TPU v7x, 32 devices: a whole 2x2x4 slice. The times are simulated.
32 devices in a mesh: blk: 8 (over z, x), head: 4 (over y, core).
Axes of the slice: x: 2, y: 2, z: 4, core: 2. Of those that a mesh axis runs over, the one named last changes fastest.
Arguments:
- tokens: bfloat16 [4096, 512], P('blk'), may hold values from -6 to 6
- gain_attn: bfloat16 [512], replicated, may hold values from 0.5 to 1.5
- gain_ffn: bfloat16 [512], replicated, may hold values from 0.5 to 1.5
- w_qkv: bfloat16 [512, 3, 512], P(None, None, 'head'), may hold values from -0.25 to 0.25
- w_out: bfloat16 [512, 512], P('head'), may hold values from -3 to 3
- w_sort: bfloat16 [512, 512], P(None, 'head'), may hold values from -0.75 to 0.75
- w_up: bfloat16 [512, 2048], P(None, 'head'), may hold values from -0.25 to 0.25
- w_down: bfloat16 [2048, 512], P('head'), may hold values from -0.125 to 0.125
- gumbel_noise: float32 [64, 8, 64], P('blk', 'head'), may hold values from -1.4 to 7, as said below
- partner: int32 [64, 8], P(None, 'head'), may hold values from 0 to 63
- cotangent: bfloat16 [4096, 512], P('blk'), may hold values from -6 to 6
Outputs:
- output: float32 [4096, 512], P('blk')
- d_tokens: float32 [4096, 512], P('blk')
- g_gain_attn: float32 [512], replicated
- g_gain_ffn: float32 [512], replicated
- g_qkv: float32 [512, 3, 512], P(None, None, 'head')
- g_out: float32 [512, 512], P('head')
- g_sort: float32 [512, 512], P(None, 'head')
- g_up: float32 [512, 2048], P(None, 'head')
- g_down: float32 [2048, 512], P('head')
Inputs may be any that keep to these rules, and one draw needn't show every extreme that they name: `gumbel_noise`: gumbel noise of scale one half: -0.5 log(-log u) for a uniform u. A partner is a block number of the sequence.
All inputs are finite; a program needn't handle non-finite values.
Results may differ from a plain program's by a relative error of at most 0.006.
The roundings to bfloat16 on the way count: a program that leaves them out, or rounds other values in their place, can miss the bound.
Values may be sent and summed in bfloat16 or wider, within the bound.
No kernel may reach another device: no remote copies, remote signals or barrier semaphores. Data moves between devices by JAX's collectives and lax.ppermute only.
A program may use at most 128 MiB of HBM per device.

v0:
```python
import jax
import jax.numpy as jnp
from jax import lax
from jax.sharding import PartitionSpec as P

D = 512
DH = 64
BLOCK = 64
SINK = 8


EPS = 1e-05
TEMPER = 0.75
ROOT_HALF = 0.7071067811865476
INV_ROOT_TWO_PI = 0.3989422804014327
HIGHEST = lax.Precision.HIGHEST


def normalize(values, norm_gain):
    average = jnp.mean(values, -1, keepdims=True)
    centred = values - average
    inv_std = lax.rsqrt(jnp.mean(centred * centred, -1, keepdims=True) + EPS)
    normed = centred * inv_std
    return (normed * norm_gain, normed, inv_std)


def norm_back(d_out, normed, inv_std, norm_gain):
    d_normed = d_out * norm_gain
    return inv_std * (
        d_normed
        - jnp.mean(d_normed, -1, keepdims=True)
        - normed * jnp.mean(d_normed * normed, -1, keepdims=True)
    )


def log_total(values, axis):
    highest = jnp.max(values, axis=axis, keepdims=True)
    return highest + jnp.log(jnp.sum(jnp.exp(values - highest), axis=axis, keepdims=True))


def balancing_log_space(sort_logits):
    for sweep in range(SINK):
        sort_logits = sort_logits - log_total(sort_logits, 2)
        sort_logits = sort_logits - log_total(sort_logits, 1)
    return sort_logits


def gelu_value(values):
    return 0.5 * values * (1.0 + lax.erf(values * ROOT_HALF))


def gelu_slope(values):
    return (
        0.5 * (1.0 + lax.erf(values * ROOT_HALF))
        + values * jnp.exp(-0.5 * values * values) * INV_ROOT_TWO_PI
    )


def local(
    tokens,
    gain_attn,
    gain_ffn,
    w_qkv,
    w_out,
    w_sort,
    w_up,
    w_down,
    gumbel_noise,
    partner,
    cotangent,
):
    f32 = jnp.float32
    bf16 = jnp.bfloat16
    tok_rows = tokens.shape[0]
    blocks_dev = tok_rows // BLOCK
    heads_dev = w_out.shape[0] // DH
    width_dev = heads_dev * DH
    requests = blocks_dev * heads_dev
    dev_count = lax.axis_size("blk")
    my_index = lax.axis_index("blk")
    first_block = my_index * blocks_dev
    seq_blocks = partner.shape[0]
    scale = DH ** (-0.5)
    gain_one = gain_attn.astype(f32)
    gain_two = gain_ffn.astype(f32)
    inputs = tokens.astype(f32)
    h_one, normed_one, inv_one = normalize(inputs, gain_one)
    h_one_low = h_one.astype(bf16)
    qkv = jnp.einsum("td,dcf->tcf", h_one_low, w_qkv, preferred_element_type=f32).astype(bf16)
    summary = jnp.mean(h_one.reshape(blocks_dev, BLOCK, D), axis=1)
    sort_mat = w_sort.astype(f32)
    own_rows = (
        jnp.dot(summary, sort_mat, precision=HIGHEST).reshape(blocks_dev, heads_dev, seq_blocks)
        + gumbel_noise
    ) / TEMPER
    every_rows = lax.all_gather(own_rows, "blk", axis=0, tiled=True)
    my_partner = lax.dynamic_slice_in_dim(partner, first_block, blocks_dev, 0)

    def own_weights(sequence_rows):
        balanced_plan = balancing_log_space(sequence_rows.transpose(1, 0, 2))
        mine = lax.dynamic_slice_in_dim(jnp.exp(balanced_plan), first_block, blocks_dev, 1)
        return seq_blocks * jnp.take_along_axis(mine, my_partner.T[:, :, None], axis=2)[:, :, 0]

    weight_hb, sink_pull = jax.vjp(own_weights, every_rows)
    weight_matrix = weight_hb.T
    owner_all = (partner // blocks_dev).reshape(dev_count, requests)
    slot_all = (
        partner % blocks_dev * heads_dev + jnp.arange(heads_dev, dtype=jnp.int32)[None, :]
    ).reshape(dev_count, requests)
    owner_mine = lax.dynamic_index_in_dim(owner_all, my_index, 0, keepdims=False)
    tile_ids = jnp.arange(requests, dtype=jnp.int32)
    key_value = (
        qkv[:, 1:3]
        .reshape(blocks_dev, BLOCK, 2, heads_dev, DH)
        .transpose(0, 3, 1, 2, 4)
        .reshape(requests, BLOCK, 2 * DH)
    )
    empty_tile = jnp.zeros((), bf16)
    wanted = owner_all == my_index
    outgoing = jnp.where(
        wanted[:, :, None, None], jnp.take(key_value, slot_all, axis=0), empty_tile
    )
    incoming = lax.all_to_all(outgoing, "blk", split_axis=0, concat_axis=0, tiled=True)
    pick = jnp.broadcast_to(owner_mine[None, :, None, None], (1,) + incoming.shape[1:])
    partner_tiles = jnp.take_along_axis(incoming, pick, axis=0)[0]
    far_tiles = partner_tiles.reshape(blocks_dev, heads_dev, BLOCK, 2, DH)
    key_far = far_tiles[:, :, :, 0]
    value_far = far_tiles[:, :, :, 1]
    query_b = qkv[:, 0].reshape(blocks_dev, BLOCK, heads_dev, DH)
    key_b = qkv[:, 1].reshape(blocks_dev, BLOCK, heads_dev, DH)
    value_b = qkv[:, 2].reshape(blocks_dev, BLOCK, heads_dev, DH)
    weight_s = weight_matrix[:, :, None, None]

    def score_parts():
        near_z = scale * jnp.einsum("bqhd,bkhd->bhqk", query_b, key_b, preferred_element_type=f32)
        far_z = scale * jnp.einsum("bqhd,bhkd->bhqk", query_b, key_far, preferred_element_type=f32)
        return (near_z, far_z, jnp.concatenate([near_z, weight_s * far_z], -1))

    near_z, far_z, scores = score_parts()
    highest = jnp.max(scores, -1, keepdims=True)
    expo = jnp.exp(scores - highest)
    row_total = jnp.sum(expo, -1, keepdims=True)
    log_sum = highest + jnp.log(row_total)
    probs_low = (expo / row_total).astype(bf16)
    near_ctx = jnp.einsum(
        "bhqk,bkhd->bqhd", probs_low[..., :BLOCK], value_b, preferred_element_type=f32
    )
    far_ctx = jnp.einsum(
        "bhqk,bhkd->bqhd", probs_low[..., BLOCK:], value_far, preferred_element_type=f32
    )
    context = near_ctx + weight_matrix[:, None, :, None] * far_ctx
    context_low = context.reshape(tok_rows, width_dev).astype(bf16)
    attn = lax.psum(jnp.dot(context_low, w_out, preferred_element_type=f32), "head")
    middle = inputs + attn
    h_two, normed_two, inv_two = normalize(middle, gain_two)
    h_two_low = h_two.astype(bf16)
    hidden_pre = jnp.dot(h_two_low, w_up, preferred_element_type=f32)
    active_low = gelu_value(hidden_pre).astype(bf16)
    ffn = lax.psum(
        jnp.dot(active_low, w_down, preferred_element_type=f32).astype(jnp.bfloat16), "head"
    ).astype(jnp.float32)
    output = middle + ffn
    g_down = jnp.einsum("tf,td->fd", active_low, cotangent, preferred_element_type=f32)
    d_active = jnp.einsum("td,fd->tf", cotangent, w_down, preferred_element_type=f32)
    d_hidden = (d_active * gelu_slope(hidden_pre)).astype(bf16)
    g_up = jnp.einsum("td,tf->df", h_two_low, d_hidden, preferred_element_type=f32)
    d_h_two = lax.psum(jnp.einsum("tf,df->td", d_hidden, w_up, preferred_element_type=f32), "head")
    g_gain_two = jnp.sum(d_h_two * normed_two, 0)
    d_middle = cotangent.astype(f32) + norm_back(d_h_two, normed_two, inv_two, gain_two)
    d_attn_low = d_middle.astype(bf16)
    g_out = jnp.einsum("tf,td->fd", context_low, d_attn_low, preferred_element_type=f32)
    d_context = jnp.einsum("td,fd->tf", d_attn_low, w_out, preferred_element_type=f32).astype(bf16)
    d_context = d_context.reshape(blocks_dev, BLOCK, heads_dev, DH)
    near_z, far_z, scores = score_parts()
    probs = jnp.exp(scores - log_sum)
    probs_low = probs.astype(bf16)
    far_ctx = jnp.einsum(
        "bhqk,bhkd->bqhd", probs_low[..., BLOCK:], value_far, preferred_element_type=f32
    )
    d_probs_near = jnp.einsum("bqhd,bkhd->bhqk", d_context, value_b, preferred_element_type=f32)
    d_probs_far = weight_s * jnp.einsum(
        "bqhd,bhkd->bhqk", d_context, value_far, preferred_element_type=f32
    )
    d_probs = jnp.concatenate([d_probs_near, d_probs_far], -1)
    d_scores = probs * (d_probs - jnp.sum(d_probs * probs, -1, keepdims=True))
    d_near = d_scores[..., :BLOCK].astype(bf16)
    d_far_raw = d_scores[..., BLOCK:]
    d_far = (weight_s * d_far_raw).astype(bf16)
    d_weight = jnp.sum(d_far_raw * far_z, (2, 3)) + jnp.sum(d_context.astype(f32) * far_ctx, (1, 3))
    d_query = scale * (
        jnp.einsum("bhqk,bkhd->bqhd", d_near, key_b, preferred_element_type=f32)
        + jnp.einsum("bhqk,bhkd->bqhd", d_far, key_far, preferred_element_type=f32)
    )
    d_key = scale * jnp.einsum("bhqk,bqhd->bkhd", d_near, query_b, preferred_element_type=f32)
    d_value = jnp.einsum(
        "bhqk,bqhd->bkhd", probs_low[..., :BLOCK], d_context, preferred_element_type=f32
    )
    d_key_far = scale * jnp.einsum("bhqk,bqhd->bhkd", d_far, query_b, preferred_element_type=f32)
    d_value_far = weight_s * jnp.einsum(
        "bhqk,bqhd->bhkd", probs_low[..., BLOCK:], d_context, preferred_element_type=f32
    )
    grad_tiles = jnp.stack([d_key_far.astype(bf16), d_value_far.astype(bf16)], 3).reshape(
        requests, BLOCK * 2 * DH
    )
    peers = jnp.arange(dev_count, dtype=jnp.int32)
    outgoing_grads = jnp.where(
        (owner_mine[None, :] == peers[:, None])[:, :, None], grad_tiles[None], empty_tile
    )
    returned = lax.all_to_all(outgoing_grads, "blk", split_axis=0, concat_axis=0, tiled=True)
    selector = (owner_all == my_index)[:, :, None] & (
        slot_all[:, :, None] == tile_ids[None, None, :]
    )
    selector = selector.reshape(dev_count * requests, requests).astype(bf16)
    remote = jnp.einsum(
        "st,sf->tf",
        selector,
        returned.reshape(dev_count * requests, BLOCK * 2 * DH),
        preferred_element_type=f32,
    )
    remote = (
        remote.reshape(blocks_dev, heads_dev, BLOCK, 2, DH)
        .transpose(0, 2, 3, 1, 4)
        .reshape(tok_rows, 2, width_dev)
    )
    near_kv = (
        jnp.stack([d_key.reshape(tok_rows, width_dev), d_value.reshape(tok_rows, width_dev)], 1)
        + remote
    )
    d_qkv = jnp.concatenate([d_query.reshape(tok_rows, 1, width_dev), near_kv], 1).astype(bf16)
    g_qkv = jnp.einsum("td,tcf->dcf", h_one_low, d_qkv, preferred_element_type=f32)
    d_h_part = jnp.einsum("tcf,dcf->td", d_qkv, w_qkv, preferred_element_type=f32)
    (d_every,) = sink_pull(d_weight.T)
    d_own = lax.psum_scatter(d_every, "blk", scatter_dimension=0, tiled=True) / TEMPER
    d_flat = d_own.reshape(blocks_dev, heads_dev * seq_blocks)
    g_sort = jnp.dot(summary.T, d_flat, precision=HIGHEST)
    d_summary = jnp.dot(d_flat, sort_mat.T, precision=HIGHEST)
    d_h_part = (d_h_part.reshape(blocks_dev, BLOCK, D) + d_summary[:, None, :] / BLOCK).reshape(
        tok_rows, D
    )
    d_h_one = lax.psum(d_h_part, "head")
    g_gain_one = jnp.sum(d_h_one * normed_one, 0)
    d_tokens = d_middle + norm_back(d_h_one, normed_one, inv_one, gain_one)
    summed = lax.psum((g_gain_one, g_gain_two, g_qkv, g_out, g_sort, g_up, g_down), "blk")
    return (
        output,
        d_tokens,
        summed[0],
        summed[1],
        summed[2],
        summed[3],
        summed[4],
        summed[5],
        summed[6],
    )


def solution(mesh):
    in_specs = (
        P("blk", None),
        P(),
        P(),
        P(None, None, "head"),
        P("head", None),
        P(None, "head"),
        P(None, "head"),
        P("head", None),
        P("blk", "head", None),
        P(None, "head"),
        P("blk", None),
    )
    out_specs = (
        P("blk", None),
        P("blk", None),
        P(),
        P(),
        P(None, None, "head"),
        P("head", None),
        P(None, "head"),
        P(None, "head"),
        P("head", None),
    )
    return jax.shard_map(local, mesh=mesh, in_specs=in_specs, out_specs=out_specs, check_vma=False)
```

profile of v0, /device:TPU:0, one launch (start us, length us, event | category | flops | bytes accessed | tf_op | source)
XLA Modules:
  0.0 2535.8 jit_solution(2149323861705759468)
XLA Ops:
  11.3 1.3 fusion.26
  12.9 1.7 convolution_convert_fusion.1
  16.7 1.6 select_select_fusion
  18.3 7.4 all-to-all-start
  28.0 1.5 eq.175
  30.8 1.3 convert_element_type.126
  32.0 1.3 copy.123
  38.1 56.0 %all_gather.3 = f32[64,2,64]{2,1,0:T(2,128)S(1)} all-gather(f32[8,2,64]{2,1,0:T(2,128)S(1)} %add_multiply_fusion), channel_id=1, replica_groups=mesh['blk'=8,'head'=4] {'blk'}, dimensions={0}, use_global_device_ids=true | all-gather | bytes 36864 | tf_op jit(solution)/shard_map/all_gather | solution.py:96
  113.1 1.8 reshape_squeeze.10
  123.6 1952.6 %gather_fusion.1 = bf16[131072]{0:T(1024)(128)(2,1)} fusion(bf16[8,16,64,128]{3,2,1,0:T(8,128)(2,1)S(1)} %all-to-all-done, s32[131072]{0:T(1024)S(1)} %bitcast.149), kind=kCustom, calls=%fused_computation.1 | custom fusion | bytes 2621440 | tf_op jit(solution)/shard_map/jit(take_along_axis)/gather | solution.py:125
  2076.2 1.2 gather.18
  2078.5 1.9 fusion.141
  2082.9 1.3 fusion.154
  2085.4 34.1 %all-reduce.9.cloned.1.call-done = f32[512,512]{1,0:T(8,128)} async-done(((f32[512,512]{1,0:T(8,128)}), f32[512,512]{1,0:T(8,128)}) %all-reduce.9.cloned.1.call-update) | async-done | bytes 1048592 | tf_op jit(solution)/shard_map/psum | solution.py:153
  2119.5 1.4 fusion.140
  2121.3 1.3 multiply_convert_fusion
  2122.5 1.4 fusion.156
  2125.5 1.4 fusion.155
  2127.2 2.3 convolution_convert_fusion
  2129.5 2.3 fusion.122
  2131.8 31.7 %all-reduce.13.cloned.1.call-done = f32[512,512]{1,0:T(8,128)} async-done(((f32[512,512]{1,0:T(8,128)}), f32[512,512]{1,0:T(8,128)}) %all-reduce.13.cloned.1.call-update) | async-done | bytes 1048592 | tf_op jit(solution)/shard_map/psum | solution.py:167
  2163.5 2.3 multiply_reduce_fusion
  2167.0 33.0 %all-reduce.11.cloned.1.call-done = bf16[512,512]{1,0:T(8,128)(2,1)} async-done(((bf16[512,512]{1,0:T(8,128)(2,1)}), bf16[512,512]{1,0:T(8,128)(2,1)}) %all-reduce.11.cloned.1.call-update) | async-done | bytes 524304 | tf_op jit(solution)/shard_map/psum | solution.py:159
  2200.0 3.0 multiply_add_fusion
  2203.4 2.0 fusion.58
  2206.3 1.3 convolution_multiply_fusion.4
  2207.6 1.6 fusion.46
  2214.3 2.0 copy.136
  2216.4 2.1 reshape.658
  2240.4 2.5 broadcast_select_fusion
  2242.9 5.7 all-to-all-start.1
  2250.6 68.9 %all-reduce = f32[64,2,64]{2,1,0:T(2,128)S(1)} all-reduce(f32[64,2,64]{2,1,0:T(2,128)S(1)} %add_bitcast_fusion.1), channel_id=2, replica_groups=mesh['blk'=8,'head'=4] {'blk'}, use_global_device_ids=true, to_apply=%region_96.97.clone | all-reduce | flops 8192 | bytes 65536
  2321.3 2.0 copy.135
  2323.3 2.0 reshape.657
  2325.4 1.2 fusion.67
  2330.6 4.1 copy.119
  2334.7 3.3 convolution_bitcast_fusion.1
  2338.9 1.4 reshape.659
  2341.7 1.4 fusion
  2343.3 1.3 fusion.76
  2345.5 1.5 fusion.41
  2347.1 31.4 %all-reduce.15.cloned.1.call-done = f32[512,512]{1,0:T(8,128)} async-done(((f32[512,512]{1,0:T(8,128)}), f32[512,512]{1,0:T(8,128)}) %all-reduce.15.cloned.1.call-update) | async-done | bytes 1048592 | tf_op jit(solution)/shard_map/psum | solution.py:240
  2378.5 1.9 fusion.25
  2380.4 22.5 all-reduce.1
  2402.9 1.4 fusion.24
  2404.3 118.1 %all-reduce.17.cloned.1.call-done = (f32[512,3,128]{2,0,1:T(8,128)}, f32[128,512]{1,0:T(8,128)}, f32[512,128]{1,0:T(8,128)}, f32[512,512]{1,0:T(8,128)}, f32[512,512]{1,0:T(8,128)}) async-done(((f32[512,3,128]{2,0,1:T(8,128)}, f32[128,512]{1,0:T(8,128)}, f32[512,128]{1,0:T(8,128)}, f32[512,512]{1,0:T(8,128)}, f32[512,512]{1,0:T(8,128)}), (f32[512,3,128]{2,0,1:T(8,128)}, f32[128,512]{1,0:T(8,128)}, ...) | async-done | bytes 3407888 | tf_op jit(solution)/shard_map/psum | solution.py:243
  2522.3 2.2 copy.178
  2524.6 1.7 copy.179
  (510 shorter events, 90.2 us)
Async XLA Ops:
  7.2 2114.0 %copy-start = (bf16[512,512]{1,0:T(8,128)(2,1)S(1)}, bf16[512,512]{1,0:T(8,128)(2,1)}, u32[]{:S(2)}) copy-start(bf16[512,512]{1,0:T(8,128)(2,1)} %param.17) | copy-start | bytes 1572868
  18.3 7.4 copy-start.114
  18.3 8.7 copy-start.1
  18.3 105.3 %all-to-all-start = ((bf16[8,16,64,128]{3,2,1,0:T(8,128)(2,1)}), bf16[8,16,64,128]{3,2,1,0:T(8,128)(2,1)S(1)}, u32[]{:S(2)}, u32[]{:S(2)}) async-start(bf16[8,16,64,128]{3,2,1,0:T(8,128)(2,1)} %select_select_fusion), calls=%async_computation | async-start | bytes 4194304 | tf_op jit(solution)/shard_map/all_to_all | solution.py:123
  25.7 2093.8 %all-reduce.9.cloned.1.call-start = ((), (), s32[]{:S(2)}) async-start(), calls=%async_computation.2 | async-start | bytes 2097152 | tf_op jit(solution)/shard_map/psum | solution.py:153
  28.0 79.0 %copy-start.76 = (f32[8,512]{1,0:T(8,128)}, f32[8,512]{1,0:T(8,128)S(1)}, u32[]{:S(2)}) copy-start(f32[8,512]{1,0:T(8,128)S(1)} %bitcast_reduce_fusion) | copy-start | bytes 49156
  98.5 14.5 copy-start.5
  100.9 12.2 copy-start.7
  103.1 11.7 copy-start.9
  105.3 9.5 copy-start.11
  107.8 10.0 copy-start.138
  109.2 10.7 copy-start.20
  2082.1 37.4 %copy-start.2 = (bf16[512,512]{1,0:T(8,128)(2,1)S(1)}, bf16[512,512]{1,0:T(8,128)(2,1)}, u32[]{:S(2)}) copy-start(bf16[512,512]{1,0:T(8,128)(2,1)} %param.11) | copy-start | bytes 1572868
  2082.9 38.0 %copy-start.31 = (bf16[512,128]{0,1:T(8,128)(2,1)}, bf16[512,128]{0,1:T(8,128)(2,1)S(1)}, u32[]{:S(2)}) copy-start(bf16[512,128]{0,1:T(8,128)(2,1)S(1)} %convert_element_type.125) | copy-start | bytes 393220
  2084.2 79.3 %all-reduce.13.cloned.1.call-start = ((), (), s32[]{:S(2)}) async-start(), calls=%async_computation.4 | async-start | bytes 2097152 | tf_op jit(solution)/shard_map/psum | solution.py:167
  2126.9 73.1 %all-reduce.11.cloned.1.call-start = ((), (), s32[]{:S(2)}) async-start(), calls=%async_computation.3 | async-start | bytes 1048576 | tf_op jit(solution)/shard_map/psum | solution.py:159
  2212.9 7.1 copy-start.21
  2212.9 11.0 copy-start.14
  2212.9 11.0 copy-start.96
  2213.4 15.9 copy-start.12
  2213.4 15.9 copy-start.94
  2216.4 16.7 copy-start.10
  2216.4 16.7 copy-start.92
  2218.4 12.0 copy-start.49
  2218.5 14.6 copy-start.71
  2218.5 14.6 copy-start.47
  2218.5 15.3 copy-start.125
  2218.5 15.3 copy-start.110
  2218.5 15.6 copy-start.69
  2218.5 15.7 copy-start.8
  2218.5 15.7 copy-start.45
  2218.5 15.7 copy-start.90
  2223.1 11.8 copy-start.123
  2223.1 11.8 copy-start.108
  2225.0 10.1 copy-start.67
  2225.1 10.2 copy-start.6
  2225.1 10.2 copy-start.43
  2225.1 10.2 copy-start.88
  2228.5 7.4 copy-start.121
  2228.5 7.4 copy-start.106
  2242.9 7.0 copy-start.61
  2242.9 7.0 copy-start.24
  2242.9 7.0 copy-start.52
  2242.9 87.7 %all-to-all-start.1 = ((bf16[8,16,8192]{2,1,0:T(8,128)(2,1)}), bf16[8,16,8192]{2,1,0:T(8,128)(2,1)}, u32[]{:S(2)}, u32[]{:S(2)}) async-start(bf16[8,16,8192]{2,1,0:T(8,128)(2,1)} %broadcast_select_fusion), calls=%async_computation.1 | async-start | bytes 4194304 | tf_op jit(solution)/shard_map/all_to_all | solution.py:209
  2248.6 129.9 %all-reduce.15.cloned.1.call-start = ((), (), s32[]{:S(2)}) async-start(), calls=%async_computation.5 | async-start | bytes 2097152 | tf_op jit(solution)/shard_map/psum | solution.py:240
  2343.2 179.2 %all-reduce.17.cloned.1.call-start = ((), (), s32[]{:S(2)}) async-start(), calls=%async_computation.6 | async-start | bytes 6815744 | tf_op jit(solution)/shard_map/psum | solution.py:243
  2347.0 33.3 %copy-start.130 = (f32[512]{0:T(512)S(1)}, f32[512]{0:T(512)}, u32[]{:S(2)}) copy-start(f32[512]{0:T(512)} %get-tuple-element.9) | copy-start | bytes 6148
  2378.5 24.4 copy-start.19
  (98 other events, 247.5 us)
Sparse Core Ops, SparseCore 0:
  2084.3 35.1 all-reduce.8
  2127.0 36.4 all-reduce.12
  2166.4 33.5 all-reduce.10
  2343.3 35.1 all-reduce.14
  2383.8 138.4 all-reduce.16
where the time goes:
time: 2540 us
  local copies, waits for them, and re-layouts  2010 us (79%)
  waiting for transfers between devices  248 us (10%)
  blocking collectives  147 us (6%)
  other arithmetic  61.9 us (2%)
  matrix products  37.2 us (1%)
    gather x2, local copies, waits for them, and re-layouts, local(): partner_tiles = jnp.take_along_axis(incoming, pick, axis=0)[0]  1950 us
    psum x1, waiting for transfers between devices, local(): lax.psum((g_gain_one, g_gain_two, g_qkv, g_out, g_sort, g_up, g_down), 'b...  118 us
    unnamed x1, blocking collectives  68.9 us
    all_gather x1, blocking collectives, local(): every_rows = lax.all_gather(own_rows, 'blk', axis=0, tiled=True)  56 us
  transfers between devices with their start and end apart: 7, of which 5 were waited for; matrix products, arithmetic and copies ran while one was open for 2% of the time, Pallas kernels for 0%

commit v1 on v0

--- a/solution.py
+++ b/solution.py
@@ -121,8 +121,7 @@
         wanted[:, :, None, None], jnp.take(key_value, slot_all, axis=0), empty_tile
     )
     incoming = lax.all_to_all(outgoing, "blk", split_axis=0, concat_axis=0, tiled=True)
-    pick = jnp.broadcast_to(owner_mine[None, :, None, None], (1,) + incoming.shape[1:])
-    partner_tiles = jnp.take_along_axis(incoming, pick, axis=0)[0]
+    partner_tiles = jnp.sum(incoming, axis=0, dtype=f32).astype(bf16)
     far_tiles = partner_tiles.reshape(blocks_dev, heads_dev, BLOCK, 2, DH)
     key_far = far_tiles[:, :, :, 0]
     value_far = far_tiles[:, :, :, 1]

time: 2540 us -> 576 us (0.23)
  local copies, waits for them, and re-layouts: 2010 us -> 45.3 us
    gather x2 -> x0, local copies, waits for them, and re-layouts: 1950 us -> none  [local(): partner_tiles = jnp.take_along_axis(incoming, pick, axis=0)[0]]
  transfers between devices with their start and end apart: 7 -> 7, of which waited for: 5 -> 5; matrix products, arithmetic and copies ran while one was open for 2% -> 7% of each run, Pallas kernels for 0% -> 0%
where the time goes in v1:
time: 576 us; the launch traced here: 572 us
  waiting for transfers between devices  248 us (43%)
  blocking collectives  158 us (27%)
  other arithmetic  55.5 us (10%)
  local copies, waits for them, and re-layouts  45.3 us (8%)
  matrix products  34.2 us (6%)
  between operations  17.2 us (3%)
  starting transfers between devices  13.5 us (2%)
    psum x1, waiting for transfers between devices, local(): lax.psum((g_gain_one, g_gain_two, g_qkv, g_out, g_sort, g_up, g_down), 'b...  118 us
    unnamed x1, blocking collectives  68.9 us
    all_gather x1, blocking collectives, local(): every_rows = lax.all_gather(own_rows, 'blk', axis=0, tiled=True)  66.2 us
    psum x1, waiting for transfers between devices, local(): lax.psum(jnp.dot(context_low, w_out, preferred_element_type=f32), 'head')  34 us
    psum x1, waiting for transfers between devices, local(): lax.psum(jnp.dot(active_low, w_down, preferred_element_type=f32).astype(j...  33 us
    psum x1, waiting for transfers between devices, local(): lax.psum(jnp.einsum('tf,df->td', d_hidden, w_up, preferred_element_type=f...  31.8 us
    psum x1, waiting for transfers between devices, local(): d_h_one = lax.psum(d_h_part, 'head')  31.5 us
    psum x1, blocking collectives, local(): lax.psum((g_gain_one, g_gain_two, g_qkv, g_out, g_sort, g_up, g_down), 'b...  22.5 us
  transfers between devices with their start and end apart: 7, of which 5 were waited for; matrix products, arithmetic and copies ran while one was open for 7% of the time, Pallas kernels for 0%

profile of v1, /device:TPU:0, one launch (start us, length us, event | category | flops | bytes accessed | tf_op | source)
XLA Modules:
  0.0 571.6 jit_solution(285192011136925193)
XLA Ops:
  9.6 1.2 convert_reduce_fusion
  10.8 1.3 fusion.26
  12.4 1.7 convolution_convert_fusion.1
  16.9 1.6 select_select_fusion
  18.5 7.4 %all-to-all-start = ((bf16[8,16,64,128]{3,2,1,0:T(8,128)(2,1)}), bf16[8,16,64,128]{3,2,1,0:T(8,128)(2,1)}, u32[]{:S(2)}, u32[]{:S(2)}) async-start(bf16[8,16,64,128]{3,2,1,0:T(8,128)(2,1)} %select_select_fusion), calls=%async_computation | async-start | bytes 4194304 | tf_op jit(solution)/shard_map/all_to_all | solution.py:123
  28.0 66.2 %all_gather.3 = f32[64,2,64]{2,1,0:T(2,128)S(1)} all-gather(f32[8,2,64]{2,1,0:T(2,128)S(1)} %add_multiply_fusion), channel_id=1, replica_groups=mesh['blk'=8,'head'=4] {'blk'}, dimensions={0}, use_global_device_ids=true | all-gather | bytes 36864 | tf_op jit(solution)/shard_map/all_gather | solution.py:96
  112.7 2.0 reduce_sum.708
  114.9 1.9 fusion.144
  117.2 2.2 fusion.134
  121.5 1.3 fusion.147
  124.1 34.0 %all-reduce.9.cloned.1.call-done = f32[512,512]{1,0:T(8,128)} async-done(((f32[512,512]{1,0:T(8,128)}), f32[512,512]{1,0:T(8,128)}) %all-reduce.9.cloned.1.call-update) | async-done | bytes 1048592 | tf_op jit(solution)/shard_map/psum | solution.py:152
  158.1 1.4 fusion.133
  159.8 1.3 multiply_convert_fusion
  161.1 1.5 fusion.149
  164.0 1.4 fusion.148
  165.8 2.3 convolution_convert_fusion
  168.0 2.3 fusion.115
  170.4 31.8 %all-reduce.13.cloned.1.call-done = f32[512,512]{1,0:T(8,128)} async-done(((f32[512,512]{1,0:T(8,128)}), f32[512,512]{1,0:T(8,128)}) %all-reduce.13.cloned.1.call-update) | async-done | bytes 1048592 | tf_op jit(solution)/shard_map/psum | solution.py:166
  202.2 2.3 multiply_reduce_fusion
  205.6 33.0 %all-reduce.11.cloned.1.call-done = bf16[512,512]{1,0:T(8,128)(2,1)} async-done(((bf16[512,512]{1,0:T(8,128)(2,1)}), bf16[512,512]{1,0:T(8,128)(2,1)}) %all-reduce.11.cloned.1.call-update) | async-done | bytes 524304 | tf_op jit(solution)/shard_map/psum | solution.py:158
  238.7 3.0 multiply_add_fusion
  243.6 2.0 fusion.51
  246.8 1.6 fusion.37
  253.5 2.0 copy.135
  255.5 2.1 reshape.610
  263.2 1.1 convert_reduce_fusion.15
  268.5 1.1 convert_reduce_fusion.13
  278.5 1.2 broadcast_in_dim.119
  279.7 2.5 broadcast_select_fusion
  282.2 5.7 all-to-all-start.1
  289.9 68.9 %all-reduce = f32[64,2,64]{2,1,0:T(2,128)S(1)} all-reduce(f32[64,2,64]{2,1,0:T(2,128)S(1)} %add_bitcast_fusion), channel_id=2, replica_groups=mesh['blk'=8,'head'=4] {'blk'}, use_global_device_ids=true, to_apply=%region_97.98.clone | all-reduce | flops 8192 | bytes 65536
  360.0 2.0 copy.134
  362.0 2.0 reshape.609
  364.3 1.5 fusion.19
  366.4 4.1 copy.120
  370.5 3.3 convolution_bitcast_fusion.1
  374.7 1.4 reshape.611
  376.1 1.2 fusion.31
  377.5 1.4 fusion
  379.0 1.3 fusion.70
  381.3 1.5 fusion.32
  382.8 31.5 %all-reduce.15.cloned.1.call-done = f32[512,512]{1,0:T(8,128)} async-done(((f32[512,512]{1,0:T(8,128)}), f32[512,512]{1,0:T(8,128)}) %all-reduce.15.cloned.1.call-update) | async-done | bytes 1048592 | tf_op jit(solution)/shard_map/psum | solution.py:239
  414.3 1.9 fusion.25
  416.2 22.5 %all-reduce.1 = (f32[512]{0:T(512)}, f32[512]{0:T(512)}) all-reduce(f32[512]{0:T(512)S(1)} %get-tuple-element.11, f32[512]{0:T(512)S(1)} %copy-done.130), channel_id=1, replica_groups=mesh['blk'=8,'head'=4] {'blk'}, use_global_device_ids=true, to_apply=%region_102.103 | all-reduce | flops 1024 | bytes 8192 | tf_op jit(solution)/shard_map/psum | solution.py:242
  438.7 1.4 fusion.24
  440.0 118.1 %all-reduce.17.cloned.1.call-done = (f32[512,3,128]{2,0,1:T(8,128)}, f32[128,512]{1,0:T(8,128)}, f32[512,128]{1,0:T(8,128)}, f32[512,512]{1,0:T(8,128)}, f32[512,512]{1,0:T(8,128)}) async-done(((f32[512,3,128]{2,0,1:T(8,128)}, f32[128,512]{1,0:T(8,128)}, f32[512,128]{1,0:T(8,128)}, f32[512,512]{1,0:T(8,128)}, f32[512,512]{1,0:T(8,128)}), (f32[512,3,128]{2,0,1:T(8,128)}, f32[128,512]{1,0:T(8,128)}, ...) | async-done | bytes 3407888 | tf_op jit(solution)/shard_map/psum | solution.py:242
  558.1 2.2 copy.183
  560.3 1.7 copy.184
  (498 shorter events, 66.3 us)
Async XLA Ops:
  7.2 152.6 %copy-start = (bf16[512,512]{1,0:T(8,128)(2,1)S(1)}, bf16[512,512]{1,0:T(8,128)(2,1)}, u32[]{:S(2)}) copy-start(bf16[512,512]{1,0:T(8,128)(2,1)} %param.17) | copy-start | bytes 1572868
  9.6 16.4 %copy-start.96 = (f32[512]{0:T(512)}, f32[512]{0:T(512)S(1)}, u32[]{:S(2)}) copy-start(f32[512]{0:T(512)S(1)} %convert_element_type.121) | copy-start | bytes 6148
  10.8 15.2 %copy-start.77 = (f32[512]{0:T(512)}, f32[512]{0:T(512)S(1)}, u32[]{:S(2)}) copy-start(f32[512]{0:T(512)S(1)} %broadcast_multiply_fusion.6) | copy-start | bytes 6148
  12.1 13.8 %copy-start.98 = (f32[512]{0:T(512)}, f32[512]{0:T(512)S(1)}, u32[]{:S(2)}) copy-start(f32[512]{0:T(512)S(1)} %add_rsqrt_fusion.1) | copy-start | bytes 6148
  18.5 7.5 %copy-start.1 = (bf16[512,512]{1,0:T(8,128)(2,1)S(1)}, bf16[512,512]{1,0:T(8,128)(2,1)}, u32[]{:S(2)}) copy-start(bf16[512,512]{1,0:T(8,128)(2,1)} %param.11) | copy-start | bytes 1572868
  18.5 8.5 %copy-start.113 = (s32[64,2]{0,1:T(2,128)S(1)}, s32[64,2]{0,1:T(2,128)}, u32[]{:S(2)}) copy-start(s32[64,2]{0,1:T(2,128)} %param.20) | copy-start | bytes 1540
  18.5 8.7 %copy-start.136 = (bf16[512]{0:T(512)(128)(2,1)S(1)}, bf16[512]{0:T(512)(128)(2,1)}, u32[]{:S(2)}) copy-start(bf16[512]{0:T(512)(128)(2,1)} %param.13) | copy-start | bytes 3076
  18.5 9.3 %copy-start.56 = (bf16[512,128]{1,0:T(8,128)(2,1)S(1)}, bf16[512,128]{1,0:T(8,128)(2,1)}, u32[]{:S(2)}) copy-start(bf16[512,128]{1,0:T(8,128)(2,1)} %param.16) | copy-start | bytes 393220
  18.5 9.5 %copy-start.129 = (f32[8,2,64]{2,1,0:T(2,128)S(1)}, f32[8,2,64]{2,1,0:T(2,128)}, u32[]{:S(2)}) copy-start(f32[8,2,64]{2,1,0:T(2,128)} %param.19) | copy-start | bytes 12292
  18.5 94.2 %all-to-all-start = ((bf16[8,16,64,128]{3,2,1,0:T(8,128)(2,1)}), bf16[8,16,64,128]{3,2,1,0:T(8,128)(2,1)}, u32[]{:S(2)}, u32[]{:S(2)}) async-start(bf16[8,16,64,128]{3,2,1,0:T(8,128)(2,1)} %select_select_fusion), calls=%async_computation | async-start | bytes 4194304 | tf_op jit(solution)/shard_map/all_to_all | solution.py:123
  25.9 132.2 %all-reduce.9.cloned.1.call-start = ((), (), s32[]{:S(2)}) async-start(), calls=%async_computation.2 | async-start | bytes 2097152 | tf_op jit(solution)/shard_map/psum | solution.py:152
  26.3 75.2 %copy-start.75 = (f32[8,512]{1,0:T(8,128)}, f32[8,512]{1,0:T(8,128)S(1)}, u32[]{:S(2)}) copy-start(f32[8,512]{1,0:T(8,128)S(1)} %bitcast_reduce_fusion) | copy-start | bytes 49156
  98.2 11.6 %copy-start.32 = (bf16[512,3,128]{2,0,1:T(8,128)(2,1)S(1)}, bf16[512,3,128]{2,0,1:T(8,128)(2,1)}, u32[]{:S(2)}) copy-start(bf16[512,3,128]{2,0,1:T(8,128)(2,1)} %copy-done.31) | copy-start | bytes 1179652
  102.5 7.4 %copy-start.46 = (f32[2,64]{0,1:T(8,128)}, f32[2,64]{0,1:T(8,128)S(1)}, u32[]{:S(2)}) copy-start(f32[2,64]{0,1:T(8,128)S(1)} %fusion.67) | copy-start | bytes 1540
  110.0 10.4 %copy-start.24 = (bf16[8,64,2,64]{3,2,1,0:T(2,128)(2,1)}, bf16[8,64,2,64]{3,2,1,0:T(2,128)(2,1)S(1)}, u32[]{:S(2)}) copy-start(bf16[8,64,2,64]{3,2,1,0:T(2,128)(2,1)S(1)} %reshape_squeeze.9) | copy-start | bytes 393220
  121.4 38.0 %copy-start.29 = (bf16[512,128]{0,1:T(8,128)(2,1)}, bf16[512,128]{0,1:T(8,128)(2,1)S(1)}, u32[]{:S(2)}) copy-start(bf16[512,128]{0,1:T(8,128)(2,1)S(1)} %convert_element_type.127) | copy-start | bytes 393220
  122.8 79.4 %all-reduce.13.cloned.1.call-start = ((), (), s32[]{:S(2)}) async-start(), calls=%async_computation.4 | async-start | bytes 2097152 | tf_op jit(solution)/shard_map/psum | solution.py:166
  165.5 73.2 %all-reduce.11.cloned.1.call-start = ((), (), s32[]{:S(2)}) async-start(), calls=%async_computation.3 | async-start | bytes 1048576 | tf_op jit(solution)/shard_map/psum | solution.py:158
  252.0 11.1 %copy-start.13 = (f32[2,64,64]{2,0,1:T(2,128)S(1)}, f32[2,64,64]{2,0,1:T(2,128)}, u32[]{:S(2)}) copy-start(f32[2,64,64]{2,0,1:T(2,128)} %copy-done.12) | copy-start | bytes 98308
  252.1 11.1 %copy-start.95 = (f32[2,64]{1,0:T(2,128)S(1)}, f32[2,64]{1,0:T(2,128)}, u32[]{:S(2)}) copy-start(f32[2,64]{1,0:T(2,128)} %copy-done.94) | copy-start | bytes 1540
  252.6 15.9 %copy-start.11 = (f32[2,64,64]{2,0,1:T(2,128)S(1)}, f32[2,64,64]{2,0,1:T(2,128)}, u32[]{:S(2)}) copy-start(f32[2,64,64]{2,0,1:T(2,128)} %copy-done.10) | copy-start | bytes 98308
  252.6 15.9 %copy-start.93 = (f32[2,64]{1,0:T(2,128)S(1)}, f32[2,64]{1,0:T(2,128)}, u32[]{:S(2)}) copy-start(f32[2,64]{1,0:T(2,128)} %copy-done.92) | copy-start | bytes 1540
  255.5 16.8 %copy-start.9 = (f32[2,64,64]{2,0,1:T(2,128)S(1)}, f32[2,64,64]{2,0,1:T(2,128)}, u32[]{:S(2)}) copy-start(f32[2,64,64]{2,0,1:T(2,128)} %copy-done.8) | copy-start | bytes 98308
  255.5 16.8 %copy-start.91 = (f32[2,64]{1,0:T(2,128)S(1)}, f32[2,64]{1,0:T(2,128)}, u32[]{:S(2)}) copy-start(f32[2,64]{1,0:T(2,128)} %copy-done.90) | copy-start | bytes 1540
  257.6 12.1 %copy-start.49 = (f32[2,64]{0,1:T(8,128)S(1)}, f32[2,64]{0,1:T(8,128)}, u32[]{:S(2)}) copy-start(f32[2,64]{0,1:T(8,128)} %copy-done.48) | copy-start | bytes 1540
  257.6 14.7 %copy-start.70 = (f32[2,64]{0,1:T(8,128)S(1)}, f32[2,64]{0,1:T(8,128)}, u32[]{:S(2)}) copy-start(f32[2,64]{0,1:T(8,128)} %copy-done.69) | copy-start | bytes 1540
  257.6 14.8 %copy-start.47 = (f32[2,64]{0,1:T(8,128)S(1)}, f32[2,64]{0,1:T(8,128)}, u32[]{:S(2)}) copy-start(f32[2,64]{0,1:T(8,128)} %copy-done.46) | copy-start | bytes 1540
  257.6 15.4 %copy-start.124 = (f32[2,64]{1,0:T(2,128)S(1)}, f32[2,64]{1,0:T(2,128)}, u32[]{:S(2)}) copy-start(f32[2,64]{1,0:T(2,128)} %copy-done.123) | copy-start | bytes 1540
  257.6 15.5 %copy-start.109 = (f32[2,64]{1,0:T(2,128)S(1)}, f32[2,64]{1,0:T(2,128)}, u32[]{:S(2)}) copy-start(f32[2,64]{1,0:T(2,128)} %copy-done.108) | copy-start | bytes 1540
  257.6 15.8 %copy-start.68 = (f32[2,64]{0,1:T(8,128)S(1)}, f32[2,64]{0,1:T(8,128)}, u32[]{:S(2)}) copy-start(f32[2,64]{0,1:T(8,128)} %copy-done.67) | copy-start | bytes 1540
  257.6 15.8 %copy-start.7 = (f32[2,64,64]{2,0,1:T(2,128)S(1)}, f32[2,64,64]{2,0,1:T(2,128)}, u32[]{:S(2)}) copy-start(f32[2,64,64]{2,0,1:T(2,128)} %copy-done.6) | copy-start | bytes 98308
  257.6 15.8 %copy-start.45 = (f32[2,64]{0,1:T(8,128)S(1)}, f32[2,64]{0,1:T(8,128)}, u32[]{:S(2)}) copy-start(f32[2,64]{0,1:T(8,128)} %copy-done.44) | copy-start | bytes 1540
  257.6 15.8 %copy-start.89 = (f32[2,64]{1,0:T(2,128)S(1)}, f32[2,64]{1,0:T(2,128)}, u32[]{:S(2)}) copy-start(f32[2,64]{1,0:T(2,128)} %copy-done.88) | copy-start | bytes 1540
  262.3 11.8 %copy-start.122 = (f32[2,64]{1,0:T(2,128)S(1)}, f32[2,64]{1,0:T(2,128)}, u32[]{:S(2)}) copy-start(f32[2,64]{1,0:T(2,128)} %copy-done.121) | copy-start | bytes 1540
  262.4 11.8 %copy-start.107 = (f32[2,64]{1,0:T(2,128)S(1)}, f32[2,64]{1,0:T(2,128)}, u32[]{:S(2)}) copy-start(f32[2,64]{1,0:T(2,128)} %copy-done.106) | copy-start | bytes 1540
  264.3 10.2 %copy-start.66 = (f32[2,64]{0,1:T(8,128)S(1)}, f32[2,64]{0,1:T(8,128)}, u32[]{:S(2)}) copy-start(f32[2,64]{0,1:T(8,128)} %copy-done.65) | copy-start | bytes 1540
  264.3 10.2 %copy-start.5 = (f32[2,64,64]{2,0,1:T(2,128)S(1)}, f32[2,64,64]{2,0,1:T(2,128)}, u32[]{:S(2)}) copy-start(f32[2,64,64]{2,0,1:T(2,128)} %copy-done.4) | copy-start | bytes 98308
  264.3 10.2 %copy-start.43 = (f32[2,64]{0,1:T(8,128)S(1)}, f32[2,64]{0,1:T(8,128)}, u32[]{:S(2)}) copy-start(f32[2,64]{0,1:T(8,128)} %copy-done.42) | copy-start | bytes 1540
  264.3 10.2 %copy-start.87 = (f32[2,64]{1,0:T(2,128)S(1)}, f32[2,64]{1,0:T(2,128)}, u32[]{:S(2)}) copy-start(f32[2,64]{1,0:T(2,128)} %copy-done.86) | copy-start | bytes 1540
  267.7 7.5 %copy-start.120 = (f32[2,64]{1,0:T(2,128)S(1)}, f32[2,64]{1,0:T(2,128)}, u32[]{:S(2)}) copy-start(f32[2,64]{1,0:T(2,128)} %copy-done.119) | copy-start | bytes 1540
  267.7 7.5 %copy-start.105 = (f32[2,64]{1,0:T(2,128)S(1)}, f32[2,64]{1,0:T(2,128)}, u32[]{:S(2)}) copy-start(f32[2,64]{1,0:T(2,128)} %copy-done.104) | copy-start | bytes 1540
  282.2 84.2 %all-to-all-start.1 = ((bf16[8,16,8192]{2,1,0:T(8,128)(2,1)}), bf16[8,16,8192]{2,1,0:T(8,128)(2,1)}, u32[]{:S(2)}, u32[]{:S(2)}) async-start(bf16[8,16,8192]{2,1,0:T(8,128)(2,1)} %broadcast_select_fusion), calls=%async_computation.1 | async-start | bytes 4194304 | tf_op jit(solution)/shard_map/all_to_all | solution.py:208
  287.9 126.4 %all-reduce.15.cloned.1.call-start = ((), (), s32[]{:S(2)}) async-start(), calls=%async_computation.5 | async-start | bytes 2097152 | tf_op jit(solution)/shard_map/psum | solution.py:239
  289.0 75.0 %copy-start.21 = (bf16[8,64,2,64]{1,3,2,0:T(8,128)(2,1)S(1)}, bf16[8,64,2,64]{1,3,2,0:T(8,128)(2,1)}, u32[]{:S(2)}) copy-start(bf16[8,64,2,64]{1,3,2,0:T(8,128)(2,1)} %copy-done.20) | copy-start | bytes 393220
  358.9 7.3 %copy-start.80 = (f32[8,128]{1,0:T(8,128)}, f32[8,128]{1,0:T(8,128)S(1)}, u32[]{:S(2)}) copy-start(f32[8,128]{1,0:T(8,128)S(1)} %reshape.583) | copy-start | bytes 12292
  378.9 179.2 %all-reduce.17.cloned.1.call-start = ((), (), s32[]{:S(2)}) async-start(), calls=%async_computation.6 | async-start | bytes 6815744 | tf_op jit(solution)/shard_map/psum | solution.py:242
  382.8 33.4 %copy-start.130 = (f32[512]{0:T(512)S(1)}, f32[512]{0:T(512)}, u32[]{:S(2)}) copy-start(f32[512]{0:T(512)} %get-tuple-element.9) | copy-start | bytes 6148
  414.3 24.4 %copy-start.15 = (f32[512,512]{1,0:T(8,128)S(1)}, f32[512,512]{1,0:T(8,128)}, u32[]{:S(2)}) copy-start(f32[512,512]{1,0:T(8,128)} %all-reduce.15.cloned.1.call-done) | copy-start | bytes 3145732
  (97 other events, 275.5 us)
Sparse Core Ops, SparseCore 0:
  122.9 35.1 all-reduce.8
  165.6 36.4 all-reduce.12
  205.1 33.5 all-reduce.10
  379.1 35.1 all-reduce.14
  419.6 138.4 all-reduce.16

commit v2 on v1

--- a/solution.py
+++ b/solution.py
@@ -1,6 +1,11 @@
+import functools
+import math
+
 import jax
 import jax.numpy as jnp
 from jax import lax
+from jax.experimental import pallas as pl
+from jax.experimental.pallas import tpu as pltpu
 from jax.sharding import PartitionSpec as P
 
 D = 512
@@ -14,6 +19,7 @@
 ROOT_HALF = 0.7071067811865476
 INV_ROOT_TWO_PI = 0.3989422804014327
 HIGHEST = lax.Precision.HIGHEST
+VMEM_LIMIT = 48 * 1024 * 1024
 
 
 def normalize(values, norm_gain):
@@ -253,6 +259,647 @@
     )
 
 
+def mask_pair(values, near):
+    zero = jnp.zeros_like(values)
+    return jnp.where(near, values, zero), jnp.where(near, zero, values)
+
+
+def first_lanes():
+    return lax.broadcasted_iota(jnp.int32, (1, 2 * DH), 1) < DH
+
+
+def dot_nn(a, b):
+    return lax.dot_general(a, b, (((1,), (0,)), ((), ())), preferred_element_type=jnp.float32)
+
+
+def dot_nt(a, b):
+    return lax.dot_general(a, b, (((1,), (1,)), ((), ())), preferred_element_type=jnp.float32)
+
+
+def dot_tn(a, b):
+    return lax.dot_general(a, b, (((0,), (0,)), ((), ())), preferred_element_type=jnp.float32)
+
+
+def three_parts(values):
+    high = values.astype(jnp.bfloat16)
+    rest = values - high.astype(jnp.float32)
+    mid = rest.astype(jnp.bfloat16)
+    low = (rest - mid.astype(jnp.float32)).astype(jnp.bfloat16)
+    return high, mid, low
+
+
+def norm_parts(values):
+    centred = values - jnp.mean(values, -1, keepdims=True)
+    inv_std = lax.rsqrt(jnp.mean(centred * centred, -1, keepdims=True) + EPS)
+    return centred * inv_std, inv_std
+
+
+def head_kernel(tokens, gain, noise, h_one, payload):
+    f32 = jnp.float32
+    rows = tokens.shape[0]
+    normed, _ = norm_parts(tokens[...].astype(f32))
+    h = normed * gain[...].astype(f32)
+    h_one[...] = h.astype(jnp.bfloat16)
+    payload[:, :D] = jnp.mean(h.reshape(rows // BLOCK, BLOCK, D), axis=1)
+    nb = noise.shape[2]
+    payload[:, D : D + nb] = noise[:, 0, :]
+    payload[:, D + nb :] = noise[:, 1, :]
+
+
+def project_kernel(*refs):
+    *pieces, weight, out = refs
+    at = 0
+    for piece in pieces:
+        for start in range(0, piece.shape[0], 2 * BLOCK):
+            rows = piece[start : start + 2 * BLOCK, :]
+            out[at : at + 2 * BLOCK, :] = dot_nn(rows, weight[...]).astype(jnp.bfloat16)
+            at += 2 * BLOCK
+
+
+def sink_kernel(near_rows, far_rows, w_sort, partner, summary, steps, scale_rows, weight_rows):
+    f32 = jnp.float32
+    me = lax.axis_index("blk")
+    nb = partner.shape[0]
+    per = near_rows.shape[0] // 4
+    noise = weight_rows
+    for j in range(8):
+        source = near_rows if j < 4 else far_rows
+        piece = source[(j % 4) * per : (j % 4 + 1) * per, :]
+        distance = (0, 1, 2, 3, 4, 5, 6, 7)[j]
+        at = pl.multiple_of((me ^ distance) * per, per)
+        summary[pl.ds(at, per), :] = piece[:, :D]
+        noise[pl.ds(at, per), :] = piece[:, D:]
+    parts = three_parts(summary[...])
+    logits = sum(dot_nn(part, w_sort[...]) for part in parts[::-1])
+    logits = (logits + noise[...]) / TEMPER
+    plan = jnp.stack([logits[:, :nb], logits[:, nb:]])
+    for sweep in range(SINK):
+        for k, axis in enumerate((2, 1)):
+            plan = plan - log_total(plan, axis)
+            steps[2 * sweep + k] = jnp.exp(plan)
+    final = jnp.exp(plan)
+    lanes = lax.broadcasted_iota(jnp.int32, (nb, nb), 1)
+    picked = []
+    for h in range(2):
+        chosen = partner[:, h : h + 1] == lanes
+        picked.append(
+            nb * jnp.sum(jnp.where(chosen, final[h], 0.0), axis=1, keepdims=True)
+        )
+    ones = jnp.ones((nb, DH), f32)
+    scale_rows[...] = jnp.concatenate([ones, picked[0] * ones, ones, picked[1] * ones], 1)
+    weight_rows[...] = jnp.concatenate([picked[0] * ones, picked[1] * ones], 1)
+
+
+def ring_of(position):
+    return jnp.where(position < 4, 2 * position, 2 * (7 - position) + 1)
+
+
+def place_of(index):
+    return jnp.where(index % 2 == 0, index // 2, 7 - index // 2)
+
+
+def spread(pieces, full, span, core):
+    place = place_of(lax.axis_index("blk"))
+    for start, rows, ref, ref_start, step in pieces:
+        owner = ring_of((place - step + 8) % 8)
+        at = pl.multiple_of(owner * span + start, rows)
+        full[pl.ds(at, rows), :] = ref[ref_start : ref_start + rows, :]
+
+
+def far_near(table, at, lanes):
+    return table[pl.ds(pl.multiple_of(at * BLOCK, BLOCK), BLOCK), lanes]
+
+
+def block_operands(qkv, block, first, second, near):
+    k_lanes, v_lanes = slice(2 * DH, 4 * DH), slice(4 * DH, 6 * DH)
+    query = far_near(qkv, block, slice(0, 2 * DH))
+    keys, values = [], []
+    for lanes, store in ((k_lanes, keys), (v_lanes, values)):
+        own0, own1 = mask_pair(far_near(qkv, block, lanes), near)
+        far0, _ = mask_pair(far_near(qkv, first, lanes), near)
+        _, far1 = mask_pair(far_near(qkv, second, lanes), near)
+        store.extend([own0, far0, own1, far1])
+    return query, keys, values
+
+
+def block_probs(query, keys, scale_row):
+    z = dot_nt(query, jnp.concatenate(keys, 0)) * (DH**-0.5)
+    scores = z * scale_row
+    probs = []
+    for h in range(2):
+        part = scores[:, h * 2 * DH : (h + 1) * 2 * DH]
+        expo = jnp.exp(part - jnp.max(part, -1, keepdims=True))
+        probs.append(expo / jnp.sum(expo, -1, keepdims=True))
+    return z, probs
+
+
+def attend_kernel(own, step1, step2, step3, step4, partner, scale_rows, weight_rows, qkv, context):
+    me = lax.axis_index("blk")
+    core = lax.axis_index("head") % 2
+    place = place_of(me)
+    rows = own.shape[0]
+    half = rows // 2
+    quarter = rows // 4
+
+    def put(owner, start, n, ref, ref_start):
+        at = pl.multiple_of(owner * rows + start, n)
+        qkv[pl.ds(at, n), :] = ref[ref_start : ref_start + n, :]
+
+    put(me, 0, rows, own, 0)
+    for step, ref in ((1, step1), (2, step2), (3, step3)):
+        for side, owner in enumerate(
+            (ring_of((place + 8 - step) % 8), ring_of((place + step) % 8))
+        ):
+            put(owner, core * half, half, ref, side * 2 * half)
+            put(owner, (1 - core) * half, half, ref, side * 2 * half + half)
+    owner = ring_of((place + 4) % 8)
+    put(owner, core * half, quarter, step4, 0)
+    put(owner, (1 - core) * half, quarter, step4, quarter)
+    put(owner, core * half + quarter, quarter, step4, 2 * quarter)
+    put(owner, (1 - core) * half + quarter, quarter, step4, 3 * quarter)
+    near = first_lanes()
+    for i in range(rows // BLOCK):
+        block = me * (rows // BLOCK) + i
+        query, keys, values = block_operands(
+            qkv, block, partner[block, 0], partner[block, 1], near
+        )
+        scale_row = scale_rows[pl.ds(block, 1), :]
+        weight_row = weight_rows[pl.ds(block, 1), :]
+        _, probs = block_probs(query, keys, scale_row)
+        probs_low = jnp.concatenate([p.astype(jnp.bfloat16) for p in probs], 1)
+        none = jnp.zeros_like(values[0])
+        table = jnp.concatenate(
+            [
+                jnp.concatenate([values[0], none, values[2], none], 0),
+                jnp.concatenate([none, values[1], none, values[3]], 0),
+            ],
+            1,
+        )
+        out = dot_nn(probs_low, table)
+        ctx = out[:, : 2 * DH] + weight_row * out[:, 2 * DH :]
+        context[i * BLOCK : (i + 1) * BLOCK, :] = ctx.astype(jnp.bfloat16)
+
+
+def feed_kernel(
+    tokens, cotangent, gain, ctx0, ctx1, ctx2, ctx3, wo0, wo1, wo2, wo3, up_a, up_b, down_a, down_b,
+    middle, h_two, active, d_hidden, ffn, d_h_two,
+    ctx_full, wo_full, up_full, down_full,
+):
+    f32, bf16 = jnp.float32, jnp.bfloat16
+    hd = lax.axis_index("head")
+    row = hd // 2
+    width = ctx0.shape[1]
+    ff = up_a.shape[1]
+    for j, (c, w) in enumerate(((ctx0, wo0), (ctx1, wo1), (ctx2, wo2), (ctx3, wo3))):
+        at = pl.multiple_of((hd ^ j) * width, width)
+        ctx_full[:, pl.ds(at, width)] = c[...]
+        wo_full[pl.ds(at, width), :] = w[...]
+    for j, (u, w) in enumerate(((up_a, down_a), (up_b, down_b))):
+        at = pl.multiple_of((row ^ j) * ff, ff)
+        up_full[:, pl.ds(at, ff)] = u[...]
+        down_full[pl.ds(at, ff), :] = w[...]
+    chunk = 256
+    for start in range(0, tokens.shape[0], chunk):
+        sl = slice(start, start + chunk)
+        mid = tokens[sl, :].astype(f32) + dot_nn(ctx_full[sl, :], wo_full[...])
+        middle[sl, :] = mid
+        normed, _ = norm_parts(mid)
+        low = (normed * gain[...].astype(f32)).astype(bf16)
+        h_two[sl, :] = low
+        ffn_sum = None
+        back_sum = None
+        for j in range(2):
+            cols = slice(j * ff, (j + 1) * ff)
+            pre = dot_nn(low, up_full[:, cols])
+            d_act = dot_nt(cotangent[sl, :], down_full[cols, :])
+            bell = 0.5 * (1.0 + lax.erf(pre * ROOT_HALF))
+            act = (pre * bell).astype(bf16)
+            slope = bell + pre * jnp.exp(-0.5 * pre * pre) * INV_ROOT_TWO_PI
+            d_pre = (d_act * slope).astype(bf16)
+
+            @pl.when(row == j)
+            def _():
+                active[sl, :] = act
+                d_hidden[sl, :] = d_pre
+
+            f = dot_nn(act, down_full[cols, :])
+            b = dot_nt(d_pre, up_full[:, cols])
+            ffn_sum = f if ffn_sum is None else ffn_sum + f
+            back_sum = b if back_sum is None else back_sum + b
+        ffn[sl, :] = ffn_sum
+        d_h_two[sl, :] = back_sum
+
+
+def back_kernel(middle, own, other, cotangent, gain, w_out, d_middle, d_low, d_ctx, g_gain):
+    f32, bf16 = jnp.float32, jnp.bfloat16
+    normed, inv = norm_parts(middle[...])
+    d_h = own[...] + other[...]
+    g_gain[...] = jnp.broadcast_to(jnp.sum(d_h * normed, 0, keepdims=True), g_gain.shape)
+    d_mid = cotangent[...].astype(f32) + norm_back(d_h, normed, inv, gain[...].astype(f32))
+    d_middle[...] = d_mid
+    low = d_mid.astype(bf16)
+    d_low[...] = low
+    d_ctx[...] = dot_nt(low, w_out[...]).astype(bf16)
+
+
+def grads_kernel(h_two, d_hidden, active, cotangent, context, d_low, keep, send, total):
+    f = h_two.shape[1]
+    total[:f, :] = dot_tn(h_two[...], d_hidden[...])
+    ff = active.shape[1]
+    total[f : f + ff, :] = dot_tn(active[...], cotangent[...])
+    total[f + ff :, :] = dot_tn(context[...], d_low[...])
+    bit = lax.axis_index("blk") & 1
+    half = keep.shape[0]
+    keep[...] = total[pl.ds(pl.multiple_of(bit * half, 16), half), :]
+    send[...] = total[pl.ds(pl.multiple_of((1 - bit) * half, 16), half), :].astype(jnp.bfloat16)
+
+
+def merge_kernel(shift, held, arrived, keep, send, total):
+    total[...] = held[...] + arrived[...].astype(jnp.float32)
+    bit = (lax.axis_index("blk") >> shift) & 1
+    half = keep.shape[0]
+    keep[...] = total[pl.ds(pl.multiple_of(bit * half, 16), half), :]
+    send[...] = total[pl.ds(pl.multiple_of((1 - bit) * half, 16), half), :].astype(jnp.bfloat16)
+
+
+def lay_kernel(here, there, g_up, g_down, g_out, total):
+    me = lax.axis_index("blk")
+    n = here.shape[0] // 4
+    for j in range(8):
+        ref = here if j < 4 else there
+        source = me ^ ((0, 4, 2, 6)[j % 4] + j // 4)
+        at = (source & 1) * (4 * n) + ((source >> 1) & 1) * (2 * n) + (source >> 2) * n
+        total[pl.ds(pl.multiple_of(at, 16), n), :] = ref[(j % 4) * n : (j % 4 + 1) * n, :]
+    f = g_up.shape[0]
+    ff = g_down.shape[0]
+    g_up[...] = total[:f, :].astype(jnp.float32)
+    g_down[...] = total[f : f + ff, :].astype(jnp.float32)
+    g_out[...] = total[f + ff :, :].astype(jnp.float32)
+
+
+def pull_kernel(
+    qkv, own, f1, b1, f2, b2, f3, b3, f4, b4, partner, scale_rows, weight_rows,
+    d_qkv, d_weight, d_ctx, acc_k, acc_v,
+):
+    f32, bf16 = jnp.float32, jnp.bfloat16
+    me = lax.axis_index("blk")
+    place = place_of(me)
+    rows = own.shape[0]
+    half = rows // 2
+
+    def put(owner, start, ref):
+        n = ref.shape[0]
+        d_ctx[pl.ds(pl.multiple_of(owner * rows + start, n), n), :] = ref[...]
+
+    put(me, 0, own)
+    for step, (f, b) in enumerate(((f1, b1), (f2, b2), (f3, b3)), 1):
+        put(ring_of((place + 8 - step) % 8), 0, f)
+        put(ring_of((place + step) % 8), 0, b)
+    far = ring_of((place + 4) % 8)
+    put(far, 0, f4)
+    put(far, half, b4)
+    near = first_lanes()
+    acc_k[...] = jnp.zeros_like(acc_k)
+    acc_v[...] = jnp.zeros_like(acc_v)
+    scale = DH**-0.5
+
+    def add(acc, at, tile):
+        place_at = pl.ds(pl.multiple_of(at * BLOCK, BLOCK), BLOCK)
+        acc[place_at, :] += tile
+
+    def one(block):
+        first, second = partner[block, 0], partner[block, 1]
+        query, keys, values = block_operands(qkv, block, first, second, near)
+        scale_row = scale_rows[pl.ds(block, 1), :]
+        weight_row = weight_rows[pl.ds(block, 1), :]
+        z, probs = block_probs(query, keys, scale_row)
+        probs = jnp.concatenate(probs, 1)
+        probs_low = probs.astype(bf16)
+        d_out = far_near(d_ctx, block, slice(0, 2 * DH))
+        d_raw = dot_nt(d_out, jnp.concatenate(values, 0))
+        d_probs = d_raw * scale_row
+        weighted = d_probs * probs
+        sums = [
+            jnp.sum(weighted[:, h * 2 * DH : (h + 1) * 2 * DH], -1, keepdims=True) for h in range(2)
+        ]
+        spread_sums = jnp.concatenate([jnp.broadcast_to(s, (BLOCK, 2 * DH)) for s in sums], 1)
+        d_scores = probs * (d_probs - spread_sums)
+        d_z = (d_scores * scale_row).astype(bf16)
+        d_weight[pl.ds(block, 1), :] = jnp.sum(
+            d_scores * z + probs_low.astype(f32) * d_raw, 0, keepdims=True
+        )
+        d_query = dot_nn(d_z, jnp.concatenate(keys, 0)) * scale
+        at = pl.ds(pl.multiple_of(block * BLOCK, BLOCK), BLOCK)
+        d_qkv[at, : 2 * DH] = d_query.astype(bf16)
+        d_keys = dot_tn(d_z, query) * scale
+        d_values = dot_tn(probs_low, d_out)
+        for acc, grads, far_scale in ((acc_k, d_keys, None), (acc_v, d_values, weight_row)):
+            parts = [grads[i * BLOCK : (i + 1) * BLOCK, :] for i in range(4)]
+            far0, far1 = parts[1], parts[3]
+            if far_scale is not None:
+                far0, far1 = far0 * far_scale, far1 * far_scale
+            far0 = far0.astype(bf16).astype(f32)
+            far1 = far1.astype(bf16).astype(f32)
+            add(acc, block, jnp.where(near, parts[0], parts[2]))
+            add(acc, first, jnp.where(near, far0, 0.0))
+            add(acc, second, jnp.where(near, 0.0, far1))
+
+    def body(i, _):
+        one(i)
+        return 0
+
+    lax.fori_loop(0, partner.shape[0], body, 0, unroll=2)
+    d_qkv[:, 2 * DH : 4 * DH] = acc_k[...].astype(bf16)
+    d_qkv[:, 4 * DH :] = acc_v[...].astype(bf16)
+
+
+def sink_back_kernel(d_weight, steps, partner, summary, d_flat, g_sort):
+    nb = partner.shape[0]
+    lanes = lax.broadcasted_iota(jnp.int32, (nb, nb), 1)
+    grads = []
+    for h in range(2):
+        chosen = partner[:, h : h + 1] == lanes
+        total = jnp.sum(
+            d_weight[:, (2 * h + 1) * DH : (2 * h + 2) * DH], axis=1, keepdims=True
+        )
+        grads.append(jnp.where(chosen, nb * total, 0.0))
+    last = steps.shape[0] - 1
+    grad = jnp.stack(grads) * steps[last]
+    for t in range(last, -1, -1):
+        grad = grad - steps[t] * jnp.sum(grad, axis=1 if t % 2 else 2, keepdims=True)
+    flat = jnp.concatenate([grad[0], grad[1]], 1) / TEMPER
+    d_flat[...] = flat
+    g_sort[...] = lax.dot_general(
+        summary[...],
+        flat,
+        (((0,), (0,)), ((), ())),
+        precision=HIGHEST,
+        preferred_element_type=jnp.float32,
+    )
+
+
+def weight_kernel(*refs):
+    own, f1, b1, f2, b2, f3, b3, f4, b4, xf1, xb1, xf2, xb2, xf3, xb3, xf4, xb4 = refs[:17]
+    d_qkv, g_qkv, h_all = refs[17:]
+    me = lax.axis_index("blk")
+    core = lax.axis_index("head") % 2
+    place = place_of(me)
+    rows = own.shape[0]
+    half, quarter = rows // 2, rows // 4
+
+    def put(owner, start, ref):
+        n = ref.shape[0]
+        h_all[pl.ds(pl.multiple_of(owner * rows + start, n), n), :] = ref[...]
+
+    put(me, 0, own)
+    for step, (f, b, xf, xb) in enumerate(
+        ((f1, b1, xf1, xb1), (f2, b2, xf2, xb2), (f3, b3, xf3, xb3)), 1
+    ):
+        for owner, a, o in (
+            (ring_of((place + 8 - step) % 8), f, xf),
+            (ring_of((place + step) % 8), b, xb),
+        ):
+            put(owner, core * half, a)
+            put(owner, (1 - core) * half, o)
+    far = ring_of((place + 4) % 8)
+    put(far, core * half, f4)
+    put(far, (1 - core) * half, xf4)
+    put(far, core * half + quarter, b4)
+    put(far, (1 - core) * half + quarter, xb4)
+    out = dot_tn(h_all[...], d_qkv[...])
+    width = g_qkv.shape[2]
+    for i in range(3):
+        g_qkv[:, i, :] = out[:, i * width : (i + 1) * width]
+
+
+def input_kernel(dq_a, dq_b, w_a, w_b, flat_a, flat_b, sort_a, sort_b, d_h, dq_full, w_full, flat_full, sort_full):
+    row = lax.axis_index("head") // 2
+    width = dq_a.shape[1]
+    for j, (g, w) in enumerate(((dq_a, w_a), (dq_b, w_b))):
+        at = pl.multiple_of((row ^ j) * width, width)
+        dq_full[:, pl.ds(at, width)] = g[...]
+        w_full[:, pl.ds(at, width)] = w[...]
+    part = dot_nt(dq_full[...], w_full[...])
+    nb = flat_a.shape[1]
+    for j, (flat, sort) in enumerate(((flat_a, sort_a), (flat_b, sort_b))):
+        at = pl.multiple_of((row ^ j) * nb, nb)
+        flat_full[:, pl.ds(at, nb)] = flat[...]
+        sort_full[:, pl.ds(at, nb)] = sort[...]
+    d_sum = sum(dot_nt(p, sort_full[...]) for p in three_parts(flat_full[...])[::-1]) / BLOCK
+    blocks = d_sum.shape[0]
+    for i in range(blocks):
+        sl = slice(i * BLOCK, (i + 1) * BLOCK)
+        d_h[sl, :] = part[sl, :] + d_sum[i : i + 1, :]
+
+
+def end_kernel(tokens, gain, own, other, d_middle, d_tokens, g_gain):
+    f32 = jnp.float32
+    normed, inv = norm_parts(tokens[...].astype(f32))
+    d_h = own[...] + other[...]
+    g_gain[...] = jnp.broadcast_to(jnp.sum(d_h * normed, 0, keepdims=True), g_gain.shape)
+    d_tokens[...] = d_middle[...] + norm_back(d_h, normed, inv, gain[...].astype(f32))
+
+
+VMEM_SPEC = pl.BlockSpec(memory_space=pltpu.VMEM)
+SMEM_SPEC = pl.BlockSpec(memory_space=pltpu.SMEM)
+
+
+def call(kernel, outs, *args, scratch=(), smem=(), flops=0, name=None):
+    shapes = [jax.ShapeDtypeStruct(s, d) for s, d in outs]
+    moved = sum(a.size * a.dtype.itemsize for a in args) + sum(
+        math.prod(s) * jnp.dtype(d).itemsize for s, d in outs
+    )
+    result = pl.pallas_call(
+        kernel,
+        out_shape=shapes,
+        in_specs=[SMEM_SPEC if i in smem else VMEM_SPEC for i in range(len(args))],
+        out_specs=[VMEM_SPEC] * len(shapes),
+        scratch_shapes=[pltpu.VMEM(s, d) for s, d in scratch],
+        compiler_params=pltpu.CompilerParams(vmem_limit_bytes=VMEM_LIMIT),
+
+        name=name,
+    )(*args)
+    return result[0] if len(shapes) == 1 else result
+
+
+RING = (0, 2, 4, 6, 7, 5, 3, 1)
+
+
+def local_eight(
+    tokens, gain_attn, gain_ffn, w_qkv, w_out, w_sort, w_up, w_down, gumbel_noise, partner, cotangent
+):
+    f32, bf16 = jnp.float32, jnp.bfloat16
+    rows = tokens.shape[0]
+    blocks = rows // BLOCK
+    width = w_out.shape[0]
+    ff = w_up.shape[1]
+    nb = partner.shape[0]
+    total = nb * BLOCK
+    half, quarter = rows // 2, rows // 4
+    core = lax.axis_index("head") % 2
+
+    def ahead(v):
+        return lax.ppermute(v, "blk", [(RING[i], RING[(i + 1) % 8]) for i in range(8)])
+
+    def behind(v):
+        return lax.ppermute(v, "blk", [(RING[i], RING[(i - 1) % 8]) for i in range(8)])
+
+    def swap_head(v, j):
+        return lax.ppermute(v, "head", [(i, i ^ j) for i in range(4)])
+
+    def swap_blk(v, j):
+        return lax.ppermute(v, "blk", [(i, i ^ j) for i in range(8)])
+
+    gain_one = gain_attn.reshape(1, D)
+    gain_two = gain_ffn.reshape(1, D)
+    w_in = w_qkv.reshape(D, 3 * width)
+
+    h_one, payload = call(
+        head_kernel, [((rows, D), bf16), ((blocks, D + 2 * nb), f32)], tokens, gain_one, gumbel_noise,
+        name="norm_one",
+    )
+    mine = lax.dynamic_slice_in_dim(h_one, core * half, half, 0)
+    ring_f, ring_b = [mine], [mine]
+    for step in range(3):
+        ring_f.append(ahead(ring_f[-1]))
+        ring_b.append(behind(ring_b[-1]))
+    ring_f.append(ahead(ring_f[-1][:quarter]))
+    ring_b.append(behind(ring_b[-1][quarter:]))
+    ring_f, ring_b = ring_f[1:], ring_b[1:]
+    other_f = [swap_head(v, 1) for v in ring_f]
+    other_b = [swap_head(v, 1) for v in ring_b]
+
+    pay = jnp.concatenate([payload, swap_blk(payload, 1)], 0)
+    pay = jnp.concatenate([pay, swap_blk(pay, 2)], 0)
+    pay_far = swap_blk(pay, 4)
+
+    wo_y = swap_head(w_out, 2)
+    wo_c = swap_head(w_out, 1)
+    wo_yc = swap_head(wo_y, 1)
+    up_y = swap_head(w_up, 2)
+    down_y = swap_head(w_down, 2)
+    in_y = swap_head(w_in, 2)
+    sort_y = swap_head(w_sort, 2)
+
+    project = lambda *v: call(
+        project_kernel, [((sum(x.shape[0] for x in v), 3 * width), bf16)], *v, w_in, name="project",
+        flops=2 * sum(x.shape[0] for x in v) * 3 * width * D,
+    )
+    qkv_own = project(h_one)
+    qkv_steps = [
+        project(ring_f[s], other_f[s], ring_b[s], other_b[s]) for s in range(4)
+    ]
+    summary, steps, scale_rows, weight_rows = call(
+        sink_kernel,
+        [
+            ((nb, D), f32),
+            ((2 * SINK, 2, nb, nb), f32),
+            ((nb, 4 * DH), f32),
+            ((nb, 2 * DH), f32),
+        ],
+        pay, pay_far, w_sort, partner, name="sinkhorn",
+    )
+    qkv, context = call(
+        attend_kernel,
+        [((total, 3 * width), bf16), ((rows, width), bf16)],
+        qkv_own, *qkv_steps, partner, scale_rows, weight_rows, smem=(5,), name="attend",
+    )
+    ctx_y = swap_head(context, 2)
+    ctx_c = swap_head(context, 1)
+    ctx_yc = swap_head(ctx_y, 1)
+    middle, h_two, active, d_hidden, ffn, d_h_two = call(
+        feed_kernel,
+        [
+            ((rows, D), f32),
+            ((rows, D), bf16),
+            ((rows, ff), bf16),
+            ((rows, ff), bf16),
+            ((rows, D), f32),
+            ((rows, D), f32),
+        ],
+        tokens, cotangent, gain_two, context, ctx_c, ctx_y, ctx_yc, w_out, wo_c, wo_y, wo_yc,
+        w_up, up_y, w_down, down_y,
+        scratch=[((rows, 4 * width), bf16), ((4 * width, D), bf16), ((D, 2 * ff), bf16), ((2 * ff, D), bf16)],
+        name="feed", flops=18 * rows * D * ff,
+    )
+    d_h_two_other = swap_head(d_h_two, 1)
+    ffn_other = swap_head(ffn, 1)
+    d_middle, d_low, d_ctx, g_two = call(
+        back_kernel,
+        [((rows, D), f32), ((rows, D), bf16), ((rows, width), bf16), ((8, D), f32)],
+        middle, d_h_two, d_h_two_other, cotangent, gain_two, w_out, name="back",
+    )
+    out_f, out_b = [d_ctx], [d_ctx]
+    for step in range(3):
+        out_f.append(ahead(out_f[-1]))
+        out_b.append(behind(out_b[-1]))
+    out_f.append(ahead(out_f[-1][:half]))
+    out_b.append(behind(out_b[-1][half:]))
+    stack = D + ff + width
+    keep, send = call(
+        grads_kernel,
+        [((stack // 2, D), f32), ((stack // 2, D), bf16)],
+        h_two, d_hidden, active, cotangent, context, d_low,
+        scratch=[((stack, D), f32)], name="grads", flops=2 * rows * D * stack,
+    )
+    for shift in (1, 2):
+        n = keep.shape[0]
+        keep, send = call(
+            functools.partial(merge_kernel, shift),
+            [((n // 2, D), f32), ((n // 2, D), bf16)],
+            keep, swap_blk(send, 1 << (shift - 1)), scratch=[((n, D), f32)], name="merge",
+        )
+    owned = (keep + swap_blk(send, 4).astype(f32)).astype(bf16)
+    owned = jnp.concatenate([owned, swap_blk(owned, 4)], 0)
+    owned = jnp.concatenate([owned, swap_blk(owned, 2)], 0)
+    g_up, g_down, g_out = call(
+        lay_kernel,
+        [((D, ff), f32), ((ff, D), f32), ((width, D), f32)],
+        owned, swap_blk(owned, 1), scratch=[((stack, D), bf16)], name="lay",
+    )
+    output = middle + (ffn + ffn_other)
+    d_qkv, d_weight = call(
+        pull_kernel,
+        [((total, 3 * width), bf16), ((nb, 4 * DH), f32)],
+        qkv, d_ctx, out_f[1], out_b[1], out_f[2], out_b[2], out_f[3], out_b[3], out_f[4], out_b[4],
+        partner, scale_rows, weight_rows, smem=(10,),
+        scratch=[((total, width), bf16), ((total, width), f32), ((total, width), f32)],
+        name="pull",
+    )
+    d_flat, g_sort = call(
+        sink_back_kernel,
+        [((nb, 2 * nb), f32), ((D, 2 * nb), f32)],
+        d_weight, steps, partner, summary, name="sinkhorn_back",
+    )
+    me = lax.axis_index("blk")
+    d_mine = lax.dynamic_slice_in_dim(d_qkv, me * rows, rows, 0)
+    flat_mine = lax.dynamic_slice_in_dim(d_flat, me * blocks, blocks, 0)
+    d_mine_y = swap_head(d_mine, 2)
+    flat_y = swap_head(flat_mine, 2)
+    d_h = call(
+        input_kernel, [((rows, D), f32)],
+        d_mine, d_mine_y, w_in, in_y, flat_mine, flat_y, w_sort, sort_y,
+        scratch=[
+            ((rows, 6 * width), bf16), ((D, 6 * width), bf16), ((blocks, 4 * nb), f32), ((D, 4 * nb), bf16),
+        ],
+        name="input_back",
+    )
+    d_tokens, g_one = call(
+        end_kernel, [((rows, D), f32), ((8, D), f32)],
+        tokens, gain_one, d_h, swap_head(d_h, 1), d_middle, name="norm_one_back",
+    )
+    gains = jnp.concatenate([g_one, g_two], 1)
+    for j in (1, 2, 4):
+        gains = gains + swap_blk(gains, j)
+    g_qkv = call(
+        weight_kernel, [((D, 3, width), f32)],
+        h_one, ring_f[0], ring_b[0], ring_f[1], ring_b[1], ring_f[2], ring_b[2], ring_f[3], ring_b[3],
+        other_f[0], other_b[0], other_f[1], other_b[1], other_f[2], other_b[2], other_f[3], other_b[3],
+        d_qkv, scratch=[((total, D), bf16)], name="weights",
+    )
+    return output, d_tokens, gains[0, :D], gains[0, D:], g_qkv, g_out, g_sort, g_up, g_down
+
+
 def solution(mesh):
     in_specs = (
         P("blk", None),
@@ -278,4 +925,5 @@
         P(None, "head"),
         P("head", None),
     )
-    return jax.shard_map(local, mesh=mesh, in_specs=in_specs, out_specs=out_specs, check_vma=False)
+    plan = local_eight if mesh.shape["blk"] == 8 and mesh.shape["head"] == 4 else local
+    return jax.shard_map(plan, mesh=mesh, in_specs=in_specs, out_specs=out_specs, check_vma=False)

time: 576 us -> 229 us (0.40)
  waiting for transfers between devices: 248 us -> 83.8 us
  blocking collectives: 158 us -> 0 us
  Pallas kernels: 0 us -> 73.6 us
  other arithmetic: 55.5 us -> 1.45 us
  matrix products: 34.2 us -> 0 us
  starting transfers between devices: 13.5 us -> 41.6 us
  local copies, waits for them, and re-layouts: 45.3 us -> 26.2 us
  between operations: 17.2 us -> 1.37 us
    psum x5 -> x0, waiting for transfers between devices: 248 us -> none  [the longest x1 118 us: local(): lax.psum((g_gain_one, g_gain_two, g_qkv, g_out, g_sort, g_up, g_down), 'b...]
    ppermute x0 -> x51, waiting for transfers between devices: none -> 83.8 us  [the longest x12 47.9 us: swap_blk(): return lax.ppermute(v, 'blk', [(i, i ^ j) for i in range(8)])]
    pallas_call x0 -> x19, Pallas kernels: none -> 73.6 us  [call(): pl.pallas_call(kernel, out_shape=shapes, in_specs=[SMEM_SPEC if i in smem...]
    unnamed x1 -> x0, blocking collectives: 68.9 us -> none
    all_gather x1 -> x0, blocking collectives: 66.2 us -> none  [local(): every_rows = lax.all_gather(own_rows, 'blk', axis=0, tiled=True)]
    ppermute x0 -> x51, starting transfers between devices: none -> 41.6 us  [the longest x8 11.5 us: behind(): lax.ppermute(v, 'blk', [(RING[i], RING[(i - 1) % 8]) for i in range(8)])]
    dot_general x29 -> x0, matrix products: 34.2 us -> none  [the longest x1 3.32 us: local(): jnp.einsum('st,sf->tf', selector, returned.reshape(dev_count * requests,...]
    reduce_sum x58 -> x0, other arithmetic: 29.8 us -> none  [the longest x8 4.11 us: balancing_log_space(): sort_logits = sort_logits - log_total(sort_logits, 1)]
  transfers between devices with their start and end apart: 7 -> 51, of which waited for: 5 -> 19; matrix products, arithmetic and copies ran while one was open for 7% -> 2% of each run, Pallas kernels for 0% -> 28%
where the time goes in v2:
time: 229 us; the launch traced here: 228 us
  waiting for transfers between devices  83.8 us (37%)
  Pallas kernels  73.6 us (32%)
  starting transfers between devices  41.6 us (18%)
  local copies, waits for them, and re-layouts  26.2 us (11%)
    pallas_call x19, Pallas kernels, call(): pl.pallas_call(kernel, out_shape=shapes, in_specs=[SMEM_SPEC if i in smem...  73.6 us
    ppermute x12, waiting for transfers between devices, swap_blk(): return lax.ppermute(v, 'blk', [(i, i ^ j) for i in range(8)])  47.9 us
    unnamed x138, local copies, waits for them, and re-layouts  23.4 us
    ppermute x8, waiting for transfers between devices, ahead(): lax.ppermute(v, 'blk', [(RING[i], RING[(i + 1) % 8]) for i in range(8)])  18.9 us
    ppermute x23, waiting for transfers between devices, swap_head(): return lax.ppermute(v, 'head', [(i, i ^ j) for i in range(4)])  17 us
    ppermute x8, starting transfers between devices, behind(): lax.ppermute(v, 'blk', [(RING[i], RING[(i - 1) % 8]) for i in range(8)])  11.5 us
    ppermute x12, starting transfers between devices, swap_blk(): return lax.ppermute(v, 'blk', [(i, i ^ j) for i in range(8)])  11 us
    ppermute x23, starting transfers between devices, swap_head(): return lax.ppermute(v, 'head', [(i, i ^ j) for i in range(4)])  10.9 us
  transfers between devices with their start and end apart: 51, of which 19 were waited for; matrix products, arithmetic and copies ran while one was open for 2% of the time, Pallas kernels for 28%

profile of v2, /device:TPU:0, one launch (start us, length us, event | category | flops | bytes accessed | tf_op | source)
XLA Modules:
  0.0 228.0 jit_solution(5500251131217726686)
XLA Ops:
  3.5 3.1 %collective-permute-start = (bf16[256,512]{1,0:T(8,128)(2,1)S(1)}, bf16[256,512]{1,0:T(8,128)(2,1)S(1)}, u32[]{:S(2)}, u32[]{:S(2)}) collective-permute-start(bf16[256,512]{1,0:T(8,128)(2,1)S(1)} %constant_dynamic-slice_fusion.2), channel_id=1, source_target_pairs={{0,8},{8,16},{16,24},{24,28},{28,20},{20,12},{12,4},{4,0},{1,9},{9... | collective-permute-start | bytes 786440 | tf_op jit(solution)/shard_map/ppermute | solution.py:742
  6.6 6.2 %collective-permute-done.refs_0_.refs_1_ = bf16[256,512]{1,0:T(8,128)(2,1)S(1)} collective-permute-done((bf16[256,512]{1,0:T(8,128)(2,1)S(1)}, bf16[256,512]{1,0:T(8,128)(2,1)S(1)}, u32[]{:S(2)}, u32[]{:S(2)}) %collective-permute-start) | collective-permute-done | bytes 262176 | tf_op jit(solution)/shard_map/ppermute | solution.py:742
  12.8 1.8 collective-permute-start.4
  14.9 1.8 collective-permute-start.6
  16.7 4.1 %collective-permute-done.16 = f32[8,640]{1,0:T(8,128)S(1)} collective-permute-done((f32[8,640]{1,0:T(8,128)S(1)}, f32[8,640]{1,0:T(8,128)S(1)}, u32[]{:S(2)}, u32[]{:S(2)}) %collective-permute-start.16) | collective-permute-done | bytes 20512 | tf_op jit(solution)/shard_map/ppermute | solution.py:751
  20.8 2.0 collective-permute-start.8
  26.1 10.1 %collective-permute-done.18.far_rows = f32[32,640]{1,0:T(8,128)S(1)} collective-permute-done((f32[32,640]{1,0:T(8,128)S(1)}, f32[32,640]{1,0:T(8,128)S(1)}, u32[]{:S(2)}, u32[]{:S(2)}) %collective-permute-start.18) | collective-permute-done | bytes 81952 | tf_op jit(solution)/shard_map/ppermute | solution.py:751
  37.4 2.1 collective-permute-start.14
  39.5 3.3 %collective-permute-done.12.refs_0_.refs_7_ = bf16[128,512]{1,0:T(8,128)(2,1)S(1)} collective-permute-done((bf16[128,512]{1,0:T(8,128)(2,1)S(1)}, bf16[128,512]{1,0:T(8,128)(2,1)S(1)}, u32[]{:S(2)}, u32[]{:S(2)}) %collective-permute-start.12) | collective-permute-done | bytes 131104 | tf_op jit(solution)/shard_map/ppermute | solution.py:742
  45.4 1.5 collective-permute-start.25
  50.0 3.0 %sinkhorn.1 = (f32[64,512]{1,0:T(8,128)S(1)}, f32[16,2,64,64]{3,2,1,0:T(8,128)S(1)}, f32[64,256]{1,0:T(8,128)S(1)}, f32[64,128]{1,0:T(8,128)S(1)}) custom-call(f32[32,640]{1,0:T(8,128)S(1)} %constant_dynamic-update-slice_fusion.near_rows, f32[32,640]{1,0:T(8,128)S(1)} %copy-done.56, bf16[512,128]{1,0:T(8,128)(2,1)} %sort_a.1, s32[64,2]{1,0:T(8,128)S(1)} %copy.33.partner), custom_call_target="tpu_custom_call" | custom-call | tf_op jit(solution)/shard_map/sinkhorn/pallas_call | solution.py:712
  57.1 1.4 project.9.step4
  58.5 1.6 collective-permute-start.23
  60.1 1.7 project.8.step3
  61.9 3.7 %attend.1 = (bf16[4096,384]{1,0:T(8,128)(2,1)}, bf16[512,128]{1,0:T(8,128)(2,1)S(1)}) custom-call(bf16[512,384]{1,0:T(8,128)(2,1)S(1)} %project.5.own, bf16[1024,384]{1,0:T(8,128)(2,1)S(1)} %project.6.step1, bf16[1024,384]{1,0:T(8,128)(2,1)S(1)} %project.7.step2, bf16[1024,384]{1,0:T(8,128)(2,1)S(1)} %project.8.step3, bf16[512,384]{1,0:T(8,128)(2,1)S(1)} %project.9.step4, ...), custom_call_target="tpu_custom_call" | custom-call | tf_op jit(solution)/shard_map/attend/pallas_call | solution.py:712
  66.1 8.3 %collective-permute-done.23.wo2 = bf16[128,512]{1,0:T(8,128)(2,1)S(1)} collective-permute-done((bf16[128,512]{1,0:T(8,128)(2,1)S(1)}, bf16[128,512]{1,0:T(8,128)(2,1)S(1)}, u32[]{:S(2)}, u32[]{:S(2)}) %collective-permute-start.23) | collective-permute-done | bytes 131104 | tf_op jit(solution)/shard_map/ppermute | solution.py:748
  74.9 1.8 collective-permute-done.20.ctx2
  76.8 1.3 collective-permute-done.21.ctx3
  78.1 7.4 %feed.1 = (f32[512,512]{1,0:T(8,128)}, bf16[512,512]{1,0:T(8,128)(2,1)S(1)}, bf16[512,512]{1,0:T(8,128)(2,1)S(1)}, bf16[512,512]{1,0:T(8,128)(2,1)S(1)}, f32[512,512]{1,0:T(8,128)}, /*index=5*/f32[512,512]{1,0:T(8,128)}) custom-call(bf16[512,512]{1,0:T(8,128)(2,1)S(1)} %copy-done.1, bf16[512,512]{1,0:T(8,128)(2,1)S(1)} %copy-done.2, ...), custom_call_target="tpu_custom_call" | custom-call | tf_op jit(solution)/shard_map/feed/pallas_call | solution.py:712
  85.7 2.7 %collective-permute-done.28.other = f32[512,512]{1,0:T(8,128)S(1)} collective-permute-done((f32[512,512]{1,0:T(8,128)}, f32[512,512]{1,0:T(8,128)S(1)}, u32[]{:S(2)}, u32[]{:S(2)}) %collective-permute-start.28) | collective-permute-done | bytes 1048608 | tf_op jit(solution)/shard_map/ppermute | solution.py:748
  93.7 1.7 collective-permute-start.30
  95.4 3.5 %collective-permute-done.29.f1 = bf16[512,128]{1,0:T(8,128)(2,1)S(1)} collective-permute-done((bf16[512,128]{1,0:T(8,128)(2,1)S(1)}, bf16[512,128]{1,0:T(8,128)(2,1)S(1)}, u32[]{:S(2)}, u32[]{:S(2)}) %collective-permute-start.29) | collective-permute-done | bytes 131104 | tf_op jit(solution)/shard_map/ppermute | solution.py:742
  99.2 1.7 collective-permute-start.32
  101.0 2.9 %collective-permute-done.31.f2 = bf16[512,128]{1,0:T(8,128)(2,1)S(1)} collective-permute-done((bf16[512,128]{1,0:T(8,128)(2,1)S(1)}, bf16[512,128]{1,0:T(8,128)(2,1)S(1)}, u32[]{:S(2)}, u32[]{:S(2)}) %collective-permute-start.31) | collective-permute-done | bytes 131104 | tf_op jit(solution)/shard_map/ppermute | solution.py:742
  104.2 1.7 collective-permute-start.34
  105.9 2.9 %collective-permute-done.33.f3 = bf16[512,128]{1,0:T(8,128)(2,1)S(1)} collective-permute-done((bf16[512,128]{1,0:T(8,128)(2,1)S(1)}, bf16[512,128]{1,0:T(8,128)(2,1)S(1)}, u32[]{:S(2)}, u32[]{:S(2)}) %collective-permute-start.33) | collective-permute-done | bytes 131104 | tf_op jit(solution)/shard_map/ppermute | solution.py:742
  110.4 1.7 collective-permute-start.36
  112.2 1.9 grads.1
  114.1 1.6 collective-permute-start.38
  120.3 37.0 %pull.1 = (bf16[4096,384]{1,0:T(8,128)(2,1)S(1)}, f32[64,256]{1,0:T(8,128)S(1)}) custom-call(bf16[4096,384]{1,0:T(8,128)(2,1)} %get-tuple-element.49.qkv, bf16[512,128]{1,0:T(8,128)(2,1)S(1)} %copy-done.46, bf16[512,128]{1,0:T(8,128)(2,1)S(1)} %copy-done.48, bf16[512,128]{1,0:T(8,128)(2,1)S(1)} %copy-done.50, bf16[512,128]{1,0:T(8,128)(2,1)S(1)} %copy-done.52, ...), custom_call_target="tpu_custom_call" | custom-call | tf_op jit(solution)/shard_map/pull/pallas_call | solution.py:712
  157.3 1.7 copy-done.5
  164.9 2.1 sinkhorn_back.1
  167.8 1.5 collective-permute-done.40.sort_b
  169.3 1.3 collective-permute-done.39.flat_b
  170.6 2.2 input_back.1.own
  172.9 1.4 merge.2
  175.5 8.3 %collective-permute-done.46.arrived = bf16[288,512]{1,0:T(8,128)(2,1)S(1)} collective-permute-done((bf16[288,512]{1,0:T(8,128)(2,1)S(1)}, bf16[288,512]{1,0:T(8,128)(2,1)S(1)}, u32[]{:S(2)}, u32[]{:S(2)}) %collective-permute-start.46) | collective-permute-done | bytes 294944 | tf_op jit(solution)/shard_map/ppermute | solution.py:751
  183.9 2.3 %collective-permute-start.47 = (bf16[144,512]{1,0:T(8,128)(2,1)S(1)}, bf16[144,512]{1,0:T(8,128)(2,1)S(1)}, u32[]{:S(2)}, u32[]{:S(2)}) collective-permute-start(bf16[144,512]{1,0:T(8,128)(2,1)S(1)} %get-tuple-element.70), channel_id=1, source_target_pairs={{0,16},{4,20},{8,24},{12,28},{16,0},{20,4},{24,8},{28,12},{1,17},{... | collective-permute-start | bytes 442376 | tf_op jit(solution)/shard_map/ppermute | solution.py:751
  186.2 7.3 %collective-permute-done.47 = bf16[144,512]{1,0:T(8,128)(2,1)S(1)} collective-permute-done((bf16[144,512]{1,0:T(8,128)(2,1)S(1)}, bf16[144,512]{1,0:T(8,128)(2,1)S(1)}, u32[]{:S(2)}, u32[]{:S(2)}) %collective-permute-start.47) | collective-permute-done | bytes 147488 | tf_op jit(solution)/shard_map/ppermute | solution.py:751
  193.5 9.0 %collective-permute-done.48 = bf16[144,512]{1,0:T(8,128)(2,1)S(1)} collective-permute-done((bf16[144,512]{1,0:T(8,128)(2,1)S(1)}, bf16[144,512]{1,0:T(8,128)(2,1)S(1)}, u32[]{:S(2)}, u32[]{:S(2)}) %collective-permute-start.48) | collective-permute-done | bytes 147488 | tf_op jit(solution)/shard_map/ppermute | solution.py:751
  202.7 1.8 norm_one_back.1
  204.5 1.5 collective-permute-start.42
  205.9 4.3 %collective-permute-done.49 = bf16[288,512]{1,0:T(8,128)(2,1)S(1)} collective-permute-done((bf16[288,512]{1,0:T(8,128)(2,1)S(1)}, bf16[288,512]{1,0:T(8,128)(2,1)S(1)}, u32[]{:S(2)}, u32[]{:S(2)}) %collective-permute-start.49) | collective-permute-done | bytes 294944 | tf_op jit(solution)/shard_map/ppermute | solution.py:751
  210.2 2.8 %collective-permute-start.50 = (bf16[576,512]{1,0:T(8,128)(2,1)S(1)}, bf16[576,512]{1,0:T(8,128)(2,1)S(1)}, u32[]{:S(2)}, u32[]{:S(2)}) collective-permute-start(bf16[576,512]{1,0:T(8,128)(2,1)S(1)} %pad_maximum_fusion.here), channel_id=1, source_target_pairs={{0,4},{4,0},{8,12},{12,8},{16,20},{20,16},{24,28},{28,24},{1,5},{5... | collective-permute-start | bytes 1769480 | tf_op jit(solution)/shard_map/ppermute | solution.py:751
  213.4 3.6 %collective-permute-done.43 = f32[8,1024]{1,0:T(8,128)S(1)} collective-permute-done((f32[8,1024]{1,0:T(8,128)S(1)}, f32[8,1024]{1,0:T(8,128)S(1)}, u32[]{:S(2)}, u32[]{:S(2)}) %collective-permute-start.43) | collective-permute-done | bytes 32800 | tf_op jit(solution)/shard_map/ppermute | solution.py:751
  218.3 1.3 add_add_fusion
  219.8 5.1 %weights.1 = f32[512,3,128]{2,1,0:T(4,128)S(1)} custom-call(bf16[512,512]{1,0:T(8,128)(2,1)S(1)} %get-tuple-element.42.refs_0_, bf16[256,512]{1,0:T(8,128)(2,1)S(1)} %copy-done.10, bf16[256,512]{1,0:T(8,128)(2,1)S(1)} %copy-done.12, bf16[256,512]{1,0:T(8,128)(2,1)S(1)} %copy-done.14, bf16[256,512]{1,0:T(8,128)(2,1)S(1)} %copy-done.16, ...), custom_call_target="tpu_custom_call" | custom-call | tf_op jit(solution)/shard_map/weights/pallas_call | solution.py:712
  226.4 1.6 lay.1
  (232 shorter events, 41.9 us)
Async XLA Ops:
  3.5 9.3 %collective-permute-start = (bf16[256,512]{1,0:T(8,128)(2,1)S(1)}, bf16[256,512]{1,0:T(8,128)(2,1)S(1)}, u32[]{:S(2)}, u32[]{:S(2)}) collective-permute-start(bf16[256,512]{1,0:T(8,128)(2,1)S(1)} %constant_dynamic-slice_fusion.2), channel_id=1, source_target_pairs={{0,8},{8,16},{16,24},{24,28},{28,20},{20,12},{12,4},{4,0},{1,9},{9... | collective-permute-start | bytes 786440 | tf_op jit(solution)/shard_map/ppermute | solution.py:742
  6.6 8.3 %collective-permute-start.2 = (bf16[256,512]{1,0:T(8,128)(2,1)S(1)}, bf16[256,512]{1,0:T(8,128)(2,1)S(1)}, u32[]{:S(2)}, u32[]{:S(2)}) collective-permute-start(bf16[256,512]{1,0:T(8,128)(2,1)S(1)} %constant_dynamic-slice_fusion.2), channel_id=1, source_target_pairs={{0,4},{8,0},{16,8},{24,16},{28,24},{20,28},{12,20},{4,12},{1,5},{9... | collective-permute-start | bytes 786440 | tf_op jit(solution)/shard_map/ppermute | solution.py:745
  12.8 7.9 %collective-permute-start.4 = (bf16[256,512]{1,0:T(8,128)(2,1)S(1)}, bf16[256,512]{1,0:T(8,128)(2,1)S(1)}, u32[]{:S(2)}, u32[]{:S(2)}) collective-permute-start(bf16[256,512]{1,0:T(8,128)(2,1)S(1)} %collective-permute-done.refs_0_.refs_1_), channel_id=1, source_target_pairs={{0,8},{8,16},{16,24},{24,28},{28,20},{20,12},{12,4},{4,0},{1,9},{9... | collective-permute-start | bytes 786440 | tf_op jit(solution)/shard_map/ppermute | solution.py:742
  14.7 6.1 %collective-permute-start.16 = (f32[8,640]{1,0:T(8,128)S(1)}, f32[8,640]{1,0:T(8,128)S(1)}, u32[]{:S(2)}, u32[]{:S(2)}) collective-permute-start(f32[8,640]{1,0:T(8,128)S(1)} %get-tuple-element.43), channel_id=1, source_target_pairs={{0,4},{4,0},{8,12},{12,8},{16,20},{20,16},{24,28},{28,24},{1,5},{5... | collective-permute-start | bytes 61448 | tf_op jit(solution)/shard_map/ppermute | solution.py:751
  14.9 7.9 %collective-permute-start.6 = (bf16[256,512]{1,0:T(8,128)(2,1)S(1)}, bf16[256,512]{1,0:T(8,128)(2,1)S(1)}, u32[]{:S(2)}, u32[]{:S(2)}) collective-permute-start(bf16[256,512]{1,0:T(8,128)(2,1)S(1)} %collective-permute-done.2.refs_2_), channel_id=1, source_target_pairs={{0,4},{8,0},{16,8},{24,16},{28,24},{20,28},{12,20},{4,12},{1,5},{9... | collective-permute-start | bytes 786440 | tf_op jit(solution)/shard_map/ppermute | solution.py:745
  20.8 4.0 %collective-permute-start.17 = (f32[16,640]{1,0:T(8,128)S(1)}, f32[16,640]{1,0:T(8,128)S(1)}, u32[]{:S(2)}, u32[]{:S(2)}) collective-permute-start(f32[16,640]{1,0:T(8,128)S(1)} %pad_maximum_fusion.2), channel_id=1, source_target_pairs={{0,8},{4,12},{8,0},{12,4},{16,24},{20,28},{24,16},{28,20},{1,9},{5... | collective-permute-start | bytes 122888 | tf_op jit(solution)/shard_map/ppermute | solution.py:751
  20.8 16.0 %collective-permute-start.8 = (bf16[256,512]{1,0:T(8,128)(2,1)S(1)}, bf16[256,512]{1,0:T(8,128)(2,1)S(1)}, u32[]{:S(2)}, u32[]{:S(2)}) collective-permute-start(bf16[256,512]{1,0:T(8,128)(2,1)S(1)} %collective-permute-done.4.refs_0_.refs_3_), channel_id=1, source_target_pairs={{0,8},{8,16},{16,24},{24,28},{28,20},{20,12},{12,4},{4,0},{1,9},{9... | collective-permute-start | bytes 786440 | tf_op jit(solution)/shard_map/ppermute | solution.py:742
  22.8 14.6 %collective-permute-start.1 = (bf16[256,512]{1,0:T(8,128)(2,1)S(1)}, bf16[256,512]{1,0:T(8,128)(2,1)S(1)}, u32[]{:S(2)}, u32[]{:S(2)}) collective-permute-start(bf16[256,512]{1,0:T(8,128)(2,1)S(1)} %collective-permute-done.refs_0_.refs_1_), channel_id=1, source_target_pairs={{0,1},{1,0},{2,3},{3,2},{4,5},{5,4},{6,7},{7,6},{8,9},{9,8},{10,11... | collective-permute-start | bytes 786440 | tf_op jit(solution)/shard_map/ppermute | solution.py:748
  22.8 14.5 %collective-permute-start.10 = (bf16[256,512]{1,0:T(8,128)(2,1)S(1)}, bf16[256,512]{1,0:T(8,128)(2,1)S(1)}, u32[]{:S(2)}, u32[]{:S(2)}) collective-permute-start(bf16[256,512]{1,0:T(8,128)(2,1)S(1)} %collective-permute-done.6.refs_2_.refs_4_), channel_id=1, source_target_pairs={{0,4},{8,0},{16,8},{24,16},{28,24},{20,28},{12,20},{4,12},{1,5},{9... | collective-permute-start | bytes 786440 | tf_op jit(solution)/shard_map/ppermute | solution.py:745
  24.8 11.3 %collective-permute-start.18 = (f32[32,640]{1,0:T(8,128)S(1)}, f32[32,640]{1,0:T(8,128)S(1)}, u32[]{:S(2)}, u32[]{:S(2)}) collective-permute-start(f32[32,640]{1,0:T(8,128)S(1)} %constant_dynamic-update-slice_fusion.near_rows), channel_id=1, source_target_pairs={{0,16},{4,20},{8,24},{12,28},{16,0},{20,4},{24,8},{28,12},{1,17},{... | collective-permute-start | bytes 245768 | tf_op jit(solution)/shard_map/ppermute | solution.py:751
  26.1 17.4 %collective-permute-start.3 = (bf16[256,512]{1,0:T(8,128)(2,1)S(1)}, bf16[256,512]{1,0:T(8,128)(2,1)S(1)}, u32[]{:S(2)}, u32[]{:S(2)}) collective-permute-start(bf16[256,512]{1,0:T(8,128)(2,1)S(1)} %collective-permute-done.2.refs_2_), channel_id=1, source_target_pairs={{0,1},{1,0},{2,3},{3,2},{4,5},{5,4},{6,7},{7,6},{8,9},{9,8},{10,11... | collective-permute-start | bytes 786440 | tf_op jit(solution)/shard_map/ppermute | solution.py:748
  36.8 7.2 %collective-permute-start.5 = (bf16[256,512]{1,0:T(8,128)(2,1)S(1)}, bf16[256,512]{1,0:T(8,128)(2,1)S(1)}, u32[]{:S(2)}, u32[]{:S(2)}) collective-permute-start(bf16[256,512]{1,0:T(8,128)(2,1)S(1)} %collective-permute-done.4.refs_0_.refs_3_), channel_id=1, source_target_pairs={{0,1},{1,0},{2,3},{3,2},{4,5},{5,4},{6,7},{7,6},{8,9},{9,8},{10,11... | collective-permute-start | bytes 786440 | tf_op jit(solution)/shard_map/ppermute | solution.py:748
  36.8 7.9 %collective-permute-start.7 = (bf16[256,512]{1,0:T(8,128)(2,1)S(1)}, bf16[256,512]{1,0:T(8,128)(2,1)S(1)}, u32[]{:S(2)}, u32[]{:S(2)}) collective-permute-start(bf16[256,512]{1,0:T(8,128)(2,1)S(1)} %collective-permute-done.6.refs_2_.refs_4_), channel_id=1, source_target_pairs={{0,1},{1,0},{2,3},{3,2},{4,5},{5,4},{6,7},{7,6},{8,9},{9,8},{10,11... | collective-permute-start | bytes 786440 | tf_op jit(solution)/shard_map/ppermute | solution.py:748
  37.3 5.5 %collective-permute-start.12 = (bf16[128,512]{1,0:T(8,128)(2,1)S(1)}, bf16[128,512]{1,0:T(8,128)(2,1)S(1)}, u32[]{:S(2)}, u32[]{:S(2)}) collective-permute-start(bf16[128,512]{1,0:T(8,128)(2,1)S(1)} %slice.24), channel_id=1, source_target_pairs={{0,8},{8,16},{16,24},{24,28},{28,20},{20,12},{12,4},{4,0},{1,9},{9... | collective-permute-start | bytes 393224 | tf_op jit(solution)/shard_map/ppermute | solution.py:742
  37.4 9.5 %collective-permute-start.14 = (bf16[128,512]{1,0:T(8,128)(2,1)S(1)}, bf16[128,512]{1,0:T(8,128)(2,1)}, u32[]{:S(2)}, u32[]{:S(2)}) collective-permute-start(bf16[128,512]{1,0:T(8,128)(2,1)S(1)} %slice.25), channel_id=1, source_target_pairs={{0,4},{8,0},{16,8},{24,16},{28,24},{20,28},{12,20},{4,12},{1,5},{9... | collective-permute-start | bytes 393224 | tf_op jit(solution)/shard_map/ppermute | solution.py:745
  42.8 4.7 %collective-permute-start.13 = (bf16[128,512]{1,0:T(8,128)(2,1)S(1)}, bf16[128,512]{1,0:T(8,128)(2,1)S(1)}, u32[]{:S(2)}, u32[]{:S(2)}) collective-permute-start(bf16[128,512]{1,0:T(8,128)(2,1)S(1)} %collective-permute-done.12.refs_0_.refs_7_), channel_id=1, source_target_pairs={{0,1},{1,0},{2,3},{3,2},{4,5},{5,4},{6,7},{7,6},{8,9},{9,8},{10,11... | collective-permute-start | bytes 393224 | tf_op jit(solution)/shard_map/ppermute | solution.py:748
  43.4 15.1 %collective-permute-start.9 = (bf16[256,512]{1,0:T(8,128)(2,1)S(1)}, bf16[256,512]{1,0:T(8,128)(2,1)}, u32[]{:S(2)}, u32[]{:S(2)}) collective-permute-start(bf16[256,512]{1,0:T(8,128)(2,1)S(1)} %collective-permute-done.8.refs_0_.refs_5_), channel_id=1, source_target_pairs={{0,1},{1,0},{2,3},{3,2},{4,5},{5,4},{6,7},{7,6},{8,9},{9,8},{10,11... | collective-permute-start | bytes 786440 | tf_op jit(solution)/shard_map/ppermute | solution.py:748
  44.6 15.5 %collective-permute-start.11 = (bf16[256,512]{1,0:T(8,128)(2,1)S(1)}, bf16[256,512]{1,0:T(8,128)(2,1)}, u32[]{:S(2)}, u32[]{:S(2)}) collective-permute-start(bf16[256,512]{1,0:T(8,128)(2,1)S(1)} %collective-permute-done.10.refs_2_.refs_6_), channel_id=1, source_target_pairs={{0,1},{1,0},{2,3},{3,2},{4,5},{5,4},{6,7},{7,6},{8,9},{9,8},{10,11... | collective-permute-start | bytes 786440 | tf_op jit(solution)/shard_map/ppermute | solution.py:748
  45.4 31.4 %collective-permute-start.25 = (bf16[512,512]{1,0:T(8,128)(2,1)}, bf16[512,512]{1,0:T(8,128)(2,1)}, u32[]{:S(2)}, u32[]{:S(2)}) collective-permute-start(bf16[512,512]{1,0:T(8,128)(2,1)} %up_a.1), channel_id=1, source_target_pairs={{0,2},{1,3},{2,0},{3,1},{4,6},{5,7},{6,4},{7,5},{8,10},{9,11},{10,... | collective-permute-start | bytes 1572872 | tf_op jit(solution)/shard_map/ppermute | solution.py:748
  46.9 29.9 %collective-permute-start.26 = (bf16[512,512]{1,0:T(8,128)(2,1)}, bf16[512,512]{1,0:T(8,128)(2,1)}, u32[]{:S(2)}, u32[]{:S(2)}) collective-permute-start(bf16[512,512]{1,0:T(8,128)(2,1)} %down_a.1), channel_id=1, source_target_pairs={{0,2},{1,3},{2,0},{3,1},{4,6},{5,7},{6,4},{7,5},{8,10},{9,11},{10,... | collective-permute-start | bytes 1572872 | tf_op jit(solution)/shard_map/ppermute | solution.py:748
  48.1 8.3 %collective-permute-start.15 = (bf16[128,512]{1,0:T(8,128)(2,1)}, bf16[128,512]{1,0:T(8,128)(2,1)}, u32[]{:S(2)}, u32[]{:S(2)}) collective-permute-start(bf16[128,512]{1,0:T(8,128)(2,1)} %collective-permute-done.14.refs_2_.refs_8_), channel_id=1, source_target_pairs={{0,1},{1,0},{2,3},{3,2},{4,5},{5,4},{6,7},{7,6},{8,9},{9,8},{10,11... | collective-permute-start | bytes 393224 | tf_op jit(solution)/shard_map/ppermute | solution.py:748
  56.6 17.8 %collective-permute-start.22 = (bf16[128,512]{1,0:T(8,128)(2,1)S(1)}, bf16[128,512]{1,0:T(8,128)(2,1)S(1)}, u32[]{:S(2)}, u32[]{:S(2)}) collective-permute-start(bf16[128,512]{1,0:T(8,128)(2,1)S(1)} %copy-done.38), channel_id=1, source_target_pairs={{0,1},{1,0},{2,3},{3,2},{4,5},{5,4},{6,7},{7,6},{8,9},{9,8},{10,11... | collective-permute-start | bytes 393224 | tf_op jit(solution)/shard_map/ppermute | solution.py:748
  58.5 15.9 %collective-permute-start.23 = (bf16[128,512]{1,0:T(8,128)(2,1)S(1)}, bf16[128,512]{1,0:T(8,128)(2,1)S(1)}, u32[]{:S(2)}, u32[]{:S(2)}) collective-permute-start(bf16[128,512]{1,0:T(8,128)(2,1)S(1)} %copy-done.38), channel_id=1, source_target_pairs={{0,2},{1,3},{2,0},{3,1},{4,6},{5,7},{6,4},{7,5},{8,10},{9,11},{10,... | collective-permute-start | bytes 393224 | tf_op jit(solution)/shard_map/ppermute | solution.py:748
  65.6 11.2 %collective-permute-start.20 = (bf16[512,128]{1,0:T(8,128)(2,1)S(1)}, bf16[512,128]{1,0:T(8,128)(2,1)S(1)}, u32[]{:S(2)}, u32[]{:S(2)}) collective-permute-start(bf16[512,128]{1,0:T(8,128)(2,1)S(1)} %get-tuple-element.46.ctx0.context), channel_id=1, source_target_pairs={{0,2},{1,3},{2,0},{3,1},{4,6},{5,7},{6,4},{7,5},{8,10},{9,11},{10,... | collective-permute-start | bytes 393224 | tf_op jit(solution)/shard_map/ppermute | solution.py:748
  85.5 2.9 %collective-permute-start.28 = (f32[512,512]{1,0:T(8,128)}, f32[512,512]{1,0:T(8,128)S(1)}, u32[]{:S(2)}, u32[]{:S(2)}) collective-permute-start(f32[512,512]{1,0:T(8,128)} %get-tuple-element.50.own), channel_id=1, source_target_pairs={{0,1},{1,0},{2,3},{3,2},{4,5},{5,4},{6,7},{7,6},{8,9},{9,8},{10,11... | collective-permute-start | bytes 3145736 | tf_op jit(solution)/shard_map/ppermute | solution.py:748
  93.4 5.5 %collective-permute-start.29 = (bf16[512,128]{1,0:T(8,128)(2,1)S(1)}, bf16[512,128]{1,0:T(8,128)(2,1)S(1)}, u32[]{:S(2)}, u32[]{:S(2)}) collective-permute-start(bf16[512,128]{1,0:T(8,128)(2,1)S(1)} %get-tuple-element.51.own), channel_id=1, source_target_pairs={{0,8},{8,16},{16,24},{24,28},{28,20},{20,12},{12,4},{4,0},{1,9},{9... | collective-permute-start | bytes 393224 | tf_op jit(solution)/shard_map/ppermute | solution.py:742
  93.7 5.6 %collective-permute-start.30 = (bf16[512,128]{1,0:T(8,128)(2,1)S(1)}, bf16[512,128]{1,0:T(8,128)(2,1)S(1)}, u32[]{:S(2)}, u32[]{:S(2)}) collective-permute-start(bf16[512,128]{1,0:T(8,128)(2,1)S(1)} %get-tuple-element.51.own), channel_id=1, source_target_pairs={{0,4},{8,0},{16,8},{24,16},{28,24},{20,28},{12,20},{4,12},{1,5},{9... | collective-permute-start | bytes 393224 | tf_op jit(solution)/shard_map/ppermute | solution.py:745
  98.9 5.0 %collective-permute-start.31 = (bf16[512,128]{1,0:T(8,128)(2,1)S(1)}, bf16[512,128]{1,0:T(8,128)(2,1)S(1)}, u32[]{:S(2)}, u32[]{:S(2)}) collective-permute-start(bf16[512,128]{1,0:T(8,128)(2,1)S(1)} %collective-permute-done.29.f1), channel_id=1, source_target_pairs={{0,8},{8,16},{16,24},{24,28},{28,20},{20,12},{12,4},{4,0},{1,9},{9... | collective-permute-start | bytes 393224 | tf_op jit(solution)/shard_map/ppermute | solution.py:742
  99.2 5.0 %collective-permute-start.32 = (bf16[512,128]{1,0:T(8,128)(2,1)S(1)}, bf16[512,128]{1,0:T(8,128)(2,1)S(1)}, u32[]{:S(2)}, u32[]{:S(2)}) collective-permute-start(bf16[512,128]{1,0:T(8,128)(2,1)S(1)} %collective-permute-done.30.b1), channel_id=1, source_target_pairs={{0,4},{8,0},{16,8},{24,16},{28,24},{20,28},{12,20},{4,12},{1,5},{9... | collective-permute-start | bytes 393224 | tf_op jit(solution)/shard_map/ppermute | solution.py:745
  103.9 5.0 %collective-permute-start.33 = (bf16[512,128]{1,0:T(8,128)(2,1)S(1)}, bf16[512,128]{1,0:T(8,128)(2,1)S(1)}, u32[]{:S(2)}, u32[]{:S(2)}) collective-permute-start(bf16[512,128]{1,0:T(8,128)(2,1)S(1)} %collective-permute-done.31.f2), channel_id=1, source_target_pairs={{0,8},{8,16},{16,24},{24,28},{28,20},{20,12},{12,4},{4,0},{1,9},{9... | collective-permute-start | bytes 393224 | tf_op jit(solution)/shard_map/ppermute | solution.py:742
  104.2 5.6 %collective-permute-start.34 = (bf16[512,128]{1,0:T(8,128)(2,1)S(1)}, bf16[512,128]{1,0:T(8,128)(2,1)S(1)}, u32[]{:S(2)}, u32[]{:S(2)}) collective-permute-start(bf16[512,128]{1,0:T(8,128)(2,1)S(1)} %collective-permute-done.32.b2), channel_id=1, source_target_pairs={{0,4},{8,0},{16,8},{24,16},{28,24},{20,28},{12,20},{4,12},{1,5},{9... | collective-permute-start | bytes 393224 | tf_op jit(solution)/shard_map/ppermute | solution.py:745
  109.5 6.2 %collective-permute-start.35 = (bf16[256,128]{1,0:T(8,128)(2,1)}, bf16[256,128]{1,0:T(8,128)(2,1)}, u32[]{:S(2)}, u32[]{:S(2)}) collective-permute-start(bf16[256,128]{1,0:T(8,128)(2,1)} %slice.26), channel_id=1, source_target_pairs={{0,8},{8,16},{16,24},{24,28},{28,20},{20,12},{12,4},{4,0},{1,9},{9... | collective-permute-start | bytes 196616 | tf_op jit(solution)/shard_map/ppermute | solution.py:742
  110.4 5.3 %collective-permute-start.36 = (bf16[256,128]{1,0:T(8,128)(2,1)}, bf16[256,128]{1,0:T(8,128)(2,1)}, u32[]{:S(2)}, u32[]{:S(2)}) collective-permute-start(bf16[256,128]{1,0:T(8,128)(2,1)} %slice.27), channel_id=1, source_target_pairs={{0,4},{8,0},{16,8},{24,16},{28,24},{20,28},{12,20},{4,12},{1,5},{9... | collective-permute-start | bytes 196616 | tf_op jit(solution)/shard_map/ppermute | solution.py:745
  114.1 58.8 %collective-permute-start.45 = (bf16[576,512]{1,0:T(8,128)(2,1)}, bf16[576,512]{1,0:T(8,128)(2,1)}, u32[]{:S(2)}, u32[]{:S(2)}) collective-permute-start(bf16[576,512]{1,0:T(8,128)(2,1)} %get-tuple-element.66), channel_id=1, source_target_pairs={{0,4},{4,0},{8,12},{12,8},{16,20},{20,16},{24,28},{28,24},{1,5},{5... | collective-permute-start | bytes 1769480 | tf_op jit(solution)/shard_map/ppermute | solution.py:751
  114.1 55.1 %collective-permute-start.38 = (bf16[512,384]{1,0:T(8,128)(2,1)S(1)}, bf16[512,384]{1,0:T(8,128)(2,1)}, u32[]{:S(2)}, u32[]{:S(2)}) collective-permute-start(bf16[512,384]{1,0:T(8,128)(2,1)S(1)} %copy.27.refs_1_.refs_4_.w_a), channel_id=1, source_target_pairs={{0,2},{1,3},{2,0},{3,1},{4,6},{5,7},{6,4},{7,5},{8,10},{9,11},{10,... | collective-permute-start | bytes 1179656 | tf_op jit(solution)/shard_map/ppermute | solution.py:748
  159.1 11.5 %collective-permute-start.37 = (bf16[512,384]{1,0:T(8,128)(2,1)S(1)}, bf16[512,384]{1,0:T(8,128)(2,1)}, u32[]{:S(2)}, u32[]{:S(2)}) collective-permute-start(bf16[512,384]{1,0:T(8,128)(2,1)S(1)} %constant_dynamic-slice_fusion.1.dq_a), channel_id=1, source_target_pairs={{0,2},{1,3},{2,0},{3,1},{4,6},{5,7},{6,4},{7,5},{8,10},{9,11},{10,... | collective-permute-start | bytes 1179656 | tf_op jit(solution)/shard_map/ppermute | solution.py:748
  159.9 9.4 %collective-permute-start.40 = (bf16[512,128]{1,0:T(8,128)(2,1)}, bf16[512,128]{1,0:T(8,128)(2,1)}, u32[]{:S(2)}, u32[]{:S(2)}) collective-permute-start(bf16[512,128]{1,0:T(8,128)(2,1)} %sort_a.1), channel_id=1, source_target_pairs={{0,2},{1,3},{2,0},{3,1},{4,6},{5,7},{6,4},{7,5},{8,10},{9,11},{10,... | collective-permute-start | bytes 393224 | tf_op jit(solution)/shard_map/ppermute | solution.py:748
  167.0 3.6 %collective-permute-start.39 = (f32[8,128]{1,0:T(8,128)S(1)}, f32[8,128]{1,0:T(8,128)S(1)}, u32[]{:S(2)}, u32[]{:S(2)}) collective-permute-start(f32[8,128]{1,0:T(8,128)S(1)} %constant_dynamic-slice_fusion.flat_a), channel_id=1, source_target_pairs={{0,2},{1,3},{2,0},{3,1},{4,6},{5,7},{6,4},{7,5},{8,10},{9,11},{10,... | collective-permute-start | bytes 12296 | tf_op jit(solution)/shard_map/ppermute | solution.py:748
  172.8 29.9 %collective-permute-start.41 = (f32[512,512]{1,0:T(8,128)S(1)}, f32[512,512]{1,0:T(8,128)S(1)}, u32[]{:S(2)}, u32[]{:S(2)}) collective-permute-start(f32[512,512]{1,0:T(8,128)S(1)} %input_back.1.own), channel_id=1, source_target_pairs={{0,1},{1,0},{2,3},{3,2},{4,5},{5,4},{6,7},{7,6},{8,9},{9,8},{10,11... | collective-permute-start | bytes 3145736 | tf_op jit(solution)/shard_map/ppermute | solution.py:748
  174.3 9.5 %collective-permute-start.46 = (bf16[288,512]{1,0:T(8,128)(2,1)S(1)}, bf16[288,512]{1,0:T(8,128)(2,1)S(1)}, u32[]{:S(2)}, u32[]{:S(2)}) collective-permute-start(bf16[288,512]{1,0:T(8,128)(2,1)S(1)} %get-tuple-element.68), channel_id=1, source_target_pairs={{0,8},{4,12},{8,0},{12,4},{16,24},{20,28},{24,16},{28,20},{1,9},{5... | collective-permute-start | bytes 884744 | tf_op jit(solution)/shard_map/ppermute | solution.py:751
  183.9 9.6 %collective-permute-start.47 = (bf16[144,512]{1,0:T(8,128)(2,1)S(1)}, bf16[144,512]{1,0:T(8,128)(2,1)S(1)}, u32[]{:S(2)}, u32[]{:S(2)}) collective-permute-start(bf16[144,512]{1,0:T(8,128)(2,1)S(1)} %get-tuple-element.70), channel_id=1, source_target_pairs={{0,16},{4,20},{8,24},{12,28},{16,0},{20,4},{24,8},{28,12},{1,17},{... | collective-permute-start | bytes 442376 | tf_op jit(solution)/shard_map/ppermute | solution.py:751
  186.2 32.2 %collective-permute-start.27 = (f32[512,512]{1,0:T(8,128)S(1)}, f32[512,512]{1,0:T(8,128)S(1)}, u32[]{:S(2)}, u32[]{:S(2)}) collective-permute-start(f32[512,512]{1,0:T(8,128)S(1)} %copy-done.62), channel_id=1, source_target_pairs={{0,1},{1,0},{2,3},{3,2},{4,5},{5,4},{6,7},{7,6},{8,9},{9,8},{10,11... | collective-permute-start | bytes 3145736 | tf_op jit(solution)/shard_map/ppermute | solution.py:748
  193.5 9.1 %collective-permute-start.48 = (bf16[144,512]{1,0:T(8,128)(2,1)S(1)}, bf16[144,512]{1,0:T(8,128)(2,1)S(1)}, u32[]{:S(2)}, u32[]{:S(2)}) collective-permute-start(bf16[144,512]{1,0:T(8,128)(2,1)S(1)} %add_convert_fusion), channel_id=1, source_target_pairs={{0,16},{4,20},{8,24},{12,28},{16,0},{20,4},{24,8},{28,12},{1,17},{... | collective-permute-start | bytes 442376 | tf_op jit(solution)/shard_map/ppermute | solution.py:751
  202.6 7.6 %collective-permute-start.49 = (bf16[288,512]{1,0:T(8,128)(2,1)S(1)}, bf16[288,512]{1,0:T(8,128)(2,1)S(1)}, u32[]{:S(2)}, u32[]{:S(2)}) collective-permute-start(bf16[288,512]{1,0:T(8,128)(2,1)S(1)} %pad_maximum_fusion.1), channel_id=1, source_target_pairs={{0,8},{4,12},{8,0},{12,4},{16,24},{20,28},{24,16},{28,20},{1,9},{5... | collective-permute-start | bytes 884744 | tf_op jit(solution)/shard_map/ppermute | solution.py:751
  204.5 8.6 %collective-permute-start.42 = (f32[8,1024]{1,0:T(8,128)S(1)}, f32[8,1024]{1,0:T(8,128)S(1)}, u32[]{:S(2)}, u32[]{:S(2)}) collective-permute-start(f32[8,1024]{1,0:T(8,128)S(1)} %constant_dynamic-update-slice_fusion.3), channel_id=1, source_target_pairs={{0,4},{4,0},{8,12},{12,8},{16,20},{20,16},{24,28},{28,24},{1,5},{5... | collective-permute-start | bytes 98312 | tf_op jit(solution)/shard_map/ppermute | solution.py:751
  210.2 16.2 %collective-permute-start.50 = (bf16[576,512]{1,0:T(8,128)(2,1)S(1)}, bf16[576,512]{1,0:T(8,128)(2,1)S(1)}, u32[]{:S(2)}, u32[]{:S(2)}) collective-permute-start(bf16[576,512]{1,0:T(8,128)(2,1)S(1)} %pad_maximum_fusion.here), channel_id=1, source_target_pairs={{0,4},{4,0},{8,12},{12,8},{16,20},{20,16},{24,28},{28,24},{1,5},{5... | collective-permute-start | bytes 1769480 | tf_op jit(solution)/shard_map/ppermute | solution.py:751
  213.1 4.0 %collective-permute-start.43 = (f32[8,1024]{1,0:T(8,128)S(1)}, f32[8,1024]{1,0:T(8,128)S(1)}, u32[]{:S(2)}, u32[]{:S(2)}) collective-permute-start(f32[8,1024]{1,0:T(8,128)S(1)} %add.37), channel_id=1, source_target_pairs={{0,8},{4,12},{8,0},{12,4},{16,24},{20,28},{24,16},{28,20},{1,9},{5... | collective-permute-start | bytes 98312 | tf_op jit(solution)/shard_map/ppermute | solution.py:751
  217.2 8.7 %collective-permute-start.44 = (f32[8,1024]{1,0:T(8,128)S(1)}, f32[8,1024]{1,0:T(8,128)S(1)}, u32[]{:S(2)}, u32[]{:S(2)}) collective-permute-start(f32[8,1024]{1,0:T(8,128)S(1)} %add.38), channel_id=1, source_target_pairs={{0,16},{4,20},{8,24},{12,28},{16,0},{20,4},{24,8},{28,12},{1,17},{... | collective-permute-start | bytes 98312 | tf_op jit(solution)/shard_map/ppermute | solution.py:751
  (69 other events, 489.7 us)

commit v3 on v1

--- a/solution.py
+++ b/solution.py
@@ -1,6 +1,11 @@
+import functools
+import math
+
 import jax
 import jax.numpy as jnp
 from jax import lax
+from jax.experimental import pallas as pl
+from jax.experimental.pallas import tpu as pltpu
 from jax.sharding import PartitionSpec as P
 
 D = 512
@@ -253,6 +258,836 @@
     )
 
 
+def mask_pair(values, near):
+    zero = jnp.zeros_like(values)
+    return jnp.where(near, values, zero), jnp.where(near, zero, values)
+
+
+def first_lanes():
+    return lax.broadcasted_iota(jnp.int32, (1, 2 * DH), 1) < DH
+
+
+def dot_nn(a, b):
+    return lax.dot_general(a, b, (((1,), (0,)), ((), ())), preferred_element_type=jnp.float32)
+
+
+def dot_nt(a, b):
+    return lax.dot_general(a, b, (((1,), (1,)), ((), ())), preferred_element_type=jnp.float32)
+
+
+def dot_tn(a, b):
+    return lax.dot_general(a, b, (((0,), (0,)), ((), ())), preferred_element_type=jnp.float32)
+
+
+def three_parts(values):
+    high = values.astype(jnp.bfloat16)
+    rest = values - high.astype(jnp.float32)
+    mid = rest.astype(jnp.bfloat16)
+    low = (rest - mid.astype(jnp.float32)).astype(jnp.bfloat16)
+    return high, mid, low
+
+
+def norm_parts(values):
+    centred = values - jnp.mean(values, -1, keepdims=True)
+    inv_std = lax.rsqrt(jnp.mean(centred * centred, -1, keepdims=True) + EPS)
+    return centred * inv_std, inv_std
+
+
+def head_kernel(tokens, gain, noise, h_one, packed, summary, own_noise):
+    f32, bf16 = jnp.float32, jnp.bfloat16
+    core = lax.axis_index("head") % 2
+    rows = tokens.shape[0]
+    half, quarter = rows // 2, rows // 4
+    normed, _ = norm_parts(tokens[...].astype(f32))
+    h = normed * gain[...].astype(f32)
+    h_one[...] = h.astype(bf16)
+    summary[...] = jnp.mean(h.reshape(rows // BLOCK, BLOCK, D), axis=1)
+    blocks = half // BLOCK
+    mine = jnp.where(core == 0, summary[:blocks, :], summary[blocks:, :])
+    lines = []
+    for r in range(2):
+        few = noise.shape[0] // 2
+        lines.append(
+            jnp.concatenate(
+                [noise[r * few + i, h : h + 1, :] for i in range(few) for h in range(2)], 1
+            )
+        )
+    for at, values in ((0, mine), (quarter + EXTRA, jnp.concatenate(lines, 0))):
+        start = pl.multiple_of(core * half + (0 if at == 0 else quarter), quarter)
+        packed[at : at + quarter, :] = h_one[pl.ds(start, quarter), :]
+        if at:
+            own_noise[...] = values
+        parts = [p.astype(f32) for p in three_parts(values)]
+        empty = jnp.zeros((EXTRA - 3 * values.shape[0], D), f32)
+        packed[at + quarter : at + quarter + EXTRA, :] = jnp.concatenate(parts + [empty], 0).astype(bf16)
+
+
+def wide(weight):
+    return jnp.concatenate([weight[i] for i in range(3)], 1)
+
+
+def project_own_kernel(h_one, weight, out):
+    for start in range(0, h_one.shape[0], 2 * BLOCK):
+        sl = slice(start, start + 2 * BLOCK)
+        out[sl, :] = dot_nn(h_one[sl, :], wide(weight)).astype(jnp.bfloat16)
+
+
+def project_kernel(f, xf, b, xb, weight, out, extra):
+    quarter = f.shape[0] // 2 - EXTRA
+    to = 0
+    for piece in (f, xf, b, xb):
+        for at in (0, quarter + EXTRA):
+            out[to : to + quarter, :] = dot_nn(
+                piece[at : at + quarter, :], wide(weight)
+            ).astype(jnp.bfloat16)
+            to += quarter
+    to = 0
+    for piece in (f, xf, b, xb):
+        for at in (quarter, 2 * quarter + EXTRA):
+            extra[to : to + EXTRA, :] = piece[at : at + EXTRA, :]
+            to += EXTRA
+
+
+def ring_of(position):
+    return jnp.where(position < 4, 2 * position, 2 * (7 - position) + 1)
+
+
+def place_of(index):
+    return jnp.where(index % 2 == 0, index // 2, 7 - index // 2)
+
+
+def far_near(table, at, lanes):
+    return table[pl.ds(pl.multiple_of(at * BLOCK, BLOCK), BLOCK), lanes]
+
+
+def block_operands(qkv, block, first, second, near):
+    k_lanes, v_lanes = slice(2 * DH, 4 * DH), slice(4 * DH, 6 * DH)
+    query = far_near(qkv, block, slice(0, 2 * DH))
+    keys, values = [], []
+    for lanes, store in ((k_lanes, keys), (v_lanes, values)):
+        own0, own1 = mask_pair(far_near(qkv, block, lanes), near)
+        far0, _ = mask_pair(far_near(qkv, first, lanes), near)
+        _, far1 = mask_pair(far_near(qkv, second, lanes), near)
+        store.extend([own0, far0, own1, far1])
+    return query, keys, values
+
+
+def block_probs(scores):
+    probs = []
+    for h in range(2):
+        part = scores[:, h * 2 * DH : (h + 1) * 2 * DH]
+        expo = jnp.exp(part - jnp.max(part, -1, keepdims=True))
+        probs.append(expo / jnp.sum(expo, -1, keepdims=True))
+    return probs
+
+
+def choices(partner, h):
+    nb = partner.shape[1]
+    sides = lax.broadcasted_iota(jnp.int32, (nb, nb), 0)
+    hot = (sides == partner[h : h + 1, :]).astype(jnp.bfloat16)
+    same = sides == lax.broadcasted_iota(jnp.int32, (nb, nb), 1)
+    return dot_nt(same.astype(jnp.bfloat16), hot)
+
+
+def joined(rows, count):
+    parts = rows.astype(jnp.float32)
+    return (parts[:count] + parts[count : 2 * count]) + parts[2 * count : 3 * count]
+
+
+def attend_kernel(
+    own, step1, step2, step3, extra1, extra2, extra3, f4, b4, xf4, xb4, weight, w_sort,
+    own_summary, own_noise, partner, partner_rows,
+    qkv, context, summary, steps, scale_rows, weight_rows, noise,
+):
+    f32, bf16 = jnp.float32, jnp.bfloat16
+    me = lax.axis_index("blk")
+    core = lax.axis_index("head") % 2
+    place = place_of(me)
+    nb = partner_rows.shape[1]
+    rows = own.shape[0]
+    half, quarter = rows // 2, rows // 4
+    blocks = rows // BLOCK
+    few = blocks // 2
+
+    def put_noise(owner, values):
+        lines = [
+            values[r : r + 1, i * 2 * nb : (i + 1) * 2 * nb] for r in range(2) for i in range(few)
+        ]
+        at = pl.multiple_of(owner * blocks, blocks)
+        noise[pl.ds(at, blocks), :] = jnp.concatenate(lines, 0)
+
+    def put_summary(owner, mine, other):
+        both = jnp.where(
+            core == 0, jnp.concatenate([mine, other], 0), jnp.concatenate([other, mine], 0)
+        )
+        summary[pl.ds(pl.multiple_of(owner * blocks, blocks), blocks), :] = both
+
+    summary[pl.ds(pl.multiple_of(me * blocks, blocks), blocks), :] = own_summary[...]
+    put_noise(me, own_noise[...])
+    qkv[pl.ds(pl.multiple_of(me * rows, rows), rows), :] = own[...]
+    for step, ref, extra in ((1, step1, extra1), (2, step2, extra2), (3, step3, extra3)):
+        owners = (ring_of((place + 8 - step) % 8), ring_of((place + step) % 8))
+        for way, owner in enumerate(owners):
+            for side, number in ((core, 0), (1 - core, 1)):
+                at = pl.multiple_of(owner * rows + side * half, half)
+                slot = 2 * way + number
+                qkv[pl.ds(at, half), :] = ref[slot * half : (slot + 1) * half, :]
+            lines = [extra[(4 * way + k) * EXTRA : (4 * way + k + 1) * EXTRA, :] for k in range(3)]
+            put_summary(owner, joined(lines[0], few), joined(lines[2], few))
+            put_noise(owner, joined(lines[1], 2))
+    owner = ring_of((place + 4) % 8)
+    for side, front, back in ((core, f4, b4), (1 - core, xf4, xb4)):
+        for k, piece in enumerate((front, back)):
+            at = pl.multiple_of(owner * rows + side * half + k * quarter, quarter)
+            qkv[pl.ds(at, quarter), :] = dot_nn(piece[:quarter, :], wide(weight)).astype(bf16)
+    put_summary(owner, joined(f4[quarter:, :], few), joined(xf4[quarter:, :], few))
+    put_noise(owner, joined(b4[quarter:, :], 2))
+
+    parts = three_parts(summary[...])
+    logits = sum(dot_nn(part, w_sort[...]) for part in parts[::-1])
+    logits = (logits + noise[...]) / TEMPER
+    plan = jnp.stack([logits[:, :nb], logits[:, nb:]])
+    for sweep in range(SINK):
+        for k, axis in enumerate((2, 1)):
+            plan = plan - log_total(plan, axis)
+            steps[2 * sweep + k] = jnp.exp(plan)
+    final = jnp.exp(plan)
+    picked = []
+    for h in range(2):
+        chosen = choices(partner_rows, h)
+        picked.append(nb * jnp.sum(chosen * final[h], axis=1, keepdims=True))
+    ones = jnp.ones((nb, DH), f32)
+    scale_rows[...] = jnp.concatenate([ones, picked[0] * ones, ones, picked[1] * ones], 1)
+    weight_rows[...] = jnp.concatenate([picked[0] * ones, picked[1] * ones], 1)
+
+    near = first_lanes()
+    work = []
+    for i in range(blocks):
+        block = me * blocks + i
+        query, keys, values = block_operands(
+            qkv, block, partner[0, block], partner[1, block], near
+        )
+        none = jnp.zeros_like(values[0])
+        table = jnp.concatenate(
+            [
+                jnp.concatenate([values[0], none, values[2], none], 0),
+                jnp.concatenate([none, values[1], none, values[3]], 0),
+            ],
+            1,
+        )
+        z = dot_nt(query, jnp.concatenate(keys, 0)) * (DH**-0.5)
+        work.append((block, z, table))
+    probs = [block_probs(z * scale_rows[pl.ds(block, 1), :]) for block, z, _ in work]
+    outs = [
+        dot_nn(jnp.concatenate([p.astype(bf16) for p in prob], 1), table)
+        for prob, (_, _, table) in zip(probs, work)
+    ]
+    for i, (out, (block, _, _)) in enumerate(zip(outs, work)):
+        ctx = out[:, : 2 * DH] + weight_rows[pl.ds(block, 1), :] * out[:, 2 * DH :]
+        context[i * BLOCK : (i + 1) * BLOCK, :] = ctx.astype(bf16)
+
+
+def feed_kernel(
+    tokens, cotangent, gain, ctx0, ctx1, ctx2, ctx3, wo0, wo1, wo2, wo3, up_a, up_b, down_a, down_b,
+    middle, h_two, active, d_hidden, ffn, d_h_two,
+    ctx_full, wo_full, up_full, down_full, act_full, d_full,
+):
+    f32, bf16 = jnp.float32, jnp.bfloat16
+    hd = lax.axis_index("head")
+    row = hd // 2
+    width = ctx0.shape[1]
+    ff = up_a.shape[1]
+    for j, (c, w) in enumerate(((ctx0, wo0), (ctx1, wo1), (ctx2, wo2), (ctx3, wo3))):
+        at = pl.multiple_of((hd ^ j) * width, width)
+        ctx_full[:, pl.ds(at, width)] = c[...]
+        wo_full[pl.ds(at, width), :] = w[...]
+    for j, (u, w) in enumerate(((up_a, down_a), (up_b, down_b))):
+        at = pl.multiple_of((row ^ j) * ff, ff)
+        up_full[:, pl.ds(at, ff)] = u[...]
+        down_full[pl.ds(at, ff), :] = w[...]
+    chunk = 256
+    for start in range(0, tokens.shape[0], chunk):
+        sl = slice(start, start + chunk)
+        mid = tokens[sl, :].astype(f32) + dot_nn(ctx_full[sl, :], wo_full[...])
+        middle[sl, :] = mid
+        normed, _ = norm_parts(mid)
+        low = (normed * gain[...].astype(f32)).astype(bf16)
+        h_two[sl, :] = low
+        ffn_sum = None
+        back_sum = None
+        for j in range(2):
+            cols = slice(j * ff, (j + 1) * ff)
+            pre = dot_nn(low, up_full[:, cols])
+            d_act = dot_nt(cotangent[sl, :], down_full[cols, :])
+            bell = 0.5 * (1.0 + lax.erf(pre * ROOT_HALF))
+            act = (pre * bell).astype(bf16)
+            slope = bell + pre * jnp.exp(-0.5 * pre * pre) * INV_ROOT_TWO_PI
+            d_pre = (d_act * slope).astype(bf16)
+            act_full[sl, cols] = act
+            d_full[sl, cols] = d_pre
+            f = dot_nn(act, down_full[cols, :])
+            b = dot_nt(d_pre, up_full[:, cols])
+            ffn_sum = f if ffn_sum is None else ffn_sum + f
+            back_sum = b if back_sum is None else back_sum + b
+        ffn[sl, :] = ffn_sum
+        d_h_two[sl, :] = back_sum
+    mine = pl.ds(pl.multiple_of(row * ff, ff), ff)
+    active[...] = act_full[:, mine]
+    d_hidden[...] = d_full[:, mine]
+
+
+def back_kernel(middle, own, other, cotangent, gain, w_out, d_middle, d_low, d_ctx, g_gain):
+    f32, bf16 = jnp.float32, jnp.bfloat16
+    normed, inv = norm_parts(middle[...])
+    d_h = own[...] + other[...]
+    g_gain[...] = jnp.broadcast_to(jnp.sum(d_h * normed, 0, keepdims=True), g_gain.shape)
+    d_mid = cotangent[...].astype(f32) + norm_back(d_h, normed, inv, gain[...].astype(f32))
+    d_middle[...] = d_mid
+    low = d_mid.astype(bf16)
+    d_low[...] = low
+    d_ctx[...] = dot_nt(low, w_out[...]).astype(bf16)
+
+
+def grads_kernel(h_two, d_hidden, active, cotangent, *refs):
+    keeps, sends, (own, other) = refs[:4], refs[4:8], refs[8:]
+    me = lax.axis_index("blk")
+    bit, z = me & 1, me >> 1
+    up = dot_tn(h_two[...], d_hidden[...])
+    down = dot_tn(active[...], cotangent[...])
+    own[...] = jnp.where(bit == 0, up, down)
+    other[...] = jnp.where(bit == 0, down, up)
+    n = keeps[0].shape[0]
+    for j in range(4):
+        at = pl.ds(pl.multiple_of((z ^ j) * n, n), n)
+        keeps[j][...] = own[at, :]
+        sends[j][...] = other[at, :].astype(jnp.bfloat16)
+
+
+def out_grad_kernel(context, d_low, keep, send, total):
+    bit = lax.axis_index("blk") & 1
+    total[...] = dot_tn(context[...], d_low[...])
+    half = keep.shape[0]
+    keep[...] = total[pl.ds(pl.multiple_of(bit * half, half), half), :]
+    send[...] = total[pl.ds(pl.multiple_of((1 - bit) * half, half), half), :].astype(jnp.bfloat16)
+
+
+def out_part(j, keep_out, arrived_out, total):
+    total[...] = keep_out[...] + arrived_out[...].astype(jnp.float32)
+    n = total.shape[0] // 4
+    z = lax.axis_index("blk") >> 1
+    return total[pl.ds(pl.multiple_of((z ^ j) * n, n), n), :]
+
+
+def join_kernel(j, keep, arrived, keep_out, arrived_out, out, total):
+    n = keep.shape[0]
+    out[:n, :] = (keep[...] + arrived[...].astype(jnp.float32)).astype(jnp.bfloat16)
+    out[n:, :] = out_part(j, keep_out, arrived_out, total).astype(jnp.bfloat16)
+
+
+def total_kernel(keep, arrived, keep_out, arrived_out, one, two, three, out, total):
+    f32 = jnp.float32
+    n = keep.shape[0]
+    own = jnp.concatenate(
+        [keep[...] + arrived[...].astype(f32), out_part(0, keep_out, arrived_out, total)], 0
+    )
+    own = (own + one[...].astype(f32)) + (two[...].astype(f32) + three[...].astype(f32))
+    out[...] = own.astype(jnp.bfloat16)
+
+
+def lay_kernel(own, z1, z2, z3, x0, x1, x2, x3, g_up, g_down, g_out):
+    f32 = jnp.float32
+    me = lax.axis_index("blk")
+    z = me >> 1
+    n = g_up.shape[0] // 4
+    few = g_out.shape[0] // 8
+    for j in range(4):
+        at = pl.ds(pl.multiple_of((z ^ j) * n, n), n)
+        mine, other = ((own, x0), (z1, x1), (z2, x2), (z3, x3))[j]
+        first = jnp.where(me & 1 == 0, mine[...].astype(f32), other[...].astype(f32))
+        second = jnp.where(me & 1 == 0, other[...].astype(f32), mine[...].astype(f32))
+        g_up[at, :] = first[:n]
+        g_down[at, :] = second[:n]
+        to = pl.multiple_of((z ^ j) * few, few)
+        g_out[pl.ds(to, few), :] = first[n:]
+        g_out[pl.ds(pl.multiple_of(to + 4 * few, few), few), :] = second[n:]
+
+
+def halve_kernel(f, b, front, back):
+    n = front.shape[0]
+    front[...] = f[:n, :]
+    back[...] = b[n:, :]
+
+
+def add_kernel(*refs):
+    *terms, out = refs
+    total = terms[0][...]
+    for term in terms[1:]:
+        total = total + term[...]
+    out[...] = total
+
+
+def gains_kernel(here, one, two, three, first, second):
+    total = (here[...] + one[...]) + (two[...] + three[...])
+    first[...] = total[0, :]
+    second[...] = total[8, :]
+
+
+def pull_kernel(pieces, *refs):
+    f32, bf16 = jnp.float32, jnp.bfloat16
+    count = len(pieces)
+    outs = refs[:count]
+    qkv, partner, scale_rows, weight_rows, near_out, low_out, d_weight = refs[count:]
+    place = place_of(lax.axis_index("blk"))
+    near = first_lanes()
+    scale = DH**-0.5
+    to = 0
+    for (step, start), d_ctx in zip(pieces, outs):
+        owner = ring_of((place + 8 - step) % 8)
+        for group in range(0, d_ctx.shape[0] // BLOCK, 4):
+            work = []
+            for i in range(group, group + 4):
+                block = owner * (SHARD // BLOCK) + start // BLOCK + i
+                query, keys, values = block_operands(
+                    qkv, block, partner[0, block], partner[1, block], near
+                )
+                work.append(
+                    dict(
+                        query=query,
+                        keys=jnp.concatenate(keys, 0),
+                        values=jnp.concatenate(values, 0),
+                        scale=scale_rows[pl.ds(block, 1), :],
+                        weight=weight_rows[pl.ds(block, 1), :],
+                        d_out=d_ctx[i * BLOCK : (i + 1) * BLOCK, :],
+                    )
+                )
+            for w in work:
+                w["z"] = dot_nt(w["query"], w["keys"]) * scale
+            for w in work:
+                w["raw"] = dot_nt(w["d_out"], w["values"])
+            for w in work:
+                w["probs"] = block_probs(w["z"] * w["scale"])
+            for w in work:
+                d_z, low, d_w = [], [], []
+                for h in range(2):
+                    sl = slice(h * 2 * DH, (h + 1) * 2 * DH)
+                    probs = w["probs"][h]
+                    d_probs = w["raw"][:, sl] * w["scale"][:, sl]
+                    d_scores = probs * (d_probs - jnp.sum(d_probs * probs, -1, keepdims=True))
+                    d_z.append((d_scores * w["scale"][:, sl]).astype(bf16))
+                    low.append(probs.astype(bf16))
+                    d_w.append(
+                        jnp.sum(
+                            d_scores * w["z"][:, sl] + low[h].astype(f32) * w["raw"][:, sl],
+                            0,
+                            keepdims=True,
+                        )
+                    )
+                w["d_z"], w["low"] = jnp.concatenate(d_z, 1), jnp.concatenate(low, 1)
+                w["d_w"] = jnp.concatenate(d_w, 1)
+            for w in work:
+                w["d_query"] = dot_nn(w["d_z"], w["keys"]) * scale
+            for w in work:
+                w["d_keys"] = dot_tn(w["d_z"], w["query"]) * scale
+            for w in work:
+                w["d_values"] = dot_tn(w["low"], w["d_out"])
+            for w in work:
+                at = slice(to * BLOCK, (to + 1) * BLOCK)
+                d_weight[to : to + 1, :] = w["d_w"]
+                low_out[at, : 2 * DH] = w["d_query"].astype(bf16)
+                for k, name in enumerate(("d_keys", "d_values")):
+                    parts = [w[name][i * BLOCK : (i + 1) * BLOCK, :] for i in range(4)]
+                    near_out[at, k * 2 * DH : (k + 1) * 2 * DH] = jnp.where(near, parts[0], parts[2])
+                    far = jnp.where(near, parts[1], parts[3])
+                    if k == 1:
+                        far = far * w["weight"]
+                    low_out[at, (k + 1) * 2 * DH : (k + 2) * 2 * DH] = far.astype(bf16)
+                to += 1
+
+
+def collect_kernel(pieces, *refs):
+    f32, bf16 = jnp.float32, jnp.bfloat16
+    count = len(pieces)
+    nears, lows, d_weights = refs[:count], refs[count : 2 * count], refs[2 * count : 3 * count]
+    partner, d_qkv, d_mine, d_weight, acc, far = refs[3 * count :]
+    me = lax.axis_index("blk")
+    place = place_of(me)
+    for parts, near_ref, low_ref, w_ref in zip(pieces, nears, lows, d_weights):
+        at = 0
+        for step, start, n in parts:
+            owner = ring_of((place + 8 - step) % 8)
+            to = pl.ds(pl.multiple_of(owner * SHARD + start, n), n)
+            acc[to, :] = near_ref[at : at + n, :]
+            far[to, :] = low_ref[at : at + n, 2 * DH :]
+            d_qkv[to, : 2 * DH] = low_ref[at : at + n, : 2 * DH]
+            if start == 0:
+                nb = SHARD // BLOCK
+                first = pl.multiple_of(owner * nb, nb)
+                d_weight[pl.ds(first, nb), :] = w_ref[at // BLOCK : at // BLOCK + nb, :]
+            at += n
+    near = first_lanes()
+    both = jnp.concatenate([near, near], 1)
+
+    def body(block, _):
+        tile = far[pl.ds(pl.multiple_of(block * BLOCK, BLOCK), BLOCK), :].astype(f32)
+        for h, kept in ((0, jnp.where(both, tile, 0.0)), (1, jnp.where(both, 0.0, tile))):
+            to = pl.ds(pl.multiple_of(partner[h, block] * BLOCK, BLOCK), BLOCK)
+            acc[to, :] += kept
+        return 0
+
+    lax.fori_loop(0, partner.shape[1], body, 0, unroll=4)
+    d_qkv[:, 2 * DH :] = acc[...].astype(bf16)
+    d_mine[...] = d_qkv[pl.ds(pl.multiple_of(me * SHARD, SHARD), SHARD), :]
+
+
+def sink_back_kernel(d_weight, steps, partner, summary, d_mine, g_sort, d_flat):
+    nb = partner.shape[1]
+    grads = []
+    for h in range(2):
+        total = jnp.sum(
+            d_weight[:, (2 * h + 1) * DH : (2 * h + 2) * DH], axis=1, keepdims=True
+        )
+        grads.append(choices(partner, h) * (nb * total))
+    last = steps.shape[0] - 1
+    grad = jnp.stack(grads) * steps[last]
+    for t in range(last, -1, -1):
+        grad = grad - steps[t] * jnp.sum(grad, axis=1 if t % 2 else 2, keepdims=True)
+    flat = jnp.concatenate([grad[0], grad[1]], 1) / TEMPER
+    d_flat[...] = flat
+    n = d_mine.shape[0]
+    d_mine[...] = d_flat[pl.ds(pl.multiple_of(lax.axis_index("blk") * n, n), n), :]
+    g_sort[...] = lax.dot_general(
+        summary[...],
+        flat,
+        (((0,), (0,)), ((), ())),
+        precision=HIGHEST,
+        preferred_element_type=jnp.float32,
+    )
+
+
+def weight_kernel(*refs):
+    own, f1, b1, f2, b2, f3, b3, f4, b4, xf1, xb1, xf2, xb2, xf3, xb3, xf4, xb4 = refs[:17]
+    d_qkv, g_qkv, h_all = refs[17:]
+    me = lax.axis_index("blk")
+    core = lax.axis_index("head") % 2
+    place = place_of(me)
+    rows = own.shape[0]
+    half, quarter = rows // 2, rows // 4
+
+    def put(owner, start, ref):
+        for at in range(0, ref.shape[0], quarter + EXTRA):
+            to = pl.multiple_of(owner * rows + start + (quarter if at else 0), quarter)
+            h_all[pl.ds(to, quarter), :] = ref[at : at + quarter, :]
+
+    h_all[pl.ds(pl.multiple_of(me * rows, rows), rows), :] = own[...]
+    for step, (f, b, xf, xb) in enumerate(
+        ((f1, b1, xf1, xb1), (f2, b2, xf2, xb2), (f3, b3, xf3, xb3)), 1
+    ):
+        for owner, a, o in (
+            (ring_of((place + 8 - step) % 8), f, xf),
+            (ring_of((place + step) % 8), b, xb),
+        ):
+            put(owner, core * half, a)
+            put(owner, (1 - core) * half, o)
+    far = ring_of((place + 4) % 8)
+    put(far, core * half, f4)
+    put(far, (1 - core) * half, xf4)
+    put(far, core * half + quarter, b4)
+    put(far, (1 - core) * half + quarter, xb4)
+    out = dot_tn(h_all[...], d_qkv[...])
+    width = g_qkv.shape[2]
+    for i in range(3):
+        g_qkv[i] = out[:, i * width : (i + 1) * width]
+
+
+def input_kernel(dq_a, dq_b, w_a, w_b, flat_a, flat_b, sort_a, sort_b, d_h, dq_full, w_full, flat_full, sort_full):
+    row = lax.axis_index("head") // 2
+    width = dq_a.shape[1]
+    for j, (g, w) in enumerate(((dq_a, w_a), (dq_b, w_b))):
+        at = pl.multiple_of((row ^ j) * width, width)
+        dq_full[:, pl.ds(at, width)] = g[...]
+        w_full[:, pl.ds(at, width)] = wide(w)
+    part = dot_nt(dq_full[...], w_full[...])
+    nb = flat_a.shape[1]
+    for j, (flat, sort) in enumerate(((flat_a, sort_a), (flat_b, sort_b))):
+        at = pl.multiple_of((row ^ j) * nb, nb)
+        flat_full[:, pl.ds(at, nb)] = flat[...]
+        sort_full[:, pl.ds(at, nb)] = sort[...]
+    d_sum = sum(dot_nt(p, sort_full[...]) for p in three_parts(flat_full[...])[::-1]) / BLOCK
+    blocks = d_sum.shape[0]
+    for i in range(blocks):
+        sl = slice(i * BLOCK, (i + 1) * BLOCK)
+        d_h[sl, :] = part[sl, :] + d_sum[i : i + 1, :]
+
+
+def end_kernel(tokens, gain, own, other, d_middle, g_two, d_tokens, g_gain):
+    f32 = jnp.float32
+    normed, inv = norm_parts(tokens[...].astype(f32))
+    d_h = own[...] + other[...]
+    g_gain[:8, :] = jnp.broadcast_to(jnp.sum(d_h * normed, 0, keepdims=True), g_two.shape)
+    g_gain[8:, :] = g_two[...]
+    d_tokens[...] = d_middle[...] + norm_back(d_h, normed, inv, gain[...].astype(f32))
+
+
+VMEM_SPEC = pl.BlockSpec(memory_space=pltpu.VMEM)
+SMEM_SPEC = pl.BlockSpec(memory_space=pltpu.SMEM)
+
+
+def call(kernel, outs, *args, scratch=(), smem=(), limit=16, name=None):
+    shapes = [jax.ShapeDtypeStruct(s, d) for s, d in outs]
+    result = pl.pallas_call(
+        kernel,
+        out_shape=shapes,
+        in_specs=[SMEM_SPEC if i in smem else VMEM_SPEC for i in range(len(args))],
+        out_specs=[VMEM_SPEC] * len(shapes),
+        scratch_shapes=[pltpu.VMEM(s, d) for s, d in scratch],
+        compiler_params=pltpu.CompilerParams(vmem_limit_bytes=limit * 1024 * 1024),
+        name=name,
+    )(*args)
+    return result[0] if len(shapes) == 1 else result
+
+
+def tie(*values):
+    return lax.optimization_barrier(values)
+
+
+def after(value, *others):
+    return lax.optimization_barrier((value,) + others)[0]
+
+
+RING = (0, 2, 4, 6, 7, 5, 3, 1)
+SHARD = 512
+EXTRA = 16
+
+
+def local_eight(
+    tokens, gain_attn, gain_ffn, w_qkv, w_out, w_sort, w_up, w_down, gumbel_noise, partner, cotangent
+):
+    f32, bf16 = jnp.float32, jnp.bfloat16
+    rows = tokens.shape[0]
+    blocks = rows // BLOCK
+    width = w_out.shape[0]
+    ff = w_up.shape[1]
+    nb = partner.shape[0]
+    total = nb * BLOCK
+    half, quarter = rows // 2, rows // 4
+    core = lax.axis_index("head") % 2
+
+    def ahead(v):
+        return lax.ppermute(v, "blk", [(RING[i], RING[(i + 1) % 8]) for i in range(8)])
+
+    def behind(v):
+        return lax.ppermute(v, "blk", [(RING[i], RING[(i - 1) % 8]) for i in range(8)])
+
+    def swap_head(v, j):
+        return lax.ppermute(v, "head", [(i, i ^ j) for i in range(4)])
+
+    def swap_blk(v, j):
+        return lax.ppermute(v, "blk", [(i, i ^ j) for i in range(8)])
+
+    w_in = w_qkv.transpose(1, 0, 2)
+    partner_s = partner.T
+
+    h_one, packed, own_summary, noise = call(
+        head_kernel,
+        [((rows, D), bf16), ((half + 2 * EXTRA, D), bf16), ((blocks, D), f32), ((2, D), f32)],
+        tokens, gain_attn, gumbel_noise, name="norm_one",
+    )
+
+    def project(pieces):
+        return call(
+            project_kernel, [((2 * rows, 3 * width), bf16), ((8 * EXTRA, D), bf16)],
+            *pieces, w_in, name="project",
+        )
+
+    f, b = ahead(packed), behind(packed)
+    up_y = swap_head(after(w_up, packed), 2)
+    qkv_own = call(project_own_kernel, [((rows, 3 * width), bf16)], h_one, w_in, name="project_own")
+    f1, b1, _ = tie(f, b, qkv_own)
+    f, b = ahead(f1), behind(b1)
+    wo_y = swap_head(after(w_out, f1, b1), 2)
+    f2, b2, _ = tie(f, b, up_y)
+    f, b = ahead(f2), behind(b2)
+    down_y = swap_head(after(w_down, f2, b2), 2)
+    f3, b3, _ = tie(f, b, wo_y)
+    f, b = call(
+        halve_kernel, [((quarter + EXTRA, D), bf16)] * 2, f3, b3, name="halve"
+    )
+    f4, b4 = ahead(f), behind(b)
+    cross = [swap_head(after(v, f), 1) for v in (f1, b1, f2, b2, f3, b3)]
+    wo_c = swap_head(after(w_out, f), 1)
+    wo_yc = swap_head(after(wo_y, f), 1)
+    xf1, xb1, xf2, xb2, xf3, xb3 = cross
+    projected = [
+        project((f1, xf1, b1, xb1)), project((f2, xf2, b2, xb2)), project((f3, xf3, b3, xb3)),
+    ]
+    f4, b4 = tie(f4, b4, wo_c, wo_yc, *[p[0] for p in projected])[:2]
+    xf4, xb4 = swap_head(f4, 1), swap_head(b4, 1)
+    qkv, context, summary, steps, scale_rows, weight_rows = call(
+        attend_kernel,
+        [
+            ((total, 3 * width), bf16),
+            ((rows, width), bf16),
+            ((nb, D), f32),
+            ((2 * SINK, 2, nb, nb), f32),
+            ((nb, 4 * DH), f32),
+            ((nb, 2 * DH), f32),
+        ],
+        qkv_own, *[p[0] for p in projected], *[p[1] for p in projected],
+        f4, b4, xf4, xb4, w_in, w_sort, own_summary, noise, partner_s, partner_s,
+        smem=(15,), scratch=[((nb, 2 * nb), f32)], name="attend",
+    )
+    ctx_y, ctx_c = swap_head(context, 2), swap_head(context, 1)
+    ctx_yc = swap_head(ctx_y, 1)
+    middle, h_two, active, d_hidden, ffn, d_h_two = call(
+        feed_kernel,
+        [
+            ((rows, D), f32),
+            ((rows, D), bf16),
+            ((rows, ff), bf16),
+            ((rows, ff), bf16),
+            ((rows, D), f32),
+            ((rows, D), f32),
+        ],
+        tokens, cotangent, gain_ffn, context, ctx_c, ctx_y, ctx_yc, w_out, wo_c, wo_y, wo_yc,
+        w_up, up_y, w_down, down_y,
+        scratch=[
+            ((rows, 4 * width), bf16), ((4 * width, D), bf16), ((D, 2 * ff), bf16), ((2 * ff, D), bf16),
+            ((rows, 2 * ff), bf16), ((rows, 2 * ff), bf16),
+        ],
+        name="feed",
+    )
+    d_h_two_other = swap_head(d_h_two, 1)
+    piece, few = D // 4, width // 8
+    parts = call(
+        grads_kernel,
+        [((piece, D), f32)] * 4 + [((piece, D), bf16)] * 4,
+        h_two, d_hidden, active, cotangent, scratch=[((D, D), f32), ((D, D), f32)], name="grads",
+    )
+    keeps, sends = parts[:4], parts[4:]
+    d_h_two_other, _ = tie(d_h_two_other, keeps[0])
+    d_middle, d_low, d_ctx, g_two = call(
+        back_kernel,
+        [((rows, D), f32), ((rows, D), bf16), ((rows, width), bf16), ((8, D), f32)],
+        middle, d_h_two, d_h_two_other, cotangent, gain_ffn, w_out, name="back",
+    )
+
+    plans = [[(0, 0)]] + [[(k, 0), (-k, 0)] for k in (1, 2, 3)] + [[(4, 0), (4, half)]]
+    pulled = []
+
+    def pull(given):
+        plan = plans[len(pulled)]
+        n = sum(a.shape[0] for a in given)
+        pulled.append(
+            call(
+                functools.partial(pull_kernel, tuple(plan)),
+                [((n, 4 * DH), f32), ((n, 6 * DH), bf16), ((n // BLOCK, 4 * DH), f32)],
+                *given, qkv, partner_s, scale_rows, weight_rows, smem=(len(given) + 1,), name="pull",
+            )
+        )
+        return pulled[-1][0]
+
+    f, b = ahead(d_ctx), behind(d_ctx)
+    keep_out, send_out = call(
+        out_grad_kernel, [((width // 2, D), f32), ((width // 2, D), bf16)], context, d_low,
+        scratch=[((width, D), f32)], name="out_grad",
+    )
+    arrived_out = swap_blk(send_out, 1)
+    arrived = [None] * 4
+    sent = []
+    order = (1, 2, 3, 0)
+    given = [d_ctx]
+    arrays = [given]
+    ready = (d_ctx,)
+    for step in range(4):
+        j = order[step]
+        arrived[j] = swap_blk(after(sends[j], *ready), 1)
+        extra = []
+        if step:
+            j = order[step - 1]
+            summed = call(
+                functools.partial(join_kernel, j), [((piece + few, D), bf16)],
+                keeps[j], arrived[j], keep_out, arrived_out, scratch=[((4 * few, D), f32)], name="join",
+            )
+            sent.append(swap_blk(summed, 2 * j))
+            extra.append(summed)
+        done = pull(given)
+        if step == 0:
+            in_y = swap_head(after(w_in, d_ctx), 2)
+        if step == 1:
+            sort_y = swap_head(after(w_sort, f), 2)
+            ffn_other = swap_head(after(ffn, f), 1)
+            extra.append(in_y)
+        if step < 3:
+            extra.append(arrived[order[step]])
+        if step == 0:
+            extra.append(arrived_out)
+        f, b = tie(f, b, done, *extra)[:2]
+        given = [f, b]
+        arrays.append(given)
+        ready = (f, b)
+        if step < 2:
+            f, b = ahead(f), behind(b)
+        elif step == 2:
+            f, b = call(halve_kernel, [((half, width), bf16)] * 2, f, b, name="halve")
+            f, b = ahead(f), behind(b)
+    pull(given)
+    spans = tuple(
+        tuple((step, start, a.shape[0]) for (step, start), a in zip(plan, given))
+        for plan, given in zip(plans, arrays)
+    )
+    d_qkv, d_mine, d_weight = call(
+        functools.partial(collect_kernel, spans),
+        [((total, 3 * width), bf16), ((rows, 3 * width), bf16), ((nb, 4 * DH), f32)],
+        *[p[k] for k in range(3) for p in pulled], partner_s, smem=(15,),
+        scratch=[((total, 4 * DH), f32), ((total, 4 * DH), bf16)], name="collect",
+    )
+    d_mine_y = swap_head(d_mine, 2)
+    owned = call(
+        total_kernel, [((piece + few, D), bf16)],
+        keeps[0], arrived[0], keep_out, arrived_out, *sent, scratch=[((4 * few, D), f32)], name="total",
+    )
+    own_x, z1, z2, z3 = swap_blk(owned, 1), swap_blk(owned, 2), swap_blk(owned, 4), swap_blk(owned, 6)
+    flat_mine, g_sort = call(
+        sink_back_kernel,
+        [((blocks, 2 * nb), f32), ((D, 2 * nb), f32)],
+        after(d_weight, owned), steps, partner_s, summary, scratch=[((nb, 2 * nb), f32)],
+        name="sinkhorn_back",
+    )
+    flat_y = swap_head(flat_mine, 2)
+    d_h = call(
+        input_kernel, [((rows, D), f32)],
+        d_mine, d_mine_y, w_in, in_y, flat_mine, flat_y, w_sort, sort_y,
+        scratch=[
+            ((rows, 6 * width), bf16), ((D, 6 * width), bf16), ((blocks, 4 * nb), f32), ((D, 4 * nb), bf16),
+        ],
+        name="input_back",
+    )
+    d_h_other = swap_head(d_h, 1)
+    g_qkv = call(
+        weight_kernel, [((3, D, width), f32)],
+        h_one, f1, b1, f2, b2, f3, b3, f4, b4, xf1, xb1, xf2, xb2, xf3, xb3, xf4, xb4,
+        after(d_qkv, flat_mine), scratch=[((total, D), bf16)], limit=24, name="weights",
+    )
+    d_h_other, g_qkv, z1 = tie(d_h_other, g_qkv, z1)
+    d_tokens, gains = call(
+        end_kernel, [((rows, D), f32), ((16, D), f32)],
+        tokens, gain_attn, d_h, d_h_other, d_middle, g_two, name="norm_one_back",
+    )
+    gains = call(add_kernel, [((16, D), f32)], gains, swap_blk(gains, 1), name="add_gains")
+    gains1, gains2, gains3 = swap_blk(gains, 2), swap_blk(gains, 4), swap_blk(gains, 6)
+    x1, x2, x3 = swap_blk(z1, 1), swap_blk(z2, 1), swap_blk(z3, 1)
+    output = call(add_kernel, [((rows, D), f32)], after(ffn, d_h_other), ffn_other, middle, name="output")
+    g_up, g_down, g_out = call(
+        lay_kernel,
+        [((D, ff), f32), ((ff, D), f32), ((width, D), f32)],
+        owned, z1, z2, z3, own_x, x1, x2, x3, name="lay",
+    )
+    g_one, g_two = call(
+        gains_kernel, [((D,), f32), ((D,), f32)], gains, gains1, gains2, gains3, name="gains"
+    )
+    return output, d_tokens, g_one, g_two, g_qkv.transpose(1, 0, 2), g_out, g_sort, g_up, g_down
+
+
 def solution(mesh):
     in_specs = (
         P("blk", None),
@@ -278,4 +1113,5 @@
         P(None, "head"),
         P("head", None),
     )
-    return jax.shard_map(local, mesh=mesh, in_specs=in_specs, out_specs=out_specs, check_vma=False)
+    plan = local_eight if mesh.shape["blk"] == 8 and mesh.shape["head"] == 4 else local
+    return jax.shard_map(plan, mesh=mesh, in_specs=in_specs, out_specs=out_specs, check_vma=False)

time: 576 us -> 154 us (0.27)
  waiting for transfers between devices: 248 us -> 51.7 us
  blocking collectives: 158 us -> 0 us
  other arithmetic: 55.5 us -> 0 us
  starting transfers between devices: 13.5 us -> 54.9 us
  Pallas kernels: 0 us -> 41.1 us
  local copies, waits for them, and re-layouts: 45.3 us -> 4.45 us
  matrix products: 34.2 us -> 0 us
  between operations: 17.2 us -> 1.04 us
    psum x5 -> x0, waiting for transfers between devices: 248 us -> none  [the longest x1 118 us: local(): lax.psum((g_gain_one, g_gain_two, g_qkv, g_out, g_sort, g_up, g_down), 'b...]
    unnamed x1 -> x0, blocking collectives: 68.9 us -> none
    all_gather x1 -> x0, blocking collectives: 66.2 us -> none  [local(): every_rows = lax.all_gather(own_rows, 'blk', axis=0, tiled=True)]
    ppermute x0 -> x58, starting transfers between devices: none -> 54.9 us  [the longest x19 22.9 us: swap_blk(): return lax.ppermute(v, 'blk', [(i, i ^ j) for i in range(8)])]
    ppermute x0 -> x58, waiting for transfers between devices: none -> 51.7 us  [the longest x19 19.8 us: swap_blk(): return lax.ppermute(v, 'blk', [(i, i ^ j) for i in range(8)])]
    pallas_call x0 -> x30, Pallas kernels: none -> 41.1 us  [call(): pl.pallas_call(kernel, out_shape=shapes, in_specs=[SMEM_SPEC if i in smem...]
    dot_general x29 -> x0, matrix products: 34.2 us -> none  [the longest x1 3.32 us: local(): jnp.einsum('st,sf->tf', selector, returned.reshape(dev_count * requests,...]
    reduce_sum x58 -> x0, other arithmetic: 29.8 us -> none  [the longest x8 4.11 us: balancing_log_space(): sort_logits = sort_logits - log_total(sort_logits, 1)]
  transfers between devices with their start and end apart: 7 -> 58, of which waited for: 5 -> 27; matrix products, arithmetic and copies ran while one was open for 7% -> 0% of each run, Pallas kernels for 0% -> 18%
where the time goes in v3:
time: 154 us; the launch traced here: 153 us
  starting transfers between devices  54.9 us (36%)
  waiting for transfers between devices  51.7 us (34%)
  Pallas kernels  41.1 us (27%)
  local copies, waits for them, and re-layouts  4.45 us (3%)
    pallas_call x30, Pallas kernels, call(): pl.pallas_call(kernel, out_shape=shapes, in_specs=[SMEM_SPEC if i in smem...  41.1 us
    ppermute x19, starting transfers between devices, swap_blk(): return lax.ppermute(v, 'blk', [(i, i ^ j) for i in range(8)])  22.9 us
    ppermute x19, waiting for transfers between devices, swap_blk(): return lax.ppermute(v, 'blk', [(i, i ^ j) for i in range(8)])  19.8 us
    ppermute x23, waiting for transfers between devices, swap_head(): return lax.ppermute(v, 'head', [(i, i ^ j) for i in range(4)])  19.1 us
    ppermute x23, starting transfers between devices, swap_head(): return lax.ppermute(v, 'head', [(i, i ^ j) for i in range(4)])  14.7 us
    ppermute x8, starting transfers between devices, ahead(): lax.ppermute(v, 'blk', [(RING[i], RING[(i + 1) % 8]) for i in range(8)])  10.4 us
    ppermute x8, waiting for transfers between devices, ahead(): lax.ppermute(v, 'blk', [(RING[i], RING[(i + 1) % 8]) for i in range(8)])  8.28 us
    ppermute x8, starting transfers between devices, behind(): lax.ppermute(v, 'blk', [(RING[i], RING[(i - 1) % 8]) for i in range(8)])  6.92 us
  transfers between devices with their start and end apart: 58, of which 27 were waited for; matrix products, arithmetic and copies ran while one was open for 0% of the time, Pallas kernels for 18%

profile of v3, /device:TPU:0, one launch (start us, length us, event | category | flops | bytes accessed | tf_op | source)
XLA Modules:
  0.0 153.2 jit_solution(12159456757803947515)
XLA Ops:
  3.6 3.1 %collective-permute-start = (bf16[288,512]{1,0:T(8,128)(2,1)S(1)}, bf16[288,512]{1,0:T(8,128)(2,1)S(1)}, u32[]{:S(2)}, u32[]{:S(2)}) collective-permute-start(bf16[288,512]{1,0:T(8,128)(2,1)S(1)} %get-tuple-element.118), channel_id=1, source_target_pairs={{0,8},{8,16},{16,24},{24,28},{28,20},{20,12},{12,4},{4,0},{1,9},{9... | collective-permute-start | bytes 884744 | tf_op jit(solution)/shard_map/ppermute | solution.py:876
  6.6 2.0 %collective-permute-start.4 = (bf16[512,512]{1,0:T(8,128)(2,1)}, bf16[512,512]{1,0:T(8,128)(2,1)S(1)}, u32[]{:S(2)}, u32[]{:S(2)}) collective-permute-start(bf16[512,512]{1,0:T(8,128)(2,1)} %up_a.1), channel_id=1, source_target_pairs={{0,2},{1,3},{2,0},{3,1},{4,6},{5,7},{6,4},{7,5},{8,10},{9,11},{10,... | collective-permute-start | bytes 1572872 | tf_op jit(solution)/shard_map/ppermute | solution.py:882
  10.0 3.5 %collective-permute-done.f.refs_1_ = bf16[288,512]{1,0:T(8,128)(2,1)S(1)} collective-permute-done((bf16[288,512]{1,0:T(8,128)(2,1)S(1)}, bf16[288,512]{1,0:T(8,128)(2,1)S(1)}, u32[]{:S(2)}, u32[]{:S(2)}) %collective-permute-start) | collective-permute-done | bytes 294944 | tf_op jit(solution)/shard_map/ppermute | solution.py:876
  13.6 1.5 %collective-permute-done.1.b.refs_2_ = bf16[288,512]{1,0:T(8,128)(2,1)S(1)} collective-permute-done((bf16[288,512]{1,0:T(8,128)(2,1)S(1)}, bf16[288,512]{1,0:T(8,128)(2,1)S(1)}, u32[]{:S(2)}, u32[]{:S(2)}) %collective-permute-start.1) | collective-permute-done | bytes 294944 | tf_op jit(solution)/shard_map/ppermute | solution.py:879
  15.1 1.6 %collective-permute-start.2 = (bf16[288,512]{1,0:T(8,128)(2,1)S(1)}, bf16[288,512]{1,0:T(8,128)(2,1)S(1)}, u32[]{:S(2)}, u32[]{:S(2)}) collective-permute-start(bf16[288,512]{1,0:T(8,128)(2,1)S(1)} %collective-permute-done.f.refs_1_), channel_id=1, source_target_pairs={{0,8},{8,16},{16,24},{24,28},{28,20},{20,12},{12,4},{4,0},{1,9},{9... | collective-permute-start | bytes 884744 | tf_op jit(solution)/shard_map/ppermute | solution.py:876
  17.1 3.1 %collective-permute-done.4.up_b = bf16[512,512]{1,0:T(8,128)(2,1)S(1)} collective-permute-done((bf16[512,512]{1,0:T(8,128)(2,1)}, bf16[512,512]{1,0:T(8,128)(2,1)S(1)}, u32[]{:S(2)}, u32[]{:S(2)}) %collective-permute-start.4) | collective-permute-done | bytes 524320 | tf_op jit(solution)/shard_map/ppermute | solution.py:882
  20.2 2.4 %collective-permute-done.2.f.refs_3_ = bf16[288,512]{1,0:T(8,128)(2,1)S(1)} collective-permute-done((bf16[288,512]{1,0:T(8,128)(2,1)S(1)}, bf16[288,512]{1,0:T(8,128)(2,1)S(1)}, u32[]{:S(2)}, u32[]{:S(2)}) %collective-permute-start.2) | collective-permute-done | bytes 294944 | tf_op jit(solution)/shard_map/ppermute | solution.py:876
  24.0 1.6 %collective-permute-start.5 = (bf16[288,512]{1,0:T(8,128)(2,1)S(1)}, bf16[288,512]{1,0:T(8,128)(2,1)S(1)}, u32[]{:S(2)}, u32[]{:S(2)}) collective-permute-start(bf16[288,512]{1,0:T(8,128)(2,1)S(1)} %collective-permute-done.2.f.refs_3_), channel_id=1, source_target_pairs={{0,8},{8,16},{16,24},{24,28},{28,20},{20,12},{12,4},{4,0},{1,9},{9... | collective-permute-start | bytes 884744 | tf_op jit(solution)/shard_map/ppermute | solution.py:876
  26.0 1.5 collective-permute-start.7
  27.5 3.7 %collective-permute-done.7.wo2 = bf16[128,512]{1,0:T(8,128)(2,1)S(1)} collective-permute-done((bf16[128,512]{1,0:T(8,128)(2,1)}, bf16[128,512]{1,0:T(8,128)(2,1)S(1)}, u32[]{:S(2)}, u32[]{:S(2)}) %collective-permute-start.7) | collective-permute-done | bytes 131104 | tf_op jit(solution)/shard_map/ppermute | solution.py:882
  34.4 1.5 collective-permute-start.14
  36.9 1.5 collective-permute-start.23
  43.3 3.7 %attend.1 = (bf16[4096,384]{1,0:T(8,128)(2,1)S(1)}, bf16[512,128]{1,0:T(8,128)(2,1)S(1)}, f32[64,512]{1,0:T(8,128)S(1)}, f32[16,2,64,64]{3,2,1,0:T(8,128)S(1)}, ...) custom-call(bf16[512,384]{1,0:T(8,128)(2,1)S(1)} %project_own.1.own, bf16[1024,384]{1,0:T(8,128)(2,1)S(1)} %get-tuple-element.130.step1, ...), custom_call_target="tpu_custom_call" | custom-call | tf_op jit(solution)/shard_map/attend/pallas_call | solution.py:837
  48.4 5.5 %collective-permute-done.21.ctx2 = bf16[512,128]{1,0:T(8,128)(2,1)S(1)} collective-permute-done((bf16[512,128]{1,0:T(8,128)(2,1)S(1)}, bf16[512,128]{1,0:T(8,128)(2,1)S(1)}, u32[]{:S(2)}, u32[]{:S(2)}) %collective-permute-start.21) | collective-permute-done | bytes 131104 | tf_op jit(solution)/shard_map/ppermute | solution.py:882
  55.2 4.2 %feed.1 = (f32[512,512]{1,0:T(8,128)S(1)}, bf16[512,512]{1,0:T(8,128)(2,1)S(1)}, bf16[512,512]{1,0:T(8,128)(2,1)S(1)}, bf16[512,512]{1,0:T(8,128)(2,1)S(1)}, f32...) custom-call(bf16[512,512]{1,0:T(8,128)(2,1)S(1)} %copy-done.4, bf16[512,512]{1,0:T(8,128)(2,1)S(1)} %copy-done.5, ...), custom_call_target="tpu_custom_call" | custom-call | tf_op jit(solution)/shard_map/feed/pallas_call | solution.py:837
  60.6 1.6 %collective-permute-done.24.other = f32[512,512]{1,0:T(8,128)S(1)} collective-permute-done((f32[512,512]{1,0:T(8,128)S(1)}, f32[512,512]{1,0:T(8,128)S(1)}, u32[]{:S(2)}, u32[]{:S(2)}) %collective-permute-start.24) | collective-permute-done | bytes 1048608 | tf_op jit(solution)/shard_map/ppermute | solution.py:882
  63.1 1.6 %collective-permute-start.31 = (bf16[3,512,128]{2,1,0:T(8,128)(2,1)S(1)}, bf16[3,512,128]{2,1,0:T(8,128)(2,1)S(1)}, u32[]{:S(2)}, u32[]{:S(2)}) collective-permute-start(bf16[3,512,128]{2,1,0:T(8,128)(2,1)S(1)} %bitcast.8), channel_id=1, source_target_pairs={{0,2},{1,3},{2,0},{3,1},{4,6},{5,7},{6,4},{7,5},{8,10},{9,11},{10,... | collective-permute-start | bytes 1179656 | tf_op jit(solution)/shard_map/ppermute | solution.py:882
  67.5 1.6 %collective-permute-start.28 = (bf16[64,512]{1,0:T(8,128)(2,1)S(1)}, bf16[64,512]{1,0:T(8,128)(2,1)S(1)}, u32[]{:S(2)}, u32[]{:S(2)}) collective-permute-start(bf16[64,512]{1,0:T(8,128)(2,1)S(1)} %get-tuple-element.165), channel_id=1, source_target_pairs={{0,4},{4,0},{8,12},{12,8},{16,20},{20,16},{24,28},{28,24},{1,5},{5... | collective-permute-start | bytes 196616 | tf_op jit(solution)/shard_map/ppermute | solution.py:885
  69.2 1.9 %pull.5 = (f32[512,256]{1,0:T(8,128)S(1)}, bf16[512,384]{1,0:T(8,128)(2,1)S(1)}, f32[8,256]{1,0:T(8,128)S(1)}) custom-call(bf16[512,128]{1,0:T(8,128)(2,1)S(1)} %get-tuple-element.157.refs_0_, bf16[4096,384]{1,0:T(8,128)(2,1)S(1)} %get-tuple-element.158.refs_1_.refs_2_, s32[2,64]{1,0:T(2,128)S(1)} %bitcast.12, ...), custom_call_target="tpu_custom_call" | custom-call | tf_op jit(solution)/shard_map/pull/pallas_call | solution.py:837
  71.1 3.1 %collective-permute-done.28.arrived_out = bf16[64,512]{1,0:T(8,128)(2,1)S(1)} collective-permute-done((bf16[64,512]{1,0:T(8,128)(2,1)S(1)}, bf16[64,512]{1,0:T(8,128)(2,1)S(1)}, u32[]{:S(2)}, u32[]{:S(2)}) %collective-permute-start.28) | collective-permute-done | bytes 65568 | tf_op jit(solution)/shard_map/ppermute | solution.py:885
  75.0 1.8 %collective-permute-start.30 = (bf16[512,128]{1,0:T(8,128)(2,1)S(1)}, bf16[512,128]{1,0:T(8,128)(2,1)S(1)}, u32[]{:S(2)}, u32[]{:S(2)}) collective-permute-start(bf16[512,128]{1,0:T(8,128)(2,1)S(1)} %collective-permute-done.26.refs_1_), channel_id=1, source_target_pairs={{0,4},{8,0},{16,8},{24,16},{28,24},{20,28},{12,20},{4,12},{1,5},{9... | collective-permute-start | bytes 393224 | tf_op jit(solution)/shard_map/ppermute | solution.py:879
  76.8 3.2 %pull.6 = (f32[1024,256]{1,0:T(8,128)S(1)}, bf16[1024,384]{1,0:T(8,128)(2,1)S(1)}, f32[16,256]{1,0:T(8,128)S(1)}) custom-call(bf16[512,128]{1,0:T(8,128)(2,1)S(1)} %collective-permute-done.25.refs_0_, bf16[512,128]{1,0:T(8,128)(2,1)S(1)} %collective-permute-done.26.refs_1_, bf16[4096,384]{1,0:T(8,128)(2,1)S(1)} %get-tuple-element.158.refs_1_.refs_2_, ...), custom_call_target="tpu_custom_call" | custom-call | tf_op jit(solution)/shard_map/pull/pallas_call | solution.py:837
  84.1 3.2 %pull.7 = (f32[1024,256]{1,0:T(8,128)S(1)}, bf16[1024,384]{1,0:T(8,128)(2,1)S(1)}, f32[16,256]{1,0:T(8,128)S(1)}) custom-call(bf16[512,128]{1,0:T(8,128)(2,1)S(1)} %collective-permute-done.29.refs_0_, bf16[512,128]{1,0:T(8,128)(2,1)S(1)} %collective-permute-done.30.refs_1_, bf16[4096,384]{1,0:T(8,128)(2,1)S(1)} %get-tuple-element.158.refs_1_.refs_2_, ...), custom_call_target="tpu_custom_call" | custom-call | tf_op jit(solution)/shard_map/pull/pallas_call | solution.py:837
  89.0 2.0 %collective-permute-start.37 = (bf16[256,128]{1,0:T(8,128)(2,1)S(1)}, bf16[256,128]{1,0:T(8,128)(2,1)S(1)}, u32[]{:S(2)}, u32[]{:S(2)}) collective-permute-start(bf16[256,128]{1,0:T(8,128)(2,1)S(1)} %get-tuple-element.184), channel_id=1, source_target_pairs={{0,4},{8,0},{16,8},{24,16},{28,24},{20,28},{12,20},{4,12},{1,5},{9... | collective-permute-start | bytes 196616 | tf_op jit(solution)/shard_map/ppermute | solution.py:879
  90.9 3.2 %pull.8 = (f32[1024,256]{1,0:T(8,128)S(1)}, bf16[1024,384]{1,0:T(8,128)(2,1)S(1)}, f32[16,256]{1,0:T(8,128)S(1)}) custom-call(bf16[512,128]{1,0:T(8,128)(2,1)S(1)} %collective-permute-done.33.refs_0_.f, bf16[512,128]{1,0:T(8,128)(2,1)S(1)} %collective-permute-done.34.refs_1_.b, bf16[4096,384]{1,0:T(8,128)(2,1)S(1)} %get-tuple-element.158.refs_1_.refs_2_, ...), custom_call_target="tpu_custom_call" | custom-call | tf_op jit(solution)/shard_map/pull/pallas_call | solution.py:837
  94.2 2.0 %pull.9 = (f32[512,256]{1,0:T(8,128)S(1)}, bf16[512,384]{1,0:T(8,128)(2,1)S(1)}, f32[8,256]{1,0:T(8,128)S(1)}) custom-call(bf16[256,128]{1,0:T(8,128)(2,1)S(1)} %collective-permute-done.36.refs_0_, bf16[256,128]{1,0:T(8,128)(2,1)S(1)} %collective-permute-done.37.refs_1_, bf16[4096,384]{1,0:T(8,128)(2,1)S(1)} %get-tuple-element.158.refs_1_.refs_2_, ...), custom_call_target="tpu_custom_call" | custom-call | tf_op jit(solution)/shard_map/pull/pallas_call | solution.py:837
  96.2 2.5 %collect.1 = (bf16[4096,384]{1,0:T(8,128)(2,1)S(1)}, bf16[512,384]{1,0:T(8,128)(2,1)S(1)}, f32[64,256]{1,0:T(8,128)S(1)}) custom-call(f32[512,256]{1,0:T(8,128)S(1)} %get-tuple-element.161.refs_0_, f32[1024,256]{1,0:T(8,128)S(1)} %get-tuple-element.168.refs_1_, f32[1024,256]{1,0:T(8,128)S(1)} %get-tuple-element.176.refs_2_, ...), custom_call_target="tpu_custom_call" | custom-call | tf_op jit(solution)/shard_map/collect/pallas_call | solution.py:837
  99.5 1.5 collective-permute-start.41
  101.0 2.6 %collective-permute-start.42 = (bf16[144,512]{1,0:T(8,128)(2,1)S(1)}, bf16[144,512]{1,0:T(8,128)(2,1)S(1)}, u32[]{:S(2)}, u32[]{:S(2)}) collective-permute-start(bf16[144,512]{1,0:T(8,128)(2,1)S(1)} %join.5), channel_id=1, source_target_pairs={{0,24},{4,28},{8,16},{12,20},{16,8},{20,12},{24,0},{28,4},{1,25},{... | collective-permute-start | bytes 442376 | tf_op jit(solution)/shard_map/ppermute | solution.py:885
  104.9 1.5 %collective-permute-start.44 = (bf16[512,128]{1,0:T(8,128)(2,1)S(1)}, bf16[512,128]{1,0:T(8,128)(2,1)S(1)}, u32[]{:S(2)}, u32[]{:S(2)}) collective-permute-start(bf16[512,128]{1,0:T(8,128)(2,1)S(1)} %copy-done.9), channel_id=1, source_target_pairs={{0,2},{1,3},{2,0},{3,1},{4,6},{5,7},{6,4},{7,5},{8,10},{9,11},{10,... | collective-permute-start | bytes 393224 | tf_op jit(solution)/shard_map/ppermute | solution.py:882
  106.4 2.8 %collective-permute-done.41.two = bf16[144,512]{1,0:T(8,128)(2,1)S(1)} collective-permute-done((bf16[144,512]{1,0:T(8,128)(2,1)S(1)}, bf16[144,512]{1,0:T(8,128)(2,1)S(1)}, u32[]{:S(2)}, u32[]{:S(2)}) %collective-permute-start.41) | collective-permute-done | bytes 147488 | tf_op jit(solution)/shard_map/ppermute | solution.py:885
  109.3 2.1 %sinkhorn_back.1 = (f32[8,128]{1,0:T(8,128)S(1)}, f32[512,128]{1,0:T(8,128)}) custom-call(f32[64,256]{1,0:T(8,128)S(1)} %get-tuple-element.203.d_weight, f32[16,2,64,64]{3,2,1,0:T(8,128)S(1)} %get-tuple-element.204.steps, s32[2,64]{1,0:T(2,128)S(1)} %bitcast.18, f32[64,512]{1,0:T(8,128)S(1)} %get-tuple-element.205.summary), custom_call_target="tpu_custom_call" | custom-call | tf_op jit(solution)/shard_map/sinkhorn_back/pallas_call | solution.py:837
  111.4 1.6 %collective-permute-start.43 = (f32[8,128]{1,0:T(8,128)S(1)}, f32[8,128]{1,0:T(8,128)S(1)}, u32[]{:S(2)}, u32[]{:S(2)}) collective-permute-start(f32[8,128]{1,0:T(8,128)S(1)} %get-tuple-element.206.flat_a), channel_id=1, source_target_pairs={{0,2},{1,3},{2,0},{3,1},{4,6},{5,7},{6,4},{7,5},{8,10},{9,11},{10,... | collective-permute-start | bytes 12296 | tf_op jit(solution)/shard_map/ppermute | solution.py:882
  113.0 2.0 %collective-permute-done.43.flat_b = f32[8,128]{1,0:T(8,128)S(1)} collective-permute-done((f32[8,128]{1,0:T(8,128)S(1)}, f32[8,128]{1,0:T(8,128)S(1)}, u32[]{:S(2)}, u32[]{:S(2)}) %collective-permute-start.43) | collective-permute-done | bytes 4128 | tf_op jit(solution)/shard_map/ppermute | solution.py:882
  116.7 2.1 %collective-permute-start.46 = (bf16[144,512]{1,0:T(8,128)(2,1)S(1)}, bf16[144,512]{1,0:T(8,128)(2,1)S(1)}, u32[]{:S(2)}, u32[]{:S(2)}) collective-permute-start(bf16[144,512]{1,0:T(8,128)(2,1)S(1)} %total.1.own), channel_id=1, source_target_pairs={{0,8},{4,12},{8,0},{12,4},{16,24},{20,28},{24,16},{28,20},{1,9},{5... | collective-permute-start | bytes 442376 | tf_op jit(solution)/shard_map/ppermute | solution.py:885
  119.3 1.9 %collective-permute-start.53 = (bf16[144,512]{1,0:T(8,128)(2,1)S(1)}, bf16[144,512]{1,0:T(8,128)(2,1)S(1)}, u32[]{:S(2)}, u32[]{:S(2)}) collective-permute-start(bf16[144,512]{1,0:T(8,128)(2,1)S(1)} %total.1.own), channel_id=1, source_target_pairs={{0,24},{4,28},{8,16},{12,20},{16,8},{20,12},{24,0},{28,4},{1,25},{... | collective-permute-start | bytes 442376 | tf_op jit(solution)/shard_map/ppermute | solution.py:885
  121.2 3.5 %weights.1 = f32[3,512,128]{2,1,0:T(8,128)} custom-call(bf16[512,512]{1,0:T(8,128)(2,1)S(1)} %get-tuple-element.117.h_one.refs_0_, bf16[288,512]{1,0:T(8,128)(2,1)S(1)} %collective-permute-done.f.refs_1_, bf16[288,512]{1,0:T(8,128)(2,1)S(1)} %collective-permute-done.1.b.refs_2_, bf16[288,512]{1,0:T(8,128)(2,1)S(1)} %collective-permute-done.2.f.refs_3_, ...), custom_call_target="tpu_custom_call" | custom-call | tf_op jit(solution)/shard_map/weights/pallas_call | solution.py:837
  125.0 1.8 %norm_one_back.1 = (f32[512,512]{1,0:T(8,128)}, f32[16,512]{1,0:T(8,128)S(1)}) custom-call(bf16[512,512]{1,0:T(8,128)(2,1)S(1)} %copy-done.4, bf16[512]{0:T(512)(128)(2,1)S(1)} %copy-done.14, f32[512,512]{1,0:T(8,128)S(1)} %input_back.1.own, f32[512,512]{1,0:T(8,128)S(1)} %collective-permute-done.45.other, f32[512,512]{1,0:T(8,128)S(1)} %get-tuple-element.213.d_middle, ...), custom_call_target="tpu_custom_call" | custom-call | tf_op jit(solution)/shard_map/norm_one_back/pallas_call | solution.py:837
  126.8 1.5 collective-permute-start.48
  128.8 4.0 %collective-permute-done.52.z2 = bf16[144,512]{1,0:T(8,128)(2,1)S(1)} collective-permute-done((bf16[144,512]{1,0:T(8,128)(2,1)S(1)}, bf16[144,512]{1,0:T(8,128)(2,1)S(1)}, u32[]{:S(2)}, u32[]{:S(2)}) %collective-permute-start.52) | collective-permute-done | bytes 147488 | tf_op jit(solution)/shard_map/ppermute | solution.py:885
  132.8 1.6 %collective-permute-start.56 = (bf16[144,512]{1,0:T(8,128)(2,1)S(1)}, bf16[144,512]{1,0:T(8,128)(2,1)S(1)}, u32[]{:S(2)}, u32[]{:S(2)}) collective-permute-start(bf16[144,512]{1,0:T(8,128)(2,1)S(1)} %collective-permute-done.52.z2), channel_id=1, source_target_pairs={{0,4},{4,0},{8,12},{12,8},{16,20},{20,16},{24,28},{28,24},{1,5},{5... | collective-permute-start | bytes 442376 | tf_op jit(solution)/shard_map/ppermute | solution.py:885
  134.8 1.6 %collective-permute-start.55 = (bf16[144,512]{1,0:T(8,128)(2,1)S(1)}, bf16[144,512]{1,0:T(8,128)(2,1)S(1)}, u32[]{:S(2)}, u32[]{:S(2)}) collective-permute-start(bf16[144,512]{1,0:T(8,128)(2,1)S(1)} %collective-permute-done.46.z1), channel_id=1, source_target_pairs={{0,4},{4,0},{8,12},{12,8},{16,20},{20,16},{24,28},{28,24},{1,5},{5... | collective-permute-start | bytes 442376 | tf_op jit(solution)/shard_map/ppermute | solution.py:885
  137.5 3.0 %collective-permute-done.49.one = f32[16,512]{1,0:T(8,128)S(1)} collective-permute-done((f32[16,512]{1,0:T(8,128)S(1)}, f32[16,512]{1,0:T(8,128)S(1)}, u32[]{:S(2)}, u32[]{:S(2)}) %collective-permute-start.49) | collective-permute-done | bytes 32800 | tf_op jit(solution)/shard_map/ppermute | solution.py:885
  140.4 1.4 collective-permute-start.50
  141.9 3.4 %collective-permute-done.50.two = f32[16,512]{1,0:T(8,128)S(1)} collective-permute-done((f32[16,512]{1,0:T(8,128)S(1)}, f32[16,512]{1,0:T(8,128)S(1)}, u32[]{:S(2)}, u32[]{:S(2)}) %collective-permute-start.50) | collective-permute-done | bytes 32800 | tf_op jit(solution)/shard_map/ppermute | solution.py:885
  145.3 1.7 %collective-permute-start.51 = (f32[16,512]{1,0:T(8,128)S(1)}, f32[16,512]{1,0:T(8,128)S(1)}, u32[]{:S(2)}, u32[]{:S(2)}) collective-permute-start(f32[16,512]{1,0:T(8,128)S(1)} %add_gains.1.here), channel_id=1, source_target_pairs={{0,24},{4,28},{8,16},{12,20},{16,8},{20,12},{24,0},{28,4},{1,25},{... | collective-permute-start | bytes 98312 | tf_op jit(solution)/shard_map/ppermute | solution.py:885
  148.1 2.9 %collective-permute-done.51.three = f32[16,512]{1,0:T(8,128)S(1)} collective-permute-done((f32[16,512]{1,0:T(8,128)S(1)}, f32[16,512]{1,0:T(8,128)S(1)}, u32[]{:S(2)}, u32[]{:S(2)}) %collective-permute-start.51) | collective-permute-done | bytes 32800 | tf_op jit(solution)/shard_map/ppermute | solution.py:885
  151.6 1.6 %lay.1 = (f32[512,512]{1,0:T(8,128)}, f32[512,512]{1,0:T(8,128)}, f32[128,512]{1,0:T(8,128)}) custom-call(bf16[144,512]{1,0:T(8,128)(2,1)S(1)} %total.1.own, bf16[144,512]{1,0:T(8,128)(2,1)S(1)} %collective-permute-done.46.z1, bf16[144,512]{1,0:T(8,128)(2,1)S(1)} %collective-permute-done.52.z2, bf16[144,512]{1,0:T(8,128)(2,1)S(1)} %collective-permute-done.53.z3, ...), custom_call_target="tpu_custom_call" | custom-call | tf_op jit(solution)/shard_map/lay/pallas_call | solution.py:837
  (128 shorter events, 38.1 us)
Async XLA Ops:
  3.6 10.0 %collective-permute-start = (bf16[288,512]{1,0:T(8,128)(2,1)S(1)}, bf16[288,512]{1,0:T(8,128)(2,1)S(1)}, u32[]{:S(2)}, u32[]{:S(2)}) collective-permute-start(bf16[288,512]{1,0:T(8,128)(2,1)S(1)} %get-tuple-element.118), channel_id=1, source_target_pairs={{0,8},{8,16},{16,24},{24,28},{28,20},{20,12},{12,4},{4,0},{1,9},{9... | collective-permute-start | bytes 884744 | tf_op jit(solution)/shard_map/ppermute | solution.py:876
  6.6 8.5 %collective-permute-start.1 = (bf16[288,512]{1,0:T(8,128)(2,1)S(1)}, bf16[288,512]{1,0:T(8,128)(2,1)S(1)}, u32[]{:S(2)}, u32[]{:S(2)}) collective-permute-start(bf16[288,512]{1,0:T(8,128)(2,1)S(1)} %get-tuple-element.118), channel_id=1, source_target_pairs={{0,4},{8,0},{16,8},{24,16},{28,24},{20,28},{12,20},{4,12},{1,5},{9... | collective-permute-start | bytes 884744 | tf_op jit(solution)/shard_map/ppermute | solution.py:879
  6.6 13.6 %collective-permute-start.4 = (bf16[512,512]{1,0:T(8,128)(2,1)}, bf16[512,512]{1,0:T(8,128)(2,1)S(1)}, u32[]{:S(2)}, u32[]{:S(2)}) collective-permute-start(bf16[512,512]{1,0:T(8,128)(2,1)} %up_a.1), channel_id=1, source_target_pairs={{0,2},{1,3},{2,0},{3,1},{4,6},{5,7},{6,4},{7,5},{8,10},{9,11},{10,... | collective-permute-start | bytes 1572872 | tf_op jit(solution)/shard_map/ppermute | solution.py:882
  15.1 7.6 %collective-permute-start.2 = (bf16[288,512]{1,0:T(8,128)(2,1)S(1)}, bf16[288,512]{1,0:T(8,128)(2,1)S(1)}, u32[]{:S(2)}, u32[]{:S(2)}) collective-permute-start(bf16[288,512]{1,0:T(8,128)(2,1)S(1)} %collective-permute-done.f.refs_1_), channel_id=1, source_target_pairs={{0,8},{8,16},{16,24},{24,28},{28,20},{20,12},{12,4},{4,0},{1,9},{9... | collective-permute-start | bytes 884744 | tf_op jit(solution)/shard_map/ppermute | solution.py:876
  16.7 7.3 %collective-permute-start.3 = (bf16[288,512]{1,0:T(8,128)(2,1)S(1)}, bf16[288,512]{1,0:T(8,128)(2,1)S(1)}, u32[]{:S(2)}, u32[]{:S(2)}) collective-permute-start(bf16[288,512]{1,0:T(8,128)(2,1)S(1)} %collective-permute-done.1.b.refs_2_), channel_id=1, source_target_pairs={{0,4},{8,0},{16,8},{24,16},{28,24},{20,28},{12,20},{4,12},{1,5},{9... | collective-permute-start | bytes 884744 | tf_op jit(solution)/shard_map/ppermute | solution.py:879
  24.0 7.2 %collective-permute-start.5 = (bf16[288,512]{1,0:T(8,128)(2,1)S(1)}, bf16[288,512]{1,0:T(8,128)(2,1)S(1)}, u32[]{:S(2)}, u32[]{:S(2)}) collective-permute-start(bf16[288,512]{1,0:T(8,128)(2,1)S(1)} %collective-permute-done.2.f.refs_3_), channel_id=1, source_target_pairs={{0,8},{8,16},{16,24},{24,28},{28,20},{20,12},{12,4},{4,0},{1,9},{9... | collective-permute-start | bytes 884744 | tf_op jit(solution)/shard_map/ppermute | solution.py:876
  25.5 6.7 %collective-permute-start.6 = (bf16[288,512]{1,0:T(8,128)(2,1)S(1)}, bf16[288,512]{1,0:T(8,128)(2,1)S(1)}, u32[]{:S(2)}, u32[]{:S(2)}) collective-permute-start(bf16[288,512]{1,0:T(8,128)(2,1)S(1)} %collective-permute-done.3.b.refs_4_), channel_id=1, source_target_pairs={{0,4},{8,0},{16,8},{24,16},{28,24},{20,28},{12,20},{4,12},{1,5},{9... | collective-permute-start | bytes 884744 | tf_op jit(solution)/shard_map/ppermute | solution.py:879
  26.0 5.2 %collective-permute-start.7 = (bf16[128,512]{1,0:T(8,128)(2,1)}, bf16[128,512]{1,0:T(8,128)(2,1)S(1)}, u32[]{:S(2)}, u32[]{:S(2)}) collective-permute-start(bf16[128,512]{1,0:T(8,128)(2,1)} %w_out.1), channel_id=1, source_target_pairs={{0,2},{1,3},{2,0},{3,1},{4,6},{5,7},{6,4},{7,5},{8,10},{9,11},{10,... | collective-permute-start | bytes 393224 | tf_op jit(solution)/shard_map/ppermute | solution.py:882
  34.4 7.3 %collective-permute-start.14 = (bf16[144,512]{1,0:T(8,128)(2,1)S(1)}, bf16[144,512]{1,0:T(8,128)(2,1)S(1)}, u32[]{:S(2)}, u32[]{:S(2)}) collective-permute-start(bf16[144,512]{1,0:T(8,128)(2,1)S(1)} %get-tuple-element.127), channel_id=1, source_target_pairs={{0,8},{8,16},{16,24},{24,28},{28,20},{20,12},{12,4},{4,0},{1,9},{9... | collective-permute-start | bytes 442376 | tf_op jit(solution)/shard_map/ppermute | solution.py:876
  35.9 5.8 %collective-permute-start.15 = (bf16[144,512]{1,0:T(8,128)(2,1)S(1)}, bf16[144,512]{1,0:T(8,128)(2,1)S(1)}, u32[]{:S(2)}, u32[]{:S(2)}) collective-permute-start(bf16[144,512]{1,0:T(8,128)(2,1)S(1)} %get-tuple-element.140), channel_id=1, source_target_pairs={{0,4},{8,0},{16,8},{24,16},{28,24},{20,28},{12,20},{4,12},{1,5},{9... | collective-permute-start | bytes 442376 | tf_op jit(solution)/shard_map/ppermute | solution.py:879
  36.4 5.2 %collective-permute-start.17 = (bf16[128,512]{1,0:T(8,128)(2,1)S(1)}, bf16[128,512]{1,0:T(8,128)(2,1)S(1)}, u32[]{:S(2)}, u32[]{:S(2)}) collective-permute-start(bf16[128,512]{1,0:T(8,128)(2,1)S(1)} %collective-permute-done.7.wo2), channel_id=1, source_target_pairs={{0,1},{1,0},{2,3},{3,2},{4,5},{5,4},{6,7},{7,6},{8,9},{9,8},{10,11... | collective-permute-start | bytes 393224 | tf_op jit(solution)/shard_map/ppermute | solution.py:882
  36.4 5.2 %collective-permute-start.16 = (bf16[128,512]{1,0:T(8,128)(2,1)}, bf16[128,512]{1,0:T(8,128)(2,1)S(1)}, u32[]{:S(2)}, u32[]{:S(2)}) collective-permute-start(bf16[128,512]{1,0:T(8,128)(2,1)} %w_out.1), channel_id=1, source_target_pairs={{0,1},{1,0},{2,3},{3,2},{4,5},{5,4},{6,7},{7,6},{8,9},{9,8},{10,11... | collective-permute-start | bytes 393224 | tf_op jit(solution)/shard_map/ppermute | solution.py:882
  36.9 16.9 %collective-permute-start.23 = (bf16[512,512]{1,0:T(8,128)(2,1)}, bf16[512,512]{1,0:T(8,128)(2,1)S(1)}, u32[]{:S(2)}, u32[]{:S(2)}) collective-permute-start(bf16[512,512]{1,0:T(8,128)(2,1)} %down_a.1), channel_id=1, source_target_pairs={{0,2},{1,3},{2,0},{3,1},{4,6},{5,7},{6,4},{7,5},{8,10},{9,11},{10,... | collective-permute-start | bytes 1572872 | tf_op jit(solution)/shard_map/ppermute | solution.py:882
  47.0 6.8 %collective-permute-start.21 = (bf16[512,128]{1,0:T(8,128)(2,1)S(1)}, bf16[512,128]{1,0:T(8,128)(2,1)S(1)}, u32[]{:S(2)}, u32[]{:S(2)}) collective-permute-start(bf16[512,128]{1,0:T(8,128)(2,1)S(1)} %get-tuple-element.147.ctx0.context), channel_id=1, source_target_pairs={{0,2},{1,3},{2,0},{3,1},{4,6},{5,7},{6,4},{7,5},{8,10},{9,11},{10,... | collective-permute-start | bytes 393224 | tf_op jit(solution)/shard_map/ppermute | solution.py:882
  48.3 5.5 %collective-permute-start.20 = (bf16[512,128]{1,0:T(8,128)(2,1)S(1)}, bf16[512,128]{1,0:T(8,128)(2,1)S(1)}, u32[]{:S(2)}, u32[]{:S(2)}) collective-permute-start(bf16[512,128]{1,0:T(8,128)(2,1)S(1)} %get-tuple-element.147.ctx0.context), channel_id=1, source_target_pairs={{0,1},{1,0},{2,3},{3,2},{4,5},{5,4},{6,7},{7,6},{8,9},{9,8},{10,11... | collective-permute-start | bytes 393224 | tf_op jit(solution)/shard_map/ppermute | solution.py:882
  63.1 18.4 %collective-permute-start.31 = (bf16[3,512,128]{2,1,0:T(8,128)(2,1)S(1)}, bf16[3,512,128]{2,1,0:T(8,128)(2,1)S(1)}, u32[]{:S(2)}, u32[]{:S(2)}) collective-permute-start(bf16[3,512,128]{2,1,0:T(8,128)(2,1)S(1)} %bitcast.8), channel_id=1, source_target_pairs={{0,2},{1,3},{2,0},{3,1},{4,6},{5,7},{6,4},{7,5},{8,10},{9,11},{10,... | collective-permute-start | bytes 1179656 | tf_op jit(solution)/shard_map/ppermute | solution.py:882
  64.8 9.5 %collective-permute-start.27 = (bf16[128,512]{1,0:T(8,128)(2,1)S(1)}, bf16[128,512]{1,0:T(8,128)(2,1)S(1)}, u32[]{:S(2)}, u32[]{:S(2)}) collective-permute-start(bf16[128,512]{1,0:T(8,128)(2,1)S(1)} %get-tuple-element.163), channel_id=1, source_target_pairs={{0,4},{4,0},{8,12},{12,8},{16,20},{20,16},{24,28},{28,24},{1,5},{5... | collective-permute-start | bytes 393224 | tf_op jit(solution)/shard_map/ppermute | solution.py:885
  65.2 9.0 %collective-permute-start.25 = (bf16[512,128]{1,0:T(8,128)(2,1)S(1)}, bf16[512,128]{1,0:T(8,128)(2,1)S(1)}, u32[]{:S(2)}, u32[]{:S(2)}) collective-permute-start(bf16[512,128]{1,0:T(8,128)(2,1)S(1)} %get-tuple-element.157.refs_0_), channel_id=1, source_target_pairs={{0,8},{8,16},{16,24},{24,28},{28,20},{20,12},{12,4},{4,0},{1,9},{9... | collective-permute-start | bytes 393224 | tf_op jit(solution)/shard_map/ppermute | solution.py:876
  66.3 8.0 %collective-permute-start.26 = (bf16[512,128]{1,0:T(8,128)(2,1)S(1)}, bf16[512,128]{1,0:T(8,128)(2,1)S(1)}, u32[]{:S(2)}, u32[]{:S(2)}) collective-permute-start(bf16[512,128]{1,0:T(8,128)(2,1)S(1)} %get-tuple-element.157.refs_0_), channel_id=1, source_target_pairs={{0,4},{8,0},{16,8},{24,16},{28,24},{20,28},{12,20},{4,12},{1,5},{9... | collective-permute-start | bytes 393224 | tf_op jit(solution)/shard_map/ppermute | solution.py:879
  67.5 6.7 %collective-permute-start.28 = (bf16[64,512]{1,0:T(8,128)(2,1)S(1)}, bf16[64,512]{1,0:T(8,128)(2,1)S(1)}, u32[]{:S(2)}, u32[]{:S(2)}) collective-permute-start(bf16[64,512]{1,0:T(8,128)(2,1)S(1)} %get-tuple-element.165), channel_id=1, source_target_pairs={{0,4},{4,0},{8,12},{12,8},{16,20},{20,16},{24,28},{28,24},{1,5},{5... | collective-permute-start | bytes 196616 | tf_op jit(solution)/shard_map/ppermute | solution.py:885
  74.3 5.9 %collective-permute-start.32 = (bf16[128,512]{1,0:T(8,128)(2,1)S(1)}, bf16[128,512]{1,0:T(8,128)(2,1)S(1)}, u32[]{:S(2)}, u32[]{:S(2)}) collective-permute-start(bf16[128,512]{1,0:T(8,128)(2,1)S(1)} %get-tuple-element.173), channel_id=1, source_target_pairs={{0,4},{4,0},{8,12},{12,8},{16,20},{20,16},{24,28},{28,24},{1,5},{5... | collective-permute-start | bytes 393224 | tf_op jit(solution)/shard_map/ppermute | solution.py:885
  74.8 6.7 %collective-permute-start.29 = (bf16[512,128]{1,0:T(8,128)(2,1)S(1)}, bf16[512,128]{1,0:T(8,128)(2,1)S(1)}, u32[]{:S(2)}, u32[]{:S(2)}) collective-permute-start(bf16[512,128]{1,0:T(8,128)(2,1)S(1)} %collective-permute-done.25.refs_0_), channel_id=1, source_target_pairs={{0,8},{8,16},{16,24},{24,28},{28,20},{20,12},{12,4},{4,0},{1,9},{9... | collective-permute-start | bytes 393224 | tf_op jit(solution)/shard_map/ppermute | solution.py:876
  75.0 6.5 %collective-permute-start.30 = (bf16[512,128]{1,0:T(8,128)(2,1)S(1)}, bf16[512,128]{1,0:T(8,128)(2,1)S(1)}, u32[]{:S(2)}, u32[]{:S(2)}) collective-permute-start(bf16[512,128]{1,0:T(8,128)(2,1)S(1)} %collective-permute-done.26.refs_1_), channel_id=1, source_target_pairs={{0,4},{8,0},{16,8},{24,16},{28,24},{20,28},{12,20},{4,12},{1,5},{9... | collective-permute-start | bytes 393224 | tf_op jit(solution)/shard_map/ppermute | solution.py:879
  81.5 5.8 %collective-permute-start.35 = (bf16[128,512]{1,0:T(8,128)(2,1)S(1)}, bf16[128,512]{1,0:T(8,128)(2,1)S(1)}, u32[]{:S(2)}, u32[]{:S(2)}) collective-permute-start(bf16[128,512]{1,0:T(8,128)(2,1)S(1)} %get-tuple-element.179), channel_id=1, source_target_pairs={{0,4},{4,0},{8,12},{12,8},{16,20},{20,16},{24,28},{28,24},{1,5},{5... | collective-permute-start | bytes 393224 | tf_op jit(solution)/shard_map/ppermute | solution.py:885
  82.1 6.2 %collective-permute-start.33 = (bf16[512,128]{1,0:T(8,128)(2,1)S(1)}, bf16[512,128]{1,0:T(8,128)(2,1)S(1)}, u32[]{:S(2)}, u32[]{:S(2)}) collective-permute-start(bf16[512,128]{1,0:T(8,128)(2,1)S(1)} %collective-permute-done.29.refs_0_), channel_id=1, source_target_pairs={{0,8},{8,16},{16,24},{24,28},{28,20},{20,12},{12,4},{4,0},{1,9},{9... | collective-permute-start | bytes 393224 | tf_op jit(solution)/shard_map/ppermute | solution.py:876
  83.3 5.5 %collective-permute-start.34 = (bf16[512,128]{1,0:T(8,128)(2,1)S(1)}, bf16[512,128]{1,0:T(8,128)(2,1)S(1)}, u32[]{:S(2)}, u32[]{:S(2)}) collective-permute-start(bf16[512,128]{1,0:T(8,128)(2,1)S(1)} %collective-permute-done.30.refs_1_), channel_id=1, source_target_pairs={{0,4},{8,0},{16,8},{24,16},{28,24},{20,28},{12,20},{4,12},{1,5},{9... | collective-permute-start | bytes 393224 | tf_op jit(solution)/shard_map/ppermute | solution.py:879
  88.9 5.3 %collective-permute-start.36 = (bf16[256,128]{1,0:T(8,128)(2,1)S(1)}, bf16[256,128]{1,0:T(8,128)(2,1)S(1)}, u32[]{:S(2)}, u32[]{:S(2)}) collective-permute-start(bf16[256,128]{1,0:T(8,128)(2,1)S(1)} %get-tuple-element.183), channel_id=1, source_target_pairs={{0,8},{8,16},{16,24},{24,28},{28,20},{20,12},{12,4},{4,0},{1,9},{9... | collective-permute-start | bytes 196616 | tf_op jit(solution)/shard_map/ppermute | solution.py:876
  89.0 5.2 %collective-permute-start.37 = (bf16[256,128]{1,0:T(8,128)(2,1)S(1)}, bf16[256,128]{1,0:T(8,128)(2,1)S(1)}, u32[]{:S(2)}, u32[]{:S(2)}) collective-permute-start(bf16[256,128]{1,0:T(8,128)(2,1)S(1)} %get-tuple-element.184), channel_id=1, source_target_pairs={{0,4},{8,0},{16,8},{24,16},{28,24},{20,28},{12,20},{4,12},{1,5},{9... | collective-permute-start | bytes 196616 | tf_op jit(solution)/shard_map/ppermute | solution.py:879
  98.7 16.4 %collective-permute-start.38 = (bf16[512,384]{1,0:T(8,128)(2,1)S(1)}, bf16[512,384]{1,0:T(8,128)(2,1)S(1)}, u32[]{:S(2)}, u32[]{:S(2)}) collective-permute-start(bf16[512,384]{1,0:T(8,128)(2,1)S(1)} %get-tuple-element.199.dq_a), channel_id=1, source_target_pairs={{0,2},{1,3},{2,0},{3,1},{4,6},{5,7},{6,4},{7,5},{8,10},{9,11},{10,... | collective-permute-start | bytes 1179656 | tf_op jit(solution)/shard_map/ppermute | solution.py:882
  99.2 5.7 %collective-permute-start.40 = (bf16[144,512]{1,0:T(8,128)(2,1)S(1)}, bf16[144,512]{1,0:T(8,128)(2,1)S(1)}, u32[]{:S(2)}, u32[]{:S(2)}) collective-permute-start(bf16[144,512]{1,0:T(8,128)(2,1)S(1)} %join.3), channel_id=1, source_target_pairs={{0,8},{4,12},{8,0},{12,4},{16,24},{20,28},{24,16},{28,20},{1,9},{5... | collective-permute-start | bytes 442376 | tf_op jit(solution)/shard_map/ppermute | solution.py:885
  99.5 9.7 %collective-permute-start.41 = (bf16[144,512]{1,0:T(8,128)(2,1)S(1)}, bf16[144,512]{1,0:T(8,128)(2,1)S(1)}, u32[]{:S(2)}, u32[]{:S(2)}) collective-permute-start(bf16[144,512]{1,0:T(8,128)(2,1)S(1)} %join.4), channel_id=1, source_target_pairs={{0,16},{4,20},{8,24},{12,28},{16,0},{20,4},{24,8},{28,12},{1,17},{... | collective-permute-start | bytes 442376 | tf_op jit(solution)/shard_map/ppermute | solution.py:885
  101.0 8.3 %collective-permute-start.42 = (bf16[144,512]{1,0:T(8,128)(2,1)S(1)}, bf16[144,512]{1,0:T(8,128)(2,1)S(1)}, u32[]{:S(2)}, u32[]{:S(2)}) collective-permute-start(bf16[144,512]{1,0:T(8,128)(2,1)S(1)} %join.5), channel_id=1, source_target_pairs={{0,24},{4,28},{8,16},{12,20},{16,8},{20,12},{24,0},{28,4},{1,25},{... | collective-permute-start | bytes 442376 | tf_op jit(solution)/shard_map/ppermute | solution.py:885
  103.6 5.7 %collective-permute-start.39 = (bf16[128,512]{1,0:T(8,128)(2,1)S(1)}, bf16[128,512]{1,0:T(8,128)(2,1)S(1)}, u32[]{:S(2)}, u32[]{:S(2)}) collective-permute-start(bf16[128,512]{1,0:T(8,128)(2,1)S(1)} %get-tuple-element.202), channel_id=1, source_target_pairs={{0,4},{4,0},{8,12},{12,8},{16,20},{20,16},{24,28},{28,24},{1,5},{5... | collective-permute-start | bytes 393224 | tf_op jit(solution)/shard_map/ppermute | solution.py:885
  104.9 8.1 %collective-permute-start.44 = (bf16[512,128]{1,0:T(8,128)(2,1)S(1)}, bf16[512,128]{1,0:T(8,128)(2,1)S(1)}, u32[]{:S(2)}, u32[]{:S(2)}) collective-permute-start(bf16[512,128]{1,0:T(8,128)(2,1)S(1)} %copy-done.9), channel_id=1, source_target_pairs={{0,2},{1,3},{2,0},{3,1},{4,6},{5,7},{6,4},{7,5},{8,10},{9,11},{10,... | collective-permute-start | bytes 393224 | tf_op jit(solution)/shard_map/ppermute | solution.py:882
  111.4 3.6 %collective-permute-start.43 = (f32[8,128]{1,0:T(8,128)S(1)}, f32[8,128]{1,0:T(8,128)S(1)}, u32[]{:S(2)}, u32[]{:S(2)}) collective-permute-start(f32[8,128]{1,0:T(8,128)S(1)} %get-tuple-element.206.flat_a), channel_id=1, source_target_pairs={{0,2},{1,3},{2,0},{3,1},{4,6},{5,7},{6,4},{7,5},{8,10},{9,11},{10,... | collective-permute-start | bytes 12296 | tf_op jit(solution)/shard_map/ppermute | solution.py:882
  116.1 8.9 %collective-permute-start.45 = (f32[512,512]{1,0:T(8,128)S(1)}, f32[512,512]{1,0:T(8,128)S(1)}, u32[]{:S(2)}, u32[]{:S(2)}) collective-permute-start(f32[512,512]{1,0:T(8,128)S(1)} %input_back.1.own), channel_id=1, source_target_pairs={{0,1},{1,0},{2,3},{3,2},{4,5},{5,4},{6,7},{7,6},{8,9},{9,8},{10,11... | collective-permute-start | bytes 3145736 | tf_op jit(solution)/shard_map/ppermute | solution.py:882
  116.2 20.3 %collective-permute-start.47 = (f32[512,512]{1,0:T(8,128)S(1)}, f32[512,512]{1,0:T(8,128)S(1)}, u32[]{:S(2)}, u32[]{:S(2)}) collective-permute-start(f32[512,512]{1,0:T(8,128)S(1)} %get-tuple-element.212.refs_0_), channel_id=1, source_target_pairs={{0,1},{1,0},{2,3},{3,2},{4,5},{5,4},{6,7},{7,6},{8,9},{9,8},{10,11... | collective-permute-start | bytes 3145736 | tf_op jit(solution)/shard_map/ppermute | solution.py:882
  116.7 8.3 %collective-permute-start.46 = (bf16[144,512]{1,0:T(8,128)(2,1)S(1)}, bf16[144,512]{1,0:T(8,128)(2,1)S(1)}, u32[]{:S(2)}, u32[]{:S(2)}) collective-permute-start(bf16[144,512]{1,0:T(8,128)(2,1)S(1)} %total.1.own), channel_id=1, source_target_pairs={{0,8},{4,12},{8,0},{12,4},{16,24},{20,28},{24,16},{28,20},{1,9},{5... | collective-permute-start | bytes 442376 | tf_op jit(solution)/shard_map/ppermute | solution.py:885
  118.8 14.0 %collective-permute-start.52 = (bf16[144,512]{1,0:T(8,128)(2,1)S(1)}, bf16[144,512]{1,0:T(8,128)(2,1)S(1)}, u32[]{:S(2)}, u32[]{:S(2)}) collective-permute-start(bf16[144,512]{1,0:T(8,128)(2,1)S(1)} %total.1.own), channel_id=1, source_target_pairs={{0,16},{4,20},{8,24},{12,28},{16,0},{20,4},{24,8},{28,12},{1,17},{... | collective-permute-start | bytes 442376 | tf_op jit(solution)/shard_map/ppermute | solution.py:885
  119.3 15.1 %collective-permute-start.53 = (bf16[144,512]{1,0:T(8,128)(2,1)S(1)}, bf16[144,512]{1,0:T(8,128)(2,1)S(1)}, u32[]{:S(2)}, u32[]{:S(2)}) collective-permute-start(bf16[144,512]{1,0:T(8,128)(2,1)S(1)} %total.1.own), channel_id=1, source_target_pairs={{0,24},{4,28},{8,16},{12,20},{16,8},{20,12},{24,0},{28,4},{1,25},{... | collective-permute-start | bytes 442376 | tf_op jit(solution)/shard_map/ppermute | solution.py:885
  126.8 8.0 %collective-permute-start.48 = (f32[16,512]{1,0:T(8,128)S(1)}, f32[16,512]{1,0:T(8,128)S(1)}, u32[]{:S(2)}, u32[]{:S(2)}) collective-permute-start(f32[16,512]{1,0:T(8,128)S(1)} %get-tuple-element.216.refs_0_), channel_id=1, source_target_pairs={{0,4},{4,0},{8,12},{12,8},{16,20},{20,16},{24,28},{28,24},{1,5},{5... | collective-permute-start | bytes 98312 | tf_op jit(solution)/shard_map/ppermute | solution.py:885
  128.3 23.3 %collective-permute-start.54 = (bf16[144,512]{1,0:T(8,128)(2,1)S(1)}, bf16[144,512]{1,0:T(8,128)(2,1)S(1)}, u32[]{:S(2)}, u32[]{:S(2)}) collective-permute-start(bf16[144,512]{1,0:T(8,128)(2,1)S(1)} %total.1.own), channel_id=1, source_target_pairs={{0,4},{4,0},{8,12},{12,8},{16,20},{20,16},{24,28},{28,24},{1,5},{5... | collective-permute-start | bytes 442376 | tf_op jit(solution)/shard_map/ppermute | solution.py:885
  132.8 18.8 %collective-permute-start.56 = (bf16[144,512]{1,0:T(8,128)(2,1)S(1)}, bf16[144,512]{1,0:T(8,128)(2,1)S(1)}, u32[]{:S(2)}, u32[]{:S(2)}) collective-permute-start(bf16[144,512]{1,0:T(8,128)(2,1)S(1)} %collective-permute-done.52.z2), channel_id=1, source_target_pairs={{0,4},{4,0},{8,12},{12,8},{16,20},{20,16},{24,28},{28,24},{1,5},{5... | collective-permute-start | bytes 442376 | tf_op jit(solution)/shard_map/ppermute | solution.py:885
  134.4 17.2 %collective-permute-start.57 = (bf16[144,512]{1,0:T(8,128)(2,1)S(1)}, bf16[144,512]{1,0:T(8,128)(2,1)S(1)}, u32[]{:S(2)}, u32[]{:S(2)}) collective-permute-start(bf16[144,512]{1,0:T(8,128)(2,1)S(1)} %collective-permute-done.53.z3), channel_id=1, source_target_pairs={{0,4},{4,0},{8,12},{12,8},{16,20},{20,16},{24,28},{28,24},{1,5},{5... | collective-permute-start | bytes 442376 | tf_op jit(solution)/shard_map/ppermute | solution.py:885
  134.8 16.8 %collective-permute-start.55 = (bf16[144,512]{1,0:T(8,128)(2,1)S(1)}, bf16[144,512]{1,0:T(8,128)(2,1)S(1)}, u32[]{:S(2)}, u32[]{:S(2)}) collective-permute-start(bf16[144,512]{1,0:T(8,128)(2,1)S(1)} %collective-permute-done.46.z1), channel_id=1, source_target_pairs={{0,4},{4,0},{8,12},{12,8},{16,20},{20,16},{24,28},{28,24},{1,5},{5... | collective-permute-start | bytes 442376 | tf_op jit(solution)/shard_map/ppermute | solution.py:885
  136.5 4.0 %collective-permute-start.49 = (f32[16,512]{1,0:T(8,128)S(1)}, f32[16,512]{1,0:T(8,128)S(1)}, u32[]{:S(2)}, u32[]{:S(2)}) collective-permute-start(f32[16,512]{1,0:T(8,128)S(1)} %add_gains.1.here), channel_id=1, source_target_pairs={{0,8},{4,12},{8,0},{12,4},{16,24},{20,28},{24,16},{28,20},{1,9},{5... | collective-permute-start | bytes 98312 | tf_op jit(solution)/shard_map/ppermute | solution.py:885
  140.4 4.8 %collective-permute-start.50 = (f32[16,512]{1,0:T(8,128)S(1)}, f32[16,512]{1,0:T(8,128)S(1)}, u32[]{:S(2)}, u32[]{:S(2)}) collective-permute-start(f32[16,512]{1,0:T(8,128)S(1)} %add_gains.1.here), channel_id=1, source_target_pairs={{0,16},{4,20},{8,24},{12,28},{16,0},{20,4},{24,8},{28,12},{1,17},{... | collective-permute-start | bytes 98312 | tf_op jit(solution)/shard_map/ppermute | solution.py:885
  145.3 5.7 %collective-permute-start.51 = (f32[16,512]{1,0:T(8,128)S(1)}, f32[16,512]{1,0:T(8,128)S(1)}, u32[]{:S(2)}, u32[]{:S(2)}) collective-permute-start(f32[16,512]{1,0:T(8,128)S(1)} %add_gains.1.here), channel_id=1, source_target_pairs={{0,24},{4,28},{8,16},{12,20},{16,8},{20,12},{24,0},{28,4},{1,25},{... | collective-permute-start | bytes 98312 | tf_op jit(solution)/shard_map/ppermute | solution.py:885
  (25 other events, 218.5 us)

commit v4 on v1

--- a/solution.py
+++ b/solution.py
@@ -1,6 +1,11 @@
+import functools
+import math
+
 import jax
 import jax.numpy as jnp
 from jax import lax
+from jax.experimental import pallas as pl
+from jax.experimental.pallas import tpu as pltpu
 from jax.sharding import PartitionSpec as P
 
 D = 512
@@ -253,6 +258,989 @@
     )
 
 
+def mask_pair(values, near):
+    zero = jnp.zeros_like(values)
+    return jnp.where(near, values, zero), jnp.where(near, zero, values)
+
+
+def first_lanes():
+    return lax.broadcasted_iota(jnp.int32, (1, 2 * DH), 1) < DH
+
+
+def dot_nn(a, b):
+    return lax.dot_general(a, b, (((1,), (0,)), ((), ())), preferred_element_type=jnp.float32)
+
+
+def dot_nt(a, b):
+    return lax.dot_general(a, b, (((1,), (1,)), ((), ())), preferred_element_type=jnp.float32)
+
+
+def dot_tn(a, b):
+    return lax.dot_general(a, b, (((0,), (0,)), ((), ())), preferred_element_type=jnp.float32)
+
+
+def three_parts(values):
+    high = values.astype(jnp.bfloat16)
+    rest = values - high.astype(jnp.float32)
+    mid = rest.astype(jnp.bfloat16)
+    low = (rest - mid.astype(jnp.float32)).astype(jnp.bfloat16)
+    return high, mid, low
+
+
+def norm_parts(values):
+    centred = values - jnp.mean(values, -1, keepdims=True)
+    inv_std = lax.rsqrt(jnp.mean(centred * centred, -1, keepdims=True) + EPS)
+    return centred * inv_std, inv_std
+
+
+def noise_rows(noise):
+    few = noise.shape[0] // 2
+    return [
+        jnp.concatenate([noise[r * few + i, h : h + 1, :] for i in range(few) for h in range(2)], 1)
+        for r in range(2)
+    ]
+
+
+def head_kernel(tokens, gain, noise, other_noise, up, shard, summary, own_noise, up_a):
+    f32, bf16 = jnp.float32, jnp.bfloat16
+    rows = tokens.shape[0]
+    half = rows // 2
+    core = lax.axis_index("head") % 2
+    normed, _ = norm_parts(tokens[...].astype(f32))
+    h = normed * gain[...].astype(f32)
+    low = h.astype(bf16)
+    means = jnp.mean(h.reshape(rows // BLOCK, BLOCK, D), axis=1)
+    summary[...] = means
+    up_a[...] = up[: up_a.shape[0], :]
+    mine = jnp.concatenate(noise_rows(noise), 0)
+    other = jnp.concatenate(noise_rows(other_noise), 0)
+    own_noise[...] = mine
+    both = jnp.where(
+        core == 0, jnp.concatenate([mine, other], 0), jnp.concatenate([other, mine], 0)
+    )
+    few = means.shape[0] // 2
+    for k in range(2):
+        at = k * (half + EXTRA)
+        shard[at : at + half, :] = low[k * half : (k + 1) * half, :]
+        parts = [p.astype(f32) for p in three_parts(means[k * few : (k + 1) * few, :])]
+        parts += [p.astype(f32) for p in three_parts(both)] if k else [jnp.zeros((12, D), f32)]
+        parts.append(jnp.zeros((EXTRA - 24, D), f32))
+        shard[at + half : at + half + EXTRA, :] = jnp.concatenate(parts, 0).astype(bf16)
+
+
+def project_rows(rows, joint):
+    return dot_nn(rows, joint[:, : 6 * DH]).astype(jnp.bfloat16)
+
+
+def project_own_kernel(h_one, weight, w_sort, w_out, up, down, out, joint, first, second, third):
+    joint[...] = jnp.concatenate([weight[i] for i in range(3)] + [w_sort[...]], 1)
+    width = w_out.shape[0]
+    rest = first.shape[0] - width
+    first[:rest, :] = up[up.shape[0] - rest :, :]
+    first[rest:, :] = w_out[...]
+    n = second.shape[0]
+    second[...] = down[:n, :]
+    third[...] = down[n:, :]
+    project_shard(h_one, joint, out, 0)
+
+
+def project_shard(shard, joint, out, to):
+    half = shard.shape[0] // 2 - EXTRA
+    for k in range(2):
+        for start in range(0, half, 2 * BLOCK):
+            at = k * (half + EXTRA) + start
+            out[to : to + 2 * BLOCK, :] = project_rows(shard[at : at + 2 * BLOCK, :], joint)
+            to += 2 * BLOCK
+
+
+def project_kernel(mine, other, joint, out, extra):
+    size = mine.shape[0] // 2
+    for k, piece in enumerate((mine, other)):
+        project_shard(piece, joint, out, k * 2 * (size - EXTRA))
+        for m in range(2):
+            to = (2 * k + m) * EXTRA
+            extra[to : to + EXTRA, :] = piece[(m + 1) * size - EXTRA : (m + 1) * size, :]
+
+
+def half_kernel(shard, w_out, first, half, pair):
+    n, width = half.shape[0], w_out.shape[0]
+    core = lax.axis_index("head") % 2
+    half[...] = shard[pl.ds(pl.multiple_of(core * n, n), n), :]
+    pair[:width, :] = w_out[...]
+    pair[width:, :] = first[first.shape[0] - width :, :]
+
+
+def owners_of(step):
+    place = place_of(lax.axis_index("blk"))
+    core = lax.axis_index("head") % 2
+    way = jnp.where(core == 0, 8 - step, step)
+    return ring_of((place + way) % 8), ring_of((place + 8 - way) % 8)
+
+
+def ring_of(position):
+    return jnp.where(position < 4, 2 * position, 2 * (7 - position) + 1)
+
+
+def place_of(index):
+    return jnp.where(index % 2 == 0, index // 2, 7 - index // 2)
+
+
+def far_near(table, at, lanes):
+    return table[pl.ds(pl.multiple_of(at * BLOCK, BLOCK), BLOCK), lanes]
+
+
+def block_operands(qkv, block, first, second, near):
+    k_lanes, v_lanes = slice(2 * DH, 4 * DH), slice(4 * DH, 6 * DH)
+    query = far_near(qkv, block, slice(0, 2 * DH))
+    keys, values = [], []
+    for lanes, store in ((k_lanes, keys), (v_lanes, values)):
+        own0, own1 = mask_pair(far_near(qkv, block, lanes), near)
+        far0, _ = mask_pair(far_near(qkv, first, lanes), near)
+        _, far1 = mask_pair(far_near(qkv, second, lanes), near)
+        store.extend([own0, far0, own1, far1])
+    return query, keys, values
+
+
+def block_probs(scores):
+    probs = []
+    for h in range(2):
+        part = scores[:, h * 2 * DH : (h + 1) * 2 * DH]
+        expo = jnp.exp(part - jnp.max(part, -1, keepdims=True))
+        probs.append(expo / jnp.sum(expo, -1, keepdims=True))
+    return probs
+
+
+def choices(partner, h):
+    nb = partner.shape[1]
+    sides = lax.broadcasted_iota(jnp.int32, (nb, nb), 0)
+    hot = (sides == partner[h : h + 1, :]).astype(jnp.bfloat16)
+    same = sides == lax.broadcasted_iota(jnp.int32, (nb, nb), 1)
+    return dot_nt(same.astype(jnp.bfloat16), hot)
+
+
+def joined(rows, at, count):
+    parts = [rows[at + k * count : at + (k + 1) * count, :].astype(jnp.float32) for k in range(3)]
+    return (parts[0] + parts[1]) + parts[2]
+
+
+def attend_kernel(
+    own, step1, step2, step3, extra1, extra2, extra3, mine4, other4, joint, own_summary, own_noise,
+    partner, partner_rows, qkv, context, summary, steps, scale_rows, weight_rows, noise,
+):
+    f32, bf16 = jnp.float32, jnp.bfloat16
+    me = lax.axis_index("blk")
+    core = lax.axis_index("head") % 2
+    nb = partner_rows.shape[1]
+    rows = own.shape[0]
+    half = rows // 2
+    blocks = rows // BLOCK
+    few = blocks // 2
+
+    def put(owner, start, values):
+        n = values.shape[0]
+        qkv[pl.ds(pl.multiple_of(owner * rows + start, n), n), :] = values
+
+    def put_noise(owner, values):
+        lines = [
+            values[r : r + 1, i * 2 * nb : (i + 1) * 2 * nb] for r in range(2) for i in range(few)
+        ]
+        at = pl.multiple_of(owner * blocks, blocks)
+        noise[pl.ds(at, blocks), :] = jnp.concatenate(lines, 0)
+
+    def put_extra(owner, first, second):
+        at = pl.multiple_of(owner * blocks, blocks)
+        summary[pl.ds(at, blocks), :] = jnp.concatenate(
+            [joined(first, 0, few), joined(second, 0, few)], 0
+        )
+        both = joined(second, 3 * few, 4)
+        put_noise(owner, jnp.where(core == 0, both[:2], both[2:]))
+
+    put(me, 0, own[...])
+    summary[pl.ds(pl.multiple_of(me * blocks, blocks), blocks), :] = own_summary[...]
+    put_noise(me, own_noise[...])
+    for step, ref, extra in ((1, step1, extra1), (2, step2, extra2), (3, step3, extra3)):
+        for k, owner in enumerate(owners_of(step)):
+            put(owner, 0, ref[k * rows : (k + 1) * rows, :])
+            at = 2 * k * EXTRA
+            put_extra(owner, extra[at : at + EXTRA, :], extra[at + EXTRA : at + 2 * EXTRA, :])
+    owner, _ = owners_of(4)
+    for side, ref in ((core, mine4), (1 - core, other4)):
+        for start in range(0, half, 2 * BLOCK):
+            values = project_rows(ref[start : start + 2 * BLOCK, :], joint)
+            put(owner, side * half + start, values)
+    ends = [ref[half:, :].astype(f32) for ref in (mine4, other4)]
+    put_extra(
+        owner, jnp.where(core == 0, ends[0], ends[1]), jnp.where(core == 0, ends[1], ends[0])
+    )
+
+    parts = three_parts(summary[...])
+    logits = sum(dot_nn(part, joint[:, 6 * DH :]) for part in parts[::-1])
+    logits = (logits + noise[...]) / TEMPER
+    plan = jnp.stack([logits[:, :nb], logits[:, nb:]])
+    for sweep in range(SINK):
+        for k, axis in enumerate((2, 1)):
+            plan = plan - log_total(plan, axis)
+            steps[2 * sweep + k] = jnp.exp(plan)
+    final = jnp.exp(plan)
+    picked = []
+    for h in range(2):
+        picked.append(nb * jnp.sum(choices(partner_rows, h) * final[h], axis=1, keepdims=True))
+    ones = jnp.ones((nb, DH), f32)
+    scale_rows[...] = jnp.concatenate([ones, picked[0] * ones, ones, picked[1] * ones], 1)
+    weight_rows[...] = jnp.concatenate([picked[0] * ones, picked[1] * ones], 1)
+
+    near = first_lanes()
+    work = []
+    for i in range(blocks):
+        block = me * blocks + i
+        query, keys, values = block_operands(
+            qkv, block, partner[0, block], partner[1, block], near
+        )
+        none = jnp.zeros_like(values[0])
+        table = jnp.concatenate(
+            [
+                jnp.concatenate([values[0], none, values[2], none], 0),
+                jnp.concatenate([none, values[1], none, values[3]], 0),
+            ],
+            1,
+        )
+        z = dot_nt(query, jnp.concatenate(keys, 0)) * (DH**-0.5)
+        work.append((block, z, table))
+    probs = [block_probs(z * scale_rows[pl.ds(block, 1), :]) for block, z, _ in work]
+    outs = [
+        dot_nn(jnp.concatenate([p.astype(bf16) for p in prob], 1), table)
+        for prob, (_, _, table) in zip(probs, work)
+    ]
+    for i, (out, (block, _, _)) in enumerate(zip(outs, work)):
+        ctx = out[:, : 2 * DH] + weight_rows[pl.ds(block, 1), :] * out[:, 2 * DH :]
+        context[i * BLOCK : (i + 1) * BLOCK, :] = ctx.astype(bf16)
+
+
+def feed_kernel(
+    tokens, cotangent, gain, ctx0, ctx1, ctx2, ctx3, wo, wo_other, up_a, up_b, first, down_a, second, third,
+    middle, h_two, active, d_hidden, ffn, d_h_two,
+    ctx_full, wo_full, up_full, down_full, act_full, d_full,
+):
+    f32, bf16 = jnp.float32, jnp.bfloat16
+    hd = lax.axis_index("head")
+    row = hd // 2
+    width = ctx0.shape[1]
+    ff = up_a.shape[1]
+    for j, c in enumerate((ctx0, ctx1, ctx2, ctx3)):
+        at = pl.multiple_of((hd ^ j) * width, width)
+        ctx_full[:, pl.ds(at, width)] = c[...]
+        w = wo if j % 2 == 0 else wo_other
+        wo_full[pl.ds(at, width), :] = w[j // 2 * width : (j // 2 + 1) * width, :]
+    here, there = (pl.multiple_of((row ^ j) * ff, ff) for j in range(2))
+    up_full[:, pl.ds(here, ff)] = up_a[...]
+    top = up_b.shape[0]
+    up_full[:top, pl.ds(there, ff)] = up_b[...]
+    up_full[top:, pl.ds(there, ff)] = first[: up_a.shape[0] - top, :]
+    down_full[pl.ds(here, ff), :] = down_a[...]
+    n = second.shape[0]
+    down_full[pl.ds(there, n), :] = second[...]
+    down_full[pl.ds(pl.multiple_of(there + n, 32), ff - n), :] = third[...]
+    chunk = 256
+    for start in range(0, tokens.shape[0], chunk):
+        sl = slice(start, start + chunk)
+        mid = tokens[sl, :].astype(f32) + dot_nn(ctx_full[sl, :], wo_full[...])
+        middle[sl, :] = mid
+        normed, _ = norm_parts(mid)
+        low = (normed * gain[...].astype(f32)).astype(bf16)
+        h_two[sl, :] = low
+        ffn_sum = None
+        back_sum = None
+        for j in range(2):
+            cols = slice(j * ff, (j + 1) * ff)
+            pre = dot_nn(low, up_full[:, cols])
+            d_act = dot_nt(cotangent[sl, :], down_full[cols, :])
+            bell = 0.5 * (1.0 + lax.erf(pre * ROOT_HALF))
+            act = (pre * bell).astype(bf16)
+            slope = bell + pre * jnp.exp(-0.5 * pre * pre) * INV_ROOT_TWO_PI
+            d_pre = (d_act * slope).astype(bf16)
+            act_full[sl, cols] = act
+            d_full[sl, cols] = d_pre
+            f = dot_nn(act, down_full[cols, :])
+            b = dot_nt(d_pre, up_full[:, cols])
+            ffn_sum = f if ffn_sum is None else ffn_sum + f
+            back_sum = b if back_sum is None else back_sum + b
+        ffn[sl, :] = ffn_sum
+        d_h_two[sl, :] = back_sum
+    mine = pl.ds(pl.multiple_of(row * ff, ff), ff)
+    active[...] = act_full[:, mine]
+    d_hidden[...] = d_full[:, mine]
+
+
+def back_kernel(middle, own, other, cotangent, gain, w_out, d_middle, d_low, d_ctx, g_gain):
+    f32, bf16 = jnp.float32, jnp.bfloat16
+    normed, inv = norm_parts(middle[...])
+    d_h = own[...] + other[...]
+    g_gain[...] = jnp.broadcast_to(jnp.sum(d_h * normed, 0, keepdims=True), g_gain.shape)
+    d_mid = cotangent[...].astype(f32) + norm_back(d_h, normed, inv, gain[...].astype(f32))
+    d_middle[...] = d_mid
+    low = d_mid.astype(bf16)
+    d_low[...] = low
+    d_ctx[...] = dot_nt(low, w_out[...]).astype(bf16)
+
+
+def grads_kernel(h_two, d_hidden, active, cotangent, context, d_low, *refs):
+    keeps, (front, back), (up, down, out) = refs[:7], refs[7:9], refs[9:]
+    place = place_of(lax.axis_index("blk"))
+    up[...] = dot_tn(h_two[...], d_hidden[...])
+    down[...] = dot_tn(active[...], cotangent[...])
+    out[...] = dot_tn(context[...], d_low[...])
+
+    def rows_of(distance):
+        owner = ring_of((place + distance + 8) % 8)
+        parts = []
+        for ref in (up, down, out):
+            n = ref.shape[0] // 8
+            parts.append(ref[pl.ds(pl.multiple_of(owner * n, n), n), :])
+        return jnp.concatenate(parts, 0)
+
+    for ref, distance in zip(keeps, (3, 2, 1, -3, -2, -1, 0)):
+        ref[...] = rows_of(distance)
+    last = rows_of(4).astype(jnp.bfloat16)
+    n = front.shape[0]
+    front[...] = last[:n]
+    back[...] = last[n:]
+
+
+def relay_kernel(keep_f, keep_b, f, b, out_f, out_b):
+    f32 = jnp.float32
+    n, m, size = f.shape[0], b.shape[0], keep_f.shape[0]
+    out_f[...] = keep_f[...].astype(jnp.bfloat16)
+    out_b[...] = keep_b[...].astype(jnp.bfloat16)
+    out_f[:n, :] = (keep_f[:n, :] + f[...].astype(f32)).astype(jnp.bfloat16)
+    out_b[size - m :, :] = (keep_b[size - m :, :] + b[...].astype(f32)).astype(jnp.bfloat16)
+
+
+def total_kernel(keep, f, b, out):
+    f32 = jnp.float32
+    out[...] = (keep[...] + (f[...].astype(f32) + b[...].astype(f32))).astype(jnp.bfloat16)
+
+
+def cut_kernel(f, b, front, back):
+    front[...] = f[: front.shape[0], :]
+    back[...] = b[b.shape[0] - back.shape[0] :, :]
+
+
+def lay_kernel(own, f1, b1, f2, b2, f3, b3, f4, b4, g_up, g_down, g_out):
+    f32 = jnp.float32
+    place = place_of(lax.axis_index("blk"))
+    last = jnp.concatenate([f4[...], b4[...]], 0)
+    for distance, piece in (
+        (0, own[...]), (-1, f1[...]), (1, b1[...]), (-2, f2[...]), (2, b2[...]), (-3, f3[...]), (3, b3[...]),
+        (4, last),
+    ):
+        owner = ring_of((place + distance + 8) % 8)
+        start = 0
+        for ref in (g_up, g_down, g_out):
+            n = ref.shape[0] // 8
+            ref[pl.ds(pl.multiple_of(owner * n, n), n), :] = piece[start : start + n].astype(f32)
+            start += n
+
+
+def halve_kernel(f, b, front, back):
+    n = front.shape[0]
+    front[...] = f[:n, :]
+    back[...] = b[n:, :]
+
+
+def add_kernel(*refs):
+    *terms, out = refs
+    total = terms[0][...]
+    for term in terms[1:]:
+        total = total + term[...]
+    out[...] = total
+
+
+def four_kernel(here, one, two, three, out):
+    out[...] = (here[...] + one[...]) + (two[...] + three[...])
+
+
+def gains_kernel(here, other, first, second):
+    total = here[...] + other[...]
+    first[...] = total[0, :]
+    second[...] = total[8, :]
+
+
+def block_at(place, step, start, i):
+    return ring_of((place + 8 - step) % 8) * (SHARD // BLOCK) + start // BLOCK + i
+
+
+def prepare_kernel(pieces, qkv, partner, scale_rows, z_out, probs_out):
+    place = place_of(lax.axis_index("blk"))
+    near = first_lanes()
+    blocks = [(step, start, i) for step, start, n in pieces for i in range(n // BLOCK)]
+    for first in range(0, len(blocks), 8):
+        work = []
+        for step, start, i in blocks[first : first + 8]:
+            block = block_at(place, step, start, i)
+            query, keys, _ = block_operands(qkv, block, partner[0, block], partner[1, block], near)
+            work.append((query, jnp.concatenate(keys, 0), scale_rows[pl.ds(block, 1), :]))
+        z = [dot_nt(query, keys) * (DH**-0.5) for query, keys, _ in work]
+        probs = [block_probs(v * w[2]) for v, w in zip(z, work)]
+        for k in range(len(work)):
+            at = slice((first + k) * BLOCK, (first + k + 1) * BLOCK)
+            z_out[at, :] = z[k]
+            probs_out[at, :] = jnp.concatenate(probs[k], 1)
+
+
+def pull_kernel(pieces, offset, *refs):
+    f32, bf16 = jnp.float32, jnp.bfloat16
+    count = len(pieces)
+    outs, refs = refs[:count], refs[count:]
+    qkv, partner, scale_rows, weight_rows, refs = *refs[:4], refs[4:]
+    if offset is not None:
+        z_all, probs_all, refs = refs[0], refs[1], refs[2:]
+    near_out, low_out, d_weight = refs
+    place = place_of(lax.axis_index("blk"))
+    near = first_lanes()
+    scale = DH**-0.5
+    blocks = [
+        (step, start, d_ctx, i)
+        for (step, start), d_ctx in zip(pieces, outs)
+        for i in range(d_ctx.shape[0] // BLOCK)
+    ]
+    for first in range(0, len(blocks), 8):
+        work = []
+        for k, (step, start, d_ctx, i) in enumerate(blocks[first : first + 8]):
+            block = block_at(place, step, start, i)
+            query, keys, values = block_operands(
+                qkv, block, partner[0, block], partner[1, block], near
+            )
+            w = dict(
+                query=query,
+                keys=jnp.concatenate(keys, 0),
+                values=jnp.concatenate(values, 0),
+                scale=scale_rows[pl.ds(block, 1), :],
+                weight=weight_rows[pl.ds(block, 1), :],
+                d_out=d_ctx[i * BLOCK : (i + 1) * BLOCK, :],
+            )
+            if offset is not None:
+                at = slice((offset + first + k) * BLOCK, (offset + first + k + 1) * BLOCK)
+                w["z"] = z_all[at, :]
+                w["probs"] = [probs_all[at, : 2 * DH], probs_all[at, 2 * DH :]]
+            work.append(w)
+        if offset is None:
+            for w in work:
+                w["z"] = dot_nt(w["query"], w["keys"]) * scale
+        for w in work:
+            w["raw"] = dot_nt(w["d_out"], w["values"])
+        if offset is None:
+            for w in work:
+                w["probs"] = block_probs(w["z"] * w["scale"])
+        for w in work:
+            d_z, low, d_w = [], [], []
+            for h in range(2):
+                sl = slice(h * 2 * DH, (h + 1) * 2 * DH)
+                probs = w["probs"][h]
+                d_probs = w["raw"][:, sl] * w["scale"][:, sl]
+                d_scores = probs * (d_probs - jnp.sum(d_probs * probs, -1, keepdims=True))
+                d_z.append((d_scores * w["scale"][:, sl]).astype(bf16))
+                low.append(probs.astype(bf16))
+                d_w.append(
+                    jnp.sum(
+                        d_scores * w["z"][:, sl] + low[h].astype(f32) * w["raw"][:, sl],
+                        0,
+                        keepdims=True,
+                    )
+                )
+            w["d_z"], w["low"] = jnp.concatenate(d_z, 1), jnp.concatenate(low, 1)
+            w["d_w"] = jnp.concatenate(d_w, 1)
+        for w in work:
+            w["d_query"] = dot_nn(w["d_z"], w["keys"]) * scale
+        for w in work:
+            w["d_keys"] = dot_tn(w["d_z"], w["query"]) * scale
+        for w in work:
+            w["d_values"] = dot_tn(w["low"], w["d_out"])
+        for k, w in enumerate(work):
+            to = first + k
+            at = slice(to * BLOCK, (to + 1) * BLOCK)
+            d_weight[to : to + 1, :] = w["d_w"]
+            low_out[at, : 2 * DH] = w["d_query"].astype(bf16)
+            for m, name in enumerate(("d_keys", "d_values")):
+                parts = [w[name][i * BLOCK : (i + 1) * BLOCK, :] for i in range(4)]
+                near_out[at, m * 2 * DH : (m + 1) * 2 * DH] = jnp.where(near, parts[0], parts[2])
+                far = jnp.where(near, parts[1], parts[3])
+                if m == 1:
+                    far = far * w["weight"]
+                low_out[at, (m + 1) * 2 * DH : (m + 2) * 2 * DH] = far.astype(bf16)
+
+
+def collect_kernel(pieces, *refs):
+    f32, bf16 = jnp.float32, jnp.bfloat16
+    count = len(pieces)
+    nears, lows, d_weights = refs[:count], refs[count : 2 * count], refs[2 * count : 3 * count]
+    partner, partner_rows, steps, summary = refs[3 * count : 3 * count + 4]
+    d_qkv, d_mine, flat_mine, g_sort, d_weight, acc, far, d_flat = refs[3 * count + 4 :]
+    me = lax.axis_index("blk")
+    place = place_of(me)
+    for parts, near_ref, low_ref, w_ref in zip(pieces, nears, lows, d_weights):
+        at = 0
+        for step, start, n in parts:
+            owner = ring_of((place + 8 - step) % 8)
+            to = pl.ds(pl.multiple_of(owner * SHARD + start, n), n)
+            acc[to, :] = near_ref[at : at + n, :]
+            far[to, :] = low_ref[at : at + n, 2 * DH :]
+            d_qkv[to, : 2 * DH] = low_ref[at : at + n, : 2 * DH]
+            if start == 0:
+                nb = SHARD // BLOCK
+                first = pl.multiple_of(owner * nb, nb)
+                d_weight[pl.ds(first, nb), :] = w_ref[at // BLOCK : at // BLOCK + nb, :]
+            at += n
+    near = first_lanes()
+    both = jnp.concatenate([near, near], 1)
+
+    def body(block, _):
+        tile = far[pl.ds(pl.multiple_of(block * BLOCK, BLOCK), BLOCK), :].astype(f32)
+        for h, kept in ((0, jnp.where(both, tile, 0.0)), (1, jnp.where(both, 0.0, tile))):
+            to = pl.ds(pl.multiple_of(partner[h, block] * BLOCK, BLOCK), BLOCK)
+            acc[to, :] += kept
+        return 0
+
+    lax.fori_loop(0, partner.shape[1], body, 0, unroll=4)
+    d_qkv[:, 2 * DH :] = acc[...].astype(bf16)
+    d_mine[...] = d_qkv[pl.ds(pl.multiple_of(me * SHARD, SHARD), SHARD), :]
+    d_flat[...] = sink_back(d_weight[...], steps, partner_rows)
+    n = flat_mine.shape[0]
+    flat_mine[...] = d_flat[pl.ds(pl.multiple_of(me * n, n), n), :]
+    g_sort[...] = lax.dot_general(
+        summary[...],
+        d_flat[...],
+        (((0,), (0,)), ((), ())),
+        precision=HIGHEST,
+        preferred_element_type=f32,
+    )
+
+
+def sink_back(d_weight, steps, partner):
+    nb = partner.shape[1]
+    grads = []
+    for h in range(2):
+        total = jnp.sum(
+            d_weight[:, (2 * h + 1) * DH : (2 * h + 2) * DH], axis=1, keepdims=True
+        )
+        grads.append(choices(partner, h) * (nb * total))
+    last = steps.shape[0] - 1
+    grad = jnp.stack(grads) * steps[last]
+    for t in range(last, -1, -1):
+        grad = grad - steps[t] * jnp.sum(grad, axis=1 if t % 2 else 2, keepdims=True)
+    return jnp.concatenate([grad[0], grad[1]], 1) / TEMPER
+
+
+def weight_kernel(own, m1, o1, m2, o2, m3, o3, m4, o4, d_qkv, g_qkv, h_all):
+    me = lax.axis_index("blk")
+    core = lax.axis_index("head") % 2
+    half = m4.shape[0] - EXTRA
+    rows = 2 * half
+
+    def put(owner, start, ref):
+        for k in range(ref.shape[0] // (half + EXTRA)):
+            at = pl.ds(pl.multiple_of(owner * rows + start + k * half, half), half)
+            h_all[at, :] = ref[k * (half + EXTRA) : k * (half + EXTRA) + half, :]
+
+    put(me, 0, own)
+    for step, refs in ((1, (m1, o1)), (2, (m2, o2)), (3, (m3, o3))):
+        for owner, ref in zip(owners_of(step), refs):
+            put(owner, 0, ref)
+    owner, _ = owners_of(4)
+    put(owner, core * half, m4)
+    put(owner, (1 - core) * half, o4)
+    out = dot_tn(h_all[...], d_qkv[...])
+    width = g_qkv.shape[2]
+    for i in range(3):
+        g_qkv[i] = out[:, i * width : (i + 1) * width]
+
+
+def input_kernel(dq_a, dq_b, joint_a, joint_b, flat_a, flat_b, d_h, dq_full, w_full, flat_full, sort_full):
+    row = lax.axis_index("head") // 2
+    width, nb = dq_a.shape[1], flat_a.shape[1]
+    sides = ((dq_a, joint_a, flat_a), (dq_b, joint_b, flat_b))
+    for j, (g, joint, flat) in enumerate(sides):
+        at = pl.multiple_of((row ^ j) * width, width)
+        dq_full[:, pl.ds(at, width)] = g[...]
+        w_full[:, pl.ds(at, width)] = joint[:, :width]
+        at = pl.multiple_of((row ^ j) * nb, nb)
+        flat_full[:, pl.ds(at, nb)] = flat[...]
+        sort_full[:, pl.ds(at, nb)] = joint[:, width:]
+    part = dot_nt(dq_full[...], w_full[...])
+    d_sum = sum(dot_nt(p, sort_full[...]) for p in three_parts(flat_full[...])[::-1]) / BLOCK
+    blocks = d_sum.shape[0]
+    for i in range(blocks):
+        sl = slice(i * BLOCK, (i + 1) * BLOCK)
+        d_h[sl, :] = part[sl, :] + d_sum[i : i + 1, :]
+
+
+def gain_kernel(tokens, d_mine, flat_mine, joint, g_two, out):
+    width = d_mine.shape[1]
+    normed, _ = norm_parts(tokens[...].astype(jnp.float32))
+    part = dot_nt(d_mine[...], joint[:, :width])
+    d_sum = sum(dot_nt(p, joint[:, width:]) for p in three_parts(flat_mine[...])[::-1]) / BLOCK
+    blocks = d_sum.shape[0]
+    sums = jnp.sum(part * normed, 0, keepdims=True)
+    means = jnp.sum(normed.reshape(blocks, BLOCK, D), 1)
+    sums = sums + jnp.sum(d_sum * means, 0, keepdims=True)
+    out[:8, :] = jnp.broadcast_to(sums, g_two.shape)
+    out[8:, :] = jnp.where(lax.axis_index("head") == 0, g_two[...], 0.0)
+
+
+def end_kernel(tokens, gain, own, other, d_middle, d_tokens):
+    f32 = jnp.float32
+    normed, inv = norm_parts(tokens[...].astype(f32))
+    d_h = own[...] + other[...]
+    d_tokens[...] = d_middle[...] + norm_back(d_h, normed, inv, gain[...].astype(f32))
+
+
+VMEM_SPEC = pl.BlockSpec(memory_space=pltpu.VMEM)
+SMEM_SPEC = pl.BlockSpec(memory_space=pltpu.SMEM)
+ANY_SPEC = pl.BlockSpec(memory_space=pltpu.HBM)
+
+
+def fetch(pairs, sems, first=0):
+    copies = []
+    for k, (source, target) in enumerate(pairs):
+        copies.append(pltpu.make_async_copy(source, target, sems.at[first + k]))
+        copies[-1].start()
+    return copies
+
+
+def wait_all(copies):
+    for copy in copies:
+        copy.wait()
+
+
+def call(kernel, outs, *args, scratch=(), smem=(), cold=(), raw=(), out_cold=(), limit=16, name=None):
+    cost = int(1e3 * TIMES[name])
+    shapes = [jax.ShapeDtypeStruct(s, d) for s, d in outs]
+    specs = [
+        SMEM_SPEC if i in smem else ANY_SPEC if i in cold or i in raw else VMEM_SPEC
+        for i in range(len(args))
+    ]
+    out_specs = [ANY_SPEC if i in out_cold else VMEM_SPEC for i in range(len(outs))]
+    buffers = [pltpu.VMEM(args[i].shape, args[i].dtype) for i in cold]
+    buffers += [pltpu.VMEM(*outs[i]) for i in out_cold]
+    sem_count = len(cold) + len(out_cold)
+    sems = [pltpu.SemaphoreType.DMA((sem_count,))] if sem_count else []
+    own = [pltpu.SemaphoreType.DMA((40,))] if raw else []
+
+    def body(*refs):
+        refs = list(refs)
+        ins, results = refs[: len(args)], refs[len(args) : len(args) + len(outs)]
+        rest = refs[len(args) + len(outs) :]
+        mine, rest = rest[: len(scratch)], rest[len(scratch) :]
+        room, rest = rest[: len(buffers)], rest[len(buffers) :]
+        copies = []
+        if cold:
+            copies = fetch([(ins[i], room[k]) for k, i in enumerate(cold)], rest[0])
+            for k, i in enumerate(cold):
+                ins[i] = room[k]
+        targets = list(results)
+        for k, i in enumerate(out_cold):
+            results[i] = room[len(cold) + k]
+        wait_all(copies)
+        kernel(*ins, *results, *mine, *(rest[-1:] if raw else []))
+        if out_cold:
+            wait_all(fetch([(results[i], targets[i]) for i in out_cold], rest[0], len(cold)))
+
+    result = pl.pallas_call(
+        body,
+        out_shape=shapes,
+        in_specs=specs,
+        out_specs=out_specs,
+        scratch_shapes=[pltpu.VMEM(s, d) for s, d in scratch] + buffers + sems + own,
+        compiler_params=pltpu.CompilerParams(vmem_limit_bytes=limit * 1024 * 1024),
+        cost_estimate=pl.CostEstimate(
+            flops=cost * FLOPS, bytes_accessed=cost * BYTES, transcendentals=0
+        ),
+        name=name,
+    )(*args)
+    return result[0] if len(shapes) == 1 else result
+
+
+TIMES = {
+    "norm_one": 1.7,
+    "project_own": 0.45,
+    "project": 0.7,
+    "attend": 4.2,
+    "prepare": 2.9,
+    "feed": 4.2,
+    "back": 1.2,
+    "pull": 2.4,
+    "grads": 0.95,
+    "relay": 0.2,
+    "collect": 4.5,
+    "sinkhorn_back": 2.05,
+    "total": 0.25,
+    "input_back": 1.0,
+    "gain_part": 0.8,
+    "weights": 3.6,
+    "norm_one_back": 1.7,
+    "output": 1.1,
+    "lay": 1.6,
+    "gains": 0.6,
+    "halve": 0.1,
+    "half": 0.1,
+    "pair": 0.1,
+    "add_gains": 0.1,
+    "sum_gains": 0.1,
+}
+FLOPS, BYTES = 1150000, 3690
+
+
+def tie(*values):
+    return lax.optimization_barrier(values)
+
+
+def after(value, *others):
+    return lax.optimization_barrier((value,) + others)[0]
+
+
+RING = (0, 2, 4, 6, 7, 5, 3, 1)
+SHARD = 512
+EXTRA = 32
+
+
+def local_eight(
+    tokens, gain_attn, gain_ffn, w_qkv, w_out, w_sort, w_up, w_down, gumbel_noise, partner, cotangent
+):
+    f32, bf16 = jnp.float32, jnp.bfloat16
+    rows = tokens.shape[0]
+    blocks = rows // BLOCK
+    width = w_out.shape[0]
+    ff = w_up.shape[1]
+    nb = partner.shape[0]
+    total = nb * BLOCK
+    half, quarter = rows // 2, rows // 4
+    core = lax.axis_index("head") % 2
+
+    def ahead(v):
+        return lax.ppermute(v, "blk", [(RING[i], RING[(i + 1) % 8]) for i in range(8)])
+
+    def behind(v):
+        return lax.ppermute(v, "blk", [(RING[i], RING[(i - 1) % 8]) for i in range(8)])
+
+    def swap_head(v, j):
+        return lax.ppermute(v, "head", [(i, i ^ j) for i in range(4)])
+
+    def swap_blk(v, j):
+        return lax.ppermute(v, "blk", [(i, i ^ j) for i in range(8)])
+
+    w_in = w_qkv.transpose(1, 0, 2)
+    partner_s = partner.T
+
+    def along(v):
+        pairs = []
+        for i in range(8):
+            for h in range(4):
+                to = RING[(i + 1) % 8] if h % 2 == 0 else RING[(i - 1) % 8]
+                pairs.append((RING[i] * 4 + h, to * 4 + h))
+        return lax.ppermute(v, ("blk", "head"), pairs)
+
+    shard, own_summary, own_noise, up_0 = call(
+        head_kernel,
+        [((rows + 2 * EXTRA, D), bf16), ((blocks, D), f32), ((2, D), f32), ((320, ff), bf16)],
+        tokens, gain_attn, gumbel_noise, swap_head(gumbel_noise, 1), w_up,
+        cold=(0, 1, 2, 3, 4), limit=62, name="norm_one",
+    )
+
+    def project(mine, other):
+        return call(
+            project_kernel, [((2 * rows, 3 * width), bf16), ((4 * EXTRA, D), bf16)], mine, other, joint,
+            name="project",
+        )
+
+    m1 = along(shard)
+    up_y0 = swap_head(up_0, 2)
+    qkv_own, joint, first, second, third = call(
+        project_own_kernel,
+        [
+            ((rows, 3 * width), bf16), ((D, 3 * width + 2 * nb), bf16),
+            ((D - 320 + width, D), bf16), ((352, D), bf16), ((ff - 352, D), bf16),
+        ],
+        shard, w_in, w_sort, w_out, w_up, w_down, name="project_own",
+    )
+    m1, up_y0, qkv_own = tie(m1, up_y0, qkv_own)
+    m2 = along(m1)
+    first_y = swap_head(after(first, m1), 2)
+    m2, first_y = tie(m2, first_y)
+    m3 = along(m2)
+    second_y = swap_head(after(second, m2), 2)
+    m3, second_y = tie(m3, second_y)
+    half_3, wo = call(
+        half_kernel, [((half + EXTRA, D), bf16), ((2 * width, D), bf16)], m3, w_out, first_y, name="half"
+    )
+    m4 = along(half_3)
+    third_y = swap_head(after(third, m3), 2)
+    o1 = swap_head(after(m1, half_3), 1)
+    o2 = swap_head(after(m2, half_3), 1)
+    o3 = swap_head(after(m3, half_3), 1)
+    qkv1 = project(m1, o1)
+    qkv2 = project(m2, o2)
+    qkv3 = project(m3, o3)
+    m4, third_y, _, _, _ = tie(m4, third_y, qkv1[0], qkv2[0], qkv3[0])
+    o4 = swap_head(m4, 1)
+    qkv, context, summary, steps, scale_rows, weight_rows = call(
+        attend_kernel,
+        [
+            ((total, 3 * width), bf16), ((rows, width), bf16), ((nb, D), f32),
+            ((2 * SINK, 2, nb, nb), f32), ((nb, 4 * DH), f32), ((nb, 2 * DH), f32),
+        ],
+        qkv_own, qkv1[0], qkv2[0], qkv3[0], qkv1[1], qkv2[1], qkv3[1], m4, o4, joint, own_summary, own_noise,
+        partner_s, partner_s, smem=(12,), scratch=[((nb, 2 * nb), f32)], name="attend",
+    )
+    ctx_y, ctx_c = swap_head(context, 2), swap_head(context, 1)
+    wo_other = swap_head(after(wo, context), 1)
+    prepared = ((3, 0, rows), (-3, 0, rows), (4, 0, rows))
+    amount = sum(n for _, _, n in prepared)
+    z_all, probs_all = call(
+        functools.partial(prepare_kernel, prepared), [((amount, 4 * DH), f32)] * 2,
+        qkv, partner_s, scale_rows, smem=(1,), name="prepare",
+    )
+    ctx_y, ctx_c, z_all = tie(ctx_y, ctx_c, z_all)
+    ctx_yc = swap_head(ctx_y, 1)
+    middle, h_two, active, d_hidden, ffn, d_h_two = call(
+        feed_kernel,
+        [
+            ((rows, D), f32),
+            ((rows, D), bf16),
+            ((rows, ff), bf16),
+            ((rows, ff), bf16),
+            ((rows, D), f32),
+            ((rows, D), f32),
+        ],
+        tokens, cotangent, gain_ffn, context, ctx_c, ctx_y, ctx_yc, wo, wo_other,
+        w_up, up_y0, first_y, w_down, second_y, third_y,
+        scratch=[
+            ((rows, 4 * width), bf16), ((4 * width, D), bf16), ((D, 2 * ff), bf16), ((2 * ff, D), bf16),
+            ((rows, 2 * ff), bf16), ((rows, 2 * ff), bf16),
+        ],
+        name="feed",
+    )
+    d_h_two_other = swap_head(d_h_two, 1)
+    d_middle, d_low, d_ctx, g_two = call(
+        back_kernel,
+        [((rows, D), f32), ((rows, D), bf16), ((rows, width), bf16), ((8, D), f32)],
+        middle, d_h_two, d_h_two_other, cotangent, gain_ffn, w_out, name="back",
+    )
+
+    plans = [[(0, 0)]] + [[(k, 0), (-k, 0)] for k in (1, 2, 3)] + [[(4, 0), (4, half)]]
+    offsets = (None, None, None, 0, 2 * blocks)
+    pulled = []
+
+    def pull(given):
+        plan, offset = plans[len(pulled)], offsets[len(pulled)]
+        n = sum(a.shape[0] for a in given)
+        pulled.append(
+            call(
+                functools.partial(pull_kernel, tuple(plan), offset),
+                [((n, 4 * DH), f32), ((n, 6 * DH), bf16), ((n // BLOCK, 4 * DH), f32)],
+                *given, qkv, partner_s, scale_rows, weight_rows,
+                *([] if offset is None else [z_all, probs_all]),
+                smem=(len(given) + 1,), name="pull",
+            )
+        )
+        return pulled[-1][0]
+
+    piece = (D + ff + width) // 8
+    front = 80
+    parts = call(
+        grads_kernel,
+        [((piece, D), f32)] * 7 + [((front, D), bf16), ((piece - front, D), bf16)],
+        h_two, d_hidden, active, cotangent, context, d_low,
+        scratch=[((D, ff), f32), ((ff, D), f32), ((width, D), f32)], name="grads",
+    )
+    keeps, (sum_f, sum_b) = parts[:7], parts[7:]
+    given = [d_ctx]
+    arrays = [given]
+    d_ctx, sum_f, sum_b = tie(d_ctx, sum_f, sum_b)
+    f = b = d_ctx
+    joint_y = swap_head(after(joint, sum_f), 2)
+    for step in range(4):
+        if step == 3:
+            f, b = call(halve_kernel, [((half, width), bf16)] * 2, f, b, name="halve")
+        f, b = ahead(f), behind(b)
+        sum_f, sum_b = ahead(sum_f), behind(sum_b)
+        done = pull(given)
+        hold = [joint_y] if step == 2 else []
+        f, b, sum_f, sum_b, _ = tie(f, b, sum_f, sum_b, done, *hold)[:5]
+        given = [f, b]
+        arrays.append(given)
+        if step < 3:
+            sum_f, sum_b = call(
+                relay_kernel, [((piece, D), bf16)] * 2, keeps[step], keeps[step + 3], sum_f, sum_b,
+                name="relay",
+            )
+    owned = call(total_kernel, [((piece, D), bf16)], keeps[6], sum_f, sum_b, name="total")
+    wf1, wb1 = ahead(owned), behind(owned)
+    pull(given)
+    spans = tuple(
+        tuple((step, start, a.shape[0]) for (step, start), a in zip(plan, given))
+        for plan, given in zip(plans, arrays)
+    )
+    d_qkv, d_mine, flat_mine, g_sort = call(
+        functools.partial(collect_kernel, spans),
+        [
+            ((total, 3 * width), bf16), ((rows, 3 * width), bf16), ((blocks, 2 * nb), f32), ((D, 2 * nb), f32),
+        ],
+        *[p[k] for k in range(3) for p in pulled], partner_s, partner_s, steps, summary, smem=(15,),
+        scratch=[
+            ((nb, 4 * DH), f32), ((total, 4 * DH), f32), ((total, 4 * DH), bf16), ((nb, 2 * nb), f32),
+        ],
+        name="collect",
+    )
+    wf1, wb1, d_mine, flat_mine = tie(wf1, wb1, d_mine, flat_mine)
+    wf2, wb2 = ahead(wf1), behind(wb1)
+    d_mine_y, flat_y = swap_head(d_mine, 2), swap_head(flat_mine, 2)
+    gains_a = call(
+        gain_kernel, [((16, D), f32)], tokens, d_mine, flat_mine, joint, g_two, name="gain_part"
+    )
+    gains_x = swap_blk(gains_a, 1)
+    gains = call(add_kernel, [((16, D), f32)], gains_a, gains_x, name="add_gains")
+    wf2, wb2, d_mine_y, flat_y, gains = tie(wf2, wb2, d_mine_y, flat_y, gains)
+    wf3, wb3 = ahead(wf2), behind(wb2)
+    gains1, gains2, gains3 = swap_blk(gains, 2), swap_blk(gains, 4), swap_blk(gains, 6)
+    d_h = call(
+        input_kernel, [((rows, D), f32)],
+        d_mine, d_mine_y, joint, joint_y, flat_mine, flat_y,
+        scratch=[
+            ((rows, 6 * width), bf16), ((D, 6 * width), bf16), ((blocks, 4 * nb), f32), ((D, 4 * nb), bf16),
+        ],
+        name="input_back",
+    )
+    d_h_other = swap_head(d_h, 1)
+    g_qkv = call(
+        weight_kernel, [((3, D, width), f32)],
+        shard, m1, o1, m2, o2, m3, o3, m4, o4, after(d_qkv, d_h),
+        scratch=[((total, D), bf16)], limit=24, name="weights",
+    )
+    wf3, wb3, gains1, gains2, gains3, d_h_other, g_qkv = tie(
+        wf3, wb3, gains1, gains2, gains3, d_h_other, g_qkv
+    )
+    cut_f, cut_b = call(
+        cut_kernel, [((front, D), bf16), ((piece - front, D), bf16)], wf3, wb3, name="halve"
+    )
+    wf4, wb4 = ahead(cut_f), behind(cut_b)
+    gains = call(four_kernel, [((16, D), f32)], gains, gains1, gains2, gains3, name="sum_gains")
+    gains_y = swap_head(gains, 2)
+    d_tokens = call(
+        end_kernel, [((rows, D), f32)],
+        tokens, gain_attn, d_h, d_h_other, d_middle, name="norm_one_back",
+    )
+    ffn_other = swap_head(after(ffn, wf3), 1)
+    gains = call(add_kernel, [((16, D), f32)], gains, gains_y, name="add_gains")
+    gains_c = swap_head(gains, 1)
+    output = call(add_kernel, [((rows, D), f32)], ffn, ffn_other, middle, name="output")
+    g_up, g_down, g_out = call(
+        lay_kernel,
+        [((D, ff), f32), ((ff, D), f32), ((width, D), f32)],
+        owned, wf1, wb1, wf2, wb2, wf3, wb3, wf4, wb4, name="lay",
+    )
+    g_one, g_two = call(gains_kernel, [((D,), f32), ((D,), f32)], gains, gains_c, name="gains")
+    return output, d_tokens, g_one, g_two, g_qkv.transpose(1, 0, 2), g_out, g_sort, g_up, g_down
+
+
 def solution(mesh):
     in_specs = (
         P("blk", None),
@@ -278,4 +1266,5 @@
         P(None, "head"),
         P("head", None),
     )
-    return jax.shard_map(local, mesh=mesh, in_specs=in_specs, out_specs=out_specs, check_vma=False)
+    plan = local_eight if mesh.shape["blk"] == 8 and mesh.shape["head"] == 4 else local
+    return jax.shard_map(plan, mesh=mesh, in_specs=in_specs, out_specs=out_specs, check_vma=False)

time: 576 us -> 141 us (0.24)
  waiting for transfers between devices: 248 us -> 44.8 us
  blocking collectives: 158 us -> 0 us
  other arithmetic: 55.5 us -> 0 us
  Pallas kernels: 0 us -> 43.7 us
  local copies, waits for them, and re-layouts: 45.3 us -> 1.72 us
  starting transfers between devices: 13.5 us -> 49.5 us
  matrix products: 34.2 us -> 0 us
  between operations: 17.2 us -> 1.06 us
    psum x5 -> x0, waiting for transfers between devices: 248 us -> none  [the longest x1 118 us: local(): lax.psum((g_gain_one, g_gain_two, g_qkv, g_out, g_sort, g_up, g_down), 'b...]
    unnamed x1 -> x0, blocking collectives: 68.9 us -> none
    all_gather x1 -> x0, blocking collectives: 66.2 us -> none  [local(): every_rows = lax.all_gather(own_rows, 'blk', axis=0, tiled=True)]
    ppermute x0 -> x53, starting transfers between devices: none -> 49.5 us  [the longest x12 16 us: behind(): lax.ppermute(v, 'blk', [(RING[i], RING[(i - 1) % 8]) for i in range(8)])]
    ppermute x0 -> x53, waiting for transfers between devices: none -> 44.8 us  [the longest x21 36.2 us: swap_head(): return lax.ppermute(v, 'head', [(i, i ^ j) for i in range(4)])]
    pallas_call x0 -> x33, Pallas kernels: none -> 43.7 us  [call(): pl.pallas_call(body, out_shape=shapes, in_specs=specs, out_specs=out_spec...]
    dot_general x29 -> x0, matrix products: 34.2 us -> none  [the longest x1 3.32 us: local(): jnp.einsum('st,sf->tf', selector, returned.reshape(dev_count * requests,...]
    reduce_sum x58 -> x0, other arithmetic: 29.8 us -> none  [the longest x8 4.11 us: balancing_log_space(): sort_logits = sort_logits - log_total(sort_logits, 1)]
  transfers between devices with their start and end apart: 7 -> 53, of which waited for: 5 -> 19; matrix products, arithmetic and copies ran while one was open for 7% -> 0% of each run, Pallas kernels for 0% -> 21%
where the time goes in v4:
time: 141 us
  starting transfers between devices  49.5 us (35%)
  waiting for transfers between devices  44.8 us (32%)
  Pallas kernels  43.7 us (31%)
  local copies, waits for them, and re-layouts  1.72 us (1%)
    pallas_call x33, Pallas kernels, call(): pl.pallas_call(body, out_shape=shapes, in_specs=specs, out_specs=out_spec...  43.7 us
    ppermute x21, waiting for transfers between devices, swap_head(): return lax.ppermute(v, 'head', [(i, i ^ j) for i in range(4)])  36.2 us
    ppermute x12, starting transfers between devices, behind(): lax.ppermute(v, 'blk', [(RING[i], RING[(i - 1) % 8]) for i in range(8)])  16 us
    ppermute x21, starting transfers between devices, swap_head(): return lax.ppermute(v, 'head', [(i, i ^ j) for i in range(4)])  15 us
    ppermute x12, starting transfers between devices, ahead(): lax.ppermute(v, 'blk', [(RING[i], RING[(i + 1) % 8]) for i in range(8)])  8.75 us
    ppermute x4, starting transfers between devices, swap_blk(): return lax.ppermute(v, 'blk', [(i, i ^ j) for i in range(8)])  5.39 us
    ppermute x4, starting transfers between devices, along(): return lax.ppermute(v, ('blk', 'head'), pairs)  4.44 us
    ppermute x12, waiting for transfers between devices, ahead(): lax.ppermute(v, 'blk', [(RING[i], RING[(i + 1) % 8]) for i in range(8)])  3.18 us
  transfers between devices with their start and end apart: 53, of which 19 were waited for; matrix products, arithmetic and copies ran while one was open for 0% of the time, Pallas kernels for 21%

profile of v4, /device:TPU:0, one launch (start us, length us, event | category | flops | bytes accessed | tf_op | source)
XLA Modules:
  0.0 140.8 jit_solution(10811936932970946220)
XLA Ops:
  1.2 1.0 collective-permute-done.refs_3_
  2.9 2.6 %norm_one.1 = (bf16[576,512]{1,0:T(8,128)(2,1)}, f32[8,512]{1,0:T(8,128)}, f32[2,512]{1,0:T(2,128)}, bf16[320,512]{1,0:T(8,128)(2,1)}) custom-call(bf16[512,512]{1,0:T(8,128)(2,1)} %refs_0_.7, bf16[512]{0:T(512)(128)(2,1)} %refs_1_.7, f32[8,2,64]{2,1,0:T(2,128)} %refs_2_.3, f32[8,2,64]{2,1,0:T(2,128)} %copy-done.14, bf16[512,512]{1,0:T(8,128)(2,1)} %refs_9_.1), custom_call_target="tpu_custom_call" | custom-call | flops 1955000064 | bytes 6273000 | tf_op jit(solution)/shard_map/norm_one/pallas_call | solution.py:947
  5.5 3.0 %collective-permute-start.1 = (bf16[576,512]{1,0:T(8,128)(2,1)}, bf16[576,512]{1,0:T(8,128)(2,1)S(1)}, u32[]{:S(2)}, u32[]{:S(2)}) collective-permute-start(bf16[576,512]{1,0:T(8,128)(2,1)} %get-tuple-element.144.refs_0_), channel_id=1, source_target_pairs={{0,8},{1,5},{2,10},{3,7},{8,16},{9,1},{10,18},{11,3},{16,24},{17,9... | collective-permute-start | bytes 1769480 | tf_op jit(solution)/shard_map/ppermute | solution.py:1039
  8.5 1.5 %collective-permute-start.2 = (bf16[320,512]{1,0:T(8,128)(2,1)}, bf16[320,512]{1,0:T(8,128)(2,1)S(1)}, u32[]{:S(2)}, u32[]{:S(2)}) collective-permute-start(bf16[320,512]{1,0:T(8,128)(2,1)} %get-tuple-element.145), channel_id=1, source_target_pairs={{0,2},{1,3},{2,0},{3,1},{4,6},{5,7},{6,4},{7,5},{8,10},{9,11},{10,... | collective-permute-start | bytes 983048 | tf_op jit(solution)/shard_map/ppermute | solution.py:1025
  10.0 1.1 copy-done
  11.6 6.5 %collective-permute-done.2.refs_10_ = bf16[320,512]{1,0:T(8,128)(2,1)S(1)} collective-permute-done((bf16[320,512]{1,0:T(8,128)(2,1)}, bf16[320,512]{1,0:T(8,128)(2,1)S(1)}, u32[]{:S(2)}, u32[]{:S(2)}) %collective-permute-start.2) | collective-permute-done | bytes 327712 | tf_op jit(solution)/shard_map/ppermute | solution.py:1025
  18.6 1.6 %collective-permute-start.4 = (bf16[320,512]{1,0:T(8,128)(2,1)S(1)}, bf16[320,512]{1,0:T(8,128)(2,1)S(1)}, u32[]{:S(2)}, u32[]{:S(2)}) collective-permute-start(bf16[320,512]{1,0:T(8,128)(2,1)S(1)} %get-tuple-element.150), channel_id=1, source_target_pairs={{0,2},{1,3},{2,0},{3,1},{4,6},{5,7},{6,4},{7,5},{8,10},{9,11},{10,... | collective-permute-start | bytes 983048 | tf_op jit(solution)/shard_map/ppermute | solution.py:1025
  20.2 8.7 %collective-permute-done.4.refs_2_.refs_11_ = bf16[320,512]{1,0:T(8,128)(2,1)S(1)} collective-permute-done((bf16[320,512]{1,0:T(8,128)(2,1)S(1)}, bf16[320,512]{1,0:T(8,128)(2,1)S(1)}, u32[]{:S(2)}, u32[]{:S(2)}) %collective-permute-start.4) | collective-permute-done | bytes 327712 | tf_op jit(solution)/shard_map/ppermute | solution.py:1025
  28.9 1.7 %collective-permute-start.6 = (bf16[352,512]{1,0:T(8,128)(2,1)S(1)}, bf16[352,512]{1,0:T(8,128)(2,1)S(1)}, u32[]{:S(2)}, u32[]{:S(2)}) collective-permute-start(bf16[352,512]{1,0:T(8,128)(2,1)S(1)} %get-tuple-element.153), channel_id=1, source_target_pairs={{0,2},{1,3},{2,0},{3,1},{4,6},{5,7},{6,4},{7,5},{8,10},{9,11},{10,... | collective-permute-start | bytes 1081352 | tf_op jit(solution)/shard_map/ppermute | solution.py:1025
  30.6 9.1 %collective-permute-done.6.refs_13_ = bf16[352,512]{1,0:T(8,128)(2,1)S(1)} collective-permute-done((bf16[352,512]{1,0:T(8,128)(2,1)S(1)}, bf16[352,512]{1,0:T(8,128)(2,1)S(1)}, u32[]{:S(2)}, u32[]{:S(2)}) %collective-permute-start.6) | collective-permute-done | bytes 360480 | tf_op jit(solution)/shard_map/ppermute | solution.py:1025
  41.6 1.7 %collective-permute-start.11 = (bf16[160,512]{1,0:T(8,128)(2,1)S(1)}, bf16[160,512]{1,0:T(8,128)(2,1)S(1)}, u32[]{:S(2)}, u32[]{:S(2)}) collective-permute-start(bf16[160,512]{1,0:T(8,128)(2,1)S(1)} %get-tuple-element.168), channel_id=1, source_target_pairs={{0,2},{1,3},{2,0},{3,1},{4,6},{5,7},{6,4},{7,5},{8,10},{9,11},{10,... | collective-permute-start | bytes 491528 | tf_op jit(solution)/shard_map/ppermute | solution.py:1025
  45.5 2.8 %collective-permute-done.11.refs_14_ = bf16[160,512]{1,0:T(8,128)(2,1)S(1)} collective-permute-done((bf16[160,512]{1,0:T(8,128)(2,1)S(1)}, bf16[160,512]{1,0:T(8,128)(2,1)S(1)}, u32[]{:S(2)}, u32[]{:S(2)}) %collective-permute-start.11) | collective-permute-done | bytes 163872 | tf_op jit(solution)/shard_map/ppermute | solution.py:1025
  48.5 1.4 %collective-permute-done.12.refs_8_ = bf16[288,512]{1,0:T(8,128)(2,1)S(1)} collective-permute-done((bf16[288,512]{1,0:T(8,128)(2,1)S(1)}, bf16[288,512]{1,0:T(8,128)(2,1)S(1)}, u32[]{:S(2)}, u32[]{:S(2)}) %collective-permute-start.12) | collective-permute-done | bytes 294944 | tf_op jit(solution)/shard_map/ppermute | solution.py:1025
  50.0 3.7 %attend.1 = (bf16[4096,384]{1,0:T(8,128)(2,1)S(1)}, bf16[512,128]{1,0:T(8,128)(2,1)S(1)}, f32[64,512]{1,0:T(8,128)S(1)}, f32[16,2,64,64]{3,2,1,0:T(8,128)S(1)}, ...) custom-call(bf16[512,384]{1,0:T(8,128)(2,1)S(1)} %get-tuple-element.147.refs_0_, ...), custom_call_target="tpu_custom_call" | custom-call | flops 4830000128 | bytes 15498000 | tf_op jit(solution)/shard_map/attend/pallas_call | solution.py:947
  53.6 1.8 %collective-permute-start.13 = (bf16[512,128]{1,0:T(8,128)(2,1)S(1)}, bf16[512,128]{1,0:T(8,128)(2,1)S(1)}, u32[]{:S(2)}, u32[]{:S(2)}) collective-permute-start(bf16[512,128]{1,0:T(8,128)(2,1)S(1)} %get-tuple-element.172.refs_3_.refs_4_), channel_id=1, source_target_pairs={{0,2},{1,3},{2,0},{3,1},{4,6},{5,7},{6,4},{7,5},{8,10},{9,11},{10,... | collective-permute-start | bytes 393224 | tf_op jit(solution)/shard_map/ppermute | solution.py:1025
  56.0 2.8 %prepare.1 = (f32[1536,256]{1,0:T(8,128)S(1)}, f32[1536,256]{1,0:T(8,128)S(1)}) custom-call(bf16[4096,384]{1,0:T(8,128)(2,1)S(1)} %get-tuple-element.173.refs_0_.refs_1_.refs_2_, s32[2,64]{1,0:T(2,128)S(1)} %bitcast.6, f32[64,256]{1,0:T(8,128)S(1)} %get-tuple-element.174.refs_2_.refs_3_.refs_4_), custom_call_target="tpu_custom_call" | custom-call | flops 3335000064 | bytes 10701000 | tf_op jit(solution)/shard_map/prepare/pallas_call | solution.py:947
  59.3 1.3 collective-permute-done.15.refs_6_
  60.6 4.2 %feed.1 = (f32[512,512]{1,0:T(8,128)S(1)}, bf16[512,512]{1,0:T(8,128)(2,1)S(1)}, bf16[512,512]{1,0:T(8,128)(2,1)S(1)}, bf16[512,512]{1,0:T(8,128)(2,1)S(1)}, f32...) custom-call(bf16[512,512]{1,0:T(8,128)(2,1)S(1)} %copy-done.8, bf16[512,512]{1,0:T(8,128)(2,1)S(1)} %copy-done.7, ...), custom_call_target="tpu_custom_call" | custom-call | flops 4830000128 | bytes 15498000 | tf_op jit(solution)/shard_map/feed/pallas_call | solution.py:947
  65.0 2.5 %collective-permute-done.17.refs_2_ = f32[512,512]{1,0:T(8,128)S(1)} collective-permute-done((f32[512,512]{1,0:T(8,128)S(1)}, f32[512,512]{1,0:T(8,128)S(1)}, u32[]{:S(2)}, u32[]{:S(2)}) %collective-permute-start.17) | collective-permute-done | bytes 1048608 | tf_op jit(solution)/shard_map/ppermute | solution.py:1025
  69.6 1.9 %collective-permute-start.19 = (bf16[512,128]{1,0:T(8,128)(2,1)S(1)}, bf16[512,128]{1,0:T(8,128)(2,1)S(1)}, u32[]{:S(2)}, u32[]{:S(2)}) collective-permute-start(bf16[512,128]{1,0:T(8,128)(2,1)S(1)} %get-tuple-element.194.refs_0_), channel_id=1, source_target_pairs={{0,4},{8,0},{16,8},{24,16},{28,24},{20,28},{12,20},{4,12},{1,5},{9... | collective-permute-start | bytes 393224 | tf_op jit(solution)/shard_map/ppermute | solution.py:1022
  71.6 1.9 %collective-permute-start.21 = (bf16[64,512]{1,0:T(8,128)(2,1)S(1)}, bf16[64,512]{1,0:T(8,128)(2,1)S(1)}, u32[]{:S(2)}, u32[]{:S(2)}) collective-permute-start(bf16[64,512]{1,0:T(8,128)(2,1)S(1)} %get-tuple-element.196), channel_id=1, source_target_pairs={{0,4},{8,0},{16,8},{24,16},{28,24},{20,28},{12,20},{4,12},{1,5},{9... | collective-permute-start | bytes 196616 | tf_op jit(solution)/shard_map/ppermute | solution.py:1022
  73.5 1.8 %pull.5 = (f32[512,256]{1,0:T(8,128)S(1)}, bf16[512,384]{1,0:T(8,128)(2,1)S(1)}, f32[8,256]{1,0:T(8,128)S(1)}) custom-call(bf16[512,128]{1,0:T(8,128)(2,1)S(1)} %get-tuple-element.194.refs_0_, bf16[4096,384]{1,0:T(8,128)(2,1)S(1)} %get-tuple-element.173.refs_0_.refs_1_.refs_2_, s32[2,64]{1,0:T(2,128)S(1)} %bitcast.7, ...), custom_call_target="tpu_custom_call" | custom-call | flops 2760000000 | bytes 8856000 | tf_op jit(solution)/shard_map/pull/pallas_call | solution.py:947
  75.2 1.9 %collective-permute-start.30 = (bf16[512,512]{1,0:T(8,128)(2,1)S(1)}, bf16[512,512]{1,0:T(8,128)(2,1)S(1)}, u32[]{:S(2)}, u32[]{:S(2)}) collective-permute-start(bf16[512,512]{1,0:T(8,128)(2,1)S(1)} %get-tuple-element.217.refs_2_.refs_9_.refs_3_), channel_id=1, source_target_pairs={{0,2},{1,3},{2,0},{3,1},{4,6},{5,7},{6,4},{7,5},{8,10},{9,11},{10,... | collective-permute-start | bytes 1572872 | tf_op jit(solution)/shard_map/ppermute | solution.py:1025
  77.3 1.9 %collective-permute-start.23 = (bf16[512,128]{1,0:T(8,128)(2,1)S(1)}, bf16[512,128]{1,0:T(8,128)(2,1)S(1)}, u32[]{:S(2)}, u32[]{:S(2)}) collective-permute-start(bf16[512,128]{1,0:T(8,128)(2,1)S(1)} %collective-permute-done.19.refs_1_), channel_id=1, source_target_pairs={{0,4},{8,0},{16,8},{24,16},{28,24},{20,28},{12,20},{4,12},{1,5},{9... | collective-permute-start | bytes 393224 | tf_op jit(solution)/shard_map/ppermute | solution.py:1022
  79.5 1.9 %collective-permute-start.25 = (bf16[144,512]{1,0:T(8,128)(2,1)S(1)}, bf16[144,512]{1,0:T(8,128)(2,1)S(1)}, u32[]{:S(2)}, u32[]{:S(2)}) collective-permute-start(bf16[144,512]{1,0:T(8,128)(2,1)S(1)} %get-tuple-element.206), channel_id=1, source_target_pairs={{0,4},{8,0},{16,8},{24,16},{28,24},{20,28},{12,20},{4,12},{1,5},{9... | collective-permute-start | bytes 442376 | tf_op jit(solution)/shard_map/ppermute | solution.py:1022
  81.3 2.8 %pull.6 = (f32[1024,256]{1,0:T(8,128)S(1)}, bf16[1024,384]{1,0:T(8,128)(2,1)S(1)}, f32[16,256]{1,0:T(8,128)S(1)}) custom-call(bf16[512,128]{1,0:T(8,128)(2,1)S(1)} %collective-permute-done.18.refs_0_, bf16[512,128]{1,0:T(8,128)(2,1)S(1)} %collective-permute-done.19.refs_1_, bf16[4096,384]{1,0:T(8,128)(2,1)S(1)} %get-tuple-element.173.refs_0_.refs_1_.refs_2_, ...), custom_call_target="tpu_custom_call" | custom-call | flops 2760000000 | bytes 8856000 | tf_op jit(solution)/shard_map/pull/pallas_call | solution.py:947
  85.3 1.7 %collective-permute-start.27 = (bf16[512,128]{1,0:T(8,128)(2,1)S(1)}, bf16[512,128]{1,0:T(8,128)(2,1)S(1)}, u32[]{:S(2)}, u32[]{:S(2)}) collective-permute-start(bf16[512,128]{1,0:T(8,128)(2,1)S(1)} %collective-permute-done.23.refs_1_), channel_id=1, source_target_pairs={{0,4},{8,0},{16,8},{24,16},{28,24},{20,28},{12,20},{4,12},{1,5},{9... | collective-permute-start | bytes 393224 | tf_op jit(solution)/shard_map/ppermute | solution.py:1022
  87.4 1.7 %collective-permute-start.29 = (bf16[144,512]{1,0:T(8,128)(2,1)S(1)}, bf16[144,512]{1,0:T(8,128)(2,1)S(1)}, u32[]{:S(2)}, u32[]{:S(2)}) collective-permute-start(bf16[144,512]{1,0:T(8,128)(2,1)S(1)} %get-tuple-element.215), channel_id=1, source_target_pairs={{0,4},{8,0},{16,8},{24,16},{28,24},{20,28},{12,20},{4,12},{1,5},{9... | collective-permute-start | bytes 442376 | tf_op jit(solution)/shard_map/ppermute | solution.py:1022
  89.1 2.8 %pull.7 = (f32[1024,256]{1,0:T(8,128)S(1)}, bf16[1024,384]{1,0:T(8,128)(2,1)S(1)}, f32[16,256]{1,0:T(8,128)S(1)}) custom-call(bf16[512,128]{1,0:T(8,128)(2,1)S(1)} %collective-permute-done.22.refs_0_, bf16[512,128]{1,0:T(8,128)(2,1)S(1)} %collective-permute-done.23.refs_1_, bf16[4096,384]{1,0:T(8,128)(2,1)S(1)} %get-tuple-element.173.refs_0_.refs_1_.refs_2_, ...), custom_call_target="tpu_custom_call" | custom-call | flops 2760000000 | bytes 8856000 | tf_op jit(solution)/shard_map/pull/pallas_call | solution.py:947
  93.3 1.4 collective-permute-start.32
  95.5 1.4 collective-permute-start.34
  96.8 2.2 %pull.8 = (f32[1024,256]{1,0:T(8,128)S(1)}, bf16[1024,384]{1,0:T(8,128)(2,1)S(1)}, f32[16,256]{1,0:T(8,128)S(1)}) custom-call(bf16[512,128]{1,0:T(8,128)(2,1)S(1)} %collective-permute-done.26.refs_0_, bf16[512,128]{1,0:T(8,128)(2,1)S(1)} %collective-permute-done.27.refs_1_, bf16[4096,384]{1,0:T(8,128)(2,1)S(1)} %get-tuple-element.173.refs_0_.refs_1_.refs_2_, ...), custom_call_target="tpu_custom_call" | custom-call | flops 2760000000 | bytes 8856000 | tf_op jit(solution)/shard_map/pull/pallas_call | solution.py:947
  99.1 2.2 %collective-permute-done.33.refs_1_ = bf16[144,512]{1,0:T(8,128)(2,1)S(1)} collective-permute-done((bf16[144,512]{1,0:T(8,128)(2,1)S(1)}, bf16[144,512]{1,0:T(8,128)(2,1)S(1)}, u32[]{:S(2)}, u32[]{:S(2)}) %collective-permute-start.33) | collective-permute-done | bytes 147488 | tf_op jit(solution)/shard_map/ppermute | solution.py:1019
  102.2 1.7 %collective-permute-start.35 = (bf16[144,512]{1,0:T(8,128)(2,1)S(1)}, bf16[144,512]{1,0:T(8,128)(2,1)S(1)}, u32[]{:S(2)}, u32[]{:S(2)}) collective-permute-start(bf16[144,512]{1,0:T(8,128)(2,1)S(1)} %total.1.refs_0_), channel_id=1, source_target_pairs={{0,8},{8,16},{16,24},{24,28},{28,20},{20,12},{12,4},{4,0},{1,9},{9... | collective-permute-start | bytes 442376 | tf_op jit(solution)/shard_map/ppermute | solution.py:1019
  104.3 1.5 %pull.9 = (f32[512,256]{1,0:T(8,128)S(1)}, bf16[512,384]{1,0:T(8,128)(2,1)S(1)}, f32[8,256]{1,0:T(8,128)S(1)}) custom-call(bf16[256,128]{1,0:T(8,128)(2,1)S(1)} %collective-permute-done.31.refs_0_, bf16[256,128]{1,0:T(8,128)(2,1)S(1)} %collective-permute-done.32.refs_1_, bf16[4096,384]{1,0:T(8,128)(2,1)S(1)} %get-tuple-element.173.refs_0_.refs_1_.refs_2_, ...), custom_call_target="tpu_custom_call" | custom-call | flops 2760000000 | bytes 8856000 | tf_op jit(solution)/shard_map/pull/pallas_call | solution.py:947
  105.8 4.5 %collect.1 = (bf16[4096,384]{1,0:T(8,128)(2,1)S(1)}, bf16[512,384]{1,0:T(8,128)(2,1)S(1)}, f32[8,128]{1,0:T(8,128)S(1)}, f32[512,128]{1,0:T(8,128)}) custom-call(f32[512,256]{1,0:T(8,128)S(1)} %get-tuple-element.198.refs_0_, f32[1024,256]{1,0:T(8,128)S(1)} %get-tuple-element.207.refs_1_, f32[1024,256]{1,0:T(8,128)S(1)} %get-tuple-element.216.refs_2_, ...), custom_call_target="tpu_custom_call" | custom-call | flops 5175000064 | bytes 16605000 | tf_op jit(solution)/shard_map/collect/pallas_call | solution.py:947
  110.3 1.9 %collective-permute-start.39 = (bf16[512,384]{1,0:T(8,128)(2,1)S(1)}, bf16[512,384]{1,0:T(8,128)(2,1)S(1)}, u32[]{:S(2)}, u32[]{:S(2)}) collective-permute-start(bf16[512,384]{1,0:T(8,128)(2,1)S(1)} %get-tuple-element.252.refs_1_.refs_0_), channel_id=1, source_target_pairs={{0,2},{1,3},{2,0},{3,1},{4,6},{5,7},{6,4},{7,5},{8,10},{9,11},{10,... | collective-permute-start | bytes 1179656 | tf_op jit(solution)/shard_map/ppermute | solution.py:1025
  112.2 1.5 %collective-permute-start.37 = (bf16[144,512]{1,0:T(8,128)(2,1)S(1)}, bf16[144,512]{1,0:T(8,128)(2,1)S(1)}, u32[]{:S(2)}, u32[]{:S(2)}) collective-permute-start(bf16[144,512]{1,0:T(8,128)(2,1)S(1)} %collective-permute-done.35.refs_1_), channel_id=1, source_target_pairs={{0,8},{8,16},{16,24},{24,28},{28,20},{20,12},{12,4},{4,0},{1,9},{9... | collective-permute-start | bytes 442376 | tf_op jit(solution)/shard_map/ppermute | solution.py:1019
  116.0 2.8 %collective-permute-done.41.refs_1_ = f32[16,512]{1,0:T(8,128)S(1)} collective-permute-done((f32[16,512]{1,0:T(8,128)S(1)}, f32[16,512]{1,0:T(8,128)S(1)}, u32[]{:S(2)}, u32[]{:S(2)}) %collective-permute-start.41) | collective-permute-done | bytes 32800 | tf_op jit(solution)/shard_map/ppermute | solution.py:1028
  120.4 2.0 %collective-permute-start.44 = (f32[16,512]{1,0:T(8,128)S(1)}, f32[16,512]{1,0:T(8,128)S(1)}, u32[]{:S(2)}, u32[]{:S(2)}) collective-permute-start(f32[16,512]{1,0:T(8,128)S(1)} %add_gains.2.refs_0_), channel_id=1, source_target_pairs={{0,8},{4,12},{8,0},{12,4},{16,24},{20,28},{24,16},{28,20},{1,9},{5... | collective-permute-start | bytes 98312 | tf_op jit(solution)/shard_map/ppermute | solution.py:1028
  122.4 2.2 %collective-permute-start.45 = (f32[16,512]{1,0:T(8,128)S(1)}, f32[16,512]{1,0:T(8,128)S(1)}, u32[]{:S(2)}, u32[]{:S(2)}) collective-permute-start(f32[16,512]{1,0:T(8,128)S(1)} %add_gains.2.refs_0_), channel_id=1, source_target_pairs={{0,16},{4,20},{8,24},{12,28},{16,0},{20,4},{24,8},{28,12},{1,17},{... | collective-permute-start | bytes 98312 | tf_op jit(solution)/shard_map/ppermute | solution.py:1028
  126.9 3.5 %weights.1 = f32[3,512,128]{2,1,0:T(8,128)} custom-call(bf16[576,512]{1,0:T(8,128)(2,1)S(1)} %copy-done.1, bf16[576,512]{1,0:T(8,128)(2,1)S(1)} %collective-permute-done.1.refs_0_.refs_1_, bf16[576,512]{1,0:T(8,128)(2,1)S(1)} %collective-permute-done.7.refs_1_.refs_2_, bf16[576,512]{1,0:T(8,128)(2,1)S(1)} %collective-permute-done.3.refs_0_.refs_3_, ...), custom_call_target="tpu_custom_call" | custom-call | flops 4140000000 | bytes 13284000 | tf_op jit(solution)/shard_map/weights/pallas_call | solution.py:947
  130.5 1.2 collective-permute-done.43.refs_1_.refs_6_
  132.0 1.6 %collective-permute-start.51 = (bf16[80,512]{1,0:T(8,128)(2,1)S(1)}, bf16[80,512]{1,0:T(8,128)(2,1)S(1)}, u32[]{:S(2)}, u32[]{:S(2)}) collective-permute-start(bf16[80,512]{1,0:T(8,128)(2,1)S(1)} %get-tuple-element.273), channel_id=1, source_target_pairs={{0,8},{8,16},{16,24},{24,28},{28,20},{20,12},{12,4},{4,0},{1,9},{9... | collective-permute-start | bytes 245768 | tf_op jit(solution)/shard_map/ppermute | solution.py:1019
  134.1 1.6 %collective-permute-done.49.refs_1_ = f32[16,512]{1,0:T(8,128)S(1)} collective-permute-done((f32[16,512]{1,0:T(8,128)S(1)}, f32[16,512]{1,0:T(8,128)S(1)}, u32[]{:S(2)}, u32[]{:S(2)}) %collective-permute-start.49) | collective-permute-done | bytes 32800 | tf_op jit(solution)/shard_map/ppermute | solution.py:1025
  135.7 1.7 %norm_one_back.1 = f32[512,512]{1,0:T(8,128)} custom-call(bf16[512,512]{1,0:T(8,128)(2,1)S(1)} %copy-done.8, bf16[512]{0:T(512)(128)(2,1)S(1)} %copy-done.11, f32[512,512]{1,0:T(8,128)S(1)} %input_back.1.refs_2_, f32[512,512]{1,0:T(8,128)S(1)} %collective-permute-done.47.refs_3_, f32[512,512]{1,0:T(8,128)S(1)} %get-tuple-element.265.refs_4_), custom_call_target="tpu_custom_call" | custom-call | flops 1955000064 | bytes 6273000 | tf_op jit(solution)/shard_map/norm_one_back/pallas_call | solution.py:947
  138.0 1.6 %lay.1 = (f32[512,512]{1,0:T(8,128)}, f32[512,512]{1,0:T(8,128)}, f32[128,512]{1,0:T(8,128)}) custom-call(bf16[144,512]{1,0:T(8,128)(2,1)S(1)} %total.1.refs_0_, bf16[144,512]{1,0:T(8,128)(2,1)S(1)} %collective-permute-done.35.refs_1_, bf16[144,512]{1,0:T(8,128)(2,1)S(1)} %collective-permute-done.36.refs_2_, ...), custom_call_target="tpu_custom_call" | custom-call | flops 1840000000 | bytes 5904000 | tf_op jit(solution)/shard_map/lay/pallas_call | solution.py:947
  139.6 1.1 output.1
  (121 shorter events, 22.8 us)
Async XLA Ops:
  5.5 12.6 %collective-permute-start.1 = (bf16[576,512]{1,0:T(8,128)(2,1)}, bf16[576,512]{1,0:T(8,128)(2,1)S(1)}, u32[]{:S(2)}, u32[]{:S(2)}) collective-permute-start(bf16[576,512]{1,0:T(8,128)(2,1)} %get-tuple-element.144.refs_0_), channel_id=1, source_target_pairs={{0,8},{1,5},{2,10},{3,7},{8,16},{9,1},{10,18},{11,3},{16,24},{17,9... | collective-permute-start | bytes 1769480 | tf_op jit(solution)/shard_map/ppermute | solution.py:1039
  8.5 9.6 %collective-permute-start.2 = (bf16[320,512]{1,0:T(8,128)(2,1)}, bf16[320,512]{1,0:T(8,128)(2,1)S(1)}, u32[]{:S(2)}, u32[]{:S(2)}) collective-permute-start(bf16[320,512]{1,0:T(8,128)(2,1)} %get-tuple-element.145), channel_id=1, source_target_pairs={{0,2},{1,3},{2,0},{3,1},{4,6},{5,7},{6,4},{7,5},{8,10},{9,11},{10,... | collective-permute-start | bytes 983048 | tf_op jit(solution)/shard_map/ppermute | solution.py:1025
  18.1 10.8 %collective-permute-start.3 = (bf16[576,512]{1,0:T(8,128)(2,1)S(1)}, bf16[576,512]{1,0:T(8,128)(2,1)S(1)}, u32[]{:S(2)}, u32[]{:S(2)}) collective-permute-start(bf16[576,512]{1,0:T(8,128)(2,1)S(1)} %collective-permute-done.1.refs_0_.refs_1_), channel_id=1, source_target_pairs={{0,8},{1,5},{2,10},{3,7},{8,16},{9,1},{10,18},{11,3},{16,24},{17,9... | collective-permute-start | bytes 1769480 | tf_op jit(solution)/shard_map/ppermute | solution.py:1039
  18.6 10.3 %collective-permute-start.4 = (bf16[320,512]{1,0:T(8,128)(2,1)S(1)}, bf16[320,512]{1,0:T(8,128)(2,1)S(1)}, u32[]{:S(2)}, u32[]{:S(2)}) collective-permute-start(bf16[320,512]{1,0:T(8,128)(2,1)S(1)} %get-tuple-element.150), channel_id=1, source_target_pairs={{0,2},{1,3},{2,0},{3,1},{4,6},{5,7},{6,4},{7,5},{8,10},{9,11},{10,... | collective-permute-start | bytes 983048 | tf_op jit(solution)/shard_map/ppermute | solution.py:1025
  28.9 10.8 %collective-permute-start.5 = (bf16[576,512]{1,0:T(8,128)(2,1)S(1)}, bf16[576,512]{1,0:T(8,128)(2,1)S(1)}, u32[]{:S(2)}, u32[]{:S(2)}) collective-permute-start(bf16[576,512]{1,0:T(8,128)(2,1)S(1)} %collective-permute-done.3.refs_0_.refs_3_), channel_id=1, source_target_pairs={{0,8},{1,5},{2,10},{3,7},{8,16},{9,1},{10,18},{11,3},{16,24},{17,9... | collective-permute-start | bytes 1769480 | tf_op jit(solution)/shard_map/ppermute | solution.py:1039
  28.9 10.8 %collective-permute-start.6 = (bf16[352,512]{1,0:T(8,128)(2,1)S(1)}, bf16[352,512]{1,0:T(8,128)(2,1)S(1)}, u32[]{:S(2)}, u32[]{:S(2)}) collective-permute-start(bf16[352,512]{1,0:T(8,128)(2,1)S(1)} %get-tuple-element.153), channel_id=1, source_target_pairs={{0,2},{1,3},{2,0},{3,1},{4,6},{5,7},{6,4},{7,5},{8,10},{9,11},{10,... | collective-permute-start | bytes 1081352 | tf_op jit(solution)/shard_map/ppermute | solution.py:1025
  39.8 3.6 %collective-permute-start.7 = (bf16[576,512]{1,0:T(8,128)(2,1)S(1)}, bf16[576,512]{1,0:T(8,128)(2,1)S(1)}, u32[]{:S(2)}, u32[]{:S(2)}) collective-permute-start(bf16[576,512]{1,0:T(8,128)(2,1)S(1)} %collective-permute-done.1.refs_0_.refs_1_), channel_id=1, source_target_pairs={{0,1},{1,0},{2,3},{3,2},{4,5},{5,4},{6,7},{7,6},{8,9},{9,8},{10,11... | collective-permute-start | bytes 1769480 | tf_op jit(solution)/shard_map/ppermute | solution.py:1025
  40.1 4.0 %collective-permute-start.8 = (bf16[576,512]{1,0:T(8,128)(2,1)S(1)}, bf16[576,512]{1,0:T(8,128)(2,1)S(1)}, u32[]{:S(2)}, u32[]{:S(2)}) collective-permute-start(bf16[576,512]{1,0:T(8,128)(2,1)S(1)} %collective-permute-done.3.refs_0_.refs_3_), channel_id=1, source_target_pairs={{0,1},{1,0},{2,3},{3,2},{4,5},{5,4},{6,7},{7,6},{8,9},{9,8},{10,11... | collective-permute-start | bytes 1769480 | tf_op jit(solution)/shard_map/ppermute | solution.py:1025
  40.3 4.5 %collective-permute-start.9 = (bf16[576,512]{1,0:T(8,128)(2,1)S(1)}, bf16[576,512]{1,0:T(8,128)(2,1)S(1)}, u32[]{:S(2)}, u32[]{:S(2)}) collective-permute-start(bf16[576,512]{1,0:T(8,128)(2,1)S(1)} %collective-permute-done.5.refs_0_.refs_5_), channel_id=1, source_target_pairs={{0,1},{1,0},{2,3},{3,2},{4,5},{5,4},{6,7},{7,6},{8,9},{9,8},{10,11... | collective-permute-start | bytes 1769480 | tf_op jit(solution)/shard_map/ppermute | solution.py:1025
  40.6 7.8 %collective-permute-start.10 = (bf16[288,512]{1,0:T(8,128)(2,1)S(1)}, bf16[288,512]{1,0:T(8,128)(2,1)S(1)}, u32[]{:S(2)}, u32[]{:S(2)}) collective-permute-start(bf16[288,512]{1,0:T(8,128)(2,1)S(1)} %get-tuple-element.156), channel_id=1, source_target_pairs={{0,8},{1,5},{2,10},{3,7},{8,16},{9,1},{10,18},{11,3},{16,24},{17,9... | collective-permute-start | bytes 884744 | tf_op jit(solution)/shard_map/ppermute | solution.py:1039
  41.6 6.8 %collective-permute-start.11 = (bf16[160,512]{1,0:T(8,128)(2,1)S(1)}, bf16[160,512]{1,0:T(8,128)(2,1)S(1)}, u32[]{:S(2)}, u32[]{:S(2)}) collective-permute-start(bf16[160,512]{1,0:T(8,128)(2,1)S(1)} %get-tuple-element.168), channel_id=1, source_target_pairs={{0,2},{1,3},{2,0},{3,1},{4,6},{5,7},{6,4},{7,5},{8,10},{9,11},{10,... | collective-permute-start | bytes 491528 | tf_op jit(solution)/shard_map/ppermute | solution.py:1025
  53.6 5.6 %collective-permute-start.13 = (bf16[512,128]{1,0:T(8,128)(2,1)S(1)}, bf16[512,128]{1,0:T(8,128)(2,1)S(1)}, u32[]{:S(2)}, u32[]{:S(2)}) collective-permute-start(bf16[512,128]{1,0:T(8,128)(2,1)S(1)} %get-tuple-element.172.refs_3_.refs_4_), channel_id=1, source_target_pairs={{0,2},{1,3},{2,0},{3,1},{4,6},{5,7},{6,4},{7,5},{8,10},{9,11},{10,... | collective-permute-start | bytes 393224 | tf_op jit(solution)/shard_map/ppermute | solution.py:1025
  55.4 3.8 %collective-permute-start.14 = (bf16[512,128]{1,0:T(8,128)(2,1)S(1)}, bf16[512,128]{1,0:T(8,128)(2,1)S(1)}, u32[]{:S(2)}, u32[]{:S(2)}) collective-permute-start(bf16[512,128]{1,0:T(8,128)(2,1)S(1)} %get-tuple-element.172.refs_3_.refs_4_), channel_id=1, source_target_pairs={{0,1},{1,0},{2,3},{3,2},{4,5},{5,4},{6,7},{7,6},{8,9},{9,8},{10,11... | collective-permute-start | bytes 393224 | tf_op jit(solution)/shard_map/ppermute | solution.py:1025
  55.5 3.8 %collective-permute-start.16 = (bf16[256,512]{1,0:T(8,128)(2,1)S(1)}, bf16[256,512]{1,0:T(8,128)(2,1)S(1)}, u32[]{:S(2)}, u32[]{:S(2)}) collective-permute-start(bf16[256,512]{1,0:T(8,128)(2,1)S(1)} %get-tuple-element.179.refs_7_), channel_id=1, source_target_pairs={{0,1},{1,0},{2,3},{3,2},{4,5},{5,4},{6,7},{7,6},{8,9},{9,8},{10,11... | collective-permute-start | bytes 786440 | tf_op jit(solution)/shard_map/ppermute | solution.py:1025
  69.4 7.7 %collective-permute-start.18 = (bf16[512,128]{1,0:T(8,128)(2,1)S(1)}, bf16[512,128]{1,0:T(8,128)(2,1)S(1)}, u32[]{:S(2)}, u32[]{:S(2)}) collective-permute-start(bf16[512,128]{1,0:T(8,128)(2,1)S(1)} %get-tuple-element.194.refs_0_), channel_id=1, source_target_pairs={{0,8},{8,16},{16,24},{24,28},{28,20},{20,12},{12,4},{4,0},{1,9},{9... | collective-permute-start | bytes 393224 | tf_op jit(solution)/shard_map/ppermute | solution.py:1019
  69.6 7.5 %collective-permute-start.19 = (bf16[512,128]{1,0:T(8,128)(2,1)S(1)}, bf16[512,128]{1,0:T(8,128)(2,1)S(1)}, u32[]{:S(2)}, u32[]{:S(2)}) collective-permute-start(bf16[512,128]{1,0:T(8,128)(2,1)S(1)} %get-tuple-element.194.refs_0_), channel_id=1, source_target_pairs={{0,4},{8,0},{16,8},{24,16},{28,24},{20,28},{12,20},{4,12},{1,5},{9... | collective-permute-start | bytes 393224 | tf_op jit(solution)/shard_map/ppermute | solution.py:1022
  71.5 5.7 %collective-permute-start.20 = (bf16[80,512]{1,0:T(8,128)(2,1)S(1)}, bf16[80,512]{1,0:T(8,128)(2,1)S(1)}, u32[]{:S(2)}, u32[]{:S(2)}) collective-permute-start(bf16[80,512]{1,0:T(8,128)(2,1)S(1)} %get-tuple-element.195), channel_id=1, source_target_pairs={{0,8},{8,16},{16,24},{24,28},{28,20},{20,12},{12,4},{4,0},{1,9},{9... | collective-permute-start | bytes 245768 | tf_op jit(solution)/shard_map/ppermute | solution.py:1019
  71.6 5.5 %collective-permute-start.21 = (bf16[64,512]{1,0:T(8,128)(2,1)S(1)}, bf16[64,512]{1,0:T(8,128)(2,1)S(1)}, u32[]{:S(2)}, u32[]{:S(2)}) collective-permute-start(bf16[64,512]{1,0:T(8,128)(2,1)S(1)} %get-tuple-element.196), channel_id=1, source_target_pairs={{0,4},{8,0},{16,8},{24,16},{28,24},{20,28},{12,20},{4,12},{1,5},{9... | collective-permute-start | bytes 196616 | tf_op jit(solution)/shard_map/ppermute | solution.py:1022
  75.2 17.3 %collective-permute-start.30 = (bf16[512,512]{1,0:T(8,128)(2,1)S(1)}, bf16[512,512]{1,0:T(8,128)(2,1)S(1)}, u32[]{:S(2)}, u32[]{:S(2)}) collective-permute-start(bf16[512,512]{1,0:T(8,128)(2,1)S(1)} %get-tuple-element.217.refs_2_.refs_9_.refs_3_), channel_id=1, source_target_pairs={{0,2},{1,3},{2,0},{3,1},{4,6},{5,7},{6,4},{7,5},{8,10},{9,11},{10,... | collective-permute-start | bytes 1572872 | tf_op jit(solution)/shard_map/ppermute | solution.py:1025
  77.1 7.0 %collective-permute-start.22 = (bf16[512,128]{1,0:T(8,128)(2,1)S(1)}, bf16[512,128]{1,0:T(8,128)(2,1)S(1)}, u32[]{:S(2)}, u32[]{:S(2)}) collective-permute-start(bf16[512,128]{1,0:T(8,128)(2,1)S(1)} %collective-permute-done.18.refs_0_), channel_id=1, source_target_pairs={{0,8},{8,16},{16,24},{24,28},{28,20},{20,12},{12,4},{4,0},{1,9},{9... | collective-permute-start | bytes 393224 | tf_op jit(solution)/shard_map/ppermute | solution.py:1019
  77.3 6.8 %collective-permute-start.23 = (bf16[512,128]{1,0:T(8,128)(2,1)S(1)}, bf16[512,128]{1,0:T(8,128)(2,1)S(1)}, u32[]{:S(2)}, u32[]{:S(2)}) collective-permute-start(bf16[512,128]{1,0:T(8,128)(2,1)S(1)} %collective-permute-done.19.refs_1_), channel_id=1, source_target_pairs={{0,4},{8,0},{16,8},{24,16},{28,24},{20,28},{12,20},{4,12},{1,5},{9... | collective-permute-start | bytes 393224 | tf_op jit(solution)/shard_map/ppermute | solution.py:1022
  79.3 5.5 %collective-permute-start.24 = (bf16[144,512]{1,0:T(8,128)(2,1)S(1)}, bf16[144,512]{1,0:T(8,128)(2,1)S(1)}, u32[]{:S(2)}, u32[]{:S(2)}) collective-permute-start(bf16[144,512]{1,0:T(8,128)(2,1)S(1)} %get-tuple-element.205), channel_id=1, source_target_pairs={{0,8},{8,16},{16,24},{24,28},{28,20},{20,12},{12,4},{4,0},{1,9},{9... | collective-permute-start | bytes 442376 | tf_op jit(solution)/shard_map/ppermute | solution.py:1019
  79.5 5.5 %collective-permute-start.25 = (bf16[144,512]{1,0:T(8,128)(2,1)S(1)}, bf16[144,512]{1,0:T(8,128)(2,1)S(1)}, u32[]{:S(2)}, u32[]{:S(2)}) collective-permute-start(bf16[144,512]{1,0:T(8,128)(2,1)S(1)} %get-tuple-element.206), channel_id=1, source_target_pairs={{0,4},{8,0},{16,8},{24,16},{28,24},{20,28},{12,20},{4,12},{1,5},{9... | collective-permute-start | bytes 442376 | tf_op jit(solution)/shard_map/ppermute | solution.py:1022
  84.9 7.0 %collective-permute-start.26 = (bf16[512,128]{1,0:T(8,128)(2,1)S(1)}, bf16[512,128]{1,0:T(8,128)(2,1)S(1)}, u32[]{:S(2)}, u32[]{:S(2)}) collective-permute-start(bf16[512,128]{1,0:T(8,128)(2,1)S(1)} %collective-permute-done.22.refs_0_), channel_id=1, source_target_pairs={{0,8},{8,16},{16,24},{24,28},{28,20},{20,12},{12,4},{4,0},{1,9},{9... | collective-permute-start | bytes 393224 | tf_op jit(solution)/shard_map/ppermute | solution.py:1019
  85.3 6.6 %collective-permute-start.27 = (bf16[512,128]{1,0:T(8,128)(2,1)S(1)}, bf16[512,128]{1,0:T(8,128)(2,1)S(1)}, u32[]{:S(2)}, u32[]{:S(2)}) collective-permute-start(bf16[512,128]{1,0:T(8,128)(2,1)S(1)} %collective-permute-done.23.refs_1_), channel_id=1, source_target_pairs={{0,4},{8,0},{16,8},{24,16},{28,24},{20,28},{12,20},{4,12},{1,5},{9... | collective-permute-start | bytes 393224 | tf_op jit(solution)/shard_map/ppermute | solution.py:1022
  87.0 5.2 %collective-permute-start.28 = (bf16[144,512]{1,0:T(8,128)(2,1)S(1)}, bf16[144,512]{1,0:T(8,128)(2,1)S(1)}, u32[]{:S(2)}, u32[]{:S(2)}) collective-permute-start(bf16[144,512]{1,0:T(8,128)(2,1)S(1)} %get-tuple-element.214), channel_id=1, source_target_pairs={{0,8},{8,16},{16,24},{24,28},{28,20},{20,12},{12,4},{4,0},{1,9},{9... | collective-permute-start | bytes 442376 | tf_op jit(solution)/shard_map/ppermute | solution.py:1019
  87.4 5.1 %collective-permute-start.29 = (bf16[144,512]{1,0:T(8,128)(2,1)S(1)}, bf16[144,512]{1,0:T(8,128)(2,1)S(1)}, u32[]{:S(2)}, u32[]{:S(2)}) collective-permute-start(bf16[144,512]{1,0:T(8,128)(2,1)S(1)} %get-tuple-element.215), channel_id=1, source_target_pairs={{0,4},{8,0},{16,8},{24,16},{28,24},{20,28},{12,20},{4,12},{1,5},{9... | collective-permute-start | bytes 442376 | tf_op jit(solution)/shard_map/ppermute | solution.py:1022
  92.6 6.5 %collective-permute-start.31 = (bf16[256,128]{1,0:T(8,128)(2,1)S(1)}, bf16[256,128]{1,0:T(8,128)(2,1)S(1)}, u32[]{:S(2)}, u32[]{:S(2)}) collective-permute-start(bf16[256,128]{1,0:T(8,128)(2,1)S(1)} %get-tuple-element.220), channel_id=1, source_target_pairs={{0,8},{8,16},{16,24},{24,28},{28,20},{20,12},{12,4},{4,0},{1,9},{9... | collective-permute-start | bytes 196616 | tf_op jit(solution)/shard_map/ppermute | solution.py:1019
  93.3 5.8 %collective-permute-start.32 = (bf16[256,128]{1,0:T(8,128)(2,1)S(1)}, bf16[256,128]{1,0:T(8,128)(2,1)S(1)}, u32[]{:S(2)}, u32[]{:S(2)}) collective-permute-start(bf16[256,128]{1,0:T(8,128)(2,1)S(1)} %get-tuple-element.221), channel_id=1, source_target_pairs={{0,4},{8,0},{16,8},{24,16},{28,24},{20,28},{12,20},{4,12},{1,5},{9... | collective-permute-start | bytes 196616 | tf_op jit(solution)/shard_map/ppermute | solution.py:1022
  94.7 6.6 %collective-permute-start.33 = (bf16[144,512]{1,0:T(8,128)(2,1)S(1)}, bf16[144,512]{1,0:T(8,128)(2,1)S(1)}, u32[]{:S(2)}, u32[]{:S(2)}) collective-permute-start(bf16[144,512]{1,0:T(8,128)(2,1)S(1)} %get-tuple-element.226), channel_id=1, source_target_pairs={{0,8},{8,16},{16,24},{24,28},{28,20},{20,12},{12,4},{4,0},{1,9},{9... | collective-permute-start | bytes 442376 | tf_op jit(solution)/shard_map/ppermute | solution.py:1019
  95.5 6.7 %collective-permute-start.34 = (bf16[144,512]{1,0:T(8,128)(2,1)S(1)}, bf16[144,512]{1,0:T(8,128)(2,1)S(1)}, u32[]{:S(2)}, u32[]{:S(2)}) collective-permute-start(bf16[144,512]{1,0:T(8,128)(2,1)S(1)} %get-tuple-element.227), channel_id=1, source_target_pairs={{0,4},{8,0},{16,8},{24,16},{28,24},{20,28},{12,20},{4,12},{1,5},{9... | collective-permute-start | bytes 442376 | tf_op jit(solution)/shard_map/ppermute | solution.py:1022
  102.2 8.1 %collective-permute-start.35 = (bf16[144,512]{1,0:T(8,128)(2,1)S(1)}, bf16[144,512]{1,0:T(8,128)(2,1)S(1)}, u32[]{:S(2)}, u32[]{:S(2)}) collective-permute-start(bf16[144,512]{1,0:T(8,128)(2,1)S(1)} %total.1.refs_0_), channel_id=1, source_target_pairs={{0,8},{8,16},{16,24},{24,28},{28,20},{20,12},{12,4},{4,0},{1,9},{9... | collective-permute-start | bytes 442376 | tf_op jit(solution)/shard_map/ppermute | solution.py:1019
  103.9 6.4 %collective-permute-start.36 = (bf16[144,512]{1,0:T(8,128)(2,1)S(1)}, bf16[144,512]{1,0:T(8,128)(2,1)S(1)}, u32[]{:S(2)}, u32[]{:S(2)}) collective-permute-start(bf16[144,512]{1,0:T(8,128)(2,1)S(1)} %total.1.refs_0_), channel_id=1, source_target_pairs={{0,4},{8,0},{16,8},{24,16},{28,24},{20,28},{12,20},{4,12},{1,5},{9... | collective-permute-start | bytes 442376 | tf_op jit(solution)/shard_map/ppermute | solution.py:1022
  110.3 9.1 %collective-permute-start.39 = (bf16[512,384]{1,0:T(8,128)(2,1)S(1)}, bf16[512,384]{1,0:T(8,128)(2,1)S(1)}, u32[]{:S(2)}, u32[]{:S(2)}) collective-permute-start(bf16[512,384]{1,0:T(8,128)(2,1)S(1)} %get-tuple-element.252.refs_1_.refs_0_), channel_id=1, source_target_pairs={{0,2},{1,3},{2,0},{3,1},{4,6},{5,7},{6,4},{7,5},{8,10},{9,11},{10,... | collective-permute-start | bytes 1179656 | tf_op jit(solution)/shard_map/ppermute | solution.py:1025
  112.2 7.2 %collective-permute-start.37 = (bf16[144,512]{1,0:T(8,128)(2,1)S(1)}, bf16[144,512]{1,0:T(8,128)(2,1)S(1)}, u32[]{:S(2)}, u32[]{:S(2)}) collective-permute-start(bf16[144,512]{1,0:T(8,128)(2,1)S(1)} %collective-permute-done.35.refs_1_), channel_id=1, source_target_pairs={{0,8},{8,16},{16,24},{24,28},{28,20},{20,12},{12,4},{4,0},{1,9},{9... | collective-permute-start | bytes 442376 | tf_op jit(solution)/shard_map/ppermute | solution.py:1019
  113.7 5.7 %collective-permute-start.38 = (bf16[144,512]{1,0:T(8,128)(2,1)S(1)}, bf16[144,512]{1,0:T(8,128)(2,1)S(1)}, u32[]{:S(2)}, u32[]{:S(2)}) collective-permute-start(bf16[144,512]{1,0:T(8,128)(2,1)S(1)} %collective-permute-done.36.refs_2_), channel_id=1, source_target_pairs={{0,4},{8,0},{16,8},{24,16},{28,24},{20,28},{12,20},{4,12},{1,5},{9... | collective-permute-start | bytes 442376 | tf_op jit(solution)/shard_map/ppermute | solution.py:1022
  114.8 4.0 %collective-permute-start.41 = (f32[16,512]{1,0:T(8,128)S(1)}, f32[16,512]{1,0:T(8,128)S(1)}, u32[]{:S(2)}, u32[]{:S(2)}) collective-permute-start(f32[16,512]{1,0:T(8,128)S(1)} %gain_part.1.refs_0_), channel_id=1, source_target_pairs={{0,4},{4,0},{8,12},{12,8},{16,20},{20,16},{24,28},{28,24},{1,5},{5... | collective-permute-start | bytes 98312 | tf_op jit(solution)/shard_map/ppermute | solution.py:1028
  115.8 3.6 %collective-permute-start.40 = (f32[8,128]{1,0:T(8,128)S(1)}, f32[8,128]{1,0:T(8,128)S(1)}, u32[]{:S(2)}, u32[]{:S(2)}) collective-permute-start(f32[8,128]{1,0:T(8,128)S(1)} %get-tuple-element.253.refs_2_.refs_4_), channel_id=1, source_target_pairs={{0,2},{1,3},{2,0},{3,1},{4,6},{5,7},{6,4},{7,5},{8,10},{9,11},{10,... | collective-permute-start | bytes 12296 | tf_op jit(solution)/shard_map/ppermute | solution.py:1025
  120.4 11.4 %collective-permute-start.47 = (f32[512,512]{1,0:T(8,128)S(1)}, f32[512,512]{1,0:T(8,128)S(1)}, u32[]{:S(2)}, u32[]{:S(2)}) collective-permute-start(f32[512,512]{1,0:T(8,128)S(1)} %input_back.1.refs_2_), channel_id=1, source_target_pairs={{0,1},{1,0},{2,3},{3,2},{4,5},{5,4},{6,7},{7,6},{8,9},{9,8},{10,11... | collective-permute-start | bytes 3145736 | tf_op jit(solution)/shard_map/ppermute | solution.py:1025
  120.4 5.5 %collective-permute-start.44 = (f32[16,512]{1,0:T(8,128)S(1)}, f32[16,512]{1,0:T(8,128)S(1)}, u32[]{:S(2)}, u32[]{:S(2)}) collective-permute-start(f32[16,512]{1,0:T(8,128)S(1)} %add_gains.2.refs_0_), channel_id=1, source_target_pairs={{0,8},{4,12},{8,0},{12,4},{16,24},{20,28},{24,16},{28,20},{1,9},{5... | collective-permute-start | bytes 98312 | tf_op jit(solution)/shard_map/ppermute | solution.py:1028
  122.4 8.0 %collective-permute-start.45 = (f32[16,512]{1,0:T(8,128)S(1)}, f32[16,512]{1,0:T(8,128)S(1)}, u32[]{:S(2)}, u32[]{:S(2)}) collective-permute-start(f32[16,512]{1,0:T(8,128)S(1)} %add_gains.2.refs_0_), channel_id=1, source_target_pairs={{0,16},{4,20},{8,24},{12,28},{16,0},{20,4},{24,8},{28,12},{1,17},{... | collective-permute-start | bytes 98312 | tf_op jit(solution)/shard_map/ppermute | solution.py:1028
  124.7 5.8 %collective-permute-start.46 = (f32[16,512]{1,0:T(8,128)S(1)}, f32[16,512]{1,0:T(8,128)S(1)}, u32[]{:S(2)}, u32[]{:S(2)}) collective-permute-start(f32[16,512]{1,0:T(8,128)S(1)} %add_gains.2.refs_0_), channel_id=1, source_target_pairs={{0,24},{4,28},{8,16},{12,20},{16,8},{20,12},{24,0},{28,4},{1,25},{... | collective-permute-start | bytes 98312 | tf_op jit(solution)/shard_map/ppermute | solution.py:1028
  124.9 5.6 %collective-permute-start.42 = (bf16[144,512]{1,0:T(8,128)(2,1)S(1)}, bf16[144,512]{1,0:T(8,128)(2,1)S(1)}, u32[]{:S(2)}, u32[]{:S(2)}) collective-permute-start(bf16[144,512]{1,0:T(8,128)(2,1)S(1)} %collective-permute-done.37.refs_3_), channel_id=1, source_target_pairs={{0,8},{8,16},{16,24},{24,28},{28,20},{20,12},{12,4},{4,0},{1,9},{9... | collective-permute-start | bytes 442376 | tf_op jit(solution)/shard_map/ppermute | solution.py:1019
  125.9 5.8 %collective-permute-start.43 = (bf16[144,512]{1,0:T(8,128)(2,1)S(1)}, bf16[144,512]{1,0:T(8,128)(2,1)S(1)}, u32[]{:S(2)}, u32[]{:S(2)}) collective-permute-start(bf16[144,512]{1,0:T(8,128)(2,1)S(1)} %collective-permute-done.38.refs_4_), channel_id=1, source_target_pairs={{0,4},{8,0},{16,8},{24,16},{28,24},{20,28},{12,20},{4,12},{1,5},{9... | collective-permute-start | bytes 442376 | tf_op jit(solution)/shard_map/ppermute | solution.py:1022
  131.7 7.9 %collective-permute-start.48 = (f32[512,512]{1,0:T(8,128)S(1)}, f32[512,512]{1,0:T(8,128)S(1)}, u32[]{:S(2)}, u32[]{:S(2)}) collective-permute-start(f32[512,512]{1,0:T(8,128)S(1)} %get-tuple-element.263.refs_0_), channel_id=1, source_target_pairs={{0,1},{1,0},{2,3},{3,2},{4,5},{5,4},{6,7},{7,6},{8,9},{9,8},{10,11... | collective-permute-start | bytes 3145736 | tf_op jit(solution)/shard_map/ppermute | solution.py:1025
  131.7 4.0 %collective-permute-start.49 = (f32[16,512]{1,0:T(8,128)S(1)}, f32[16,512]{1,0:T(8,128)S(1)}, u32[]{:S(2)}, u32[]{:S(2)}) collective-permute-start(f32[16,512]{1,0:T(8,128)S(1)} %sum_gains.1.refs_0_), channel_id=1, source_target_pairs={{0,2},{1,3},{2,0},{3,1},{4,6},{5,7},{6,4},{7,5},{8,10},{9,11},{10,... | collective-permute-start | bytes 98312 | tf_op jit(solution)/shard_map/ppermute | solution.py:1025
  132.0 6.0 %collective-permute-start.51 = (bf16[80,512]{1,0:T(8,128)(2,1)S(1)}, bf16[80,512]{1,0:T(8,128)(2,1)S(1)}, u32[]{:S(2)}, u32[]{:S(2)}) collective-permute-start(bf16[80,512]{1,0:T(8,128)(2,1)S(1)} %get-tuple-element.273), channel_id=1, source_target_pairs={{0,8},{8,16},{16,24},{24,28},{28,20},{20,12},{12,4},{4,0},{1,9},{9... | collective-permute-start | bytes 245768 | tf_op jit(solution)/shard_map/ppermute | solution.py:1019
  133.6 4.4 %collective-permute-start.52 = (bf16[64,512]{1,0:T(8,128)(2,1)S(1)}, bf16[64,512]{1,0:T(8,128)(2,1)S(1)}, u32[]{:S(2)}, u32[]{:S(2)}) collective-permute-start(bf16[64,512]{1,0:T(8,128)(2,1)S(1)} %get-tuple-element.274), channel_id=1, source_target_pairs={{0,4},{8,0},{16,8},{24,16},{28,24},{20,28},{12,20},{4,12},{1,5},{9... | collective-permute-start | bytes 196616 | tf_op jit(solution)/shard_map/ppermute | solution.py:1022
  (20 other events, 110.8 us)

commit v5 on v4

--- a/solution.py
+++ b/solution.py
@@ -301,7 +301,7 @@
     ]
 
 
-def head_kernel(tokens, gain, noise, other_noise, up, shard, summary, own_noise, up_a):
+def head_kernel(tokens, gain, noise, other_noise, first, second, summary, own_noise):
     f32, bf16 = jnp.float32, jnp.bfloat16
     rows = tokens.shape[0]
     half = rows // 2
@@ -311,7 +311,6 @@
     low = h.astype(bf16)
     means = jnp.mean(h.reshape(rows // BLOCK, BLOCK, D), axis=1)
     summary[...] = means
-    up_a[...] = up[: up_a.shape[0], :]
     mine = jnp.concatenate(noise_rows(noise), 0)
     other = jnp.concatenate(noise_rows(other_noise), 0)
     own_noise[...] = mine
@@ -319,55 +318,48 @@
         core == 0, jnp.concatenate([mine, other], 0), jnp.concatenate([other, mine], 0)
     )
     few = means.shape[0] // 2
-    for k in range(2):
-        at = k * (half + EXTRA)
-        shard[at : at + half, :] = low[k * half : (k + 1) * half, :]
+    for k, ref in enumerate((first, second)):
+        ref[:half, :] = low[k * half : (k + 1) * half, :]
         parts = [p.astype(f32) for p in three_parts(means[k * few : (k + 1) * few, :])]
         parts += [p.astype(f32) for p in three_parts(both)] if k else [jnp.zeros((12, D), f32)]
         parts.append(jnp.zeros((EXTRA - 24, D), f32))
-        shard[at + half : at + half + EXTRA, :] = jnp.concatenate(parts, 0).astype(bf16)
+        ref[half:, :] = jnp.concatenate(parts, 0).astype(bf16)
 
 
 def project_rows(rows, joint):
     return dot_nn(rows, joint[:, : 6 * DH]).astype(jnp.bfloat16)
 
 
-def project_own_kernel(h_one, weight, w_sort, w_out, up, down, out, joint, first, second, third):
+def project_own_kernel(h_first, h_second, weight, w_sort, w_out, down, out, joint, first, second):
+    width = w_out.shape[0]
+    more = first.shape[0] - width
+    first[:width, :] = w_out[...]
+    first[width:, :] = down[:more, :]
+    second[...] = down[more:, :]
     joint[...] = jnp.concatenate([weight[i] for i in range(3)] + [w_sort[...]], 1)
+    project_half(h_first, joint, out, 0)
+    project_half(h_second, joint, out, h_first.shape[0] - EXTRA)
+
+
+def project_half(piece, joint, out, to):
+    for start in range(0, piece.shape[0] - EXTRA, 2 * BLOCK):
+        rows = project_rows(piece[start : start + 2 * BLOCK, :], joint)
+        out[to + start : to + start + 2 * BLOCK, :] = rows
+
+
+def project_kernel(mine1, mine2, other1, other2, joint, out, extra):
+    half = mine1.shape[0] - EXTRA
+    for k, piece in enumerate((mine1, mine2, other1, other2)):
+        project_half(piece, joint, out, k * half)
+        extra[k * EXTRA : (k + 1) * EXTRA, :] = piece[half:, :]
+
+
+def half_kernel(first, second, w_out, w_out_y, half, pair):
     width = w_out.shape[0]
-    rest = first.shape[0] - width
-    first[:rest, :] = up[up.shape[0] - rest :, :]
-    first[rest:, :] = w_out[...]
-    n = second.shape[0]
-    second[...] = down[:n, :]
-    third[...] = down[n:, :]
-    project_shard(h_one, joint, out, 0)
-
-
-def project_shard(shard, joint, out, to):
-    half = shard.shape[0] // 2 - EXTRA
-    for k in range(2):
-        for start in range(0, half, 2 * BLOCK):
-            at = k * (half + EXTRA) + start
-            out[to : to + 2 * BLOCK, :] = project_rows(shard[at : at + 2 * BLOCK, :], joint)
-            to += 2 * BLOCK
-
-
-def project_kernel(mine, other, joint, out, extra):
-    size = mine.shape[0] // 2
-    for k, piece in enumerate((mine, other)):
-        project_shard(piece, joint, out, k * 2 * (size - EXTRA))
-        for m in range(2):
-            to = (2 * k + m) * EXTRA
-            extra[to : to + EXTRA, :] = piece[(m + 1) * size - EXTRA : (m + 1) * size, :]
-
-
-def half_kernel(shard, w_out, first, half, pair):
-    n, width = half.shape[0], w_out.shape[0]
-    core = lax.axis_index("head") % 2
-    half[...] = shard[pl.ds(pl.multiple_of(core * n, n), n), :]
+    even = lax.axis_index("head") % 2 == 0
+    half[...] = jnp.where(even, first[...], second[...])
     pair[:width, :] = w_out[...]
-    pair[width:, :] = first[first.shape[0] - width :, :]
+    pair[width:, :] = w_out_y[:width, :]
 
 
 def owners_of(step):
@@ -517,7 +509,7 @@
 
 
 def feed_kernel(
-    tokens, cotangent, gain, ctx0, ctx1, ctx2, ctx3, wo, wo_other, up_a, up_b, first, down_a, second, third,
+    tokens, cotangent, gain, ctx0, ctx1, ctx2, ctx3, wo, wo_other, up_a, up_b, down_a, first, second,
     middle, h_two, active, d_hidden, ffn, d_h_two,
     ctx_full, wo_full, up_full, down_full, act_full, d_full,
 ):
@@ -533,13 +525,11 @@
         wo_full[pl.ds(at, width), :] = w[j // 2 * width : (j // 2 + 1) * width, :]
     here, there = (pl.multiple_of((row ^ j) * ff, ff) for j in range(2))
     up_full[:, pl.ds(here, ff)] = up_a[...]
-    top = up_b.shape[0]
-    up_full[:top, pl.ds(there, ff)] = up_b[...]
-    up_full[top:, pl.ds(there, ff)] = first[: up_a.shape[0] - top, :]
+    up_full[:, pl.ds(there, ff)] = up_b[...]
     down_full[pl.ds(here, ff), :] = down_a[...]
-    n = second.shape[0]
-    down_full[pl.ds(there, n), :] = second[...]
-    down_full[pl.ds(pl.multiple_of(there + n, 32), ff - n), :] = third[...]
+    more = first.shape[0] - width
+    down_full[pl.ds(there, more), :] = first[width:, :]
+    down_full[pl.ds(pl.multiple_of(there + more, 32), ff - more), :] = second[...]
     chunk = 256
     for start in range(0, tokens.shape[0], chunk):
         sl = slice(start, start + chunk)
@@ -830,24 +820,24 @@
     return jnp.concatenate([grad[0], grad[1]], 1) / TEMPER
 
 
-def weight_kernel(own, m1, o1, m2, o2, m3, o3, m4, o4, d_qkv, g_qkv, h_all):
+def weight_kernel(*refs):
+    *halves, d_qkv, g_qkv, h_all = refs
     me = lax.axis_index("blk")
     core = lax.axis_index("head") % 2
-    half = m4.shape[0] - EXTRA
+    half = halves[0].shape[0] - EXTRA
     rows = 2 * half
 
-    def put(owner, start, ref):
-        for k in range(ref.shape[0] // (half + EXTRA)):
-            at = pl.ds(pl.multiple_of(owner * rows + start + k * half, half), half)
-            h_all[at, :] = ref[k * (half + EXTRA) : k * (half + EXTRA) + half, :]
-
-    put(me, 0, own)
-    for step, refs in ((1, (m1, o1)), (2, (m2, o2)), (3, (m3, o3))):
-        for owner, ref in zip(owners_of(step), refs):
-            put(owner, 0, ref)
+    def put(owner, side, ref):
+        at = pl.ds(pl.multiple_of(owner * rows + side * half, half), half)
+        h_all[at, :] = ref[:half, :]
+
+    owners = [me] + [owner for step in (1, 2, 3) for owner in owners_of(step)]
+    for k, owner in enumerate(owners):
+        put(owner, 0, halves[2 * k])
+        put(owner, 1, halves[2 * k + 1])
     owner, _ = owners_of(4)
-    put(owner, core * half, m4)
-    put(owner, (1 - core) * half, o4)
+    put(owner, core, halves[14])
+    put(owner, 1 - core, halves[15])
     out = dot_tn(h_all[...], d_qkv[...])
     width = g_qkv.shape[2]
     for i in range(3):
@@ -1000,6 +990,7 @@
 RING = (0, 2, 4, 6, 7, 5, 3, 1)
 SHARD = 512
 EXTRA = 32
+CUT = 320
 
 
 def local_eight(
@@ -1038,48 +1029,47 @@
                 pairs.append((RING[i] * 4 + h, to * 4 + h))
         return lax.ppermute(v, ("blk", "head"), pairs)
 
-    shard, own_summary, own_noise, up_0 = call(
+    a, b, own_summary, own_noise = call(
         head_kernel,
-        [((rows + 2 * EXTRA, D), bf16), ((blocks, D), f32), ((2, D), f32), ((320, ff), bf16)],
-        tokens, gain_attn, gumbel_noise, swap_head(gumbel_noise, 1), w_up,
-        cold=(0, 1, 2, 3, 4), limit=62, name="norm_one",
-    )
-
-    def project(mine, other):
-        return call(
-            project_kernel, [((2 * rows, 3 * width), bf16), ((4 * EXTRA, D), bf16)], mine, other, joint,
-            name="project",
-        )
-
-    m1 = along(shard)
-    up_y0 = swap_head(up_0, 2)
-    qkv_own, joint, first, second, third = call(
+        [((half + EXTRA, D), bf16)] * 2 + [((blocks, D), f32), ((2, D), f32)],
+        tokens, gain_attn, gumbel_noise, swap_head(gumbel_noise, 1),
+        cold=(0, 1, 2, 3), limit=62, name="norm_one",
+    )
+
+    mine = [(a, b)]
+    up_y = swap_head(after(w_up, a), 2)
+    a, b = along(a), along(b)
+    qkv_own, joint, first, second = call(
         project_own_kernel,
         [
-            ((rows, 3 * width), bf16), ((D, 3 * width + 2 * nb), bf16),
-            ((D - 320 + width, D), bf16), ((352, D), bf16), ((ff - 352, D), bf16),
+            ((rows, 3 * width), bf16), ((D, 3 * width + 2 * nb), bf16), ((CUT, D), bf16),
+            ((width + ff - CUT, D), bf16),
         ],
-        shard, w_in, w_sort, w_out, w_up, w_down, name="project_own",
-    )
-    m1, up_y0, qkv_own = tie(m1, up_y0, qkv_own)
-    m2 = along(m1)
-    first_y = swap_head(after(first, m1), 2)
-    m2, first_y = tie(m2, first_y)
-    m3 = along(m2)
-    second_y = swap_head(after(second, m2), 2)
-    m3, second_y = tie(m3, second_y)
+        *mine[0], w_in, w_sort, w_out, w_down, name="project_own",
+    )
+    mine.append((a, b))
+    a, b = along(a), along(b)
+    b, up_y, qkv_own = tie(b, up_y, qkv_own)
+    mine.append((a, b))
+    first_y = swap_head(after(first, a), 2)
+    a, b = along(a), along(b)
+    b, first_y = tie(b, first_y)
+    mine.append((a, b))
+    second_y = swap_head(after(second, a), 2)
     half_3, wo = call(
-        half_kernel, [((half + EXTRA, D), bf16), ((2 * width, D), bf16)], m3, w_out, first_y, name="half"
+        half_kernel, [((half + EXTRA, D), bf16), ((2 * width, D), bf16)], a, b, w_out, first_y, name="half"
     )
     m4 = along(half_3)
-    third_y = swap_head(after(third, m3), 2)
-    o1 = swap_head(after(m1, half_3), 1)
-    o2 = swap_head(after(m2, half_3), 1)
-    o3 = swap_head(after(m3, half_3), 1)
-    qkv1 = project(m1, o1)
-    qkv2 = project(m2, o2)
-    qkv3 = project(m3, o3)
-    m4, third_y, _, _, _ = tie(m4, third_y, qkv1[0], qkv2[0], qkv3[0])
+    other, projected = [], []
+    for k in (1, 2, 3):
+        other.append(tuple(swap_head(after(v, mine[min(k + 1, 3)][0]), 1) for v in mine[k]))
+        projected.append(
+            call(
+                project_kernel, [((2 * rows, 3 * width), bf16), ((4 * EXTRA, D), bf16)],
+                *mine[k], *other[-1], joint, name="project",
+            )
+        )
+    m4, second_y = tie(m4, second_y, *[p[0] for p in projected])[:2]
     o4 = swap_head(m4, 1)
     qkv, context, summary, steps, scale_rows, weight_rows = call(
         attend_kernel,
@@ -1087,7 +1077,7 @@
             ((total, 3 * width), bf16), ((rows, width), bf16), ((nb, D), f32),
             ((2 * SINK, 2, nb, nb), f32), ((nb, 4 * DH), f32), ((nb, 2 * DH), f32),
         ],
-        qkv_own, qkv1[0], qkv2[0], qkv3[0], qkv1[1], qkv2[1], qkv3[1], m4, o4, joint, own_summary, own_noise,
+        qkv_own, *[p[0] for p in projected], *[p[1] for p in projected], m4, o4, joint, own_summary, own_noise,
         partner_s, partner_s, smem=(12,), scratch=[((nb, 2 * nb), f32)], name="attend",
     )
     ctx_y, ctx_c = swap_head(context, 2), swap_head(context, 1)
@@ -1111,7 +1101,7 @@
             ((rows, D), f32),
         ],
         tokens, cotangent, gain_ffn, context, ctx_c, ctx_y, ctx_yc, wo, wo_other,
-        w_up, up_y0, first_y, w_down, second_y, third_y,
+        w_up, up_y, w_down, first_y, second_y,
         scratch=[
             ((rows, 4 * width), bf16), ((4 * width, D), bf16), ((D, 2 * ff), bf16), ((2 * ff, D), bf16),
             ((rows, 2 * ff), bf16), ((rows, 2 * ff), bf16),
@@ -1164,7 +1154,7 @@
         sum_f, sum_b = ahead(sum_f), behind(sum_b)
         done = pull(given)
         hold = [joint_y] if step == 2 else []
-        f, b, sum_f, sum_b, _ = tie(f, b, sum_f, sum_b, done, *hold)[:5]
+        sum_f, sum_b = tie(sum_f, sum_b, done, *hold)[:2]
         given = [f, b]
         arrays.append(given)
         if step < 3:
@@ -1212,7 +1202,7 @@
     d_h_other = swap_head(d_h, 1)
     g_qkv = call(
         weight_kernel, [((3, D, width), f32)],
-        shard, m1, o1, m2, o2, m3, o3, m4, o4, after(d_qkv, d_h),
+        *mine[0], *[v for k in (1, 2, 3) for v in (*mine[k], *other[k - 1])], m4, o4, after(d_qkv, d_h),
         scratch=[((total, D), bf16)], limit=24, name="weights",
     )
     wf3, wb3, gains1, gains2, gains3, d_h_other, g_qkv = tie(

time: 141 us -> 137 us (0.972)
  waiting for transfers between devices: 44.8 us -> 33.6 us
  starting transfers between devices: 49.5 us -> 56.4 us
    ppermute x21 -> x23, waiting for transfers between devices: 36.2 us -> 12.6 us  [swap_head(): return lax.ppermute(v, 'head', [(i, i ^ j) for i in range(4)])]
    ppermute x4 -> x7, waiting for transfers between devices: 0.01 us -> 11.1 us  [along(): return lax.ppermute(v, ('blk', 'head'), pairs)]
    ppermute x4 -> x7, starting transfers between devices: 4.44 us -> 13.5 us  [along(): return lax.ppermute(v, ('blk', 'head'), pairs)]
    ppermute x12, starting transfers between devices: 16 us -> 11.4 us  [behind(): lax.ppermute(v, 'blk', [(RING[i], RING[(i - 1) % 8]) for i in range(8)])]
    ppermute x12, starting transfers between devices: 8.75 us -> 13.3 us  [ahead(): lax.ppermute(v, 'blk', [(RING[i], RING[(i + 1) % 8]) for i in range(8)])]
    ppermute x12, waiting for transfers between devices: 2.54 us -> 4.82 us  [behind(): lax.ppermute(v, 'blk', [(RING[i], RING[(i - 1) % 8]) for i in range(8)])]
    ppermute x21 -> x23, starting transfers between devices: 15 us -> 13.1 us  [swap_head(): return lax.ppermute(v, 'head', [(i, i ^ j) for i in range(4)])]
  transfers between devices with their start and end apart: 53 -> 58, of which waited for: 19 -> 23; matrix products, arithmetic and copies ran while one was open for 0% -> 0% of each run, Pallas kernels for 21% -> 21%
where the time goes in v5:
time: 137 us
  starting transfers between devices  56.4 us (41%)
  Pallas kernels  43.4 us (32%)
  waiting for transfers between devices  33.6 us (25%)
  local copies, waits for them, and re-layouts  2.58 us (2%)
    pallas_call x33, Pallas kernels, call(): pl.pallas_call(body, out_shape=shapes, in_specs=specs, out_specs=out_spec...  43.4 us
    ppermute x7, starting transfers between devices, along(): return lax.ppermute(v, ('blk', 'head'), pairs)  13.5 us
    ppermute x12, starting transfers between devices, ahead(): lax.ppermute(v, 'blk', [(RING[i], RING[(i + 1) % 8]) for i in range(8)])  13.3 us
    ppermute x23, starting transfers between devices, swap_head(): return lax.ppermute(v, 'head', [(i, i ^ j) for i in range(4)])  13.1 us
    ppermute x23, waiting for transfers between devices, swap_head(): return lax.ppermute(v, 'head', [(i, i ^ j) for i in range(4)])  12.6 us
    ppermute x12, starting transfers between devices, behind(): lax.ppermute(v, 'blk', [(RING[i], RING[(i - 1) % 8]) for i in range(8)])  11.4 us
    ppermute x7, waiting for transfers between devices, along(): return lax.ppermute(v, ('blk', 'head'), pairs)  11.1 us
    ppermute x4, starting transfers between devices, swap_blk(): return lax.ppermute(v, 'blk', [(i, i ^ j) for i in range(8)])  5.15 us
  transfers between devices with their start and end apart: 58, of which 23 were waited for; matrix products, arithmetic and copies ran while one was open for 0% of the time, Pallas kernels for 21%

profile of v5, /device:TPU:0, one launch (start us, length us, event | category | flops | bytes accessed | tf_op | source)
XLA Modules:
  0.0 137.0 jit_solution(7838944283816594349)
XLA Ops:
  2.9 2.3 %norm_one.1 = (bf16[288,512]{1,0:T(8,128)(2,1)}, bf16[288,512]{1,0:T(8,128)(2,1)}, f32[8,512]{1,0:T(8,128)}, f32[2,512]{1,0:T(2,128)}) custom-call(bf16[512,512]{1,0:T(8,128)(2,1)} %refs_0_.7, bf16[512]{0:T(512)(128)(2,1)} %refs_1_.5, f32[8,2,64]{2,1,0:T(2,128)} %refs_2_.3, f32[8,2,64]{2,1,0:T(2,128)} %copy-done.16), custom_call_target="tpu_custom_call" | custom-call | flops 1955000064 | bytes 6273000 | tf_op jit(solution)/shard_map/norm_one/pallas_call | solution.py:937
  5.2 3.0 %collective-permute-start.4 = (bf16[288,512]{1,0:T(8,128)(2,1)}, bf16[288,512]{1,0:T(8,128)(2,1)S(1)}, u32[]{:S(2)}, u32[]{:S(2)}) collective-permute-start(bf16[288,512]{1,0:T(8,128)(2,1)} %get-tuple-element.137.refs_0_), channel_id=1, source_target_pairs={{0,8},{1,5},{2,10},{3,7},{8,16},{9,1},{10,18},{11,3},{16,24},{17,9... | collective-permute-start | bytes 884744 | tf_op jit(solution)/shard_map/ppermute | solution.py:1030
  8.1 1.6 %collective-permute-start.1 = (bf16[288,512]{1,0:T(8,128)(2,1)}, bf16[288,512]{1,0:T(8,128)(2,1)S(1)}, u32[]{:S(2)}, u32[]{:S(2)}) collective-permute-start(bf16[288,512]{1,0:T(8,128)(2,1)} %get-tuple-element.136.refs_1_), channel_id=1, source_target_pairs={{0,8},{1,5},{2,10},{3,7},{8,16},{9,1},{10,18},{11,3},{16,24},{17,9... | collective-permute-start | bytes 884744 | tf_op jit(solution)/shard_map/ppermute | solution.py:1030
  9.7 1.5 %collective-permute-start.3 = (bf16[512,512]{1,0:T(8,128)(2,1)S(1)}, bf16[512,512]{1,0:T(8,128)(2,1)S(1)}, u32[]{:S(2)}, u32[]{:S(2)}) collective-permute-start(bf16[512,512]{1,0:T(8,128)(2,1)S(1)} %copy-done.2), channel_id=1, source_target_pairs={{0,2},{1,3},{2,0},{3,1},{4,6},{5,7},{6,4},{7,5},{8,10},{9,11},{10,... | collective-permute-start | bytes 1572872 | tf_op jit(solution)/shard_map/ppermute | solution.py:1016
  11.2 1.7 %collective-permute-done.4.refs_0_.refs_2_ = bf16[288,512]{1,0:T(8,128)(2,1)S(1)} collective-permute-done((bf16[288,512]{1,0:T(8,128)(2,1)}, bf16[288,512]{1,0:T(8,128)(2,1)S(1)}, u32[]{:S(2)}, u32[]{:S(2)}) %collective-permute-start.4) | collective-permute-done | bytes 294944 | tf_op jit(solution)/shard_map/ppermute | solution.py:1030
  13.0 2.1 %collective-permute-start.5 = (bf16[288,512]{1,0:T(8,128)(2,1)S(1)}, bf16[288,512]{1,0:T(8,128)(2,1)S(1)}, u32[]{:S(2)}, u32[]{:S(2)}) collective-permute-start(bf16[288,512]{1,0:T(8,128)(2,1)S(1)} %collective-permute-done.4.refs_0_.refs_2_), channel_id=1, source_target_pairs={{0,8},{1,5},{2,10},{3,7},{8,16},{9,1},{10,18},{11,3},{16,24},{17,9... | collective-permute-start | bytes 884744 | tf_op jit(solution)/shard_map/ppermute | solution.py:1030
  16.1 2.1 %collective-permute-start.2 = (bf16[288,512]{1,0:T(8,128)(2,1)S(1)}, bf16[288,512]{1,0:T(8,128)(2,1)S(1)}, u32[]{:S(2)}, u32[]{:S(2)}) collective-permute-start(bf16[288,512]{1,0:T(8,128)(2,1)S(1)} %collective-permute-done.1.refs_1_.refs_3_), channel_id=1, source_target_pairs={{0,8},{1,5},{2,10},{3,7},{8,16},{9,1},{10,18},{11,3},{16,24},{17,9... | collective-permute-start | bytes 884744 | tf_op jit(solution)/shard_map/ppermute | solution.py:1030
  18.2 1.5 %collective-permute-done.5.refs_0_.refs_6_ = bf16[288,512]{1,0:T(8,128)(2,1)S(1)} collective-permute-done((bf16[288,512]{1,0:T(8,128)(2,1)S(1)}, bf16[288,512]{1,0:T(8,128)(2,1)S(1)}, u32[]{:S(2)}, u32[]{:S(2)}) %collective-permute-start.5) | collective-permute-done | bytes 294944 | tf_op jit(solution)/shard_map/ppermute | solution.py:1030
  19.7 2.1 %collective-permute-start.8 = (bf16[288,512]{1,0:T(8,128)(2,1)S(1)}, bf16[288,512]{1,0:T(8,128)(2,1)S(1)}, u32[]{:S(2)}, u32[]{:S(2)}) collective-permute-start(bf16[288,512]{1,0:T(8,128)(2,1)S(1)} %collective-permute-done.5.refs_0_.refs_6_), channel_id=1, source_target_pairs={{0,8},{1,5},{2,10},{3,7},{8,16},{9,1},{10,18},{11,3},{16,24},{17,9... | collective-permute-start | bytes 884744 | tf_op jit(solution)/shard_map/ppermute | solution.py:1030
  24.3 1.6 %collective-permute-start.11 = (bf16[288,512]{1,0:T(8,128)(2,1)S(1)}, bf16[288,512]{1,0:T(8,128)(2,1)S(1)}, u32[]{:S(2)}, u32[]{:S(2)}) collective-permute-start(bf16[288,512]{1,0:T(8,128)(2,1)S(1)} %collective-permute-done.2.refs_1_.refs_7_), channel_id=1, source_target_pairs={{0,8},{1,5},{2,10},{3,7},{8,16},{9,1},{10,18},{11,3},{16,24},{17,9... | collective-permute-start | bytes 884744 | tf_op jit(solution)/shard_map/ppermute | solution.py:1030
  25.9 1.5 %collective-permute-start.12 = (bf16[320,512]{1,0:T(8,128)(2,1)S(1)}, bf16[320,512]{1,0:T(8,128)(2,1)S(1)}, u32[]{:S(2)}, u32[]{:S(2)}) collective-permute-start(bf16[320,512]{1,0:T(8,128)(2,1)S(1)} %get-tuple-element.150), channel_id=1, source_target_pairs={{0,2},{1,3},{2,0},{3,1},{4,6},{5,7},{6,4},{7,5},{8,10},{9,11},{10,... | collective-permute-start | bytes 983048 | tf_op jit(solution)/shard_map/ppermute | solution.py:1016
  27.9 3.1 %collective-permute-done.11.refs_1_.refs_11_ = bf16[288,512]{1,0:T(8,128)(2,1)S(1)} collective-permute-done((bf16[288,512]{1,0:T(8,128)(2,1)S(1)}, bf16[288,512]{1,0:T(8,128)(2,1)S(1)}, u32[]{:S(2)}, u32[]{:S(2)}) %collective-permute-start.11) | collective-permute-done | bytes 294944 | tf_op jit(solution)/shard_map/ppermute | solution.py:1030
  31.0 2.7 %collective-permute-done.12.refs_3_.refs_12_ = bf16[320,512]{1,0:T(8,128)(2,1)S(1)} collective-permute-done((bf16[320,512]{1,0:T(8,128)(2,1)S(1)}, bf16[320,512]{1,0:T(8,128)(2,1)S(1)}, u32[]{:S(2)}, u32[]{:S(2)}) %collective-permute-start.12) | collective-permute-done | bytes 327712 | tf_op jit(solution)/shard_map/ppermute | solution.py:1016
  34.3 1.5 %collective-permute-start.16 = (bf16[320,512]{1,0:T(8,128)(2,1)S(1)}, bf16[320,512]{1,0:T(8,128)(2,1)S(1)}, u32[]{:S(2)}, u32[]{:S(2)}) collective-permute-start(bf16[320,512]{1,0:T(8,128)(2,1)S(1)} %get-tuple-element.161), channel_id=1, source_target_pairs={{0,2},{1,3},{2,0},{3,1},{4,6},{5,7},{6,4},{7,5},{8,10},{9,11},{10,... | collective-permute-start | bytes 983048 | tf_op jit(solution)/shard_map/ppermute | solution.py:1016
  39.1 3.8 %collective-permute-done.15.refs_7_.refs_14_ = bf16[288,512]{1,0:T(8,128)(2,1)S(1)} collective-permute-done((bf16[288,512]{1,0:T(8,128)(2,1)S(1)}, bf16[288,512]{1,0:T(8,128)(2,1)S(1)}, u32[]{:S(2)}, u32[]{:S(2)}) %collective-permute-start.15) | collective-permute-done | bytes 294944 | tf_op jit(solution)/shard_map/ppermute | solution.py:1030
  44.0 1.6 %collective-permute-done.17.refs_8_.refs_15_ = bf16[288,512]{1,0:T(8,128)(2,1)S(1)} collective-permute-done((bf16[288,512]{1,0:T(8,128)(2,1)S(1)}, bf16[288,512]{1,0:T(8,128)(2,1)S(1)}, u32[]{:S(2)}, u32[]{:S(2)}) %collective-permute-start.17) | collective-permute-done | bytes 294944 | tf_op jit(solution)/shard_map/ppermute | solution.py:1016
  45.6 3.7 %attend.1 = (bf16[4096,384]{1,0:T(8,128)(2,1)S(1)}, bf16[512,128]{1,0:T(8,128)(2,1)S(1)}, f32[64,512]{1,0:T(8,128)S(1)}, f32[16,2,64,64]{3,2,1,0:T(8,128)S(1)}, ...) custom-call(bf16[512,384]{1,0:T(8,128)(2,1)S(1)} %get-tuple-element.140.refs_0_, ...), custom_call_target="tpu_custom_call" | custom-call | flops 4830000128 | bytes 15498000 | tf_op jit(solution)/shard_map/attend/pallas_call | solution.py:937
  49.3 1.6 %collective-permute-start.18 = (bf16[512,128]{1,0:T(8,128)(2,1)S(1)}, bf16[512,128]{1,0:T(8,128)(2,1)S(1)}, u32[]{:S(2)}, u32[]{:S(2)}) collective-permute-start(bf16[512,128]{1,0:T(8,128)(2,1)S(1)} %get-tuple-element.165.refs_3_.refs_4_), channel_id=1, source_target_pairs={{0,2},{1,3},{2,0},{3,1},{4,6},{5,7},{6,4},{7,5},{8,10},{9,11},{10,... | collective-permute-start | bytes 393224 | tf_op jit(solution)/shard_map/ppermute | solution.py:1016
  51.4 2.8 %prepare.1 = (f32[1536,256]{1,0:T(8,128)S(1)}, f32[1536,256]{1,0:T(8,128)S(1)}) custom-call(bf16[4096,384]{1,0:T(8,128)(2,1)S(1)} %get-tuple-element.166.refs_0_.refs_1_.refs_2_, s32[2,64]{1,0:T(2,128)S(1)} %bitcast.6, f32[64,256]{1,0:T(8,128)S(1)} %get-tuple-element.167.refs_2_.refs_3_.refs_4_), custom_call_target="tpu_custom_call" | custom-call | flops 3335000064 | bytes 10701000 | tf_op jit(solution)/shard_map/prepare/pallas_call | solution.py:937
  54.9 1.3 collective-permute-done.20.refs_6_
  56.2 4.2 %feed.1 = (f32[512,512]{1,0:T(8,128)S(1)}, bf16[512,512]{1,0:T(8,128)(2,1)S(1)}, bf16[512,512]{1,0:T(8,128)(2,1)S(1)}, bf16[512,512]{1,0:T(8,128)(2,1)S(1)}, f32...) custom-call(bf16[512,512]{1,0:T(8,128)(2,1)S(1)} %copy-done.4, bf16[512,512]{1,0:T(8,128)(2,1)S(1)} %copy-done.3, ...), custom_call_target="tpu_custom_call" | custom-call | flops 4830000128 | bytes 15498000 | tf_op jit(solution)/shard_map/feed/pallas_call | solution.py:937
  60.6 2.5 %collective-permute-done.22.refs_2_ = f32[512,512]{1,0:T(8,128)S(1)} collective-permute-done((f32[512,512]{1,0:T(8,128)S(1)}, f32[512,512]{1,0:T(8,128)S(1)}, u32[]{:S(2)}, u32[]{:S(2)}) %collective-permute-start.22) | collective-permute-done | bytes 1048608 | tf_op jit(solution)/shard_map/ppermute | solution.py:1016
  65.8 1.3 collective-permute-start.28
  67.8 1.3 collective-permute-start.24
  69.1 1.8 %pull.5 = (f32[512,256]{1,0:T(8,128)S(1)}, bf16[512,384]{1,0:T(8,128)(2,1)S(1)}, f32[8,256]{1,0:T(8,128)S(1)}) custom-call(bf16[512,128]{1,0:T(8,128)(2,1)S(1)} %get-tuple-element.200.refs_0_, bf16[4096,384]{1,0:T(8,128)(2,1)S(1)} %get-tuple-element.166.refs_0_.refs_1_.refs_2_, s32[2,64]{1,0:T(2,128)S(1)} %bitcast.7, ...), custom_call_target="tpu_custom_call" | custom-call | flops 2760000000 | bytes 8856000 | tf_op jit(solution)/shard_map/pull/pallas_call | solution.py:937
  70.9 1.6 %collective-permute-start.33 = (bf16[512,512]{1,0:T(8,128)(2,1)S(1)}, bf16[512,512]{1,0:T(8,128)(2,1)S(1)}, u32[]{:S(2)}, u32[]{:S(2)}) collective-permute-start(bf16[512,512]{1,0:T(8,128)(2,1)S(1)} %get-tuple-element.207.refs_4_.refs_9_.refs_3_.refs_2_), channel_id=1, source_target_pairs={{0,2},{1,3},{2,0},{3,1},{4,6},{5,7},{6,4},{7,5},{8,10},{9,11},{10,... | collective-permute-start | bytes 1572872 | tf_op jit(solution)/shard_map/ppermute | solution.py:1016
  72.6 1.5 %collective-permute-start.25 = (bf16[144,512]{1,0:T(8,128)(2,1)S(1)}, bf16[144,512]{1,0:T(8,128)(2,1)S(1)}, u32[]{:S(2)}, u32[]{:S(2)}) collective-permute-start(bf16[144,512]{1,0:T(8,128)(2,1)S(1)} %get-tuple-element.198), channel_id=1, source_target_pairs={{0,8},{8,16},{16,24},{24,28},{28,20},{20,12},{12,4},{4,0},{1,9},{9... | collective-permute-start | bytes 442376 | tf_op jit(solution)/shard_map/ppermute | solution.py:1010
  74.6 1.4 %collective-permute-start.31 = (bf16[512,128]{1,0:T(8,128)(2,1)S(1)}, bf16[512,128]{1,0:T(8,128)(2,1)S(1)}, u32[]{:S(2)}, u32[]{:S(2)}) collective-permute-start(bf16[512,128]{1,0:T(8,128)(2,1)S(1)} %collective-permute-done.27.refs_0_), channel_id=1, source_target_pairs={{0,8},{8,16},{16,24},{24,28},{28,20},{20,12},{12,4},{4,0},{1,9},{9... | collective-permute-start | bytes 393224 | tf_op jit(solution)/shard_map/ppermute | solution.py:1010
  76.7 2.8 %pull.6 = (f32[1024,256]{1,0:T(8,128)S(1)}, bf16[1024,384]{1,0:T(8,128)(2,1)S(1)}, f32[16,256]{1,0:T(8,128)S(1)}) custom-call(bf16[512,128]{1,0:T(8,128)(2,1)S(1)} %collective-permute-done.27.refs_0_, bf16[512,128]{1,0:T(8,128)(2,1)S(1)} %collective-permute-done.28.refs_1_, bf16[4096,384]{1,0:T(8,128)(2,1)S(1)} %get-tuple-element.166.refs_0_.refs_1_.refs_2_, ...), custom_call_target="tpu_custom_call" | custom-call | flops 2760000000 | bytes 8856000 | tf_op jit(solution)/shard_map/pull/pallas_call | solution.py:937
  84.1 2.8 %pull.7 = (f32[1024,256]{1,0:T(8,128)S(1)}, bf16[1024,384]{1,0:T(8,128)(2,1)S(1)}, f32[16,256]{1,0:T(8,128)S(1)}) custom-call(bf16[512,128]{1,0:T(8,128)(2,1)S(1)} %collective-permute-done.31.refs_0_, bf16[512,128]{1,0:T(8,128)(2,1)S(1)} %collective-permute-done.32.refs_1_, bf16[4096,384]{1,0:T(8,128)(2,1)S(1)} %get-tuple-element.166.refs_0_.refs_1_.refs_2_, ...), custom_call_target="tpu_custom_call" | custom-call | flops 2760000000 | bytes 8856000 | tf_op jit(solution)/shard_map/pull/pallas_call | solution.py:937
  87.0 1.3 collective-permute-done.37.refs_1_
  88.4 1.3 collective-permute-start.40
  90.5 2.2 %pull.8 = (f32[1024,256]{1,0:T(8,128)S(1)}, bf16[1024,384]{1,0:T(8,128)(2,1)S(1)}, f32[16,256]{1,0:T(8,128)S(1)}) custom-call(bf16[512,128]{1,0:T(8,128)(2,1)S(1)} %collective-permute-done.36.refs_0_, bf16[512,128]{1,0:T(8,128)(2,1)S(1)} %collective-permute-done.37.refs_1_, bf16[4096,384]{1,0:T(8,128)(2,1)S(1)} %get-tuple-element.166.refs_0_.refs_1_.refs_2_, ...), custom_call_target="tpu_custom_call" | custom-call | flops 2760000000 | bytes 8856000 | tf_op jit(solution)/shard_map/pull/pallas_call | solution.py:937
  92.8 1.3 collective-permute-start.34
  94.9 1.5 %pull.9 = (f32[512,256]{1,0:T(8,128)S(1)}, bf16[512,384]{1,0:T(8,128)(2,1)S(1)}, f32[8,256]{1,0:T(8,128)S(1)}) custom-call(bf16[256,128]{1,0:T(8,128)(2,1)S(1)} %collective-permute-done.40.refs_0_, bf16[256,128]{1,0:T(8,128)(2,1)S(1)} %collective-permute-done.41.refs_1_, bf16[4096,384]{1,0:T(8,128)(2,1)S(1)} %get-tuple-element.166.refs_0_.refs_1_.refs_2_, ...), custom_call_target="tpu_custom_call" | custom-call | flops 2760000000 | bytes 8856000 | tf_op jit(solution)/shard_map/pull/pallas_call | solution.py:937
  96.3 2.8 %collective-permute-done.34.refs_1_ = bf16[144,512]{1,0:T(8,128)(2,1)S(1)} collective-permute-done((bf16[144,512]{1,0:T(8,128)(2,1)S(1)}, bf16[144,512]{1,0:T(8,128)(2,1)S(1)}, u32[]{:S(2)}, u32[]{:S(2)}) %collective-permute-start.34) | collective-permute-done | bytes 147488 | tf_op jit(solution)/shard_map/ppermute | solution.py:1010
  100.2 1.8 %collective-permute-start.38 = (bf16[144,512]{1,0:T(8,128)(2,1)S(1)}, bf16[144,512]{1,0:T(8,128)(2,1)S(1)}, u32[]{:S(2)}, u32[]{:S(2)}) collective-permute-start(bf16[144,512]{1,0:T(8,128)(2,1)S(1)} %total.1.refs_0_), channel_id=1, source_target_pairs={{0,8},{8,16},{16,24},{24,28},{28,20},{20,12},{12,4},{4,0},{1,9},{9... | collective-permute-start | bytes 442376 | tf_op jit(solution)/shard_map/ppermute | solution.py:1010
  102.3 4.5 %collect.1 = (bf16[4096,384]{1,0:T(8,128)(2,1)S(1)}, bf16[512,384]{1,0:T(8,128)(2,1)S(1)}, f32[8,128]{1,0:T(8,128)S(1)}, f32[512,128]{1,0:T(8,128)}) custom-call(f32[512,256]{1,0:T(8,128)S(1)} %get-tuple-element.195.refs_0_, f32[1024,256]{1,0:T(8,128)S(1)} %get-tuple-element.201.refs_1_, f32[1024,256]{1,0:T(8,128)S(1)} %get-tuple-element.206.refs_2_, ...), custom_call_target="tpu_custom_call" | custom-call | flops 5175000064 | bytes 16605000 | tf_op jit(solution)/shard_map/collect/pallas_call | solution.py:937
  107.0 1.5 %collective-permute-done.39.refs_2_ = bf16[144,512]{1,0:T(8,128)(2,1)S(1)} collective-permute-done((bf16[144,512]{1,0:T(8,128)(2,1)S(1)}, bf16[144,512]{1,0:T(8,128)(2,1)S(1)}, u32[]{:S(2)}, u32[]{:S(2)}) %collective-permute-start.39) | collective-permute-done | bytes 147488 | tf_op jit(solution)/shard_map/ppermute | solution.py:1013
  112.4 1.4 %collective-permute-start.45 = (f32[8,128]{1,0:T(8,128)S(1)}, f32[8,128]{1,0:T(8,128)S(1)}, u32[]{:S(2)}, u32[]{:S(2)}) collective-permute-start(f32[8,128]{1,0:T(8,128)S(1)} %get-tuple-element.237.refs_2_.refs_4_), channel_id=1, source_target_pairs={{0,2},{1,3},{2,0},{3,1},{4,6},{5,7},{6,4},{7,5},{8,10},{9,11},{10,... | collective-permute-start | bytes 12296 | tf_op jit(solution)/shard_map/ppermute | solution.py:1016
  113.8 1.9 %collective-permute-done.46.refs_1_ = f32[16,512]{1,0:T(8,128)S(1)} collective-permute-done((f32[16,512]{1,0:T(8,128)S(1)}, f32[16,512]{1,0:T(8,128)S(1)}, u32[]{:S(2)}, u32[]{:S(2)}) %collective-permute-start.46) | collective-permute-done | bytes 32800 | tf_op jit(solution)/shard_map/ppermute | solution.py:1019
  117.4 1.3 collective-permute-start.49
  118.6 1.3 collective-permute-start.50
  119.9 1.9 %collective-permute-start.51 = (f32[16,512]{1,0:T(8,128)S(1)}, f32[16,512]{1,0:T(8,128)S(1)}, u32[]{:S(2)}, u32[]{:S(2)}) collective-permute-start(f32[16,512]{1,0:T(8,128)S(1)} %add_gains.2.refs_0_), channel_id=1, source_target_pairs={{0,24},{4,28},{8,16},{12,20},{16,8},{20,12},{24,0},{28,4},{1,25},{... | collective-permute-start | bytes 98312 | tf_op jit(solution)/shard_map/ppermute | solution.py:1019
  122.1 1.7 %collective-permute-start.48 = (bf16[144,512]{1,0:T(8,128)(2,1)S(1)}, bf16[144,512]{1,0:T(8,128)(2,1)S(1)}, u32[]{:S(2)}, u32[]{:S(2)}) collective-permute-start(bf16[144,512]{1,0:T(8,128)(2,1)S(1)} %collective-permute-done.43.refs_4_), channel_id=1, source_target_pairs={{0,4},{8,0},{16,8},{24,16},{28,24},{20,28},{12,20},{4,12},{1,5},{9... | collective-permute-start | bytes 442376 | tf_op jit(solution)/shard_map/ppermute | solution.py:1013
  123.9 3.6 %weights.1 = f32[3,512,128]{2,1,0:T(8,128)} custom-call(bf16[288,512]{1,0:T(8,128)(2,1)S(1)} %copy-done.7, bf16[288,512]{1,0:T(8,128)(2,1)S(1)} %copy-done.9, bf16[288,512]{1,0:T(8,128)(2,1)S(1)} %collective-permute-done.4.refs_0_.refs_2_, bf16[288,512]{1,0:T(8,128)(2,1)S(1)} %collective-permute-done.1.refs_1_.refs_3_, ...), custom_call_target="tpu_custom_call" | custom-call | flops 4140000000 | bytes 13284000 | tf_op jit(solution)/shard_map/weights/pallas_call | solution.py:937
  132.0 1.7 %norm_one_back.1 = f32[512,512]{1,0:T(8,128)} custom-call(bf16[512,512]{1,0:T(8,128)(2,1)S(1)} %copy-done.4, bf16[512]{0:T(512)(128)(2,1)S(1)} %copy-done.13, f32[512,512]{1,0:T(8,128)S(1)} %input_back.1.refs_2_, f32[512,512]{1,0:T(8,128)S(1)} %collective-permute-done.52.refs_3_, f32[512,512]{1,0:T(8,128)S(1)} %get-tuple-element.249.refs_4_), custom_call_target="tpu_custom_call" | custom-call | flops 1955000064 | bytes 6273000 | tf_op jit(solution)/shard_map/norm_one_back/pallas_call | solution.py:937
  134.3 1.6 %lay.1 = (f32[512,512]{1,0:T(8,128)}, f32[512,512]{1,0:T(8,128)}, f32[128,512]{1,0:T(8,128)}) custom-call(bf16[144,512]{1,0:T(8,128)(2,1)S(1)} %total.1.refs_0_, bf16[144,512]{1,0:T(8,128)(2,1)S(1)} %collective-permute-done.38.refs_1_, bf16[144,512]{1,0:T(8,128)(2,1)S(1)} %collective-permute-done.39.refs_2_, ...), custom_call_target="tpu_custom_call" | custom-call | flops 1840000000 | bytes 5904000 | tf_op jit(solution)/shard_map/lay/pallas_call | solution.py:937
  (135 shorter events, 37.1 us)
Async XLA Ops:
  5.2 7.8 %collective-permute-start.4 = (bf16[288,512]{1,0:T(8,128)(2,1)}, bf16[288,512]{1,0:T(8,128)(2,1)S(1)}, u32[]{:S(2)}, u32[]{:S(2)}) collective-permute-start(bf16[288,512]{1,0:T(8,128)(2,1)} %get-tuple-element.137.refs_0_), channel_id=1, source_target_pairs={{0,8},{1,5},{2,10},{3,7},{8,16},{9,1},{10,18},{11,3},{16,24},{17,9... | collective-permute-start | bytes 884744 | tf_op jit(solution)/shard_map/ppermute | solution.py:1030
  8.1 8.0 %collective-permute-start.1 = (bf16[288,512]{1,0:T(8,128)(2,1)}, bf16[288,512]{1,0:T(8,128)(2,1)S(1)}, u32[]{:S(2)}, u32[]{:S(2)}) collective-permute-start(bf16[288,512]{1,0:T(8,128)(2,1)} %get-tuple-element.136.refs_1_), channel_id=1, source_target_pairs={{0,8},{1,5},{2,10},{3,7},{8,16},{9,1},{10,18},{11,3},{16,24},{17,9... | collective-permute-start | bytes 884744 | tf_op jit(solution)/shard_map/ppermute | solution.py:1030
  9.7 14.5 %collective-permute-start.3 = (bf16[512,512]{1,0:T(8,128)(2,1)S(1)}, bf16[512,512]{1,0:T(8,128)(2,1)S(1)}, u32[]{:S(2)}, u32[]{:S(2)}) collective-permute-start(bf16[512,512]{1,0:T(8,128)(2,1)S(1)} %copy-done.2), channel_id=1, source_target_pairs={{0,2},{1,3},{2,0},{3,1},{4,6},{5,7},{6,4},{7,5},{8,10},{9,11},{10,... | collective-permute-start | bytes 1572872 | tf_op jit(solution)/shard_map/ppermute | solution.py:1016
  13.0 6.7 %collective-permute-start.5 = (bf16[288,512]{1,0:T(8,128)(2,1)S(1)}, bf16[288,512]{1,0:T(8,128)(2,1)S(1)}, u32[]{:S(2)}, u32[]{:S(2)}) collective-permute-start(bf16[288,512]{1,0:T(8,128)(2,1)S(1)} %collective-permute-done.4.refs_0_.refs_2_), channel_id=1, source_target_pairs={{0,8},{1,5},{2,10},{3,7},{8,16},{9,1},{10,18},{11,3},{16,24},{17,9... | collective-permute-start | bytes 884744 | tf_op jit(solution)/shard_map/ppermute | solution.py:1030
  16.1 8.1 %collective-permute-start.2 = (bf16[288,512]{1,0:T(8,128)(2,1)S(1)}, bf16[288,512]{1,0:T(8,128)(2,1)S(1)}, u32[]{:S(2)}, u32[]{:S(2)}) collective-permute-start(bf16[288,512]{1,0:T(8,128)(2,1)S(1)} %collective-permute-done.1.refs_1_.refs_3_), channel_id=1, source_target_pairs={{0,8},{1,5},{2,10},{3,7},{8,16},{9,1},{10,18},{11,3},{16,24},{17,9... | collective-permute-start | bytes 884744 | tf_op jit(solution)/shard_map/ppermute | solution.py:1030
  19.7 8.2 %collective-permute-start.8 = (bf16[288,512]{1,0:T(8,128)(2,1)S(1)}, bf16[288,512]{1,0:T(8,128)(2,1)S(1)}, u32[]{:S(2)}, u32[]{:S(2)}) collective-permute-start(bf16[288,512]{1,0:T(8,128)(2,1)S(1)} %collective-permute-done.5.refs_0_.refs_6_), channel_id=1, source_target_pairs={{0,8},{1,5},{2,10},{3,7},{8,16},{9,1},{10,18},{11,3},{16,24},{17,9... | collective-permute-start | bytes 884744 | tf_op jit(solution)/shard_map/ppermute | solution.py:1030
  24.3 6.8 %collective-permute-start.11 = (bf16[288,512]{1,0:T(8,128)(2,1)S(1)}, bf16[288,512]{1,0:T(8,128)(2,1)S(1)}, u32[]{:S(2)}, u32[]{:S(2)}) collective-permute-start(bf16[288,512]{1,0:T(8,128)(2,1)S(1)} %collective-permute-done.2.refs_1_.refs_7_), channel_id=1, source_target_pairs={{0,8},{1,5},{2,10},{3,7},{8,16},{9,1},{10,18},{11,3},{16,24},{17,9... | collective-permute-start | bytes 884744 | tf_op jit(solution)/shard_map/ppermute | solution.py:1030
  25.9 7.9 %collective-permute-start.12 = (bf16[320,512]{1,0:T(8,128)(2,1)S(1)}, bf16[320,512]{1,0:T(8,128)(2,1)S(1)}, u32[]{:S(2)}, u32[]{:S(2)}) collective-permute-start(bf16[320,512]{1,0:T(8,128)(2,1)S(1)} %get-tuple-element.150), channel_id=1, source_target_pairs={{0,2},{1,3},{2,0},{3,1},{4,6},{5,7},{6,4},{7,5},{8,10},{9,11},{10,... | collective-permute-start | bytes 983048 | tf_op jit(solution)/shard_map/ppermute | solution.py:1016
  27.4 6.4 %collective-permute-start.6 = (bf16[288,512]{1,0:T(8,128)(2,1)S(1)}, bf16[288,512]{1,0:T(8,128)(2,1)S(1)}, u32[]{:S(2)}, u32[]{:S(2)}) collective-permute-start(bf16[288,512]{1,0:T(8,128)(2,1)S(1)} %collective-permute-done.4.refs_0_.refs_2_), channel_id=1, source_target_pairs={{0,1},{1,0},{2,3},{3,2},{4,5},{5,4},{6,7},{7,6},{8,9},{9,8},{10,11... | collective-permute-start | bytes 884744 | tf_op jit(solution)/shard_map/ppermute | solution.py:1016
  27.4 6.9 %collective-permute-start.7 = (bf16[288,512]{1,0:T(8,128)(2,1)S(1)}, bf16[288,512]{1,0:T(8,128)(2,1)S(1)}, u32[]{:S(2)}, u32[]{:S(2)}) collective-permute-start(bf16[288,512]{1,0:T(8,128)(2,1)S(1)} %collective-permute-done.1.refs_1_.refs_3_), channel_id=1, source_target_pairs={{0,1},{1,0},{2,3},{3,2},{4,5},{5,4},{6,7},{7,6},{8,9},{9,8},{10,11... | collective-permute-start | bytes 884744 | tf_op jit(solution)/shard_map/ppermute | solution.py:1016
  27.9 8.0 %collective-permute-start.10 = (bf16[288,512]{1,0:T(8,128)(2,1)S(1)}, bf16[288,512]{1,0:T(8,128)(2,1)S(1)}, u32[]{:S(2)}, u32[]{:S(2)}) collective-permute-start(bf16[288,512]{1,0:T(8,128)(2,1)S(1)} %collective-permute-done.2.refs_1_.refs_7_), channel_id=1, source_target_pairs={{0,1},{1,0},{2,3},{3,2},{4,5},{5,4},{6,7},{7,6},{8,9},{9,8},{10,11... | collective-permute-start | bytes 884744 | tf_op jit(solution)/shard_map/ppermute | solution.py:1016
  31.0 6.6 %collective-permute-start.9 = (bf16[288,512]{1,0:T(8,128)(2,1)S(1)}, bf16[288,512]{1,0:T(8,128)(2,1)S(1)}, u32[]{:S(2)}, u32[]{:S(2)}) collective-permute-start(bf16[288,512]{1,0:T(8,128)(2,1)S(1)} %collective-permute-done.5.refs_0_.refs_6_), channel_id=1, source_target_pairs={{0,1},{1,0},{2,3},{3,2},{4,5},{5,4},{6,7},{7,6},{8,9},{9,8},{10,11... | collective-permute-start | bytes 884744 | tf_op jit(solution)/shard_map/ppermute | solution.py:1016
  33.8 4.6 %collective-permute-start.13 = (bf16[288,512]{1,0:T(8,128)(2,1)S(1)}, bf16[288,512]{1,0:T(8,128)(2,1)S(1)}, u32[]{:S(2)}, u32[]{:S(2)}) collective-permute-start(bf16[288,512]{1,0:T(8,128)(2,1)S(1)} %collective-permute-done.8.refs_0_.refs_10_), channel_id=1, source_target_pairs={{0,1},{1,0},{2,3},{3,2},{4,5},{5,4},{6,7},{7,6},{8,9},{9,8},{10,11... | collective-permute-start | bytes 884744 | tf_op jit(solution)/shard_map/ppermute | solution.py:1016
  33.8 4.6 %collective-permute-start.14 = (bf16[288,512]{1,0:T(8,128)(2,1)S(1)}, bf16[288,512]{1,0:T(8,128)(2,1)S(1)}, u32[]{:S(2)}, u32[]{:S(2)}) collective-permute-start(bf16[288,512]{1,0:T(8,128)(2,1)S(1)} %collective-permute-done.11.refs_1_.refs_11_), channel_id=1, source_target_pairs={{0,1},{1,0},{2,3},{3,2},{4,5},{5,4},{6,7},{7,6},{8,9},{9,8},{10,11... | collective-permute-start | bytes 884744 | tf_op jit(solution)/shard_map/ppermute | solution.py:1016
  34.3 9.7 %collective-permute-start.16 = (bf16[320,512]{1,0:T(8,128)(2,1)S(1)}, bf16[320,512]{1,0:T(8,128)(2,1)S(1)}, u32[]{:S(2)}, u32[]{:S(2)}) collective-permute-start(bf16[320,512]{1,0:T(8,128)(2,1)S(1)} %get-tuple-element.161), channel_id=1, source_target_pairs={{0,2},{1,3},{2,0},{3,1},{4,6},{5,7},{6,4},{7,5},{8,10},{9,11},{10,... | collective-permute-start | bytes 983048 | tf_op jit(solution)/shard_map/ppermute | solution.py:1016
  35.9 7.0 %collective-permute-start.15 = (bf16[288,512]{1,0:T(8,128)(2,1)S(1)}, bf16[288,512]{1,0:T(8,128)(2,1)S(1)}, u32[]{:S(2)}, u32[]{:S(2)}) collective-permute-start(bf16[288,512]{1,0:T(8,128)(2,1)S(1)} %get-tuple-element.159), channel_id=1, source_target_pairs={{0,8},{1,5},{2,10},{3,7},{8,16},{9,1},{10,18},{11,3},{16,24},{17,9... | collective-permute-start | bytes 884744 | tf_op jit(solution)/shard_map/ppermute | solution.py:1030
  49.3 5.6 %collective-permute-start.18 = (bf16[512,128]{1,0:T(8,128)(2,1)S(1)}, bf16[512,128]{1,0:T(8,128)(2,1)S(1)}, u32[]{:S(2)}, u32[]{:S(2)}) collective-permute-start(bf16[512,128]{1,0:T(8,128)(2,1)S(1)} %get-tuple-element.165.refs_3_.refs_4_), channel_id=1, source_target_pairs={{0,2},{1,3},{2,0},{3,1},{4,6},{5,7},{6,4},{7,5},{8,10},{9,11},{10,... | collective-permute-start | bytes 393224 | tf_op jit(solution)/shard_map/ppermute | solution.py:1016
  65.0 9.7 %collective-permute-start.27 = (bf16[512,128]{1,0:T(8,128)(2,1)S(1)}, bf16[512,128]{1,0:T(8,128)(2,1)S(1)}, u32[]{:S(2)}, u32[]{:S(2)}) collective-permute-start(bf16[512,128]{1,0:T(8,128)(2,1)S(1)} %get-tuple-element.200.refs_0_), channel_id=1, source_target_pairs={{0,8},{8,16},{16,24},{24,28},{28,20},{20,12},{12,4},{4,0},{1,9},{9... | collective-permute-start | bytes 393224 | tf_op jit(solution)/shard_map/ppermute | solution.py:1010
  65.8 10.3 %collective-permute-start.28 = (bf16[512,128]{1,0:T(8,128)(2,1)S(1)}, bf16[512,128]{1,0:T(8,128)(2,1)S(1)}, u32[]{:S(2)}, u32[]{:S(2)}) collective-permute-start(bf16[512,128]{1,0:T(8,128)(2,1)S(1)} %get-tuple-element.200.refs_0_), channel_id=1, source_target_pairs={{0,4},{8,0},{16,8},{24,16},{28,24},{20,28},{12,20},{4,12},{1,5},{9... | collective-permute-start | bytes 393224 | tf_op jit(solution)/shard_map/ppermute | solution.py:1013
  67.1 5.4 %collective-permute-start.23 = (bf16[80,512]{1,0:T(8,128)(2,1)S(1)}, bf16[80,512]{1,0:T(8,128)(2,1)S(1)}, u32[]{:S(2)}, u32[]{:S(2)}) collective-permute-start(bf16[80,512]{1,0:T(8,128)(2,1)S(1)} %get-tuple-element.192), channel_id=1, source_target_pairs={{0,8},{8,16},{16,24},{24,28},{28,20},{20,12},{12,4},{4,0},{1,9},{9... | collective-permute-start | bytes 245768 | tf_op jit(solution)/shard_map/ppermute | solution.py:1010
  67.8 4.7 %collective-permute-start.24 = (bf16[64,512]{1,0:T(8,128)(2,1)S(1)}, bf16[64,512]{1,0:T(8,128)(2,1)S(1)}, u32[]{:S(2)}, u32[]{:S(2)}) collective-permute-start(bf16[64,512]{1,0:T(8,128)(2,1)S(1)} %get-tuple-element.193), channel_id=1, source_target_pairs={{0,4},{8,0},{16,8},{24,16},{28,24},{20,28},{12,20},{4,12},{1,5},{9... | collective-permute-start | bytes 196616 | tf_op jit(solution)/shard_map/ppermute | solution.py:1013
  70.9 21.8 %collective-permute-start.33 = (bf16[512,512]{1,0:T(8,128)(2,1)S(1)}, bf16[512,512]{1,0:T(8,128)(2,1)S(1)}, u32[]{:S(2)}, u32[]{:S(2)}) collective-permute-start(bf16[512,512]{1,0:T(8,128)(2,1)S(1)} %get-tuple-element.207.refs_4_.refs_9_.refs_3_.refs_2_), channel_id=1, source_target_pairs={{0,2},{1,3},{2,0},{3,1},{4,6},{5,7},{6,4},{7,5},{8,10},{9,11},{10,... | collective-permute-start | bytes 1572872 | tf_op jit(solution)/shard_map/ppermute | solution.py:1016
  72.6 6.9 %collective-permute-start.25 = (bf16[144,512]{1,0:T(8,128)(2,1)S(1)}, bf16[144,512]{1,0:T(8,128)(2,1)S(1)}, u32[]{:S(2)}, u32[]{:S(2)}) collective-permute-start(bf16[144,512]{1,0:T(8,128)(2,1)S(1)} %get-tuple-element.198), channel_id=1, source_target_pairs={{0,8},{8,16},{16,24},{24,28},{28,20},{20,12},{12,4},{4,0},{1,9},{9... | collective-permute-start | bytes 442376 | tf_op jit(solution)/shard_map/ppermute | solution.py:1010
  74.1 5.9 %collective-permute-start.26 = (bf16[144,512]{1,0:T(8,128)(2,1)S(1)}, bf16[144,512]{1,0:T(8,128)(2,1)S(1)}, u32[]{:S(2)}, u32[]{:S(2)}) collective-permute-start(bf16[144,512]{1,0:T(8,128)(2,1)S(1)} %get-tuple-element.199), channel_id=1, source_target_pairs={{0,4},{8,0},{16,8},{24,16},{28,24},{20,28},{12,20},{4,12},{1,5},{9... | collective-permute-start | bytes 442376 | tf_op jit(solution)/shard_map/ppermute | solution.py:1013
  74.6 7.4 %collective-permute-start.31 = (bf16[512,128]{1,0:T(8,128)(2,1)S(1)}, bf16[512,128]{1,0:T(8,128)(2,1)S(1)}, u32[]{:S(2)}, u32[]{:S(2)}) collective-permute-start(bf16[512,128]{1,0:T(8,128)(2,1)S(1)} %collective-permute-done.27.refs_0_), channel_id=1, source_target_pairs={{0,8},{8,16},{16,24},{24,28},{28,20},{20,12},{12,4},{4,0},{1,9},{9... | collective-permute-start | bytes 393224 | tf_op jit(solution)/shard_map/ppermute | solution.py:1010
  76.1 7.0 %collective-permute-start.32 = (bf16[512,128]{1,0:T(8,128)(2,1)S(1)}, bf16[512,128]{1,0:T(8,128)(2,1)S(1)}, u32[]{:S(2)}, u32[]{:S(2)}) collective-permute-start(bf16[512,128]{1,0:T(8,128)(2,1)S(1)} %collective-permute-done.28.refs_1_), channel_id=1, source_target_pairs={{0,4},{8,0},{16,8},{24,16},{28,24},{20,28},{12,20},{4,12},{1,5},{9... | collective-permute-start | bytes 393224 | tf_op jit(solution)/shard_map/ppermute | solution.py:1013
  80.0 12.7 %collective-permute-start.29 = (bf16[144,512]{1,0:T(8,128)(2,1)S(1)}, bf16[144,512]{1,0:T(8,128)(2,1)S(1)}, u32[]{:S(2)}, u32[]{:S(2)}) collective-permute-start(bf16[144,512]{1,0:T(8,128)(2,1)S(1)} %get-tuple-element.204), channel_id=1, source_target_pairs={{0,8},{8,16},{16,24},{24,28},{28,20},{20,12},{12,4},{4,0},{1,9},{9... | collective-permute-start | bytes 442376 | tf_op jit(solution)/shard_map/ppermute | solution.py:1010
  81.1 11.6 %collective-permute-start.30 = (bf16[144,512]{1,0:T(8,128)(2,1)S(1)}, bf16[144,512]{1,0:T(8,128)(2,1)S(1)}, u32[]{:S(2)}, u32[]{:S(2)}) collective-permute-start(bf16[144,512]{1,0:T(8,128)(2,1)S(1)} %get-tuple-element.205), channel_id=1, source_target_pairs={{0,4},{8,0},{16,8},{24,16},{28,24},{20,28},{12,20},{4,12},{1,5},{9... | collective-permute-start | bytes 442376 | tf_op jit(solution)/shard_map/ppermute | solution.py:1013
  82.1 5.0 %collective-permute-start.36 = (bf16[512,128]{1,0:T(8,128)(2,1)S(1)}, bf16[512,128]{1,0:T(8,128)(2,1)S(1)}, u32[]{:S(2)}, u32[]{:S(2)}) collective-permute-start(bf16[512,128]{1,0:T(8,128)(2,1)S(1)} %collective-permute-done.31.refs_0_), channel_id=1, source_target_pairs={{0,8},{8,16},{16,24},{24,28},{28,20},{20,12},{12,4},{4,0},{1,9},{9... | collective-permute-start | bytes 393224 | tf_op jit(solution)/shard_map/ppermute | solution.py:1010
  83.1 5.3 %collective-permute-start.37 = (bf16[512,128]{1,0:T(8,128)(2,1)S(1)}, bf16[512,128]{1,0:T(8,128)(2,1)S(1)}, u32[]{:S(2)}, u32[]{:S(2)}) collective-permute-start(bf16[512,128]{1,0:T(8,128)(2,1)S(1)} %collective-permute-done.32.refs_1_), channel_id=1, source_target_pairs={{0,4},{8,0},{16,8},{24,16},{28,24},{20,28},{12,20},{4,12},{1,5},{9... | collective-permute-start | bytes 393224 | tf_op jit(solution)/shard_map/ppermute | solution.py:1013
  88.4 6.5 %collective-permute-start.40 = (bf16[256,128]{1,0:T(8,128)(2,1)S(1)}, bf16[256,128]{1,0:T(8,128)(2,1)S(1)}, u32[]{:S(2)}, u32[]{:S(2)}) collective-permute-start(bf16[256,128]{1,0:T(8,128)(2,1)S(1)} %get-tuple-element.217), channel_id=1, source_target_pairs={{0,8},{8,16},{16,24},{24,28},{28,20},{20,12},{12,4},{4,0},{1,9},{9... | collective-permute-start | bytes 196616 | tf_op jit(solution)/shard_map/ppermute | solution.py:1010
  89.7 5.2 %collective-permute-start.41 = (bf16[256,128]{1,0:T(8,128)(2,1)S(1)}, bf16[256,128]{1,0:T(8,128)(2,1)S(1)}, u32[]{:S(2)}, u32[]{:S(2)}) collective-permute-start(bf16[256,128]{1,0:T(8,128)(2,1)S(1)} %get-tuple-element.218), channel_id=1, source_target_pairs={{0,4},{8,0},{16,8},{24,16},{28,24},{20,28},{12,20},{4,12},{1,5},{9... | collective-permute-start | bytes 196616 | tf_op jit(solution)/shard_map/ppermute | solution.py:1013
  92.8 6.4 %collective-permute-start.34 = (bf16[144,512]{1,0:T(8,128)(2,1)S(1)}, bf16[144,512]{1,0:T(8,128)(2,1)S(1)}, u32[]{:S(2)}, u32[]{:S(2)}) collective-permute-start(bf16[144,512]{1,0:T(8,128)(2,1)S(1)} %get-tuple-element.210), channel_id=1, source_target_pairs={{0,8},{8,16},{16,24},{24,28},{28,20},{20,12},{12,4},{4,0},{1,9},{9... | collective-permute-start | bytes 442376 | tf_op jit(solution)/shard_map/ppermute | solution.py:1010
  94.1 6.1 %collective-permute-start.35 = (bf16[144,512]{1,0:T(8,128)(2,1)S(1)}, bf16[144,512]{1,0:T(8,128)(2,1)S(1)}, u32[]{:S(2)}, u32[]{:S(2)}) collective-permute-start(bf16[144,512]{1,0:T(8,128)(2,1)S(1)} %get-tuple-element.211), channel_id=1, source_target_pairs={{0,4},{8,0},{16,8},{24,16},{28,24},{20,28},{12,20},{4,12},{1,5},{9... | collective-permute-start | bytes 442376 | tf_op jit(solution)/shard_map/ppermute | solution.py:1013
  100.2 6.8 %collective-permute-start.38 = (bf16[144,512]{1,0:T(8,128)(2,1)S(1)}, bf16[144,512]{1,0:T(8,128)(2,1)S(1)}, u32[]{:S(2)}, u32[]{:S(2)}) collective-permute-start(bf16[144,512]{1,0:T(8,128)(2,1)S(1)} %total.1.refs_0_), channel_id=1, source_target_pairs={{0,8},{8,16},{16,24},{24,28},{28,20},{20,12},{12,4},{4,0},{1,9},{9... | collective-permute-start | bytes 442376 | tf_op jit(solution)/shard_map/ppermute | solution.py:1010
  102.0 6.4 %collective-permute-start.39 = (bf16[144,512]{1,0:T(8,128)(2,1)S(1)}, bf16[144,512]{1,0:T(8,128)(2,1)S(1)}, u32[]{:S(2)}, u32[]{:S(2)}) collective-permute-start(bf16[144,512]{1,0:T(8,128)(2,1)S(1)} %total.1.refs_0_), channel_id=1, source_target_pairs={{0,4},{8,0},{16,8},{24,16},{28,24},{20,28},{12,20},{4,12},{1,5},{9... | collective-permute-start | bytes 442376 | tf_op jit(solution)/shard_map/ppermute | solution.py:1013
  108.5 7.8 %collective-permute-start.44 = (bf16[512,384]{1,0:T(8,128)(2,1)S(1)}, bf16[512,384]{1,0:T(8,128)(2,1)S(1)}, u32[]{:S(2)}, u32[]{:S(2)}) collective-permute-start(bf16[512,384]{1,0:T(8,128)(2,1)S(1)} %get-tuple-element.236.refs_1_.refs_0_), channel_id=1, source_target_pairs={{0,2},{1,3},{2,0},{3,1},{4,6},{5,7},{6,4},{7,5},{8,10},{9,11},{10,... | collective-permute-start | bytes 1179656 | tf_op jit(solution)/shard_map/ppermute | solution.py:1016
  109.0 7.3 %collective-permute-start.42 = (bf16[144,512]{1,0:T(8,128)(2,1)S(1)}, bf16[144,512]{1,0:T(8,128)(2,1)S(1)}, u32[]{:S(2)}, u32[]{:S(2)}) collective-permute-start(bf16[144,512]{1,0:T(8,128)(2,1)S(1)} %collective-permute-done.38.refs_1_), channel_id=1, source_target_pairs={{0,8},{8,16},{16,24},{24,28},{28,20},{20,12},{12,4},{4,0},{1,9},{9... | collective-permute-start | bytes 442376 | tf_op jit(solution)/shard_map/ppermute | solution.py:1010
  110.1 6.2 %collective-permute-start.43 = (bf16[144,512]{1,0:T(8,128)(2,1)S(1)}, bf16[144,512]{1,0:T(8,128)(2,1)S(1)}, u32[]{:S(2)}, u32[]{:S(2)}) collective-permute-start(bf16[144,512]{1,0:T(8,128)(2,1)S(1)} %collective-permute-done.39.refs_2_), channel_id=1, source_target_pairs={{0,4},{8,0},{16,8},{24,16},{28,24},{20,28},{12,20},{4,12},{1,5},{9... | collective-permute-start | bytes 442376 | tf_op jit(solution)/shard_map/ppermute | solution.py:1013
  117.3 10.7 %collective-permute-start.52 = (f32[512,512]{1,0:T(8,128)S(1)}, f32[512,512]{1,0:T(8,128)S(1)}, u32[]{:S(2)}, u32[]{:S(2)}) collective-permute-start(f32[512,512]{1,0:T(8,128)S(1)} %input_back.1.refs_2_), channel_id=1, source_target_pairs={{0,1},{1,0},{2,3},{3,2},{4,5},{5,4},{6,7},{7,6},{8,9},{9,8},{10,11... | collective-permute-start | bytes 3145736 | tf_op jit(solution)/shard_map/ppermute | solution.py:1016
  117.4 4.7 %collective-permute-start.49 = (f32[16,512]{1,0:T(8,128)S(1)}, f32[16,512]{1,0:T(8,128)S(1)}, u32[]{:S(2)}, u32[]{:S(2)}) collective-permute-start(f32[16,512]{1,0:T(8,128)S(1)} %add_gains.2.refs_0_), channel_id=1, source_target_pairs={{0,8},{4,12},{8,0},{12,4},{16,24},{20,28},{24,16},{28,20},{1,9},{5... | collective-permute-start | bytes 98312 | tf_op jit(solution)/shard_map/ppermute | solution.py:1019
  118.6 8.8 %collective-permute-start.50 = (f32[16,512]{1,0:T(8,128)S(1)}, f32[16,512]{1,0:T(8,128)S(1)}, u32[]{:S(2)}, u32[]{:S(2)}) collective-permute-start(f32[16,512]{1,0:T(8,128)S(1)} %add_gains.2.refs_0_), channel_id=1, source_target_pairs={{0,16},{4,20},{8,24},{12,28},{16,0},{20,4},{24,8},{28,12},{1,17},{... | collective-permute-start | bytes 98312 | tf_op jit(solution)/shard_map/ppermute | solution.py:1019
  119.9 7.5 %collective-permute-start.51 = (f32[16,512]{1,0:T(8,128)S(1)}, f32[16,512]{1,0:T(8,128)S(1)}, u32[]{:S(2)}, u32[]{:S(2)}) collective-permute-start(f32[16,512]{1,0:T(8,128)S(1)} %add_gains.2.refs_0_), channel_id=1, source_target_pairs={{0,24},{4,28},{8,16},{12,20},{16,8},{20,12},{24,0},{28,4},{1,25},{... | collective-permute-start | bytes 98312 | tf_op jit(solution)/shard_map/ppermute | solution.py:1019
  121.8 5.6 %collective-permute-start.47 = (bf16[144,512]{1,0:T(8,128)(2,1)S(1)}, bf16[144,512]{1,0:T(8,128)(2,1)S(1)}, u32[]{:S(2)}, u32[]{:S(2)}) collective-permute-start(bf16[144,512]{1,0:T(8,128)(2,1)S(1)} %collective-permute-done.42.refs_3_), channel_id=1, source_target_pairs={{0,8},{8,16},{16,24},{24,28},{28,20},{20,12},{12,4},{4,0},{1,9},{9... | collective-permute-start | bytes 442376 | tf_op jit(solution)/shard_map/ppermute | solution.py:1010
  122.1 5.8 %collective-permute-start.48 = (bf16[144,512]{1,0:T(8,128)(2,1)S(1)}, bf16[144,512]{1,0:T(8,128)(2,1)S(1)}, u32[]{:S(2)}, u32[]{:S(2)}) collective-permute-start(bf16[144,512]{1,0:T(8,128)(2,1)S(1)} %collective-permute-done.43.refs_4_), channel_id=1, source_target_pairs={{0,4},{8,0},{16,8},{24,16},{28,24},{20,28},{12,20},{4,12},{1,5},{9... | collective-permute-start | bytes 442376 | tf_op jit(solution)/shard_map/ppermute | solution.py:1013
  127.9 7.9 %collective-permute-start.53 = (f32[512,512]{1,0:T(8,128)S(1)}, f32[512,512]{1,0:T(8,128)S(1)}, u32[]{:S(2)}, u32[]{:S(2)}) collective-permute-start(f32[512,512]{1,0:T(8,128)S(1)} %get-tuple-element.247.refs_0_), channel_id=1, source_target_pairs={{0,1},{1,0},{2,3},{3,2},{4,5},{5,4},{6,7},{7,6},{8,9},{9,8},{10,11... | collective-permute-start | bytes 3145736 | tf_op jit(solution)/shard_map/ppermute | solution.py:1016
  129.0 5.2 %collective-permute-start.56 = (bf16[80,512]{1,0:T(8,128)(2,1)S(1)}, bf16[80,512]{1,0:T(8,128)(2,1)S(1)}, u32[]{:S(2)}, u32[]{:S(2)}) collective-permute-start(bf16[80,512]{1,0:T(8,128)(2,1)S(1)} %get-tuple-element.257), channel_id=1, source_target_pairs={{0,8},{8,16},{16,24},{24,28},{28,20},{20,12},{12,4},{4,0},{1,9},{9... | collective-permute-start | bytes 245768 | tf_op jit(solution)/shard_map/ppermute | solution.py:1010
  130.0 4.3 %collective-permute-start.57 = (bf16[64,512]{1,0:T(8,128)(2,1)S(1)}, bf16[64,512]{1,0:T(8,128)(2,1)S(1)}, u32[]{:S(2)}, u32[]{:S(2)}) collective-permute-start(bf16[64,512]{1,0:T(8,128)(2,1)S(1)} %get-tuple-element.258), channel_id=1, source_target_pairs={{0,4},{8,0},{16,8},{24,16},{28,24},{20,28},{12,20},{4,12},{1,5},{9... | collective-permute-start | bytes 196616 | tf_op jit(solution)/shard_map/ppermute | solution.py:1013
  (27 other events, 198.1 us)

commit v6 on v5

--- a/solution.py
+++ b/solution.py
@@ -360,6 +360,10 @@
     half[...] = jnp.where(even, first[...], second[...])
     pair[:width, :] = w_out[...]
     pair[width:, :] = w_out_y[:width, :]
+
+
+def turn():
+    return 1 - 2 * (lax.axis_index("head") % 2)
 
 
 def owners_of(step):
@@ -573,15 +577,19 @@
     d_ctx[...] = dot_nt(low, w_out[...]).astype(bf16)
 
 
-def grads_kernel(h_two, d_hidden, active, cotangent, context, d_low, *refs):
-    keeps, (front, back), (up, down, out) = refs[:7], refs[7:9], refs[9:]
+def stacked(rows):
+    return jnp.concatenate([rows[:, k * 2 * DH : (k + 1) * 2 * DH] for k in range(D // (2 * DH))], 0)
+
+
+def grads_kernel(h_two, d_hidden, active, cotangent, context, d_low, d_ctx, *refs):
+    keeps, (ahead, behind), (up, down, out) = refs[:7], refs[7:9], refs[9:]
     place = place_of(lax.axis_index("blk"))
     up[...] = dot_tn(h_two[...], d_hidden[...])
     down[...] = dot_tn(active[...], cotangent[...])
     out[...] = dot_tn(context[...], d_low[...])
 
     def rows_of(distance):
-        owner = ring_of((place + distance + 8) % 8)
+        owner = ring_of((place + turn() * distance + 8) % 8)
         parts = []
         for ref in (up, down, out):
             n = ref.shape[0] // 8
@@ -589,25 +597,36 @@
         return jnp.concatenate(parts, 0)
 
     for ref, distance in zip(keeps, (3, 2, 1, -3, -2, -1, 0)):
-        ref[...] = rows_of(distance)
+        ref[...] = stacked(rows_of(distance))
     last = rows_of(4).astype(jnp.bfloat16)
-    n = front.shape[0]
-    front[...] = last[:n]
-    back[...] = last[n:]
-
-
-def relay_kernel(keep_f, keep_b, f, b, out_f, out_b):
+    rows = d_ctx.shape[0]
+    n = (ahead.shape[0] - rows) // 4
+    for ref, part in ((ahead, last[:n]), (behind, last[n:])):
+        ref[:rows, :] = d_ctx[...]
+        ref[rows:, :] = stacked(part)
+
+
+def relay_kernel(start, count, at, keep, arrived, out):
+    f32, bf16 = jnp.float32, jnp.bfloat16
+    size = keep.shape[0] // 4
+    n = (arrived.shape[0] - SHARD) // 4
+    out[:count, :] = arrived[start : start + count, :]
+    out[count:, :] = keep[...].astype(bf16)
+    for k in range(4):
+        here = slice(k * size + at, k * size + at + n)
+        total = keep[here, :] + arrived[SHARD + k * n : SHARD + (k + 1) * n, :].astype(f32)
+        out[count + k * size + at : count + k * size + at + n, :] = total.astype(bf16)
+
+
+def total_kernel(keep, x, y, out):
     f32 = jnp.float32
-    n, m, size = f.shape[0], b.shape[0], keep_f.shape[0]
-    out_f[...] = keep_f[...].astype(jnp.bfloat16)
-    out_b[...] = keep_b[...].astype(jnp.bfloat16)
-    out_f[:n, :] = (keep_f[:n, :] + f[...].astype(f32)).astype(jnp.bfloat16)
-    out_b[size - m :, :] = (keep_b[size - m :, :] + b[...].astype(f32)).astype(jnp.bfloat16)
-
-
-def total_kernel(keep, f, b, out):
-    f32 = jnp.float32
-    out[...] = (keep[...] + (f[...].astype(f32) + b[...].astype(f32))).astype(jnp.bfloat16)
+    size = keep.shape[0] // 4
+    skip = x.shape[0] - 4 * size
+    for k in range(4):
+        rows = slice(k * size, (k + 1) * size)
+        there = slice(skip + k * size, skip + (k + 1) * size)
+        total = keep[rows, :] + (x[there, :].astype(f32) + y[there, :].astype(f32))
+        out[:, k * 2 * DH : (k + 1) * 2 * DH] = total.astype(jnp.bfloat16)
 
 
 def cut_kernel(f, b, front, back):
@@ -615,15 +634,18 @@
     back[...] = b[b.shape[0] - back.shape[0] :, :]
 
 
-def lay_kernel(own, f1, b1, f2, b2, f3, b3, f4, b4, g_up, g_down, g_out):
+def lay_kernel(own, f1, b1, f2, b2, f3, b3, f4, b4, gains, other, g_up, g_down, g_out, g_one, g_two):
     f32 = jnp.float32
+    total = gains[...] + other[...]
+    g_one[...] = total[0, :]
+    g_two[...] = total[8, :]
     place = place_of(lax.axis_index("blk"))
     last = jnp.concatenate([f4[...], b4[...]], 0)
     for distance, piece in (
         (0, own[...]), (-1, f1[...]), (1, b1[...]), (-2, f2[...]), (2, b2[...]), (-3, f3[...]), (3, b3[...]),
         (4, last),
     ):
-        owner = ring_of((place + distance + 8) % 8)
+        owner = ring_of((place + turn() * distance + 8) % 8)
         start = 0
         for ref in (g_up, g_down, g_out):
             n = ref.shape[0] // 8
@@ -649,14 +671,8 @@
     out[...] = (here[...] + one[...]) + (two[...] + three[...])
 
 
-def gains_kernel(here, other, first, second):
-    total = here[...] + other[...]
-    first[...] = total[0, :]
-    second[...] = total[8, :]
-
-
 def block_at(place, step, start, i):
-    return ring_of((place + 8 - step) % 8) * (SHARD // BLOCK) + start // BLOCK + i
+    return ring_of((place + 8 - turn() * step) % 8) * (SHARD // BLOCK) + start // BLOCK + i
 
 
 def prepare_kernel(pieces, qkv, partner, scale_rows, z_out, probs_out):
@@ -690,8 +706,8 @@
     scale = DH**-0.5
     blocks = [
         (step, start, d_ctx, i)
-        for (step, start), d_ctx in zip(pieces, outs)
-        for i in range(d_ctx.shape[0] // BLOCK)
+        for (step, start, n), d_ctx in zip(pieces, outs)
+        for i in range(n // BLOCK)
     ]
     for first in range(0, len(blocks), 8):
         work = []
@@ -770,7 +786,7 @@
     for parts, near_ref, low_ref, w_ref in zip(pieces, nears, lows, d_weights):
         at = 0
         for step, start, n in parts:
-            owner = ring_of((place + 8 - step) % 8)
+            owner = ring_of((place + 8 - turn() * step) % 8)
             to = pl.ds(pl.multiple_of(owner * SHARD + start, n), n)
             acc[to, :] = near_ref[at : at + n, :]
             far[to, :] = low_ref[at : at + n, 2 * DH :]
@@ -886,6 +902,7 @@
 VMEM_SPEC = pl.BlockSpec(memory_space=pltpu.VMEM)
 SMEM_SPEC = pl.BlockSpec(memory_space=pltpu.SMEM)
 ANY_SPEC = pl.BlockSpec(memory_space=pltpu.HBM)
+FREE_SPEC = pl.BlockSpec(memory_space=pl.ANY)
 
 
 def fetch(pairs, sems, first=0):
@@ -901,11 +918,11 @@
         copy.wait()
 
 
-def call(kernel, outs, *args, scratch=(), smem=(), cold=(), raw=(), out_cold=(), limit=16, name=None):
+def call(kernel, outs, *args, scratch=(), smem=(), cold=(), free=(), raw=(), out_cold=(), limit=16, name=None):
     cost = int(1e3 * TIMES[name])
     shapes = [jax.ShapeDtypeStruct(s, d) for s, d in outs]
     specs = [
-        SMEM_SPEC if i in smem else ANY_SPEC if i in cold or i in raw else VMEM_SPEC
+        SMEM_SPEC if i in smem else FREE_SPEC if i in free else ANY_SPEC if i in cold or i in raw else VMEM_SPEC
         for i in range(len(args))
     ]
     out_specs = [ANY_SPEC if i in out_cold else VMEM_SPEC for i in range(len(outs))]
@@ -957,9 +974,9 @@
     "prepare": 2.9,
     "feed": 4.2,
     "back": 1.2,
-    "pull": 2.4,
+    "pull": 0.1,
     "grads": 0.95,
-    "relay": 0.2,
+    "relay": 0.3,
     "collect": 4.5,
     "sinkhorn_back": 2.05,
     "total": 0.25,
@@ -1006,34 +1023,34 @@
     half, quarter = rows // 2, rows // 4
     core = lax.axis_index("head") % 2
 
-    def ahead(v):
-        return lax.ppermute(v, "blk", [(RING[i], RING[(i + 1) % 8]) for i in range(8)])
-
-    def behind(v):
-        return lax.ppermute(v, "blk", [(RING[i], RING[(i - 1) % 8]) for i in range(8)])
-
-    def swap_head(v, j):
-        return lax.ppermute(v, "head", [(i, i ^ j) for i in range(4)])
-
-    def swap_blk(v, j):
-        return lax.ppermute(v, "blk", [(i, i ^ j) for i in range(8)])
-
-    w_in = w_qkv.transpose(1, 0, 2)
-    partner_s = partner.T
-
-    def along(v):
+    def along(v, way=1):
         pairs = []
         for i in range(8):
             for h in range(4):
-                to = RING[(i + 1) % 8] if h % 2 == 0 else RING[(i - 1) % 8]
+                to = RING[(i + (way if h % 2 == 0 else -way)) % 8]
                 pairs.append((RING[i] * 4 + h, to * 4 + h))
         return lax.ppermute(v, ("blk", "head"), pairs)
+
+    def ahead(v):
+        return along(v)
+
+    def behind(v):
+        return along(v, -1)
+
+    def swap_head(v, j):
+        return lax.ppermute(v, "head", [(i, i ^ j) for i in range(4)])
+
+    def swap_blk(v, j):
+        return lax.ppermute(v, "blk", [(i, i ^ j) for i in range(8)])
+
+    w_in = w_qkv.transpose(1, 0, 2)
+    partner_s = partner.T
 
     a, b, own_summary, own_noise = call(
         head_kernel,
         [((half + EXTRA, D), bf16)] * 2 + [((blocks, D), f32), ((2, D), f32)],
         tokens, gain_attn, gumbel_noise, swap_head(gumbel_noise, 1),
-        cold=(0, 1, 2, 3), limit=62, name="norm_one",
+        cold=(0, 1, 2, 3), free=(3,), limit=62, name="norm_one",
     )
 
     mine = [(a, b)]
@@ -1047,9 +1064,10 @@
         ],
         *mine[0], w_in, w_sort, w_out, w_down, name="project_own",
     )
+    a, qkv_own = tie(a, qkv_own)
     mine.append((a, b))
     a, b = along(a), along(b)
-    b, up_y, qkv_own = tie(b, up_y, qkv_own)
+    b, up_y = tie(b, up_y)
     mine.append((a, b))
     first_y = swap_head(after(first, a), 2)
     a, b = along(a), along(b)
@@ -1115,13 +1133,14 @@
         middle, d_h_two, d_h_two_other, cotangent, gain_ffn, w_out, name="back",
     )
 
-    plans = [[(0, 0)]] + [[(k, 0), (-k, 0)] for k in (1, 2, 3)] + [[(4, 0), (4, half)]]
+    plans = [[(0, 0, rows)]] + [[(k, 0, rows), (-k, 0, rows)] for k in (1, 2, 3)]
+    plans.append([(4, 0, half), (4, half, half)])
     offsets = (None, None, None, 0, 2 * blocks)
     pulled = []
 
     def pull(given):
         plan, offset = plans[len(pulled)], offsets[len(pulled)]
-        n = sum(a.shape[0] for a in given)
+        n = sum(count for _, _, count in plan)
         pulled.append(
             call(
                 functools.partial(pull_kernel, tuple(plan), offset),
@@ -1137,38 +1156,37 @@
     front = 80
     parts = call(
         grads_kernel,
-        [((piece, D), f32)] * 7 + [((front, D), bf16), ((piece - front, D), bf16)],
-        h_two, d_hidden, active, cotangent, context, d_low,
+        [((4 * piece, width), f32)] * 7
+        + [((rows + 4 * front, width), bf16), ((rows + 4 * (piece - front), width), bf16)],
+        h_two, d_hidden, active, cotangent, context, d_low, d_ctx,
         scratch=[((D, ff), f32), ((ff, D), f32), ((width, D), f32)], name="grads",
     )
-    keeps, (sum_f, sum_b) = parts[:7], parts[7:]
+    keeps, (x, y) = parts[:7], parts[7:]
+
+    def relay(start, count, at, keep, arrived):
+        return call(
+            functools.partial(relay_kernel, start, count, at), [((count + 4 * piece, width), bf16)],
+            keep, arrived, name="relay",
+        )
+
     given = [d_ctx]
-    arrays = [given]
-    d_ctx, sum_f, sum_b = tie(d_ctx, sum_f, sum_b)
-    f = b = d_ctx
-    joint_y = swap_head(after(joint, sum_f), 2)
     for step in range(4):
-        if step == 3:
-            f, b = call(halve_kernel, [((half, width), bf16)] * 2, f, b, name="halve")
-        f, b = ahead(f), behind(b)
-        sum_f, sum_b = ahead(sum_f), behind(sum_b)
+        x, y = ahead(x), behind(y)
         done = pull(given)
+        given = [x, y]
+        if step == 0:
+            joint_y = swap_head(after(joint, done), 2)
         hold = [joint_y] if step == 2 else []
-        sum_f, sum_b = tie(sum_f, sum_b, done, *hold)[:2]
-        given = [f, b]
-        arrays.append(given)
+        y = tie(y, done, *hold)[0]
         if step < 3:
-            sum_f, sum_b = call(
-                relay_kernel, [((piece, D), bf16)] * 2, keeps[step], keeps[step + 3], sum_f, sum_b,
-                name="relay",
-            )
-    owned = call(total_kernel, [((piece, D), bf16)], keeps[6], sum_f, sum_b, name="total")
+            count = half if step == 2 else rows
+            x = relay(0, count, 0, keeps[step], x)
+            y = relay(rows - count, count, 0 if step else front, keeps[step + 3], y)
+    owned = call(total_kernel, [((piece, D), bf16)], keeps[6], x, y, name="total")
     wf1, wb1 = ahead(owned), behind(owned)
     pull(given)
-    spans = tuple(
-        tuple((step, start, a.shape[0]) for (step, start), a in zip(plan, given))
-        for plan, given in zip(plans, arrays)
-    )
+
+    spans = tuple(tuple(plan) for plan in plans)
     d_qkv, d_mine, flat_mine, g_sort = call(
         functools.partial(collect_kernel, spans),
         [
@@ -1181,6 +1199,8 @@
         name="collect",
     )
     wf1, wb1, d_mine, flat_mine = tie(wf1, wb1, d_mine, flat_mine)
+    ffn_other = swap_head(after(ffn, d_mine), 1)
+    output = call(add_kernel, [((rows, D), f32)], ffn, ffn_other, middle, name="output")
     wf2, wb2 = ahead(wf1), behind(wb1)
     d_mine_y, flat_y = swap_head(d_mine, 2), swap_head(flat_mine, 2)
     gains_a = call(
@@ -1188,9 +1208,11 @@
     )
     gains_x = swap_blk(gains_a, 1)
     gains = call(add_kernel, [((16, D), f32)], gains_a, gains_x, name="add_gains")
-    wf2, wb2, d_mine_y, flat_y, gains = tie(wf2, wb2, d_mine_y, flat_y, gains)
+    wf2, wb2, gains, flat_y, d_mine_y = tie(wf2, wb2, gains, flat_y, d_mine_y)
     wf3, wb3 = ahead(wf2), behind(wb2)
-    gains1, gains2, gains3 = swap_blk(gains, 2), swap_blk(gains, 4), swap_blk(gains, 6)
+    gains1 = swap_blk(gains, 2)
+    gains = call(add_kernel, [((16, D), f32)], gains, gains1, name="add_gains")
+    gains2 = swap_blk(gains, 4)
     d_h = call(
         input_kernel, [((rows, D), f32)],
         d_mine, d_mine_y, joint, joint_y, flat_mine, flat_y,
@@ -1205,29 +1227,26 @@
         *mine[0], *[v for k in (1, 2, 3) for v in (*mine[k], *other[k - 1])], m4, o4, after(d_qkv, d_h),
         scratch=[((total, D), bf16)], limit=24, name="weights",
     )
-    wf3, wb3, gains1, gains2, gains3, d_h_other, g_qkv = tie(
-        wf3, wb3, gains1, gains2, gains3, d_h_other, g_qkv
+    wf3, wb3, gains, gains2, g_qkv, d_h_other = tie(
+        wf3, wb3, gains, gains2, g_qkv, d_h_other
     )
     cut_f, cut_b = call(
         cut_kernel, [((front, D), bf16), ((piece - front, D), bf16)], wf3, wb3, name="halve"
     )
     wf4, wb4 = ahead(cut_f), behind(cut_b)
-    gains = call(four_kernel, [((16, D), f32)], gains, gains1, gains2, gains3, name="sum_gains")
+    gains = call(add_kernel, [((16, D), f32)], gains, gains2, name="add_gains")
     gains_y = swap_head(gains, 2)
     d_tokens = call(
         end_kernel, [((rows, D), f32)],
         tokens, gain_attn, d_h, d_h_other, d_middle, name="norm_one_back",
     )
-    ffn_other = swap_head(after(ffn, wf3), 1)
     gains = call(add_kernel, [((16, D), f32)], gains, gains_y, name="add_gains")
     gains_c = swap_head(gains, 1)
-    output = call(add_kernel, [((rows, D), f32)], ffn, ffn_other, middle, name="output")
-    g_up, g_down, g_out = call(
+    g_up, g_down, g_out, g_one, g_two = call(
         lay_kernel,
-        [((D, ff), f32), ((ff, D), f32), ((width, D), f32)],
-        owned, wf1, wb1, wf2, wb2, wf3, wb3, wf4, wb4, name="lay",
-    )
-    g_one, g_two = call(gains_kernel, [((D,), f32), ((D,), f32)], gains, gains_c, name="gains")
+        [((D, ff), f32), ((ff, D), f32), ((width, D), f32), ((D,), f32), ((D,), f32)],
+        owned, wf1, wb1, wf2, wb2, wf3, wb3, wf4, wb4, gains, gains_c, name="lay",
+    )
     return output, d_tokens, g_one, g_two, g_qkv.transpose(1, 0, 2), g_out, g_sort, g_up, g_down
 
 

time: 137 us -> 133 us (0.971)
  starting transfers between devices: 56.4 us -> 44.5 us
  waiting for transfers between devices: 33.6 us -> 42 us
    ppermute x24 -> x0, starting transfers between devices: 24.7 us -> none  [the longest x12 13.3 us: ahead(): lax.ppermute(v, 'blk', [(RING[i], RING[(i + 1) % 8]) for i in range(8)])]
    ppermute x7 -> x23, starting transfers between devices: 13.5 us -> 28.3 us  [along(): return lax.ppermute(v, ('blk', 'head'), pairs)]
    ppermute x7 -> x23, waiting for transfers between devices: 11.1 us -> 22.3 us  [along(): return lax.ppermute(v, ('blk', 'head'), pairs)]
    ppermute x24 -> x0, waiting for transfers between devices: 7.98 us -> none  [the longest x12 4.82 us: behind(): lax.ppermute(v, 'blk', [(RING[i], RING[(i - 1) % 8]) for i in range(8)])]
    ppermute x23, waiting for transfers between devices: 12.6 us -> 15.7 us  [swap_head(): return lax.ppermute(v, 'head', [(i, i ^ j) for i in range(4)])]
    ppermute x4 -> x3, waiting for transfers between devices: 1.87 us -> 4.03 us  [swap_blk(): return lax.ppermute(v, 'blk', [(i, i ^ j) for i in range(8)])]
    ppermute x4 -> x3, starting transfers between devices: 5.15 us -> 3.46 us  [swap_blk(): return lax.ppermute(v, 'blk', [(i, i ^ j) for i in range(8)])]
    pallas_call x33 -> x35, Pallas kernels: 43.4 us -> 42.9 us  [call(): pl.pallas_call(body, out_shape=shapes, in_specs=specs, out_specs=out_spec...]
  transfers between devices with their start and end apart: 58 -> 49, of which waited for: 23 -> 25; matrix products, arithmetic and copies ran while one was open for 0% -> 0% of each run, Pallas kernels for 21% -> 21%
where the time goes in v6:
time: 133 us
  starting transfers between devices  44.5 us (33%)
  Pallas kernels  42.9 us (32%)
  waiting for transfers between devices  42 us (32%)
  local copies, waits for them, and re-layouts  2.58 us (2%)
    pallas_call x35, Pallas kernels, call(): pl.pallas_call(body, out_shape=shapes, in_specs=specs, out_specs=out_spec...  42.9 us
    ppermute x23, starting transfers between devices, along(): return lax.ppermute(v, ('blk', 'head'), pairs)  28.3 us
    ppermute x23, waiting for transfers between devices, along(): return lax.ppermute(v, ('blk', 'head'), pairs)  22.3 us
    ppermute x23, waiting for transfers between devices, swap_head(): return lax.ppermute(v, 'head', [(i, i ^ j) for i in range(4)])  15.7 us
    ppermute x23, starting transfers between devices, swap_head(): return lax.ppermute(v, 'head', [(i, i ^ j) for i in range(4)])  12.7 us
    ppermute x3, waiting for transfers between devices, swap_blk(): return lax.ppermute(v, 'blk', [(i, i ^ j) for i in range(8)])  4.03 us
    ppermute x3, starting transfers between devices, swap_blk(): return lax.ppermute(v, 'blk', [(i, i ^ j) for i in range(8)])  3.46 us
  transfers between devices with their start and end apart: 49, of which 25 were waited for; matrix products, arithmetic and copies ran while one was open for 0% of the time, Pallas kernels for 21%

profile of v6, /device:TPU:0, one launch (start us, length us, event | category | flops | bytes accessed | tf_op | source)
XLA Modules:
  0.0 133.1 jit_solution(18255226083752148032)
XLA Ops:
  2.9 2.3 %norm_one.1 = (bf16[288,512]{1,0:T(8,128)(2,1)}, bf16[288,512]{1,0:T(8,128)(2,1)}, f32[8,512]{1,0:T(8,128)}, f32[2,512]{1,0:T(2,128)}) custom-call(bf16[512,512]{1,0:T(8,128)(2,1)} %refs_0_.7, bf16[512]{0:T(512)(128)(2,1)} %refs_1_.5, f32[8,2,64]{2,1,0:T(2,128)} %refs_2_.3, f32[8,2,64]{2,1,0:T(2,128)} %copy-done.16), custom_call_target="tpu_custom_call" | custom-call | flops 1955000064 | bytes 6273000 | tf_op jit(solution)/shard_map/norm_one/pallas_call | solution.py:954
  5.2 3.0 %collective-permute-start.1 = (bf16[288,512]{1,0:T(8,128)(2,1)}, bf16[288,512]{1,0:T(8,128)(2,1)S(1)}, u32[]{:S(2)}, u32[]{:S(2)}) collective-permute-start(bf16[288,512]{1,0:T(8,128)(2,1)} %get-tuple-element.121.refs_0_), channel_id=1, source_target_pairs={{0,8},{1,5},{2,10},{3,7},{8,16},{9,1},{10,18},{11,3},{16,24},{17,9... | collective-permute-start | bytes 884744 | tf_op jit(solution)/shard_map/ppermute | solution.py:1032
  8.1 1.6 %collective-permute-start.2 = (bf16[288,512]{1,0:T(8,128)(2,1)}, bf16[288,512]{1,0:T(8,128)(2,1)S(1)}, u32[]{:S(2)}, u32[]{:S(2)}) collective-permute-start(bf16[288,512]{1,0:T(8,128)(2,1)} %get-tuple-element.122.refs_1_), channel_id=1, source_target_pairs={{0,8},{1,5},{2,10},{3,7},{8,16},{9,1},{10,18},{11,3},{16,24},{17,9... | collective-permute-start | bytes 884744 | tf_op jit(solution)/shard_map/ppermute | solution.py:1032
  9.7 1.5 %collective-permute-start.7 = (bf16[512,512]{1,0:T(8,128)(2,1)S(1)}, bf16[512,512]{1,0:T(8,128)(2,1)S(1)}, u32[]{:S(2)}, u32[]{:S(2)}) collective-permute-start(bf16[512,512]{1,0:T(8,128)(2,1)S(1)} %copy-done.3), channel_id=1, source_target_pairs={{0,2},{1,3},{2,0},{3,1},{4,6},{5,7},{6,4},{7,5},{8,10},{9,11},{10,... | collective-permute-start | bytes 1572872 | tf_op jit(solution)/shard_map/ppermute | solution.py:1041
  13.7 1.6 %collective-permute-start.3 = (bf16[288,512]{1,0:T(8,128)(2,1)S(1)}, bf16[288,512]{1,0:T(8,128)(2,1)S(1)}, u32[]{:S(2)}, u32[]{:S(2)}) collective-permute-start(bf16[288,512]{1,0:T(8,128)(2,1)S(1)} %collective-permute-done.1.refs_0_.refs_2_), channel_id=1, source_target_pairs={{0,8},{1,5},{2,10},{3,7},{8,16},{9,1},{10,18},{11,3},{16,24},{17,9... | collective-permute-start | bytes 884744 | tf_op jit(solution)/shard_map/ppermute | solution.py:1032
  16.1 2.1 %collective-permute-start.6 = (bf16[288,512]{1,0:T(8,128)(2,1)S(1)}, bf16[288,512]{1,0:T(8,128)(2,1)S(1)}, u32[]{:S(2)}, u32[]{:S(2)}) collective-permute-start(bf16[288,512]{1,0:T(8,128)(2,1)S(1)} %collective-permute-done.2.refs_1_.refs_3_), channel_id=1, source_target_pairs={{0,8},{1,5},{2,10},{3,7},{8,16},{9,1},{10,18},{11,3},{16,24},{17,9... | collective-permute-start | bytes 884744 | tf_op jit(solution)/shard_map/ppermute | solution.py:1032
  18.2 2.2 %collective-permute-done.3.refs_0_.refs_6_ = bf16[288,512]{1,0:T(8,128)(2,1)S(1)} collective-permute-done((bf16[288,512]{1,0:T(8,128)(2,1)S(1)}, bf16[288,512]{1,0:T(8,128)(2,1)S(1)}, u32[]{:S(2)}, u32[]{:S(2)}) %collective-permute-start.3) | collective-permute-done | bytes 294944 | tf_op jit(solution)/shard_map/ppermute | solution.py:1032
  20.5 1.6 %collective-permute-start.8 = (bf16[288,512]{1,0:T(8,128)(2,1)S(1)}, bf16[288,512]{1,0:T(8,128)(2,1)S(1)}, u32[]{:S(2)}, u32[]{:S(2)}) collective-permute-start(bf16[288,512]{1,0:T(8,128)(2,1)S(1)} %collective-permute-done.3.refs_0_.refs_6_), channel_id=1, source_target_pairs={{0,8},{1,5},{2,10},{3,7},{8,16},{9,1},{10,18},{11,3},{16,24},{17,9... | collective-permute-start | bytes 884744 | tf_op jit(solution)/shard_map/ppermute | solution.py:1032
  23.6 1.6 %collective-permute-start.11 = (bf16[288,512]{1,0:T(8,128)(2,1)S(1)}, bf16[288,512]{1,0:T(8,128)(2,1)S(1)}, u32[]{:S(2)}, u32[]{:S(2)}) collective-permute-start(bf16[288,512]{1,0:T(8,128)(2,1)S(1)} %collective-permute-done.6.refs_1_.refs_7_), channel_id=1, source_target_pairs={{0,8},{1,5},{2,10},{3,7},{8,16},{9,1},{10,18},{11,3},{16,24},{17,9... | collective-permute-start | bytes 884744 | tf_op jit(solution)/shard_map/ppermute | solution.py:1032
  25.2 1.3 collective-permute-start.12
  27.2 3.2 %collective-permute-done.11.refs_1_.refs_11_ = bf16[288,512]{1,0:T(8,128)(2,1)S(1)} collective-permute-done((bf16[288,512]{1,0:T(8,128)(2,1)S(1)}, bf16[288,512]{1,0:T(8,128)(2,1)S(1)}, u32[]{:S(2)}, u32[]{:S(2)}) %collective-permute-start.11) | collective-permute-done | bytes 294944 | tf_op jit(solution)/shard_map/ppermute | solution.py:1032
  30.4 3.4 %collective-permute-done.12.refs_3_.refs_12_ = bf16[320,512]{1,0:T(8,128)(2,1)S(1)} collective-permute-done((bf16[320,512]{1,0:T(8,128)(2,1)S(1)}, bf16[320,512]{1,0:T(8,128)(2,1)S(1)}, u32[]{:S(2)}, u32[]{:S(2)}) %collective-permute-start.12) | collective-permute-done | bytes 327712 | tf_op jit(solution)/shard_map/ppermute | solution.py:1041
  34.3 1.5 %collective-permute-start.16 = (bf16[320,512]{1,0:T(8,128)(2,1)S(1)}, bf16[320,512]{1,0:T(8,128)(2,1)S(1)}, u32[]{:S(2)}, u32[]{:S(2)}) collective-permute-start(bf16[320,512]{1,0:T(8,128)(2,1)S(1)} %get-tuple-element.147), channel_id=1, source_target_pairs={{0,2},{1,3},{2,0},{3,1},{4,6},{5,7},{6,4},{7,5},{8,10},{9,11},{10,... | collective-permute-start | bytes 983048 | tf_op jit(solution)/shard_map/ppermute | solution.py:1041
  38.3 4.5 %collective-permute-done.15.refs_7_.refs_14_ = bf16[288,512]{1,0:T(8,128)(2,1)S(1)} collective-permute-done((bf16[288,512]{1,0:T(8,128)(2,1)S(1)}, bf16[288,512]{1,0:T(8,128)(2,1)S(1)}, u32[]{:S(2)}, u32[]{:S(2)}) %collective-permute-start.15) | collective-permute-done | bytes 294944 | tf_op jit(solution)/shard_map/ppermute | solution.py:1032
  44.0 1.6 %collective-permute-done.17.refs_8_.refs_15_ = bf16[288,512]{1,0:T(8,128)(2,1)S(1)} collective-permute-done((bf16[288,512]{1,0:T(8,128)(2,1)S(1)}, bf16[288,512]{1,0:T(8,128)(2,1)S(1)}, u32[]{:S(2)}, u32[]{:S(2)}) %collective-permute-start.17) | collective-permute-done | bytes 294944 | tf_op jit(solution)/shard_map/ppermute | solution.py:1041
  45.6 3.7 %attend.1 = (bf16[4096,384]{1,0:T(8,128)(2,1)S(1)}, bf16[512,128]{1,0:T(8,128)(2,1)S(1)}, f32[64,512]{1,0:T(8,128)S(1)}, f32[16,2,64,64]{3,2,1,0:T(8,128)S(1)}, ...) custom-call(bf16[512,384]{1,0:T(8,128)(2,1)S(1)} %get-tuple-element.124.refs_0_, ...), custom_call_target="tpu_custom_call" | custom-call | flops 4830000128 | bytes 15498000 | tf_op jit(solution)/shard_map/attend/pallas_call | solution.py:954
  49.2 1.6 %collective-permute-start.18 = (bf16[512,128]{1,0:T(8,128)(2,1)S(1)}, bf16[512,128]{1,0:T(8,128)(2,1)S(1)}, u32[]{:S(2)}, u32[]{:S(2)}) collective-permute-start(bf16[512,128]{1,0:T(8,128)(2,1)S(1)} %get-tuple-element.151.refs_3_.refs_4_), channel_id=1, source_target_pairs={{0,2},{1,3},{2,0},{3,1},{4,6},{5,7},{6,4},{7,5},{8,10},{9,11},{10,... | collective-permute-start | bytes 393224 | tf_op jit(solution)/shard_map/ppermute | solution.py:1041
  51.4 2.8 %prepare.1 = (f32[1536,256]{1,0:T(8,128)S(1)}, f32[1536,256]{1,0:T(8,128)S(1)}) custom-call(bf16[4096,384]{1,0:T(8,128)(2,1)S(1)} %get-tuple-element.152.refs_0_.refs_1_.refs_2_, s32[2,64]{1,0:T(2,128)S(1)} %bitcast.5, f32[64,256]{1,0:T(8,128)S(1)} %get-tuple-element.153.refs_2_.refs_3_.refs_4_), custom_call_target="tpu_custom_call" | custom-call | flops 3335000064 | bytes 10701000 | tf_op jit(solution)/shard_map/prepare/pallas_call | solution.py:954
  54.8 1.3 %collective-permute-done.20.refs_6_ = bf16[512,128]{1,0:T(8,128)(2,1)S(1)} collective-permute-done((bf16[512,128]{1,0:T(8,128)(2,1)S(1)}, bf16[512,128]{1,0:T(8,128)(2,1)S(1)}, u32[]{:S(2)}, u32[]{:S(2)}) %collective-permute-start.20) | collective-permute-done | bytes 131104 | tf_op jit(solution)/shard_map/ppermute | solution.py:1041
  56.2 4.2 %feed.1 = (f32[512,512]{1,0:T(8,128)S(1)}, bf16[512,512]{1,0:T(8,128)(2,1)S(1)}, bf16[512,512]{1,0:T(8,128)(2,1)S(1)}, bf16[512,512]{1,0:T(8,128)(2,1)S(1)}, f32...) custom-call(bf16[512,512]{1,0:T(8,128)(2,1)S(1)} %copy-done.5, bf16[512,512]{1,0:T(8,128)(2,1)S(1)} %copy-done.4, ...), custom_call_target="tpu_custom_call" | custom-call | flops 4830000128 | bytes 15498000 | tf_op jit(solution)/shard_map/feed/pallas_call | solution.py:954
  60.6 2.5 %collective-permute-done.22.refs_2_ = f32[512,512]{1,0:T(8,128)S(1)} collective-permute-done((f32[512,512]{1,0:T(8,128)S(1)}, f32[512,512]{1,0:T(8,128)S(1)}, u32[]{:S(2)}, u32[]{:S(2)}) %collective-permute-start.22) | collective-permute-done | bytes 1048608 | tf_op jit(solution)/shard_map/ppermute | solution.py:1041
  67.1 1.8 %pull.5 = (f32[512,256]{1,0:T(8,128)S(1)}, bf16[512,384]{1,0:T(8,128)(2,1)S(1)}, f32[8,256]{1,0:T(8,128)S(1)}) custom-call(bf16[512,128]{1,0:T(8,128)(2,1)S(1)} %get-tuple-element.168.refs_6_.refs_0_, bf16[4096,384]{1,0:T(8,128)(2,1)S(1)} %get-tuple-element.152.refs_0_.refs_1_.refs_2_, s32[2,64]{1,0:T(2,128)S(1)} %bitcast.6, ...), custom_call_target="tpu_custom_call" | custom-call | flops 115000000 | bytes 369000 | tf_op jit(solution)/shard_map/pull/pallas_call | solution.py:954
  68.8 3.6 %collective-permute-done.27.refs_1_ = bf16[768,128]{1,0:T(8,128)(2,1)S(1)} collective-permute-done((bf16[768,128]{1,0:T(8,128)(2,1)S(1)}, bf16[768,128]{1,0:T(8,128)(2,1)S(1)}, u32[]{:S(2)}, u32[]{:S(2)}) %collective-permute-start.27) | collective-permute-done | bytes 196640 | tf_op jit(solution)/shard_map/ppermute | solution.py:1032
  72.5 1.3 collective-permute-start.28
  74.7 1.6 %collective-permute-start.30 = (bf16[512,512]{1,0:T(8,128)(2,1)S(1)}, bf16[512,512]{1,0:T(8,128)(2,1)S(1)}, u32[]{:S(2)}, u32[]{:S(2)}) collective-permute-start(bf16[512,512]{1,0:T(8,128)(2,1)S(1)} %get-tuple-element.184.refs_4_.refs_9_.refs_3_.refs_2_), channel_id=1, source_target_pairs={{0,2},{1,3},{2,0},{3,1},{4,6},{5,7},{6,4},{7,5},{8,10},{9,11},{10,... | collective-permute-start | bytes 1572872 | tf_op jit(solution)/shard_map/ppermute | solution.py:1041
  76.2 2.8 %pull.6 = (f32[1024,256]{1,0:T(8,128)S(1)}, bf16[1024,384]{1,0:T(8,128)(2,1)S(1)}, f32[16,256]{1,0:T(8,128)S(1)}) custom-call(bf16[832,128]{1,0:T(8,128)(2,1)S(1)} %collective-permute-done.23.refs_1_.refs_0_, bf16[768,128]{1,0:T(8,128)(2,1)S(1)} %collective-permute-done.27.refs_1_, bf16[4096,384]{1,0:T(8,128)(2,1)S(1)} %get-tuple-element.152.refs_0_.refs_1_.refs_2_, ...), custom_call_target="tpu_custom_call" | custom-call | flops 115000000 | bytes 369000 | tf_op jit(solution)/shard_map/pull/pallas_call | solution.py:954
  79.1 1.9 %collective-permute-done.28.refs_1_ = bf16[1088,128]{1,0:T(8,128)(2,1)S(1)} collective-permute-done((bf16[1088,128]{1,0:T(8,128)(2,1)S(1)}, bf16[1088,128]{1,0:T(8,128)(2,1)S(1)}, u32[]{:S(2)}, u32[]{:S(2)}) %collective-permute-start.28) | collective-permute-done | bytes 278560 | tf_op jit(solution)/shard_map/ppermute | solution.py:1032
  81.0 1.6 %collective-permute-start.29 = (bf16[1088,128]{1,0:T(8,128)(2,1)S(1)}, bf16[1088,128]{1,0:T(8,128)(2,1)S(1)}, u32[]{:S(2)}, u32[]{:S(2)}) collective-permute-start(bf16[1088,128]{1,0:T(8,128)(2,1)S(1)} %relay.10), channel_id=1, source_target_pairs={{0,4},{1,9},{2,6},{3,11},{8,0},{9,17},{10,2},{11,19},{16,8},{17,25... | collective-permute-start | bytes 835592 | tf_op jit(solution)/shard_map/ppermute | solution.py:1032
  83.2 2.8 %pull.7 = (f32[1024,256]{1,0:T(8,128)S(1)}, bf16[1024,384]{1,0:T(8,128)(2,1)S(1)}, f32[16,256]{1,0:T(8,128)S(1)}) custom-call(bf16[1088,128]{1,0:T(8,128)(2,1)S(1)} %collective-permute-done.24.refs_1_.refs_0_, bf16[1088,128]{1,0:T(8,128)(2,1)S(1)} %collective-permute-done.28.refs_1_, bf16[4096,384]{1,0:T(8,128)(2,1)S(1)} %get-tuple-element.152.refs_0_.refs_1_.refs_2_, ...), custom_call_target="tpu_custom_call" | custom-call | flops 115000000 | bytes 369000 | tf_op jit(solution)/shard_map/pull/pallas_call | solution.py:954
  86.0 1.5 %collective-permute-done.30.refs_3_ = bf16[512,512]{1,0:T(8,128)(2,1)S(1)} collective-permute-done((bf16[512,512]{1,0:T(8,128)(2,1)S(1)}, bf16[512,512]{1,0:T(8,128)(2,1)S(1)}, u32[]{:S(2)}, u32[]{:S(2)}) %collective-permute-start.30) | collective-permute-done | bytes 524320 | tf_op jit(solution)/shard_map/ppermute | solution.py:1041
  88.6 1.9 %collective-permute-start.31 = (bf16[832,128]{1,0:T(8,128)(2,1)S(1)}, bf16[832,128]{1,0:T(8,128)(2,1)S(1)}, u32[]{:S(2)}, u32[]{:S(2)}) collective-permute-start(bf16[832,128]{1,0:T(8,128)(2,1)S(1)} %relay.11), channel_id=1, source_target_pairs={{0,4},{1,9},{2,6},{3,11},{8,0},{9,17},{10,2},{11,19},{16,8},{17,25... | collective-permute-start | bytes 638984 | tf_op jit(solution)/shard_map/ppermute | solution.py:1032
  90.8 2.2 %pull.8 = (f32[1024,256]{1,0:T(8,128)S(1)}, bf16[1024,384]{1,0:T(8,128)(2,1)S(1)}, f32[16,256]{1,0:T(8,128)S(1)}) custom-call(bf16[1088,128]{1,0:T(8,128)(2,1)S(1)} %collective-permute-done.25.refs_1_.refs_0_, bf16[1088,128]{1,0:T(8,128)(2,1)S(1)} %collective-permute-done.29.refs_1_, bf16[4096,384]{1,0:T(8,128)(2,1)S(1)} %get-tuple-element.152.refs_0_.refs_1_.refs_2_, ...), custom_call_target="tpu_custom_call" | custom-call | flops 115000000 | bytes 369000 | tf_op jit(solution)/shard_map/pull/pallas_call | solution.py:954
  93.0 1.5 %collective-permute-done.31.refs_2_.refs_1_ = bf16[832,128]{1,0:T(8,128)(2,1)S(1)} collective-permute-done((bf16[832,128]{1,0:T(8,128)(2,1)S(1)}, bf16[832,128]{1,0:T(8,128)(2,1)S(1)}, u32[]{:S(2)}, u32[]{:S(2)}) %collective-permute-start.31) | collective-permute-done | bytes 213024 | tf_op jit(solution)/shard_map/ppermute | solution.py:1032
  94.5 2.3 %collective-permute-done.26.refs_1_.refs_0_ = bf16[832,128]{1,0:T(8,128)(2,1)S(1)} collective-permute-done((bf16[832,128]{1,0:T(8,128)(2,1)S(1)}, bf16[832,128]{1,0:T(8,128)(2,1)S(1)}, u32[]{:S(2)}, u32[]{:S(2)}) %collective-permute-start.26) | collective-permute-done | bytes 213024 | tf_op jit(solution)/shard_map/ppermute | solution.py:1032
  97.0 2.0 %collective-permute-start.33 = (bf16[144,512]{1,0:T(8,128)(2,1)S(1)}, bf16[144,512]{1,0:T(8,128)(2,1)S(1)}, u32[]{:S(2)}, u32[]{:S(2)}) collective-permute-start(bf16[144,512]{1,0:T(8,128)(2,1)S(1)} %total.1.refs_0_), channel_id=1, source_target_pairs={{0,4},{1,9},{2,6},{3,11},{8,0},{9,17},{10,2},{11,19},{16,8},{17,25... | collective-permute-start | bytes 442376 | tf_op jit(solution)/shard_map/ppermute | solution.py:1032
  99.0 1.5 %pull.9 = (f32[512,256]{1,0:T(8,128)S(1)}, bf16[512,384]{1,0:T(8,128)(2,1)S(1)}, f32[8,256]{1,0:T(8,128)S(1)}) custom-call(bf16[832,128]{1,0:T(8,128)(2,1)S(1)} %collective-permute-done.26.refs_1_.refs_0_, bf16[832,128]{1,0:T(8,128)(2,1)S(1)} %collective-permute-done.31.refs_2_.refs_1_, bf16[4096,384]{1,0:T(8,128)(2,1)S(1)} %get-tuple-element.152.refs_0_.refs_1_.refs_2_, ...), custom_call_target="tpu_custom_call" | custom-call | flops 115000000 | bytes 369000 | tf_op jit(solution)/shard_map/pull/pallas_call | solution.py:954
  100.5 4.5 %collect.1 = (bf16[4096,384]{1,0:T(8,128)(2,1)S(1)}, bf16[512,384]{1,0:T(8,128)(2,1)S(1)}, f32[8,128]{1,0:T(8,128)S(1)}, f32[512,128]{1,0:T(8,128)}) custom-call(f32[512,256]{1,0:T(8,128)S(1)} %get-tuple-element.179.refs_0_, f32[1024,256]{1,0:T(8,128)S(1)} %get-tuple-element.181.refs_1_, f32[1024,256]{1,0:T(8,128)S(1)} %get-tuple-element.183.refs_2_, ...), custom_call_target="tpu_custom_call" | custom-call | flops 5175000064 | bytes 16605000 | tf_op jit(solution)/shard_map/collect/pallas_call | solution.py:954
  105.0 1.8 %collective-permute-start.39 = (bf16[512,384]{1,0:T(8,128)(2,1)S(1)}, bf16[512,384]{1,0:T(8,128)(2,1)S(1)}, u32[]{:S(2)}, u32[]{:S(2)}) collective-permute-start(bf16[512,384]{1,0:T(8,128)(2,1)S(1)} %get-tuple-element.205.refs_1_.refs_0_), channel_id=1, source_target_pairs={{0,2},{1,3},{2,0},{3,1},{4,6},{5,7},{6,4},{7,5},{8,10},{9,11},{10,... | collective-permute-start | bytes 1179656 | tf_op jit(solution)/shard_map/ppermute | solution.py:1041
  106.8 2.0 %collective-permute-start.36 = (bf16[144,512]{1,0:T(8,128)(2,1)S(1)}, bf16[144,512]{1,0:T(8,128)(2,1)S(1)}, u32[]{:S(2)}, u32[]{:S(2)}) collective-permute-start(bf16[144,512]{1,0:T(8,128)(2,1)S(1)} %collective-permute-done.33.refs_2_), channel_id=1, source_target_pairs={{0,4},{1,9},{2,6},{3,11},{8,0},{9,17},{10,2},{11,19},{16,8},{17,25... | collective-permute-start | bytes 442376 | tf_op jit(solution)/shard_map/ppermute | solution.py:1032
  109.4 1.5 %collective-permute-start.37 = (f32[16,512]{1,0:T(8,128)S(1)}, f32[16,512]{1,0:T(8,128)S(1)}, u32[]{:S(2)}, u32[]{:S(2)}) collective-permute-start(f32[16,512]{1,0:T(8,128)S(1)} %gain_part.1.refs_0_), channel_id=1, source_target_pairs={{0,4},{4,0},{8,12},{12,8},{16,20},{20,16},{24,28},{28,24},{1,5},{5... | collective-permute-start | bytes 98312 | tf_op jit(solution)/shard_map/ppermute | solution.py:1044
  111.0 2.4 %collective-permute-done.37.refs_1_ = f32[16,512]{1,0:T(8,128)S(1)} collective-permute-done((f32[16,512]{1,0:T(8,128)S(1)}, f32[16,512]{1,0:T(8,128)S(1)}, u32[]{:S(2)}, u32[]{:S(2)}) %collective-permute-start.37) | collective-permute-done | bytes 32800 | tf_op jit(solution)/shard_map/ppermute | solution.py:1044
  116.7 1.5 %collective-permute-start.40 = (bf16[144,512]{1,0:T(8,128)(2,1)S(1)}, bf16[144,512]{1,0:T(8,128)(2,1)S(1)}, u32[]{:S(2)}, u32[]{:S(2)}) collective-permute-start(bf16[144,512]{1,0:T(8,128)(2,1)S(1)} %collective-permute-done.35.refs_3_), channel_id=1, source_target_pairs={{0,8},{1,5},{2,10},{3,7},{8,16},{9,1},{10,18},{11,3},{16,24},{17,9... | collective-permute-start | bytes 442376 | tf_op jit(solution)/shard_map/ppermute | solution.py:1032
  118.7 1.7 %collective-permute-done.42.refs_1_ = f32[16,512]{1,0:T(8,128)S(1)} collective-permute-done((f32[16,512]{1,0:T(8,128)S(1)}, f32[16,512]{1,0:T(8,128)S(1)}, u32[]{:S(2)}, u32[]{:S(2)}) %collective-permute-start.42) | collective-permute-done | bytes 32800 | tf_op jit(solution)/shard_map/ppermute | solution.py:1044
  120.4 1.4 %collective-permute-start.43 = (f32[16,512]{1,0:T(8,128)S(1)}, f32[16,512]{1,0:T(8,128)S(1)}, u32[]{:S(2)}, u32[]{:S(2)}) collective-permute-start(f32[16,512]{1,0:T(8,128)S(1)} %add_gains.5.refs_0_), channel_id=1, source_target_pairs={{0,16},{4,20},{8,24},{12,28},{16,0},{20,4},{24,8},{28,12},{1,17},{... | collective-permute-start | bytes 98312 | tf_op jit(solution)/shard_map/ppermute | solution.py:1044
  121.8 3.6 %weights.1 = f32[3,512,128]{2,1,0:T(8,128)} custom-call(bf16[288,512]{1,0:T(8,128)(2,1)S(1)} %copy-done.8, bf16[288,512]{1,0:T(8,128)(2,1)S(1)} %copy-done.10, bf16[288,512]{1,0:T(8,128)(2,1)S(1)} %collective-permute-done.1.refs_0_.refs_2_, bf16[288,512]{1,0:T(8,128)(2,1)S(1)} %collective-permute-done.2.refs_1_.refs_3_, ...), custom_call_target="tpu_custom_call" | custom-call | flops 4140000000 | bytes 13284000 | tf_op jit(solution)/shard_map/weights/pallas_call | solution.py:954
  127.3 1.9 %collective-permute-start.46 = (bf16[64,512]{1,0:T(8,128)(2,1)S(1)}, bf16[64,512]{1,0:T(8,128)(2,1)S(1)}, u32[]{:S(2)}, u32[]{:S(2)}) collective-permute-start(bf16[64,512]{1,0:T(8,128)(2,1)S(1)} %get-tuple-element.223), channel_id=1, source_target_pairs={{0,4},{1,9},{2,6},{3,11},{8,0},{9,17},{10,2},{11,19},{16,8},{17,25... | collective-permute-start | bytes 196616 | tf_op jit(solution)/shard_map/ppermute | solution.py:1032
  129.4 1.7 %norm_one_back.1 = f32[512,512]{1,0:T(8,128)} custom-call(bf16[512,512]{1,0:T(8,128)(2,1)S(1)} %copy-done.5, bf16[512]{0:T(512)(128)(2,1)S(1)} %copy-done.13, f32[512,512]{1,0:T(8,128)S(1)} %input_back.1.refs_2_, f32[512,512]{1,0:T(8,128)S(1)} %collective-permute-done.44.refs_3_, f32[512,512]{1,0:T(8,128)S(1)} %get-tuple-element.219.refs_4_), custom_call_target="tpu_custom_call" | custom-call | flops 1955000064 | bytes 6273000 | tf_op jit(solution)/shard_map/norm_one_back/pallas_call | solution.py:954
  131.5 1.6 %lay.1 = (f32[512,512]{1,0:T(8,128)}, f32[512,512]{1,0:T(8,128)}, f32[128,512]{1,0:T(8,128)}, f32[512]{0:T(512)}, f32[512]{0:T(512)}) custom-call(bf16[144,512]{1,0:T(8,128)(2,1)S(1)} %total.1.refs_0_, bf16[144,512]{1,0:T(8,128)(2,1)S(1)} %collective-permute-done.32.refs_1_, bf16[144,512]{1,0:T(8,128)(2,1)S(1)} %collective-permute-done.33.refs_2_, ...), custom_call_target="tpu_custom_call" | custom-call | flops 1840000000 | bytes 5904000 | tf_op jit(solution)/shard_map/lay/pallas_call | solution.py:954
  (119 shorter events, 27.5 us)
Async XLA Ops:
  0.7 1.6 %collective-permute-start = (f32[8,2,64]{2,1,0:T(2,128)}, f32[8,2,64]{2,1,0:T(2,128)S(1)}, u32[]{:S(2)}, u32[]{:S(2)}) collective-permute-start(f32[8,2,64]{2,1,0:T(2,128)} %refs_2_.3), channel_id=1, source_target_pairs={{0,1},{1,0},{2,3},{3,2},{4,5},{5,4},{6,7},{7,6},{8,9},{9,8},{10,11... | collective-permute-start | bytes 12296 | tf_op jit(solution)/shard_map/ppermute | solution.py:1041
  5.2 8.5 %collective-permute-start.1 = (bf16[288,512]{1,0:T(8,128)(2,1)}, bf16[288,512]{1,0:T(8,128)(2,1)S(1)}, u32[]{:S(2)}, u32[]{:S(2)}) collective-permute-start(bf16[288,512]{1,0:T(8,128)(2,1)} %get-tuple-element.121.refs_0_), channel_id=1, source_target_pairs={{0,8},{1,5},{2,10},{3,7},{8,16},{9,1},{10,18},{11,3},{16,24},{17,9... | collective-permute-start | bytes 884744 | tf_op jit(solution)/shard_map/ppermute | solution.py:1032
  8.1 8.0 %collective-permute-start.2 = (bf16[288,512]{1,0:T(8,128)(2,1)}, bf16[288,512]{1,0:T(8,128)(2,1)S(1)}, u32[]{:S(2)}, u32[]{:S(2)}) collective-permute-start(bf16[288,512]{1,0:T(8,128)(2,1)} %get-tuple-element.122.refs_1_), channel_id=1, source_target_pairs={{0,8},{1,5},{2,10},{3,7},{8,16},{9,1},{10,18},{11,3},{16,24},{17,9... | collective-permute-start | bytes 884744 | tf_op jit(solution)/shard_map/ppermute | solution.py:1032
  9.7 13.3 %collective-permute-start.7 = (bf16[512,512]{1,0:T(8,128)(2,1)S(1)}, bf16[512,512]{1,0:T(8,128)(2,1)S(1)}, u32[]{:S(2)}, u32[]{:S(2)}) collective-permute-start(bf16[512,512]{1,0:T(8,128)(2,1)S(1)} %copy-done.3), channel_id=1, source_target_pairs={{0,2},{1,3},{2,0},{3,1},{4,6},{5,7},{6,4},{7,5},{8,10},{9,11},{10,... | collective-permute-start | bytes 1572872 | tf_op jit(solution)/shard_map/ppermute | solution.py:1041
  13.7 6.8 %collective-permute-start.3 = (bf16[288,512]{1,0:T(8,128)(2,1)S(1)}, bf16[288,512]{1,0:T(8,128)(2,1)S(1)}, u32[]{:S(2)}, u32[]{:S(2)}) collective-permute-start(bf16[288,512]{1,0:T(8,128)(2,1)S(1)} %collective-permute-done.1.refs_0_.refs_2_), channel_id=1, source_target_pairs={{0,8},{1,5},{2,10},{3,7},{8,16},{9,1},{10,18},{11,3},{16,24},{17,9... | collective-permute-start | bytes 884744 | tf_op jit(solution)/shard_map/ppermute | solution.py:1032
  16.1 7.5 %collective-permute-start.6 = (bf16[288,512]{1,0:T(8,128)(2,1)S(1)}, bf16[288,512]{1,0:T(8,128)(2,1)S(1)}, u32[]{:S(2)}, u32[]{:S(2)}) collective-permute-start(bf16[288,512]{1,0:T(8,128)(2,1)S(1)} %collective-permute-done.2.refs_1_.refs_3_), channel_id=1, source_target_pairs={{0,8},{1,5},{2,10},{3,7},{8,16},{9,1},{10,18},{11,3},{16,24},{17,9... | collective-permute-start | bytes 884744 | tf_op jit(solution)/shard_map/ppermute | solution.py:1032
  20.5 6.7 %collective-permute-start.8 = (bf16[288,512]{1,0:T(8,128)(2,1)S(1)}, bf16[288,512]{1,0:T(8,128)(2,1)S(1)}, u32[]{:S(2)}, u32[]{:S(2)}) collective-permute-start(bf16[288,512]{1,0:T(8,128)(2,1)S(1)} %collective-permute-done.3.refs_0_.refs_6_), channel_id=1, source_target_pairs={{0,8},{1,5},{2,10},{3,7},{8,16},{9,1},{10,18},{11,3},{16,24},{17,9... | collective-permute-start | bytes 884744 | tf_op jit(solution)/shard_map/ppermute | solution.py:1032
  23.6 6.7 %collective-permute-start.11 = (bf16[288,512]{1,0:T(8,128)(2,1)S(1)}, bf16[288,512]{1,0:T(8,128)(2,1)S(1)}, u32[]{:S(2)}, u32[]{:S(2)}) collective-permute-start(bf16[288,512]{1,0:T(8,128)(2,1)S(1)} %collective-permute-done.6.refs_1_.refs_7_), channel_id=1, source_target_pairs={{0,8},{1,5},{2,10},{3,7},{8,16},{9,1},{10,18},{11,3},{16,24},{17,9... | collective-permute-start | bytes 884744 | tf_op jit(solution)/shard_map/ppermute | solution.py:1032
  25.2 8.6 %collective-permute-start.12 = (bf16[320,512]{1,0:T(8,128)(2,1)S(1)}, bf16[320,512]{1,0:T(8,128)(2,1)S(1)}, u32[]{:S(2)}, u32[]{:S(2)}) collective-permute-start(bf16[320,512]{1,0:T(8,128)(2,1)S(1)} %get-tuple-element.136), channel_id=1, source_target_pairs={{0,2},{1,3},{2,0},{3,1},{4,6},{5,7},{6,4},{7,5},{8,10},{9,11},{10,... | collective-permute-start | bytes 983048 | tf_op jit(solution)/shard_map/ppermute | solution.py:1041
  26.5 7.3 %collective-permute-start.4 = (bf16[288,512]{1,0:T(8,128)(2,1)S(1)}, bf16[288,512]{1,0:T(8,128)(2,1)S(1)}, u32[]{:S(2)}, u32[]{:S(2)}) collective-permute-start(bf16[288,512]{1,0:T(8,128)(2,1)S(1)} %collective-permute-done.1.refs_0_.refs_2_), channel_id=1, source_target_pairs={{0,1},{1,0},{2,3},{3,2},{4,5},{5,4},{6,7},{7,6},{8,9},{9,8},{10,11... | collective-permute-start | bytes 884744 | tf_op jit(solution)/shard_map/ppermute | solution.py:1041
  26.5 7.8 %collective-permute-start.5 = (bf16[288,512]{1,0:T(8,128)(2,1)S(1)}, bf16[288,512]{1,0:T(8,128)(2,1)S(1)}, u32[]{:S(2)}, u32[]{:S(2)}) collective-permute-start(bf16[288,512]{1,0:T(8,128)(2,1)S(1)} %collective-permute-done.2.refs_1_.refs_3_), channel_id=1, source_target_pairs={{0,1},{1,0},{2,3},{3,2},{4,5},{5,4},{6,7},{7,6},{8,9},{9,8},{10,11... | collective-permute-start | bytes 884744 | tf_op jit(solution)/shard_map/ppermute | solution.py:1041
  27.2 8.7 %collective-permute-start.9 = (bf16[288,512]{1,0:T(8,128)(2,1)S(1)}, bf16[288,512]{1,0:T(8,128)(2,1)S(1)}, u32[]{:S(2)}, u32[]{:S(2)}) collective-permute-start(bf16[288,512]{1,0:T(8,128)(2,1)S(1)} %collective-permute-done.3.refs_0_.refs_6_), channel_id=1, source_target_pairs={{0,1},{1,0},{2,3},{3,2},{4,5},{5,4},{6,7},{7,6},{8,9},{9,8},{10,11... | collective-permute-start | bytes 884744 | tf_op jit(solution)/shard_map/ppermute | solution.py:1041
  30.4 6.5 %collective-permute-start.10 = (bf16[288,512]{1,0:T(8,128)(2,1)S(1)}, bf16[288,512]{1,0:T(8,128)(2,1)S(1)}, u32[]{:S(2)}, u32[]{:S(2)}) collective-permute-start(bf16[288,512]{1,0:T(8,128)(2,1)S(1)} %collective-permute-done.6.refs_1_.refs_7_), channel_id=1, source_target_pairs={{0,1},{1,0},{2,3},{3,2},{4,5},{5,4},{6,7},{7,6},{8,9},{9,8},{10,11... | collective-permute-start | bytes 884744 | tf_op jit(solution)/shard_map/ppermute | solution.py:1041
  33.8 3.8 %collective-permute-start.13 = (bf16[288,512]{1,0:T(8,128)(2,1)S(1)}, bf16[288,512]{1,0:T(8,128)(2,1)S(1)}, u32[]{:S(2)}, u32[]{:S(2)}) collective-permute-start(bf16[288,512]{1,0:T(8,128)(2,1)S(1)} %collective-permute-done.8.refs_0_.refs_10_), channel_id=1, source_target_pairs={{0,1},{1,0},{2,3},{3,2},{4,5},{5,4},{6,7},{7,6},{8,9},{9,8},{10,11... | collective-permute-start | bytes 884744 | tf_op jit(solution)/shard_map/ppermute | solution.py:1041
  33.8 3.8 %collective-permute-start.14 = (bf16[288,512]{1,0:T(8,128)(2,1)S(1)}, bf16[288,512]{1,0:T(8,128)(2,1)S(1)}, u32[]{:S(2)}, u32[]{:S(2)}) collective-permute-start(bf16[288,512]{1,0:T(8,128)(2,1)S(1)} %collective-permute-done.11.refs_1_.refs_11_), channel_id=1, source_target_pairs={{0,1},{1,0},{2,3},{3,2},{4,5},{5,4},{6,7},{7,6},{8,9},{9,8},{10,11... | collective-permute-start | bytes 884744 | tf_op jit(solution)/shard_map/ppermute | solution.py:1041
  34.3 9.7 %collective-permute-start.16 = (bf16[320,512]{1,0:T(8,128)(2,1)S(1)}, bf16[320,512]{1,0:T(8,128)(2,1)S(1)}, u32[]{:S(2)}, u32[]{:S(2)}) collective-permute-start(bf16[320,512]{1,0:T(8,128)(2,1)S(1)} %get-tuple-element.147), channel_id=1, source_target_pairs={{0,2},{1,3},{2,0},{3,1},{4,6},{5,7},{6,4},{7,5},{8,10},{9,11},{10,... | collective-permute-start | bytes 983048 | tf_op jit(solution)/shard_map/ppermute | solution.py:1041
  35.9 7.0 %collective-permute-start.15 = (bf16[288,512]{1,0:T(8,128)(2,1)S(1)}, bf16[288,512]{1,0:T(8,128)(2,1)S(1)}, u32[]{:S(2)}, u32[]{:S(2)}) collective-permute-start(bf16[288,512]{1,0:T(8,128)(2,1)S(1)} %get-tuple-element.145), channel_id=1, source_target_pairs={{0,8},{1,5},{2,10},{3,7},{8,16},{9,1},{10,18},{11,3},{16,24},{17,9... | collective-permute-start | bytes 884744 | tf_op jit(solution)/shard_map/ppermute | solution.py:1032
  44.0 1.6 %collective-permute-start.17 = (bf16[288,512]{1,0:T(8,128)(2,1)S(1)}, bf16[288,512]{1,0:T(8,128)(2,1)S(1)}, u32[]{:S(2)}, u32[]{:S(2)}) collective-permute-start(bf16[288,512]{1,0:T(8,128)(2,1)S(1)} %collective-permute-done.15.refs_7_.refs_14_), channel_id=1, source_target_pairs={{0,1},{1,0},{2,3},{3,2},{4,5},{5,4},{6,7},{7,6},{8,9},{9,8},{10,11... | collective-permute-start | bytes 884744 | tf_op jit(solution)/shard_map/ppermute | solution.py:1041
  49.2 5.6 %collective-permute-start.18 = (bf16[512,128]{1,0:T(8,128)(2,1)S(1)}, bf16[512,128]{1,0:T(8,128)(2,1)S(1)}, u32[]{:S(2)}, u32[]{:S(2)}) collective-permute-start(bf16[512,128]{1,0:T(8,128)(2,1)S(1)} %get-tuple-element.151.refs_3_.refs_4_), channel_id=1, source_target_pairs={{0,2},{1,3},{2,0},{3,1},{4,6},{5,7},{6,4},{7,5},{8,10},{9,11},{10,... | collective-permute-start | bytes 393224 | tf_op jit(solution)/shard_map/ppermute | solution.py:1041
  50.8 4.0 %collective-permute-start.19 = (bf16[512,128]{1,0:T(8,128)(2,1)S(1)}, bf16[512,128]{1,0:T(8,128)(2,1)S(1)}, u32[]{:S(2)}, u32[]{:S(2)}) collective-permute-start(bf16[512,128]{1,0:T(8,128)(2,1)S(1)} %get-tuple-element.151.refs_3_.refs_4_), channel_id=1, source_target_pairs={{0,1},{1,0},{2,3},{3,2},{4,5},{5,4},{6,7},{7,6},{8,9},{9,8},{10,11... | collective-permute-start | bytes 393224 | tf_op jit(solution)/shard_map/ppermute | solution.py:1041
  50.8 5.4 %collective-permute-start.21 = (bf16[256,512]{1,0:T(8,128)(2,1)S(1)}, bf16[256,512]{1,0:T(8,128)(2,1)S(1)}, u32[]{:S(2)}, u32[]{:S(2)}) collective-permute-start(bf16[256,512]{1,0:T(8,128)(2,1)S(1)} %get-tuple-element.158.refs_7_), channel_id=1, source_target_pairs={{0,1},{1,0},{2,3},{3,2},{4,5},{5,4},{6,7},{7,6},{8,9},{9,8},{10,11... | collective-permute-start | bytes 786440 | tf_op jit(solution)/shard_map/ppermute | solution.py:1041
  60.4 2.7 %collective-permute-start.22 = (f32[512,512]{1,0:T(8,128)S(1)}, f32[512,512]{1,0:T(8,128)S(1)}, u32[]{:S(2)}, u32[]{:S(2)}) collective-permute-start(f32[512,512]{1,0:T(8,128)S(1)} %get-tuple-element.166.refs_1_), channel_id=1, source_target_pairs={{0,1},{1,0},{2,3},{3,2},{4,5},{5,4},{6,7},{7,6},{8,9},{9,8},{10,11... | collective-permute-start | bytes 3145736 | tf_op jit(solution)/shard_map/ppermute | solution.py:1041
  65.0 7.5 %collective-permute-start.27 = (bf16[768,128]{1,0:T(8,128)(2,1)S(1)}, bf16[768,128]{1,0:T(8,128)(2,1)S(1)}, u32[]{:S(2)}, u32[]{:S(2)}) collective-permute-start(bf16[768,128]{1,0:T(8,128)(2,1)S(1)} %get-tuple-element.177), channel_id=1, source_target_pairs={{0,4},{1,9},{2,6},{3,11},{8,0},{9,17},{10,2},{11,19},{16,8},{17,25... | collective-permute-start | bytes 589832 | tf_op jit(solution)/shard_map/ppermute | solution.py:1032
  65.9 7.8 %collective-permute-start.23 = (bf16[832,128]{1,0:T(8,128)(2,1)S(1)}, bf16[832,128]{1,0:T(8,128)(2,1)S(1)}, u32[]{:S(2)}, u32[]{:S(2)}) collective-permute-start(bf16[832,128]{1,0:T(8,128)(2,1)S(1)} %get-tuple-element.173), channel_id=1, source_target_pairs={{0,8},{1,5},{2,10},{3,7},{8,16},{9,1},{10,18},{11,3},{16,24},{17,9... | collective-permute-start | bytes 638984 | tf_op jit(solution)/shard_map/ppermute | solution.py:1032
  72.5 8.4 %collective-permute-start.28 = (bf16[1088,128]{1,0:T(8,128)(2,1)S(1)}, bf16[1088,128]{1,0:T(8,128)(2,1)S(1)}, u32[]{:S(2)}, u32[]{:S(2)}) collective-permute-start(bf16[1088,128]{1,0:T(8,128)(2,1)S(1)} %relay.9), channel_id=1, source_target_pairs={{0,4},{1,9},{2,6},{3,11},{8,0},{9,17},{10,2},{11,19},{16,8},{17,25... | collective-permute-start | bytes 835592 | tf_op jit(solution)/shard_map/ppermute | solution.py:1032
  73.8 8.7 %collective-permute-start.24 = (bf16[1088,128]{1,0:T(8,128)(2,1)S(1)}, bf16[1088,128]{1,0:T(8,128)(2,1)S(1)}, u32[]{:S(2)}, u32[]{:S(2)}) collective-permute-start(bf16[1088,128]{1,0:T(8,128)(2,1)S(1)} %relay.6), channel_id=1, source_target_pairs={{0,8},{1,5},{2,10},{3,7},{8,16},{9,1},{10,18},{11,3},{16,24},{17,9... | collective-permute-start | bytes 835592 | tf_op jit(solution)/shard_map/ppermute | solution.py:1032
  74.7 12.8 %collective-permute-start.30 = (bf16[512,512]{1,0:T(8,128)(2,1)S(1)}, bf16[512,512]{1,0:T(8,128)(2,1)S(1)}, u32[]{:S(2)}, u32[]{:S(2)}) collective-permute-start(bf16[512,512]{1,0:T(8,128)(2,1)S(1)} %get-tuple-element.184.refs_4_.refs_9_.refs_3_.refs_2_), channel_id=1, source_target_pairs={{0,2},{1,3},{2,0},{3,1},{4,6},{5,7},{6,4},{7,5},{8,10},{9,11},{10,... | collective-permute-start | bytes 1572872 | tf_op jit(solution)/shard_map/ppermute | solution.py:1041
  81.0 7.6 %collective-permute-start.29 = (bf16[1088,128]{1,0:T(8,128)(2,1)S(1)}, bf16[1088,128]{1,0:T(8,128)(2,1)S(1)}, u32[]{:S(2)}, u32[]{:S(2)}) collective-permute-start(bf16[1088,128]{1,0:T(8,128)(2,1)S(1)} %relay.10), channel_id=1, source_target_pairs={{0,4},{1,9},{2,6},{3,11},{8,0},{9,17},{10,2},{11,19},{16,8},{17,25... | collective-permute-start | bytes 835592 | tf_op jit(solution)/shard_map/ppermute | solution.py:1032
  82.6 7.9 %collective-permute-start.25 = (bf16[1088,128]{1,0:T(8,128)(2,1)S(1)}, bf16[1088,128]{1,0:T(8,128)(2,1)S(1)}, u32[]{:S(2)}, u32[]{:S(2)}) collective-permute-start(bf16[1088,128]{1,0:T(8,128)(2,1)S(1)} %relay.7), channel_id=1, source_target_pairs={{0,8},{1,5},{2,10},{3,7},{8,16},{9,1},{10,18},{11,3},{16,24},{17,9... | collective-permute-start | bytes 835592 | tf_op jit(solution)/shard_map/ppermute | solution.py:1032
  88.6 5.9 %collective-permute-start.31 = (bf16[832,128]{1,0:T(8,128)(2,1)S(1)}, bf16[832,128]{1,0:T(8,128)(2,1)S(1)}, u32[]{:S(2)}, u32[]{:S(2)}) collective-permute-start(bf16[832,128]{1,0:T(8,128)(2,1)S(1)} %relay.11), channel_id=1, source_target_pairs={{0,4},{1,9},{2,6},{3,11},{8,0},{9,17},{10,2},{11,19},{16,8},{17,25... | collective-permute-start | bytes 638984 | tf_op jit(solution)/shard_map/ppermute | solution.py:1032
  90.5 6.3 %collective-permute-start.26 = (bf16[832,128]{1,0:T(8,128)(2,1)S(1)}, bf16[832,128]{1,0:T(8,128)(2,1)S(1)}, u32[]{:S(2)}, u32[]{:S(2)}) collective-permute-start(bf16[832,128]{1,0:T(8,128)(2,1)S(1)} %relay.8), channel_id=1, source_target_pairs={{0,8},{1,5},{2,10},{3,7},{8,16},{9,1},{10,18},{11,3},{16,24},{17,9... | collective-permute-start | bytes 638984 | tf_op jit(solution)/shard_map/ppermute | solution.py:1032
  96.9 8.1 %collective-permute-start.32 = (bf16[144,512]{1,0:T(8,128)(2,1)S(1)}, bf16[144,512]{1,0:T(8,128)(2,1)S(1)}, u32[]{:S(2)}, u32[]{:S(2)}) collective-permute-start(bf16[144,512]{1,0:T(8,128)(2,1)S(1)} %total.1.refs_0_), channel_id=1, source_target_pairs={{0,8},{1,5},{2,10},{3,7},{8,16},{9,1},{10,18},{11,3},{16,24},{17,9... | collective-permute-start | bytes 442376 | tf_op jit(solution)/shard_map/ppermute | solution.py:1032
  97.0 8.0 %collective-permute-start.33 = (bf16[144,512]{1,0:T(8,128)(2,1)S(1)}, bf16[144,512]{1,0:T(8,128)(2,1)S(1)}, u32[]{:S(2)}, u32[]{:S(2)}) collective-permute-start(bf16[144,512]{1,0:T(8,128)(2,1)S(1)} %total.1.refs_0_), channel_id=1, source_target_pairs={{0,4},{1,9},{2,6},{3,11},{8,0},{9,17},{10,2},{11,19},{16,8},{17,25... | collective-permute-start | bytes 442376 | tf_op jit(solution)/shard_map/ppermute | solution.py:1032
  105.0 9.6 %collective-permute-start.39 = (bf16[512,384]{1,0:T(8,128)(2,1)S(1)}, bf16[512,384]{1,0:T(8,128)(2,1)S(1)}, u32[]{:S(2)}, u32[]{:S(2)}) collective-permute-start(bf16[512,384]{1,0:T(8,128)(2,1)S(1)} %get-tuple-element.205.refs_1_.refs_0_), channel_id=1, source_target_pairs={{0,2},{1,3},{2,0},{3,1},{4,6},{5,7},{6,4},{7,5},{8,10},{9,11},{10,... | collective-permute-start | bytes 1179656 | tf_op jit(solution)/shard_map/ppermute | solution.py:1041
  106.8 7.8 %collective-permute-start.35 = (bf16[144,512]{1,0:T(8,128)(2,1)S(1)}, bf16[144,512]{1,0:T(8,128)(2,1)S(1)}, u32[]{:S(2)}, u32[]{:S(2)}) collective-permute-start(bf16[144,512]{1,0:T(8,128)(2,1)S(1)} %collective-permute-done.32.refs_1_), channel_id=1, source_target_pairs={{0,8},{1,5},{2,10},{3,7},{8,16},{9,1},{10,18},{11,3},{16,24},{17,9... | collective-permute-start | bytes 442376 | tf_op jit(solution)/shard_map/ppermute | solution.py:1032
  106.8 7.7 %collective-permute-start.36 = (bf16[144,512]{1,0:T(8,128)(2,1)S(1)}, bf16[144,512]{1,0:T(8,128)(2,1)S(1)}, u32[]{:S(2)}, u32[]{:S(2)}) collective-permute-start(bf16[144,512]{1,0:T(8,128)(2,1)S(1)} %collective-permute-done.33.refs_2_), channel_id=1, source_target_pairs={{0,4},{1,9},{2,6},{3,11},{8,0},{9,17},{10,2},{11,19},{16,8},{17,25... | collective-permute-start | bytes 442376 | tf_op jit(solution)/shard_map/ppermute | solution.py:1032
  109.4 4.0 %collective-permute-start.37 = (f32[16,512]{1,0:T(8,128)S(1)}, f32[16,512]{1,0:T(8,128)S(1)}, u32[]{:S(2)}, u32[]{:S(2)}) collective-permute-start(f32[16,512]{1,0:T(8,128)S(1)} %gain_part.1.refs_0_), channel_id=1, source_target_pairs={{0,4},{4,0},{8,12},{12,8},{16,20},{20,16},{24,28},{28,24},{1,5},{5... | collective-permute-start | bytes 98312 | tf_op jit(solution)/shard_map/ppermute | solution.py:1044
  110.9 3.6 %collective-permute-start.38 = (f32[8,128]{1,0:T(8,128)S(1)}, f32[8,128]{1,0:T(8,128)S(1)}, u32[]{:S(2)}, u32[]{:S(2)}) collective-permute-start(f32[8,128]{1,0:T(8,128)S(1)} %get-tuple-element.209.refs_2_.refs_4_), channel_id=1, source_target_pairs={{0,2},{1,3},{2,0},{3,1},{4,6},{5,7},{6,4},{7,5},{8,10},{9,11},{10,... | collective-permute-start | bytes 12296 | tf_op jit(solution)/shard_map/ppermute | solution.py:1041
  115.5 9.8 %collective-permute-start.44 = (f32[512,512]{1,0:T(8,128)S(1)}, f32[512,512]{1,0:T(8,128)S(1)}, u32[]{:S(2)}, u32[]{:S(2)}) collective-permute-start(f32[512,512]{1,0:T(8,128)S(1)} %input_back.1.refs_2_), channel_id=1, source_target_pairs={{0,1},{1,0},{2,3},{3,2},{4,5},{5,4},{6,7},{7,6},{8,9},{9,8},{10,11... | collective-permute-start | bytes 3145736 | tf_op jit(solution)/shard_map/ppermute | solution.py:1041
  115.6 10.3 %collective-permute-start.34 = (f32[512,512]{1,0:T(8,128)S(1)}, f32[512,512]{1,0:T(8,128)S(1)}, u32[]{:S(2)}, u32[]{:S(2)}) collective-permute-start(f32[512,512]{1,0:T(8,128)S(1)} %get-tuple-element.206.refs_0_), channel_id=1, source_target_pairs={{0,1},{1,0},{2,3},{3,2},{4,5},{5,4},{6,7},{7,6},{8,9},{9,8},{10,11... | collective-permute-start | bytes 3145736 | tf_op jit(solution)/shard_map/ppermute | solution.py:1041
  116.1 4.3 %collective-permute-start.42 = (f32[16,512]{1,0:T(8,128)S(1)}, f32[16,512]{1,0:T(8,128)S(1)}, u32[]{:S(2)}, u32[]{:S(2)}) collective-permute-start(f32[16,512]{1,0:T(8,128)S(1)} %add_gains.4.refs_0_), channel_id=1, source_target_pairs={{0,8},{4,12},{8,0},{12,4},{16,24},{20,28},{24,16},{28,20},{1,9},{5... | collective-permute-start | bytes 98312 | tf_op jit(solution)/shard_map/ppermute | solution.py:1044
  116.7 8.7 %collective-permute-start.40 = (bf16[144,512]{1,0:T(8,128)(2,1)S(1)}, bf16[144,512]{1,0:T(8,128)(2,1)S(1)}, u32[]{:S(2)}, u32[]{:S(2)}) collective-permute-start(bf16[144,512]{1,0:T(8,128)(2,1)S(1)} %collective-permute-done.35.refs_3_), channel_id=1, source_target_pairs={{0,8},{1,5},{2,10},{3,7},{8,16},{9,1},{10,18},{11,3},{16,24},{17,9... | collective-permute-start | bytes 442376 | tf_op jit(solution)/shard_map/ppermute | solution.py:1032
  118.1 7.2 %collective-permute-start.41 = (bf16[144,512]{1,0:T(8,128)(2,1)S(1)}, bf16[144,512]{1,0:T(8,128)(2,1)S(1)}, u32[]{:S(2)}, u32[]{:S(2)}) collective-permute-start(bf16[144,512]{1,0:T(8,128)(2,1)S(1)} %collective-permute-done.36.refs_4_), channel_id=1, source_target_pairs={{0,4},{1,9},{2,6},{3,11},{8,0},{9,17},{10,2},{11,19},{16,8},{17,25... | collective-permute-start | bytes 442376 | tf_op jit(solution)/shard_map/ppermute | solution.py:1032
  120.4 5.0 %collective-permute-start.43 = (f32[16,512]{1,0:T(8,128)S(1)}, f32[16,512]{1,0:T(8,128)S(1)}, u32[]{:S(2)}, u32[]{:S(2)}) collective-permute-start(f32[16,512]{1,0:T(8,128)S(1)} %add_gains.5.refs_0_), channel_id=1, source_target_pairs={{0,16},{4,20},{8,24},{12,28},{16,0},{20,4},{24,8},{28,12},{1,17},{... | collective-permute-start | bytes 98312 | tf_op jit(solution)/shard_map/ppermute | solution.py:1044
  125.4 4.0 %collective-permute-start.47 = (f32[16,512]{1,0:T(8,128)S(1)}, f32[16,512]{1,0:T(8,128)S(1)}, u32[]{:S(2)}, u32[]{:S(2)}) collective-permute-start(f32[16,512]{1,0:T(8,128)S(1)} %add_gains.6.refs_0_), channel_id=1, source_target_pairs={{0,2},{1,3},{2,0},{3,1},{4,6},{5,7},{6,4},{7,5},{8,10},{9,11},{10,... | collective-permute-start | bytes 98312 | tf_op jit(solution)/shard_map/ppermute | solution.py:1041
  127.0 4.5 %collective-permute-start.45 = (bf16[80,512]{1,0:T(8,128)(2,1)S(1)}, bf16[80,512]{1,0:T(8,128)(2,1)S(1)}, u32[]{:S(2)}, u32[]{:S(2)}) collective-permute-start(bf16[80,512]{1,0:T(8,128)(2,1)S(1)} %get-tuple-element.222), channel_id=1, source_target_pairs={{0,8},{1,5},{2,10},{3,7},{8,16},{9,1},{10,18},{11,3},{16,24},{17,9... | collective-permute-start | bytes 245768 | tf_op jit(solution)/shard_map/ppermute | solution.py:1032
  127.3 4.3 %collective-permute-start.46 = (bf16[64,512]{1,0:T(8,128)(2,1)S(1)}, bf16[64,512]{1,0:T(8,128)(2,1)S(1)}, u32[]{:S(2)}, u32[]{:S(2)}) collective-permute-start(bf16[64,512]{1,0:T(8,128)(2,1)S(1)} %get-tuple-element.223), channel_id=1, source_target_pairs={{0,4},{1,9},{2,6},{3,11},{8,0},{9,17},{10,2},{11,19},{16,8},{17,25... | collective-permute-start | bytes 196616 | tf_op jit(solution)/shard_map/ppermute | solution.py:1032
  129.4 2.2 %collective-permute-start.48 = (f32[16,512]{1,0:T(8,128)S(1)}, f32[16,512]{1,0:T(8,128)S(1)}, u32[]{:S(2)}, u32[]{:S(2)}) collective-permute-start(f32[16,512]{1,0:T(8,128)S(1)} %add_gains.7.refs_9_), channel_id=1, source_target_pairs={{0,1},{1,0},{2,3},{3,2},{4,5},{5,4},{6,7},{7,6},{8,9},{9,8},{10,11... | collective-permute-start | bytes 98312 | tf_op jit(solution)/shard_map/ppermute | solution.py:1041
  (18 other events, 124.8 us)

commit v7 on v6

--- a/solution.py
+++ b/solution.py
@@ -977,7 +977,7 @@
     "pull": 0.1,
     "grads": 0.95,
     "relay": 0.3,
-    "collect": 4.5,
+    "collect": 9.0,
     "sinkhorn_back": 2.05,
     "total": 0.25,
     "input_back": 1.0,
@@ -1007,7 +1007,7 @@
 RING = (0, 2, 4, 6, 7, 5, 3, 1)
 SHARD = 512
 EXTRA = 32
-CUT = 320
+CUT = 256
 
 
 def local_eight(

time: 133 us -> 131 us (0.985)
  waiting for transfers between devices: 42 us -> 37.4 us
  starting transfers between devices: 44.5 us -> 47.2 us
    ppermute x23, waiting for transfers between devices: 15.7 us -> 11.6 us  [swap_head(): return lax.ppermute(v, 'head', [(i, i ^ j) for i in range(4)])]
    ppermute x23, starting transfers between devices: 28.3 us -> 29.7 us  [along(): return lax.ppermute(v, ('blk', 'head'), pairs)]
  transfers between devices with their start and end apart: 49 -> 49, of which waited for: 25 -> 25; matrix products, arithmetic and copies ran while one was open for 0% -> 0% of each run, Pallas kernels for 21% -> 22%
where the time goes in v7:
time: 131 us
  starting transfers between devices  47.2 us (36%)
  Pallas kernels  42.9 us (33%)
  waiting for transfers between devices  37.4 us (29%)
  local copies, waits for them, and re-layouts  2.58 us (2%)
    pallas_call x35, Pallas kernels, call(): pl.pallas_call(body, out_shape=shapes, in_specs=specs, out_specs=out_spec...  42.9 us
    ppermute x23, starting transfers between devices, along(): return lax.ppermute(v, ('blk', 'head'), pairs)  29.7 us
    ppermute x23, waiting for transfers between devices, along(): return lax.ppermute(v, ('blk', 'head'), pairs)  22.2 us
    ppermute x23, starting transfers between devices, swap_head(): return lax.ppermute(v, 'head', [(i, i ^ j) for i in range(4)])  12.8 us
    ppermute x23, waiting for transfers between devices, swap_head(): return lax.ppermute(v, 'head', [(i, i ^ j) for i in range(4)])  11.6 us
    ppermute x3, starting transfers between devices, swap_blk(): return lax.ppermute(v, 'blk', [(i, i ^ j) for i in range(8)])  4.71 us
    ppermute x3, waiting for transfers between devices, swap_blk(): return lax.ppermute(v, 'blk', [(i, i ^ j) for i in range(8)])  3.59 us
  transfers between devices with their start and end apart: 49, of which 25 were waited for; matrix products, arithmetic and copies ran while one was open for 0% of the time, Pallas kernels for 22%

profile of v7, /device:TPU:0, one launch (start us, length us, event | category | flops | bytes accessed | tf_op | source)
XLA Modules:
  0.0 131.2 jit_solution(9451270379984000882)
XLA Ops:
  2.9 2.3 %norm_one.1 = (bf16[288,512]{1,0:T(8,128)(2,1)}, bf16[288,512]{1,0:T(8,128)(2,1)}, f32[8,512]{1,0:T(8,128)}, f32[2,512]{1,0:T(2,128)}) custom-call(bf16[512,512]{1,0:T(8,128)(2,1)} %refs_0_.7, bf16[512]{0:T(512)(128)(2,1)} %refs_1_.5, f32[8,2,64]{2,1,0:T(2,128)} %refs_2_.3, f32[8,2,64]{2,1,0:T(2,128)} %copy-done.16), custom_call_target="tpu_custom_call" | custom-call | flops 1955000064 | bytes 6273000 | tf_op jit(solution)/shard_map/norm_one/pallas_call | solution.py:954
  5.2 3.0 %collective-permute-start.1 = (bf16[288,512]{1,0:T(8,128)(2,1)}, bf16[288,512]{1,0:T(8,128)(2,1)S(1)}, u32[]{:S(2)}, u32[]{:S(2)}) collective-permute-start(bf16[288,512]{1,0:T(8,128)(2,1)} %get-tuple-element.121.refs_0_), channel_id=1, source_target_pairs={{0,8},{1,5},{2,10},{3,7},{8,16},{9,1},{10,18},{11,3},{16,24},{17,9... | collective-permute-start | bytes 884744 | tf_op jit(solution)/shard_map/ppermute | solution.py:1032
  8.1 1.6 %collective-permute-start.2 = (bf16[288,512]{1,0:T(8,128)(2,1)}, bf16[288,512]{1,0:T(8,128)(2,1)S(1)}, u32[]{:S(2)}, u32[]{:S(2)}) collective-permute-start(bf16[288,512]{1,0:T(8,128)(2,1)} %get-tuple-element.122.refs_1_), channel_id=1, source_target_pairs={{0,8},{1,5},{2,10},{3,7},{8,16},{9,1},{10,18},{11,3},{16,24},{17,9... | collective-permute-start | bytes 884744 | tf_op jit(solution)/shard_map/ppermute | solution.py:1032
  9.7 1.5 %collective-permute-start.7 = (bf16[512,512]{1,0:T(8,128)(2,1)S(1)}, bf16[512,512]{1,0:T(8,128)(2,1)S(1)}, u32[]{:S(2)}, u32[]{:S(2)}) collective-permute-start(bf16[512,512]{1,0:T(8,128)(2,1)S(1)} %copy-done.3), channel_id=1, source_target_pairs={{0,2},{1,3},{2,0},{3,1},{4,6},{5,7},{6,4},{7,5},{8,10},{9,11},{10,... | collective-permute-start | bytes 1572872 | tf_op jit(solution)/shard_map/ppermute | solution.py:1041
  13.7 1.6 %collective-permute-start.3 = (bf16[288,512]{1,0:T(8,128)(2,1)S(1)}, bf16[288,512]{1,0:T(8,128)(2,1)S(1)}, u32[]{:S(2)}, u32[]{:S(2)}) collective-permute-start(bf16[288,512]{1,0:T(8,128)(2,1)S(1)} %collective-permute-done.1.refs_0_.refs_2_), channel_id=1, source_target_pairs={{0,8},{1,5},{2,10},{3,7},{8,16},{9,1},{10,18},{11,3},{16,24},{17,9... | collective-permute-start | bytes 884744 | tf_op jit(solution)/shard_map/ppermute | solution.py:1032
  16.1 2.1 %collective-permute-start.6 = (bf16[288,512]{1,0:T(8,128)(2,1)S(1)}, bf16[288,512]{1,0:T(8,128)(2,1)S(1)}, u32[]{:S(2)}, u32[]{:S(2)}) collective-permute-start(bf16[288,512]{1,0:T(8,128)(2,1)S(1)} %collective-permute-done.2.refs_1_.refs_3_), channel_id=1, source_target_pairs={{0,8},{1,5},{2,10},{3,7},{8,16},{9,1},{10,18},{11,3},{16,24},{17,9... | collective-permute-start | bytes 884744 | tf_op jit(solution)/shard_map/ppermute | solution.py:1032
  18.2 2.2 %collective-permute-done.3.refs_0_.refs_6_ = bf16[288,512]{1,0:T(8,128)(2,1)S(1)} collective-permute-done((bf16[288,512]{1,0:T(8,128)(2,1)S(1)}, bf16[288,512]{1,0:T(8,128)(2,1)S(1)}, u32[]{:S(2)}, u32[]{:S(2)}) %collective-permute-start.3) | collective-permute-done | bytes 294944 | tf_op jit(solution)/shard_map/ppermute | solution.py:1032
  20.5 1.6 %collective-permute-start.8 = (bf16[288,512]{1,0:T(8,128)(2,1)S(1)}, bf16[288,512]{1,0:T(8,128)(2,1)S(1)}, u32[]{:S(2)}, u32[]{:S(2)}) collective-permute-start(bf16[288,512]{1,0:T(8,128)(2,1)S(1)} %collective-permute-done.3.refs_0_.refs_6_), channel_id=1, source_target_pairs={{0,8},{1,5},{2,10},{3,7},{8,16},{9,1},{10,18},{11,3},{16,24},{17,9... | collective-permute-start | bytes 884744 | tf_op jit(solution)/shard_map/ppermute | solution.py:1032
  22.0 1.3 collective-permute-start.12
  23.6 1.6 %collective-permute-start.11 = (bf16[288,512]{1,0:T(8,128)(2,1)S(1)}, bf16[288,512]{1,0:T(8,128)(2,1)S(1)}, u32[]{:S(2)}, u32[]{:S(2)}) collective-permute-start(bf16[288,512]{1,0:T(8,128)(2,1)S(1)} %collective-permute-done.6.refs_1_.refs_7_), channel_id=1, source_target_pairs={{0,8},{1,5},{2,10},{3,7},{8,16},{9,1},{10,18},{11,3},{16,24},{17,9... | collective-permute-start | bytes 884744 | tf_op jit(solution)/shard_map/ppermute | solution.py:1032
  25.7 1.5 %collective-permute-done.8.refs_0_.refs_10_ = bf16[288,512]{1,0:T(8,128)(2,1)S(1)} collective-permute-done((bf16[288,512]{1,0:T(8,128)(2,1)S(1)}, bf16[288,512]{1,0:T(8,128)(2,1)S(1)}, u32[]{:S(2)}, u32[]{:S(2)}) %collective-permute-start.8) | collective-permute-done | bytes 294944 | tf_op jit(solution)/shard_map/ppermute | solution.py:1032
  27.2 1.5 %collective-permute-done.12.refs_3_.refs_12_ = bf16[256,512]{1,0:T(8,128)(2,1)S(1)} collective-permute-done((bf16[256,512]{1,0:T(8,128)(2,1)S(1)}, bf16[256,512]{1,0:T(8,128)(2,1)S(1)}, u32[]{:S(2)}, u32[]{:S(2)}) %collective-permute-start.12) | collective-permute-done | bytes 262176 | tf_op jit(solution)/shard_map/ppermute | solution.py:1041
  28.7 1.7 %collective-permute-done.11.refs_1_.refs_11_ = bf16[288,512]{1,0:T(8,128)(2,1)S(1)} collective-permute-done((bf16[288,512]{1,0:T(8,128)(2,1)S(1)}, bf16[288,512]{1,0:T(8,128)(2,1)S(1)}, u32[]{:S(2)}, u32[]{:S(2)}) %collective-permute-start.11) | collective-permute-done | bytes 294944 | tf_op jit(solution)/shard_map/ppermute | solution.py:1032
  30.4 1.3 collective-permute-start.16
  32.2 1.8 %collective-permute-start.15 = (bf16[288,512]{1,0:T(8,128)(2,1)S(1)}, bf16[288,512]{1,0:T(8,128)(2,1)S(1)}, u32[]{:S(2)}, u32[]{:S(2)}) collective-permute-start(bf16[288,512]{1,0:T(8,128)(2,1)S(1)} %get-tuple-element.145), channel_id=1, source_target_pairs={{0,8},{1,5},{2,10},{3,7},{8,16},{9,1},{10,18},{11,3},{16,24},{17,9... | collective-permute-start | bytes 884744 | tf_op jit(solution)/shard_map/ppermute | solution.py:1032
  36.2 2.9 %collective-permute-done.15.refs_7_.refs_14_ = bf16[288,512]{1,0:T(8,128)(2,1)S(1)} collective-permute-done((bf16[288,512]{1,0:T(8,128)(2,1)S(1)}, bf16[288,512]{1,0:T(8,128)(2,1)S(1)}, u32[]{:S(2)}, u32[]{:S(2)}) %collective-permute-start.15) | collective-permute-done | bytes 294944 | tf_op jit(solution)/shard_map/ppermute | solution.py:1032
  40.2 1.6 %collective-permute-done.17.refs_8_.refs_15_ = bf16[288,512]{1,0:T(8,128)(2,1)S(1)} collective-permute-done((bf16[288,512]{1,0:T(8,128)(2,1)S(1)}, bf16[288,512]{1,0:T(8,128)(2,1)S(1)}, u32[]{:S(2)}, u32[]{:S(2)}) %collective-permute-start.17) | collective-permute-done | bytes 294944 | tf_op jit(solution)/shard_map/ppermute | solution.py:1041
  41.8 3.7 %attend.1 = (bf16[4096,384]{1,0:T(8,128)(2,1)S(1)}, bf16[512,128]{1,0:T(8,128)(2,1)S(1)}, f32[64,512]{1,0:T(8,128)S(1)}, f32[16,2,64,64]{3,2,1,0:T(8,128)S(1)}, ...) custom-call(bf16[512,384]{1,0:T(8,128)(2,1)S(1)} %get-tuple-element.124.refs_0_, ...), custom_call_target="tpu_custom_call" | custom-call | flops 4830000128 | bytes 15498000 | tf_op jit(solution)/shard_map/attend/pallas_call | solution.py:954
  45.5 1.6 %collective-permute-start.18 = (bf16[512,128]{1,0:T(8,128)(2,1)S(1)}, bf16[512,128]{1,0:T(8,128)(2,1)S(1)}, u32[]{:S(2)}, u32[]{:S(2)}) collective-permute-start(bf16[512,128]{1,0:T(8,128)(2,1)S(1)} %get-tuple-element.151.refs_3_.refs_4_), channel_id=1, source_target_pairs={{0,2},{1,3},{2,0},{3,1},{4,6},{5,7},{6,4},{7,5},{8,10},{9,11},{10,... | collective-permute-start | bytes 393224 | tf_op jit(solution)/shard_map/ppermute | solution.py:1041
  47.6 2.8 %prepare.1 = (f32[1536,256]{1,0:T(8,128)S(1)}, f32[1536,256]{1,0:T(8,128)S(1)}) custom-call(bf16[4096,384]{1,0:T(8,128)(2,1)S(1)} %get-tuple-element.152.refs_0_.refs_1_.refs_2_, s32[2,64]{1,0:T(2,128)S(1)} %bitcast.5, f32[64,256]{1,0:T(8,128)S(1)} %get-tuple-element.153.refs_2_.refs_3_.refs_4_), custom_call_target="tpu_custom_call" | custom-call | flops 3335000064 | bytes 10701000 | tf_op jit(solution)/shard_map/prepare/pallas_call | solution.py:954
  51.1 1.3 %collective-permute-done.20.refs_6_ = bf16[512,128]{1,0:T(8,128)(2,1)S(1)} collective-permute-done((bf16[512,128]{1,0:T(8,128)(2,1)S(1)}, bf16[512,128]{1,0:T(8,128)(2,1)S(1)}, u32[]{:S(2)}, u32[]{:S(2)}) %collective-permute-start.20) | collective-permute-done | bytes 131104 | tf_op jit(solution)/shard_map/ppermute | solution.py:1041
  52.4 4.2 %feed.1 = (f32[512,512]{1,0:T(8,128)S(1)}, bf16[512,512]{1,0:T(8,128)(2,1)S(1)}, bf16[512,512]{1,0:T(8,128)(2,1)S(1)}, bf16[512,512]{1,0:T(8,128)(2,1)S(1)}, f32...) custom-call(bf16[512,512]{1,0:T(8,128)(2,1)S(1)} %copy-done.5, bf16[512,512]{1,0:T(8,128)(2,1)S(1)} %copy-done.4, ...), custom_call_target="tpu_custom_call" | custom-call | flops 4830000128 | bytes 15498000 | tf_op jit(solution)/shard_map/feed/pallas_call | solution.py:954
  56.9 2.5 %collective-permute-done.22.refs_2_ = f32[512,512]{1,0:T(8,128)S(1)} collective-permute-done((f32[512,512]{1,0:T(8,128)S(1)}, f32[512,512]{1,0:T(8,128)S(1)}, u32[]{:S(2)}, u32[]{:S(2)}) %collective-permute-start.22) | collective-permute-done | bytes 1048608 | tf_op jit(solution)/shard_map/ppermute | solution.py:1041
  61.2 1.6 %collective-permute-start.27 = (bf16[768,128]{1,0:T(8,128)(2,1)S(1)}, bf16[768,128]{1,0:T(8,128)(2,1)S(1)}, u32[]{:S(2)}, u32[]{:S(2)}) collective-permute-start(bf16[768,128]{1,0:T(8,128)(2,1)S(1)} %get-tuple-element.177), channel_id=1, source_target_pairs={{0,4},{1,9},{2,6},{3,11},{8,0},{9,17},{10,2},{11,19},{16,8},{17,25... | collective-permute-start | bytes 589832 | tf_op jit(solution)/shard_map/ppermute | solution.py:1032
  63.3 1.8 %pull.5 = (f32[512,256]{1,0:T(8,128)S(1)}, bf16[512,384]{1,0:T(8,128)(2,1)S(1)}, f32[8,256]{1,0:T(8,128)S(1)}) custom-call(bf16[512,128]{1,0:T(8,128)(2,1)S(1)} %get-tuple-element.168.refs_6_.refs_0_, bf16[4096,384]{1,0:T(8,128)(2,1)S(1)} %get-tuple-element.152.refs_0_.refs_1_.refs_2_, s32[2,64]{1,0:T(2,128)S(1)} %bitcast.6, ...), custom_call_target="tpu_custom_call" | custom-call | flops 115000000 | bytes 369000 | tf_op jit(solution)/shard_map/pull/pallas_call | solution.py:954
  65.1 3.9 %collective-permute-done.27.refs_1_ = bf16[768,128]{1,0:T(8,128)(2,1)S(1)} collective-permute-done((bf16[768,128]{1,0:T(8,128)(2,1)S(1)}, bf16[768,128]{1,0:T(8,128)(2,1)S(1)}, u32[]{:S(2)}, u32[]{:S(2)}) %collective-permute-start.27) | collective-permute-done | bytes 196640 | tf_op jit(solution)/shard_map/ppermute | solution.py:1032
  69.0 1.4 %collective-permute-start.28 = (bf16[1088,128]{1,0:T(8,128)(2,1)S(1)}, bf16[1088,128]{1,0:T(8,128)(2,1)S(1)}, u32[]{:S(2)}, u32[]{:S(2)}) collective-permute-start(bf16[1088,128]{1,0:T(8,128)(2,1)S(1)} %relay.9), channel_id=1, source_target_pairs={{0,4},{1,9},{2,6},{3,11},{8,0},{9,17},{10,2},{11,19},{16,8},{17,25... | collective-permute-start | bytes 835592 | tf_op jit(solution)/shard_map/ppermute | solution.py:1032
  71.2 1.7 %collective-permute-start.30 = (bf16[512,512]{1,0:T(8,128)(2,1)S(1)}, bf16[512,512]{1,0:T(8,128)(2,1)S(1)}, u32[]{:S(2)}, u32[]{:S(2)}) collective-permute-start(bf16[512,512]{1,0:T(8,128)(2,1)S(1)} %get-tuple-element.184.refs_4_.refs_9_.refs_3_.refs_2_), channel_id=1, source_target_pairs={{0,2},{1,3},{2,0},{3,1},{4,6},{5,7},{6,4},{7,5},{8,10},{9,11},{10,... | collective-permute-start | bytes 1572872 | tf_op jit(solution)/shard_map/ppermute | solution.py:1041
  72.8 2.8 %pull.6 = (f32[1024,256]{1,0:T(8,128)S(1)}, bf16[1024,384]{1,0:T(8,128)(2,1)S(1)}, f32[16,256]{1,0:T(8,128)S(1)}) custom-call(bf16[832,128]{1,0:T(8,128)(2,1)S(1)} %collective-permute-done.23.refs_1_.refs_0_, bf16[768,128]{1,0:T(8,128)(2,1)S(1)} %collective-permute-done.27.refs_1_, bf16[4096,384]{1,0:T(8,128)(2,1)S(1)} %get-tuple-element.152.refs_0_.refs_1_.refs_2_, ...), custom_call_target="tpu_custom_call" | custom-call | flops 115000000 | bytes 369000 | tf_op jit(solution)/shard_map/pull/pallas_call | solution.py:954
  75.7 2.1 %collective-permute-done.28.refs_1_ = bf16[1088,128]{1,0:T(8,128)(2,1)S(1)} collective-permute-done((bf16[1088,128]{1,0:T(8,128)(2,1)S(1)}, bf16[1088,128]{1,0:T(8,128)(2,1)S(1)}, u32[]{:S(2)}, u32[]{:S(2)}) %collective-permute-start.28) | collective-permute-done | bytes 278560 | tf_op jit(solution)/shard_map/ppermute | solution.py:1032
  80.0 2.8 %pull.7 = (f32[1024,256]{1,0:T(8,128)S(1)}, bf16[1024,384]{1,0:T(8,128)(2,1)S(1)}, f32[16,256]{1,0:T(8,128)S(1)}) custom-call(bf16[1088,128]{1,0:T(8,128)(2,1)S(1)} %collective-permute-done.24.refs_1_.refs_0_, bf16[1088,128]{1,0:T(8,128)(2,1)S(1)} %collective-permute-done.28.refs_1_, bf16[4096,384]{1,0:T(8,128)(2,1)S(1)} %get-tuple-element.152.refs_0_.refs_1_.refs_2_, ...), custom_call_target="tpu_custom_call" | custom-call | flops 115000000 | bytes 369000 | tf_op jit(solution)/shard_map/pull/pallas_call | solution.py:954
  83.7 1.9 %collective-permute-done.29.refs_1_ = bf16[1088,128]{1,0:T(8,128)(2,1)S(1)} collective-permute-done((bf16[1088,128]{1,0:T(8,128)(2,1)S(1)}, bf16[1088,128]{1,0:T(8,128)(2,1)S(1)}, u32[]{:S(2)}, u32[]{:S(2)}) %collective-permute-start.29) | collective-permute-done | bytes 278560 | tf_op jit(solution)/shard_map/ppermute | solution.py:1032
  86.7 1.1 collective-permute-start.26
  87.9 2.2 %pull.8 = (f32[1024,256]{1,0:T(8,128)S(1)}, bf16[1024,384]{1,0:T(8,128)(2,1)S(1)}, f32[16,256]{1,0:T(8,128)S(1)}) custom-call(bf16[1088,128]{1,0:T(8,128)(2,1)S(1)} %collective-permute-done.25.refs_1_.refs_0_, bf16[1088,128]{1,0:T(8,128)(2,1)S(1)} %collective-permute-done.29.refs_1_, bf16[4096,384]{1,0:T(8,128)(2,1)S(1)} %get-tuple-element.152.refs_0_.refs_1_.refs_2_, ...), custom_call_target="tpu_custom_call" | custom-call | flops 115000000 | bytes 369000 | tf_op jit(solution)/shard_map/pull/pallas_call | solution.py:954
  90.1 1.5 %collective-permute-done.31.refs_2_.refs_1_ = bf16[832,128]{1,0:T(8,128)(2,1)S(1)} collective-permute-done((bf16[832,128]{1,0:T(8,128)(2,1)S(1)}, bf16[832,128]{1,0:T(8,128)(2,1)S(1)}, u32[]{:S(2)}, u32[]{:S(2)}) %collective-permute-start.31) | collective-permute-done | bytes 213024 | tf_op jit(solution)/shard_map/ppermute | solution.py:1032
  91.6 2.0 %collective-permute-done.26.refs_1_.refs_0_ = bf16[832,128]{1,0:T(8,128)(2,1)S(1)} collective-permute-done((bf16[832,128]{1,0:T(8,128)(2,1)S(1)}, bf16[832,128]{1,0:T(8,128)(2,1)S(1)}, u32[]{:S(2)}, u32[]{:S(2)}) %collective-permute-start.26) | collective-permute-done | bytes 213024 | tf_op jit(solution)/shard_map/ppermute | solution.py:1032
  94.2 1.5 %collective-permute-start.33 = (bf16[144,512]{1,0:T(8,128)(2,1)S(1)}, bf16[144,512]{1,0:T(8,128)(2,1)S(1)}, u32[]{:S(2)}, u32[]{:S(2)}) collective-permute-start(bf16[144,512]{1,0:T(8,128)(2,1)S(1)} %total.1.refs_0_), channel_id=1, source_target_pairs={{0,4},{1,9},{2,6},{3,11},{8,0},{9,17},{10,2},{11,19},{16,8},{17,25... | collective-permute-start | bytes 442376 | tf_op jit(solution)/shard_map/ppermute | solution.py:1032
  95.8 1.5 %pull.9 = (f32[512,256]{1,0:T(8,128)S(1)}, bf16[512,384]{1,0:T(8,128)(2,1)S(1)}, f32[8,256]{1,0:T(8,128)S(1)}) custom-call(bf16[832,128]{1,0:T(8,128)(2,1)S(1)} %collective-permute-done.26.refs_1_.refs_0_, bf16[832,128]{1,0:T(8,128)(2,1)S(1)} %collective-permute-done.31.refs_2_.refs_1_, bf16[4096,384]{1,0:T(8,128)(2,1)S(1)} %get-tuple-element.152.refs_0_.refs_1_.refs_2_, ...), custom_call_target="tpu_custom_call" | custom-call | flops 115000000 | bytes 369000 | tf_op jit(solution)/shard_map/pull/pallas_call | solution.py:954
  97.3 4.5 %collect.1 = (bf16[4096,384]{1,0:T(8,128)(2,1)S(1)}, bf16[512,384]{1,0:T(8,128)(2,1)S(1)}, f32[8,128]{1,0:T(8,128)S(1)}, f32[512,128]{1,0:T(8,128)}) custom-call(f32[512,256]{1,0:T(8,128)S(1)} %get-tuple-element.179.refs_0_, f32[1024,256]{1,0:T(8,128)S(1)} %get-tuple-element.181.refs_1_, f32[1024,256]{1,0:T(8,128)S(1)} %get-tuple-element.183.refs_2_, ...), custom_call_target="tpu_custom_call" | custom-call | flops 10350000128 | bytes 33210000 | tf_op jit(solution)/shard_map/collect/pallas_call | solution.py:954
  101.8 1.7 %collective-permute-start.39 = (bf16[512,384]{1,0:T(8,128)(2,1)S(1)}, bf16[512,384]{1,0:T(8,128)(2,1)S(1)}, u32[]{:S(2)}, u32[]{:S(2)}) collective-permute-start(bf16[512,384]{1,0:T(8,128)(2,1)S(1)} %get-tuple-element.205.refs_1_.refs_0_), channel_id=1, source_target_pairs={{0,2},{1,3},{2,0},{3,1},{4,6},{5,7},{6,4},{7,5},{8,10},{9,11},{10,... | collective-permute-start | bytes 1179656 | tf_op jit(solution)/shard_map/ppermute | solution.py:1041
  103.9 1.6 %collective-permute-start.36 = (bf16[144,512]{1,0:T(8,128)(2,1)S(1)}, bf16[144,512]{1,0:T(8,128)(2,1)S(1)}, u32[]{:S(2)}, u32[]{:S(2)}) collective-permute-start(bf16[144,512]{1,0:T(8,128)(2,1)S(1)} %collective-permute-done.33.refs_2_), channel_id=1, source_target_pairs={{0,4},{1,9},{2,6},{3,11},{8,0},{9,17},{10,2},{11,19},{16,8},{17,25... | collective-permute-start | bytes 442376 | tf_op jit(solution)/shard_map/ppermute | solution.py:1032
  107.6 2.5 %collective-permute-done.37.refs_1_ = f32[16,512]{1,0:T(8,128)S(1)} collective-permute-done((f32[16,512]{1,0:T(8,128)S(1)}, f32[16,512]{1,0:T(8,128)S(1)}, u32[]{:S(2)}, u32[]{:S(2)}) %collective-permute-start.37) | collective-permute-done | bytes 32800 | tf_op jit(solution)/shard_map/ppermute | solution.py:1044
  116.6 2.5 %collective-permute-start.43 = (f32[16,512]{1,0:T(8,128)S(1)}, f32[16,512]{1,0:T(8,128)S(1)}, u32[]{:S(2)}, u32[]{:S(2)}) collective-permute-start(f32[16,512]{1,0:T(8,128)S(1)} %add_gains.5.refs_0_), channel_id=1, source_target_pairs={{0,16},{4,20},{8,24},{12,28},{16,0},{20,4},{24,8},{28,12},{1,17},{... | collective-permute-start | bytes 98312 | tf_op jit(solution)/shard_map/ppermute | solution.py:1044
  119.2 3.6 %weights.1 = f32[3,512,128]{2,1,0:T(8,128)} custom-call(bf16[288,512]{1,0:T(8,128)(2,1)S(1)} %copy-done.8, bf16[288,512]{1,0:T(8,128)(2,1)S(1)} %copy-done.10, bf16[288,512]{1,0:T(8,128)(2,1)S(1)} %collective-permute-done.1.refs_0_.refs_2_, bf16[288,512]{1,0:T(8,128)(2,1)S(1)} %collective-permute-done.2.refs_1_.refs_3_, ...), custom_call_target="tpu_custom_call" | custom-call | flops 4140000000 | bytes 13284000 | tf_op jit(solution)/shard_map/weights/pallas_call | solution.py:954
  125.3 1.2 collective-permute-start.46
  126.8 1.7 %norm_one_back.1 = f32[512,512]{1,0:T(8,128)} custom-call(bf16[512,512]{1,0:T(8,128)(2,1)S(1)} %copy-done.5, bf16[512]{0:T(512)(128)(2,1)S(1)} %copy-done.13, f32[512,512]{1,0:T(8,128)S(1)} %input_back.1.refs_2_, f32[512,512]{1,0:T(8,128)S(1)} %collective-permute-done.44.refs_3_, f32[512,512]{1,0:T(8,128)S(1)} %get-tuple-element.219.refs_4_), custom_call_target="tpu_custom_call" | custom-call | flops 1955000064 | bytes 6273000 | tf_op jit(solution)/shard_map/norm_one_back/pallas_call | solution.py:954
  128.4 1.1 collective-permute-done.46.refs_8_
  129.6 1.6 %lay.1 = (f32[512,512]{1,0:T(8,128)}, f32[512,512]{1,0:T(8,128)}, f32[128,512]{1,0:T(8,128)}, f32[512]{0:T(512)}, f32[512]{0:T(512)}) custom-call(bf16[144,512]{1,0:T(8,128)(2,1)S(1)} %total.1.refs_0_, bf16[144,512]{1,0:T(8,128)(2,1)S(1)} %collective-permute-done.32.refs_1_, bf16[144,512]{1,0:T(8,128)(2,1)S(1)} %collective-permute-done.33.refs_2_, ...), custom_call_target="tpu_custom_call" | custom-call | flops 1840000000 | bytes 5904000 | tf_op jit(solution)/shard_map/lay/pallas_call | solution.py:954
  (119 shorter events, 31.3 us)
Async XLA Ops:
  0.7 1.6 %collective-permute-start = (f32[8,2,64]{2,1,0:T(2,128)}, f32[8,2,64]{2,1,0:T(2,128)S(1)}, u32[]{:S(2)}, u32[]{:S(2)}) collective-permute-start(f32[8,2,64]{2,1,0:T(2,128)} %refs_2_.3), channel_id=1, source_target_pairs={{0,1},{1,0},{2,3},{3,2},{4,5},{5,4},{6,7},{7,6},{8,9},{9,8},{10,11... | collective-permute-start | bytes 12296 | tf_op jit(solution)/shard_map/ppermute | solution.py:1041
  5.2 8.5 %collective-permute-start.1 = (bf16[288,512]{1,0:T(8,128)(2,1)}, bf16[288,512]{1,0:T(8,128)(2,1)S(1)}, u32[]{:S(2)}, u32[]{:S(2)}) collective-permute-start(bf16[288,512]{1,0:T(8,128)(2,1)} %get-tuple-element.121.refs_0_), channel_id=1, source_target_pairs={{0,8},{1,5},{2,10},{3,7},{8,16},{9,1},{10,18},{11,3},{16,24},{17,9... | collective-permute-start | bytes 884744 | tf_op jit(solution)/shard_map/ppermute | solution.py:1032
  8.1 8.0 %collective-permute-start.2 = (bf16[288,512]{1,0:T(8,128)(2,1)}, bf16[288,512]{1,0:T(8,128)(2,1)S(1)}, u32[]{:S(2)}, u32[]{:S(2)}) collective-permute-start(bf16[288,512]{1,0:T(8,128)(2,1)} %get-tuple-element.122.refs_1_), channel_id=1, source_target_pairs={{0,8},{1,5},{2,10},{3,7},{8,16},{9,1},{10,18},{11,3},{16,24},{17,9... | collective-permute-start | bytes 884744 | tf_op jit(solution)/shard_map/ppermute | solution.py:1032
  9.7 13.6 %collective-permute-start.7 = (bf16[512,512]{1,0:T(8,128)(2,1)S(1)}, bf16[512,512]{1,0:T(8,128)(2,1)S(1)}, u32[]{:S(2)}, u32[]{:S(2)}) collective-permute-start(bf16[512,512]{1,0:T(8,128)(2,1)S(1)} %copy-done.3), channel_id=1, source_target_pairs={{0,2},{1,3},{2,0},{3,1},{4,6},{5,7},{6,4},{7,5},{8,10},{9,11},{10,... | collective-permute-start | bytes 1572872 | tf_op jit(solution)/shard_map/ppermute | solution.py:1041
  13.7 6.8 %collective-permute-start.3 = (bf16[288,512]{1,0:T(8,128)(2,1)S(1)}, bf16[288,512]{1,0:T(8,128)(2,1)S(1)}, u32[]{:S(2)}, u32[]{:S(2)}) collective-permute-start(bf16[288,512]{1,0:T(8,128)(2,1)S(1)} %collective-permute-done.1.refs_0_.refs_2_), channel_id=1, source_target_pairs={{0,8},{1,5},{2,10},{3,7},{8,16},{9,1},{10,18},{11,3},{16,24},{17,9... | collective-permute-start | bytes 884744 | tf_op jit(solution)/shard_map/ppermute | solution.py:1032
  16.1 7.5 %collective-permute-start.6 = (bf16[288,512]{1,0:T(8,128)(2,1)S(1)}, bf16[288,512]{1,0:T(8,128)(2,1)S(1)}, u32[]{:S(2)}, u32[]{:S(2)}) collective-permute-start(bf16[288,512]{1,0:T(8,128)(2,1)S(1)} %collective-permute-done.2.refs_1_.refs_3_), channel_id=1, source_target_pairs={{0,8},{1,5},{2,10},{3,7},{8,16},{9,1},{10,18},{11,3},{16,24},{17,9... | collective-permute-start | bytes 884744 | tf_op jit(solution)/shard_map/ppermute | solution.py:1032
  20.5 6.7 %collective-permute-start.8 = (bf16[288,512]{1,0:T(8,128)(2,1)S(1)}, bf16[288,512]{1,0:T(8,128)(2,1)S(1)}, u32[]{:S(2)}, u32[]{:S(2)}) collective-permute-start(bf16[288,512]{1,0:T(8,128)(2,1)S(1)} %collective-permute-done.3.refs_0_.refs_6_), channel_id=1, source_target_pairs={{0,8},{1,5},{2,10},{3,7},{8,16},{9,1},{10,18},{11,3},{16,24},{17,9... | collective-permute-start | bytes 884744 | tf_op jit(solution)/shard_map/ppermute | solution.py:1032
  22.0 6.6 %collective-permute-start.12 = (bf16[256,512]{1,0:T(8,128)(2,1)S(1)}, bf16[256,512]{1,0:T(8,128)(2,1)S(1)}, u32[]{:S(2)}, u32[]{:S(2)}) collective-permute-start(bf16[256,512]{1,0:T(8,128)(2,1)S(1)} %get-tuple-element.136), channel_id=1, source_target_pairs={{0,2},{1,3},{2,0},{3,1},{4,6},{5,7},{6,4},{7,5},{8,10},{9,11},{10,... | collective-permute-start | bytes 786440 | tf_op jit(solution)/shard_map/ppermute | solution.py:1041
  23.6 6.7 %collective-permute-start.11 = (bf16[288,512]{1,0:T(8,128)(2,1)S(1)}, bf16[288,512]{1,0:T(8,128)(2,1)S(1)}, u32[]{:S(2)}, u32[]{:S(2)}) collective-permute-start(bf16[288,512]{1,0:T(8,128)(2,1)S(1)} %collective-permute-done.6.refs_1_.refs_7_), channel_id=1, source_target_pairs={{0,8},{1,5},{2,10},{3,7},{8,16},{9,1},{10,18},{11,3},{16,24},{17,9... | collective-permute-start | bytes 884744 | tf_op jit(solution)/shard_map/ppermute | solution.py:1032
  25.2 6.4 %collective-permute-start.4 = (bf16[288,512]{1,0:T(8,128)(2,1)S(1)}, bf16[288,512]{1,0:T(8,128)(2,1)S(1)}, u32[]{:S(2)}, u32[]{:S(2)}) collective-permute-start(bf16[288,512]{1,0:T(8,128)(2,1)S(1)} %collective-permute-done.1.refs_0_.refs_2_), channel_id=1, source_target_pairs={{0,1},{1,0},{2,3},{3,2},{4,5},{5,4},{6,7},{7,6},{8,9},{9,8},{10,11... | collective-permute-start | bytes 884744 | tf_op jit(solution)/shard_map/ppermute | solution.py:1041
  25.2 6.4 %collective-permute-start.5 = (bf16[288,512]{1,0:T(8,128)(2,1)S(1)}, bf16[288,512]{1,0:T(8,128)(2,1)S(1)}, u32[]{:S(2)}, u32[]{:S(2)}) collective-permute-start(bf16[288,512]{1,0:T(8,128)(2,1)S(1)} %collective-permute-done.2.refs_1_.refs_3_), channel_id=1, source_target_pairs={{0,1},{1,0},{2,3},{3,2},{4,5},{5,4},{6,7},{7,6},{8,9},{9,8},{10,11... | collective-permute-start | bytes 884744 | tf_op jit(solution)/shard_map/ppermute | solution.py:1041
  27.2 5.0 %collective-permute-start.9 = (bf16[288,512]{1,0:T(8,128)(2,1)S(1)}, bf16[288,512]{1,0:T(8,128)(2,1)S(1)}, u32[]{:S(2)}, u32[]{:S(2)}) collective-permute-start(bf16[288,512]{1,0:T(8,128)(2,1)S(1)} %collective-permute-done.3.refs_0_.refs_6_), channel_id=1, source_target_pairs={{0,1},{1,0},{2,3},{3,2},{4,5},{5,4},{6,7},{7,6},{8,9},{9,8},{10,11... | collective-permute-start | bytes 884744 | tf_op jit(solution)/shard_map/ppermute | solution.py:1041
  28.7 6.1 %collective-permute-start.10 = (bf16[288,512]{1,0:T(8,128)(2,1)S(1)}, bf16[288,512]{1,0:T(8,128)(2,1)S(1)}, u32[]{:S(2)}, u32[]{:S(2)}) collective-permute-start(bf16[288,512]{1,0:T(8,128)(2,1)S(1)} %collective-permute-done.6.refs_1_.refs_7_), channel_id=1, source_target_pairs={{0,1},{1,0},{2,3},{3,2},{4,5},{5,4},{6,7},{7,6},{8,9},{9,8},{10,11... | collective-permute-start | bytes 884744 | tf_op jit(solution)/shard_map/ppermute | solution.py:1041
  30.4 9.9 %collective-permute-start.16 = (bf16[384,512]{1,0:T(8,128)(2,1)S(1)}, bf16[384,512]{1,0:T(8,128)(2,1)S(1)}, u32[]{:S(2)}, u32[]{:S(2)}) collective-permute-start(bf16[384,512]{1,0:T(8,128)(2,1)S(1)} %get-tuple-element.147), channel_id=1, source_target_pairs={{0,2},{1,3},{2,0},{3,1},{4,6},{5,7},{6,4},{7,5},{8,10},{9,11},{10,... | collective-permute-start | bytes 1179656 | tf_op jit(solution)/shard_map/ppermute | solution.py:1041
  31.6 3.9 %collective-permute-start.13 = (bf16[288,512]{1,0:T(8,128)(2,1)S(1)}, bf16[288,512]{1,0:T(8,128)(2,1)S(1)}, u32[]{:S(2)}, u32[]{:S(2)}) collective-permute-start(bf16[288,512]{1,0:T(8,128)(2,1)S(1)} %collective-permute-done.8.refs_0_.refs_10_), channel_id=1, source_target_pairs={{0,1},{1,0},{2,3},{3,2},{4,5},{5,4},{6,7},{7,6},{8,9},{9,8},{10,11... | collective-permute-start | bytes 884744 | tf_op jit(solution)/shard_map/ppermute | solution.py:1041
  31.6 3.9 %collective-permute-start.14 = (bf16[288,512]{1,0:T(8,128)(2,1)S(1)}, bf16[288,512]{1,0:T(8,128)(2,1)S(1)}, u32[]{:S(2)}, u32[]{:S(2)}) collective-permute-start(bf16[288,512]{1,0:T(8,128)(2,1)S(1)} %collective-permute-done.11.refs_1_.refs_11_), channel_id=1, source_target_pairs={{0,1},{1,0},{2,3},{3,2},{4,5},{5,4},{6,7},{7,6},{8,9},{9,8},{10,11... | collective-permute-start | bytes 884744 | tf_op jit(solution)/shard_map/ppermute | solution.py:1041
  32.2 7.0 %collective-permute-start.15 = (bf16[288,512]{1,0:T(8,128)(2,1)S(1)}, bf16[288,512]{1,0:T(8,128)(2,1)S(1)}, u32[]{:S(2)}, u32[]{:S(2)}) collective-permute-start(bf16[288,512]{1,0:T(8,128)(2,1)S(1)} %get-tuple-element.145), channel_id=1, source_target_pairs={{0,8},{1,5},{2,10},{3,7},{8,16},{9,1},{10,18},{11,3},{16,24},{17,9... | collective-permute-start | bytes 884744 | tf_op jit(solution)/shard_map/ppermute | solution.py:1032
  40.2 1.6 %collective-permute-start.17 = (bf16[288,512]{1,0:T(8,128)(2,1)S(1)}, bf16[288,512]{1,0:T(8,128)(2,1)S(1)}, u32[]{:S(2)}, u32[]{:S(2)}) collective-permute-start(bf16[288,512]{1,0:T(8,128)(2,1)S(1)} %collective-permute-done.15.refs_7_.refs_14_), channel_id=1, source_target_pairs={{0,1},{1,0},{2,3},{3,2},{4,5},{5,4},{6,7},{7,6},{8,9},{9,8},{10,11... | collective-permute-start | bytes 884744 | tf_op jit(solution)/shard_map/ppermute | solution.py:1041
  45.5 5.6 %collective-permute-start.18 = (bf16[512,128]{1,0:T(8,128)(2,1)S(1)}, bf16[512,128]{1,0:T(8,128)(2,1)S(1)}, u32[]{:S(2)}, u32[]{:S(2)}) collective-permute-start(bf16[512,128]{1,0:T(8,128)(2,1)S(1)} %get-tuple-element.151.refs_3_.refs_4_), channel_id=1, source_target_pairs={{0,2},{1,3},{2,0},{3,1},{4,6},{5,7},{6,4},{7,5},{8,10},{9,11},{10,... | collective-permute-start | bytes 393224 | tf_op jit(solution)/shard_map/ppermute | solution.py:1041
  47.1 4.0 %collective-permute-start.19 = (bf16[512,128]{1,0:T(8,128)(2,1)S(1)}, bf16[512,128]{1,0:T(8,128)(2,1)S(1)}, u32[]{:S(2)}, u32[]{:S(2)}) collective-permute-start(bf16[512,128]{1,0:T(8,128)(2,1)S(1)} %get-tuple-element.151.refs_3_.refs_4_), channel_id=1, source_target_pairs={{0,1},{1,0},{2,3},{3,2},{4,5},{5,4},{6,7},{7,6},{8,9},{9,8},{10,11... | collective-permute-start | bytes 393224 | tf_op jit(solution)/shard_map/ppermute | solution.py:1041
  47.1 4.0 %collective-permute-start.21 = (bf16[256,512]{1,0:T(8,128)(2,1)S(1)}, bf16[256,512]{1,0:T(8,128)(2,1)S(1)}, u32[]{:S(2)}, u32[]{:S(2)}) collective-permute-start(bf16[256,512]{1,0:T(8,128)(2,1)S(1)} %get-tuple-element.158.refs_7_), channel_id=1, source_target_pairs={{0,1},{1,0},{2,3},{3,2},{4,5},{5,4},{6,7},{7,6},{8,9},{9,8},{10,11... | collective-permute-start | bytes 786440 | tf_op jit(solution)/shard_map/ppermute | solution.py:1041
  56.7 2.7 %collective-permute-start.22 = (f32[512,512]{1,0:T(8,128)S(1)}, f32[512,512]{1,0:T(8,128)S(1)}, u32[]{:S(2)}, u32[]{:S(2)}) collective-permute-start(f32[512,512]{1,0:T(8,128)S(1)} %get-tuple-element.166.refs_1_), channel_id=1, source_target_pairs={{0,1},{1,0},{2,3},{3,2},{4,5},{5,4},{6,7},{7,6},{8,9},{9,8},{10,11... | collective-permute-start | bytes 3145736 | tf_op jit(solution)/shard_map/ppermute | solution.py:1041
  61.2 7.7 %collective-permute-start.27 = (bf16[768,128]{1,0:T(8,128)(2,1)S(1)}, bf16[768,128]{1,0:T(8,128)(2,1)S(1)}, u32[]{:S(2)}, u32[]{:S(2)}) collective-permute-start(bf16[768,128]{1,0:T(8,128)(2,1)S(1)} %get-tuple-element.177), channel_id=1, source_target_pairs={{0,4},{1,9},{2,6},{3,11},{8,0},{9,17},{10,2},{11,19},{16,8},{17,25... | collective-permute-start | bytes 589832 | tf_op jit(solution)/shard_map/ppermute | solution.py:1032
  62.8 7.5 %collective-permute-start.23 = (bf16[832,128]{1,0:T(8,128)(2,1)S(1)}, bf16[832,128]{1,0:T(8,128)(2,1)S(1)}, u32[]{:S(2)}, u32[]{:S(2)}) collective-permute-start(bf16[832,128]{1,0:T(8,128)(2,1)S(1)} %get-tuple-element.173), channel_id=1, source_target_pairs={{0,8},{1,5},{2,10},{3,7},{8,16},{9,1},{10,18},{11,3},{16,24},{17,9... | collective-permute-start | bytes 638984 | tf_op jit(solution)/shard_map/ppermute | solution.py:1032
  69.0 8.7 %collective-permute-start.28 = (bf16[1088,128]{1,0:T(8,128)(2,1)S(1)}, bf16[1088,128]{1,0:T(8,128)(2,1)S(1)}, u32[]{:S(2)}, u32[]{:S(2)}) collective-permute-start(bf16[1088,128]{1,0:T(8,128)(2,1)S(1)} %relay.9), channel_id=1, source_target_pairs={{0,4},{1,9},{2,6},{3,11},{8,0},{9,17},{10,2},{11,19},{16,8},{17,25... | collective-permute-start | bytes 835592 | tf_op jit(solution)/shard_map/ppermute | solution.py:1032
  70.4 8.5 %collective-permute-start.24 = (bf16[1088,128]{1,0:T(8,128)(2,1)S(1)}, bf16[1088,128]{1,0:T(8,128)(2,1)S(1)}, u32[]{:S(2)}, u32[]{:S(2)}) collective-permute-start(bf16[1088,128]{1,0:T(8,128)(2,1)S(1)} %relay.6), channel_id=1, source_target_pairs={{0,8},{1,5},{2,10},{3,7},{8,16},{9,1},{10,18},{11,3},{16,24},{17,9... | collective-permute-start | bytes 835592 | tf_op jit(solution)/shard_map/ppermute | solution.py:1032
  71.2 12.6 %collective-permute-start.30 = (bf16[512,512]{1,0:T(8,128)(2,1)S(1)}, bf16[512,512]{1,0:T(8,128)(2,1)S(1)}, u32[]{:S(2)}, u32[]{:S(2)}) collective-permute-start(bf16[512,512]{1,0:T(8,128)(2,1)S(1)} %get-tuple-element.184.refs_4_.refs_9_.refs_3_.refs_2_), channel_id=1, source_target_pairs={{0,2},{1,3},{2,0},{3,1},{4,6},{5,7},{6,4},{7,5},{8,10},{9,11},{10,... | collective-permute-start | bytes 1572872 | tf_op jit(solution)/shard_map/ppermute | solution.py:1041
  77.8 7.9 %collective-permute-start.29 = (bf16[1088,128]{1,0:T(8,128)(2,1)S(1)}, bf16[1088,128]{1,0:T(8,128)(2,1)S(1)}, u32[]{:S(2)}, u32[]{:S(2)}) collective-permute-start(bf16[1088,128]{1,0:T(8,128)(2,1)S(1)} %relay.10), channel_id=1, source_target_pairs={{0,4},{1,9},{2,6},{3,11},{8,0},{9,17},{10,2},{11,19},{16,8},{17,25... | collective-permute-start | bytes 835592 | tf_op jit(solution)/shard_map/ppermute | solution.py:1032
  78.9 7.8 %collective-permute-start.25 = (bf16[1088,128]{1,0:T(8,128)(2,1)S(1)}, bf16[1088,128]{1,0:T(8,128)(2,1)S(1)}, u32[]{:S(2)}, u32[]{:S(2)}) collective-permute-start(bf16[1088,128]{1,0:T(8,128)(2,1)S(1)} %relay.7), channel_id=1, source_target_pairs={{0,8},{1,5},{2,10},{3,7},{8,16},{9,1},{10,18},{11,3},{16,24},{17,9... | collective-permute-start | bytes 835592 | tf_op jit(solution)/shard_map/ppermute | solution.py:1032
  85.7 5.9 %collective-permute-start.31 = (bf16[832,128]{1,0:T(8,128)(2,1)S(1)}, bf16[832,128]{1,0:T(8,128)(2,1)S(1)}, u32[]{:S(2)}, u32[]{:S(2)}) collective-permute-start(bf16[832,128]{1,0:T(8,128)(2,1)S(1)} %relay.11), channel_id=1, source_target_pairs={{0,4},{1,9},{2,6},{3,11},{8,0},{9,17},{10,2},{11,19},{16,8},{17,25... | collective-permute-start | bytes 638984 | tf_op jit(solution)/shard_map/ppermute | solution.py:1032
  86.7 6.9 %collective-permute-start.26 = (bf16[832,128]{1,0:T(8,128)(2,1)S(1)}, bf16[832,128]{1,0:T(8,128)(2,1)S(1)}, u32[]{:S(2)}, u32[]{:S(2)}) collective-permute-start(bf16[832,128]{1,0:T(8,128)(2,1)S(1)} %relay.8), channel_id=1, source_target_pairs={{0,8},{1,5},{2,10},{3,7},{8,16},{9,1},{10,18},{11,3},{16,24},{17,9... | collective-permute-start | bytes 638984 | tf_op jit(solution)/shard_map/ppermute | solution.py:1032
  93.7 8.1 %collective-permute-start.32 = (bf16[144,512]{1,0:T(8,128)(2,1)S(1)}, bf16[144,512]{1,0:T(8,128)(2,1)S(1)}, u32[]{:S(2)}, u32[]{:S(2)}) collective-permute-start(bf16[144,512]{1,0:T(8,128)(2,1)S(1)} %total.1.refs_0_), channel_id=1, source_target_pairs={{0,8},{1,5},{2,10},{3,7},{8,16},{9,1},{10,18},{11,3},{16,24},{17,9... | collective-permute-start | bytes 442376 | tf_op jit(solution)/shard_map/ppermute | solution.py:1032
  94.2 7.5 %collective-permute-start.33 = (bf16[144,512]{1,0:T(8,128)(2,1)S(1)}, bf16[144,512]{1,0:T(8,128)(2,1)S(1)}, u32[]{:S(2)}, u32[]{:S(2)}) collective-permute-start(bf16[144,512]{1,0:T(8,128)(2,1)S(1)} %total.1.refs_0_), channel_id=1, source_target_pairs={{0,4},{1,9},{2,6},{3,11},{8,0},{9,17},{10,2},{11,19},{16,8},{17,25... | collective-permute-start | bytes 442376 | tf_op jit(solution)/shard_map/ppermute | solution.py:1032
  101.8 9.0 %collective-permute-start.39 = (bf16[512,384]{1,0:T(8,128)(2,1)S(1)}, bf16[512,384]{1,0:T(8,128)(2,1)S(1)}, u32[]{:S(2)}, u32[]{:S(2)}) collective-permute-start(bf16[512,384]{1,0:T(8,128)(2,1)S(1)} %get-tuple-element.205.refs_1_.refs_0_), channel_id=1, source_target_pairs={{0,2},{1,3},{2,0},{3,1},{4,6},{5,7},{6,4},{7,5},{8,10},{9,11},{10,... | collective-permute-start | bytes 1179656 | tf_op jit(solution)/shard_map/ppermute | solution.py:1041
  103.4 7.3 %collective-permute-start.35 = (bf16[144,512]{1,0:T(8,128)(2,1)S(1)}, bf16[144,512]{1,0:T(8,128)(2,1)S(1)}, u32[]{:S(2)}, u32[]{:S(2)}) collective-permute-start(bf16[144,512]{1,0:T(8,128)(2,1)S(1)} %collective-permute-done.32.refs_1_), channel_id=1, source_target_pairs={{0,8},{1,5},{2,10},{3,7},{8,16},{9,1},{10,18},{11,3},{16,24},{17,9... | collective-permute-start | bytes 442376 | tf_op jit(solution)/shard_map/ppermute | solution.py:1032
  103.9 6.9 %collective-permute-start.36 = (bf16[144,512]{1,0:T(8,128)(2,1)S(1)}, bf16[144,512]{1,0:T(8,128)(2,1)S(1)}, u32[]{:S(2)}, u32[]{:S(2)}) collective-permute-start(bf16[144,512]{1,0:T(8,128)(2,1)S(1)} %collective-permute-done.33.refs_2_), channel_id=1, source_target_pairs={{0,4},{1,9},{2,6},{3,11},{8,0},{9,17},{10,2},{11,19},{16,8},{17,25... | collective-permute-start | bytes 442376 | tf_op jit(solution)/shard_map/ppermute | solution.py:1032
  106.1 4.0 %collective-permute-start.37 = (f32[16,512]{1,0:T(8,128)S(1)}, f32[16,512]{1,0:T(8,128)S(1)}, u32[]{:S(2)}, u32[]{:S(2)}) collective-permute-start(f32[16,512]{1,0:T(8,128)S(1)} %gain_part.1.refs_0_), channel_id=1, source_target_pairs={{0,4},{4,0},{8,12},{12,8},{16,20},{20,16},{24,28},{28,24},{1,5},{5... | collective-permute-start | bytes 98312 | tf_op jit(solution)/shard_map/ppermute | solution.py:1044
  107.2 3.6 %collective-permute-start.38 = (f32[8,128]{1,0:T(8,128)S(1)}, f32[8,128]{1,0:T(8,128)S(1)}, u32[]{:S(2)}, u32[]{:S(2)}) collective-permute-start(f32[8,128]{1,0:T(8,128)S(1)} %get-tuple-element.209.refs_2_.refs_4_), channel_id=1, source_target_pairs={{0,2},{1,3},{2,0},{3,1},{4,6},{5,7},{6,4},{7,5},{8,10},{9,11},{10,... | collective-permute-start | bytes 12296 | tf_op jit(solution)/shard_map/ppermute | solution.py:1041
  111.8 11.0 %collective-permute-start.44 = (f32[512,512]{1,0:T(8,128)S(1)}, f32[512,512]{1,0:T(8,128)S(1)}, u32[]{:S(2)}, u32[]{:S(2)}) collective-permute-start(f32[512,512]{1,0:T(8,128)S(1)} %input_back.1.refs_2_), channel_id=1, source_target_pairs={{0,1},{1,0},{2,3},{3,2},{4,5},{5,4},{6,7},{7,6},{8,9},{9,8},{10,11... | collective-permute-start | bytes 3145736 | tf_op jit(solution)/shard_map/ppermute | solution.py:1041
  111.9 11.4 %collective-permute-start.34 = (f32[512,512]{1,0:T(8,128)S(1)}, f32[512,512]{1,0:T(8,128)S(1)}, u32[]{:S(2)}, u32[]{:S(2)}) collective-permute-start(f32[512,512]{1,0:T(8,128)S(1)} %get-tuple-element.206.refs_0_), channel_id=1, source_target_pairs={{0,1},{1,0},{2,3},{3,2},{4,5},{5,4},{6,7},{7,6},{8,9},{9,8},{10,11... | collective-permute-start | bytes 3145736 | tf_op jit(solution)/shard_map/ppermute | solution.py:1041
  112.4 4.3 %collective-permute-start.42 = (f32[16,512]{1,0:T(8,128)S(1)}, f32[16,512]{1,0:T(8,128)S(1)}, u32[]{:S(2)}, u32[]{:S(2)}) collective-permute-start(f32[16,512]{1,0:T(8,128)S(1)} %add_gains.4.refs_0_), channel_id=1, source_target_pairs={{0,8},{4,12},{8,0},{12,4},{16,24},{20,28},{24,16},{28,20},{1,9},{5... | collective-permute-start | bytes 98312 | tf_op jit(solution)/shard_map/ppermute | solution.py:1044
  113.5 9.2 %collective-permute-start.40 = (bf16[144,512]{1,0:T(8,128)(2,1)S(1)}, bf16[144,512]{1,0:T(8,128)(2,1)S(1)}, u32[]{:S(2)}, u32[]{:S(2)}) collective-permute-start(bf16[144,512]{1,0:T(8,128)(2,1)S(1)} %collective-permute-done.35.refs_3_), channel_id=1, source_target_pairs={{0,8},{1,5},{2,10},{3,7},{8,16},{9,1},{10,18},{11,3},{16,24},{17,9... | collective-permute-start | bytes 442376 | tf_op jit(solution)/shard_map/ppermute | solution.py:1032
  114.4 8.3 %collective-permute-start.41 = (bf16[144,512]{1,0:T(8,128)(2,1)S(1)}, bf16[144,512]{1,0:T(8,128)(2,1)S(1)}, u32[]{:S(2)}, u32[]{:S(2)}) collective-permute-start(bf16[144,512]{1,0:T(8,128)(2,1)S(1)} %collective-permute-done.36.refs_4_), channel_id=1, source_target_pairs={{0,4},{1,9},{2,6},{3,11},{8,0},{9,17},{10,2},{11,19},{16,8},{17,25... | collective-permute-start | bytes 442376 | tf_op jit(solution)/shard_map/ppermute | solution.py:1032
  116.6 6.1 %collective-permute-start.43 = (f32[16,512]{1,0:T(8,128)S(1)}, f32[16,512]{1,0:T(8,128)S(1)}, u32[]{:S(2)}, u32[]{:S(2)}) collective-permute-start(f32[16,512]{1,0:T(8,128)S(1)} %add_gains.5.refs_0_), channel_id=1, source_target_pairs={{0,16},{4,20},{8,24},{12,28},{16,0},{20,4},{24,8},{28,12},{1,17},{... | collective-permute-start | bytes 98312 | tf_op jit(solution)/shard_map/ppermute | solution.py:1044
  122.8 4.0 %collective-permute-start.47 = (f32[16,512]{1,0:T(8,128)S(1)}, f32[16,512]{1,0:T(8,128)S(1)}, u32[]{:S(2)}, u32[]{:S(2)}) collective-permute-start(f32[16,512]{1,0:T(8,128)S(1)} %add_gains.6.refs_0_), channel_id=1, source_target_pairs={{0,2},{1,3},{2,0},{3,1},{4,6},{5,7},{6,4},{7,5},{8,10},{9,11},{10,... | collective-permute-start | bytes 98312 | tf_op jit(solution)/shard_map/ppermute | solution.py:1041
  124.4 5.1 %collective-permute-start.45 = (bf16[80,512]{1,0:T(8,128)(2,1)S(1)}, bf16[80,512]{1,0:T(8,128)(2,1)S(1)}, u32[]{:S(2)}, u32[]{:S(2)}) collective-permute-start(bf16[80,512]{1,0:T(8,128)(2,1)S(1)} %get-tuple-element.222), channel_id=1, source_target_pairs={{0,8},{1,5},{2,10},{3,7},{8,16},{9,1},{10,18},{11,3},{16,24},{17,9... | collective-permute-start | bytes 245768 | tf_op jit(solution)/shard_map/ppermute | solution.py:1032
  125.3 4.3 %collective-permute-start.46 = (bf16[64,512]{1,0:T(8,128)(2,1)S(1)}, bf16[64,512]{1,0:T(8,128)(2,1)S(1)}, u32[]{:S(2)}, u32[]{:S(2)}) collective-permute-start(bf16[64,512]{1,0:T(8,128)(2,1)S(1)} %get-tuple-element.223), channel_id=1, source_target_pairs={{0,4},{1,9},{2,6},{3,11},{8,0},{9,17},{10,2},{11,19},{16,8},{17,25... | collective-permute-start | bytes 196616 | tf_op jit(solution)/shard_map/ppermute | solution.py:1032
  126.7 2.8 %collective-permute-start.48 = (f32[16,512]{1,0:T(8,128)S(1)}, f32[16,512]{1,0:T(8,128)S(1)}, u32[]{:S(2)}, u32[]{:S(2)}) collective-permute-start(f32[16,512]{1,0:T(8,128)S(1)} %add_gains.7.refs_9_), channel_id=1, source_target_pairs={{0,1},{1,0},{2,3},{3,2},{4,5},{5,4},{6,7},{7,6},{8,9},{9,8},{10,11... | collective-permute-start | bytes 98312 | tf_op jit(solution)/shard_map/ppermute | solution.py:1041
  (18 other events, 121.2 us)
